TPU v7x, 32 devices: a whole 2x2x4 slice. The times are simulated.
32 devices in a mesh: dp: 8 (over y, x, core), mp: 4 (over z).
Axes of the slice: x: 2, y: 2, z: 4, core: 2. Of those that a mesh axis runs over, the one named last changes fastest.
Arguments:
- tokens: bfloat16 [8192, 2048], P(('dp', 'mp')), may hold values from -6 to 6
- norm_gain: bfloat16 [2048], replicated, may hold values from 0.5 to 1.5
- norm_bias: bfloat16 [2048], replicated, may hold values from -4 to 4
- qkv_weight: bfloat16 [3, 2048, 2048], P(None, 'dp', 'mp'), may hold values from -0.125 to 0.125
- qkv_bias: bfloat16 [3, 2048], P(None, 'mp'), may hold values from -4 to 4
- dense_weight: bfloat16 [2048, 2048], P('mp', 'dp'), may hold values from -0.5 to 0.5
- dense_bias: bfloat16 [2048], replicated, may hold values from -4 to 4
- up_weight: bfloat16 [2048, 8192], P('dp', 'mp'), may hold values from -0.125 to 0.125
- up_bias: bfloat16 [8192], P('mp'), may hold values from -6 to 6
- down_weight: bfloat16 [8192, 2048], P('mp', 'dp'), may hold values from -0.0625 to 0.0625
- down_bias: bfloat16 [2048], replicated, may hold values from -4 to 4
- cotangent: bfloat16 [8192, 2048], P(('dp', 'mp')), may hold values from -6 to 6
Outputs:
- output: bfloat16 [8192, 2048], P(('dp', 'mp'))
- grad_tokens: bfloat16 [8192, 2048], P(('dp', 'mp'))
- grad_norm_gain: float32 [2048], replicated
- grad_norm_bias: float32 [2048], replicated
- grad_qkv_weight: float32 [3, 2048, 2048], P(None, 'dp', 'mp')
- grad_qkv_bias: float32 [3, 2048], P(None, 'mp')
- grad_dense_weight: float32 [2048, 2048], P('mp', 'dp')
- grad_dense_bias: float32 [2048], replicated
- grad_up_weight: float32 [2048, 8192], P('dp', 'mp')
- grad_up_bias: float32 [8192], P('mp')
- grad_down_weight: float32 [8192, 2048], P('mp', 'dp')
- grad_down_bias: float32 [2048], replicated
All inputs are finite; a program needn't handle non-finite values.
Results may differ from a plain program's by a relative error of at most 0.013.
Values may be sent and summed in bfloat16 or wider, within the bound.
No kernel may reach another device: no remote copies, remote signals or barrier semaphores. Data moves between devices by JAX's collectives and lax.ppermute only.
A program may use at most 192 MiB of HBM per device.

v0:
```python
import jax
import jax.numpy as jnp
from jax import lax
from jax.sharding import PartitionSpec as P

HEAD_DIM = 64
ROT = 32
BLOCK = 512


EPS = 1e-05


def rotary_tables(length):
    positions = jnp.arange(length).astype(jnp.float32)
    frequency = 10000.0 ** (-jnp.arange(ROT // 2).astype(jnp.float32) * 2.0 / ROT)
    angles = positions[:, None] * frequency[None, :]
    angles = jnp.concatenate([angles, angles], axis=1)
    return (jnp.cos(angles), jnp.sin(angles))


def rotate(tensor, cosine_table, sine_table):
    leading = tensor[..., :ROT]
    turned = jnp.concatenate([-leading[..., ROT // 2 :], leading[..., : ROT // 2]], axis=-1)
    rotated = leading * cosine_table + turned * sine_table
    return jnp.concatenate([rotated, tensor[..., ROT:]], axis=-1)


def rotate_back(gradient, cosine_table, sine_table):
    leading = gradient[..., :ROT]
    product = leading * sine_table
    turned = jnp.concatenate([product[..., ROT // 2 :], -product[..., : ROT // 2]], axis=-1)
    return jnp.concatenate([leading * cosine_table + turned, gradient[..., ROT:]], axis=-1)


def masked_scores(block_query, keys, start, scale):
    length = keys.shape[1]
    rows_here = block_query.shape[1]
    row_index = start + jnp.arange(rows_here)
    columns = jnp.arange(length)
    scores = (
        jnp.einsum("hqd,hkd->hqk", block_query, keys, preferred_element_type=jnp.float32) * scale
    )
    return jnp.where(columns[None, None, :] <= row_index[None, :, None], scores, -1e30)


def attend_forward(query, keys, values):
    heads, length, width = query.shape
    count = length // BLOCK
    scale = width ** (-0.5)

    def one_block(block_index):
        start = block_index * BLOCK
        block_query = lax.dynamic_slice_in_dim(query, start, BLOCK, 1)
        masked = masked_scores(block_query, keys, start, scale)
        highest = jnp.max(masked, axis=-1)
        expon = jnp.exp(masked - highest[..., None])
        totals = jnp.sum(expon, axis=-1)
        weights = (expon / totals[..., None]).astype(jnp.bfloat16)
        result = jnp.einsum(
            "hqk,hkd->hqd", weights, values, preferred_element_type=jnp.float32
        ).astype(jnp.bfloat16)
        return (result, highest + jnp.log(totals))

    results, logsum = lax.map(one_block, jnp.arange(count))
    mixed = results.transpose(1, 0, 2, 3).reshape(heads, length, width)
    return (mixed, logsum.transpose(1, 0, 2).reshape(heads, length))


def attend_backward(query, keys, values, logsum, grad_mixed):
    heads, length, width = query.shape
    count = length // BLOCK
    scale = width ** (-0.5)

    def one_block(carry, block_index):
        grad_keys, grad_values = carry
        start = block_index * BLOCK
        block_query = lax.dynamic_slice_in_dim(query, start, BLOCK, 1)
        block_grad = lax.dynamic_slice_in_dim(grad_mixed, start, BLOCK, 1)
        block_logsum = lax.dynamic_slice_in_dim(logsum, start, BLOCK, 1)
        masked = masked_scores(block_query, keys, start, scale)
        probs = jnp.exp(masked - block_logsum[..., None])
        grad_values = grad_values + jnp.einsum(
            "hqk,hqd->hkd",
            probs.astype(jnp.bfloat16),
            block_grad,
            preferred_element_type=jnp.float32,
        )
        grad_probs = jnp.einsum(
            "hqd,hkd->hqk", block_grad, values, preferred_element_type=jnp.float32
        )
        row_delta = jnp.sum(grad_probs * probs, axis=-1, keepdims=True)
        grad_scores = (probs * (grad_probs - row_delta)).astype(jnp.bfloat16)
        grad_query = (
            jnp.einsum("hqk,hkd->hqd", grad_scores, keys, preferred_element_type=jnp.float32)
            * scale
        )
        grad_keys = (
            grad_keys
            + jnp.einsum(
                "hqk,hqd->hkd", grad_scores, block_query, preferred_element_type=jnp.float32
            )
            * scale
        )
        return ((grad_keys, grad_values), grad_query)

    zeros = jnp.zeros((heads, length, width), jnp.float32)
    (grad_keys, grad_values), grad_query = lax.scan(one_block, (zeros, zeros), jnp.arange(count))
    grad_query = grad_query.transpose(1, 0, 2, 3).reshape(heads, length, width)
    return (grad_query, grad_keys, grad_values)


def gelu_tanh(values_in):
    return jax.nn.gelu(values_in, approximate=True)


def on_device(
    tokens,
    norm_gain,
    norm_bias,
    qkv_weight,
    qkv_bias,
    dense_weight,
    dense_bias,
    up_weight,
    up_bias,
    down_weight,
    down_bias,
    cotangent,
):
    local_inputs = tokens.astype(jnp.float32)
    row_mean = jnp.mean(local_inputs, axis=1, keepdims=True)
    centered = local_inputs - row_mean
    row_var = jnp.mean(centered * centered, axis=1, keepdims=True)
    inverse_std = lax.rsqrt(row_var + EPS)
    normal_rows = centered * inverse_std
    gain_values = norm_gain.astype(jnp.float32)
    normed = (normal_rows * gain_values + norm_bias.astype(jnp.float32)).astype(jnp.bfloat16)
    seq_rows = lax.all_gather(normed, "mp", axis=0, tiled=True)
    length = seq_rows.shape[0]
    full_qkv, full_dense, full_up, full_down = (
        lax.all_gather(qkv_weight, "dp", axis=1, tiled=True),
        lax.all_gather(dense_weight, "dp", axis=1, tiled=True),
        lax.all_gather(up_weight, "dp", axis=0, tiled=True),
        lax.all_gather(down_weight, "dp", axis=1, tiled=True),
    )
    proj = (
        jnp.einsum("td,cde->cte", seq_rows, full_qkv, preferred_element_type=jnp.float32)
        + qkv_bias.astype(jnp.float32)[:, None, :]
    )
    local_width = proj.shape[2]
    local_heads = local_width // HEAD_DIM
    split = proj.reshape(3, length, local_heads, HEAD_DIM).transpose(0, 2, 1, 3)
    cosine_table, sine_table = rotary_tables(length)
    query = rotate(split[0], cosine_table, sine_table).astype(jnp.bfloat16)
    keys = rotate(split[1], cosine_table, sine_table).astype(jnp.bfloat16)
    values = split[2].astype(jnp.bfloat16)
    mixed_heads, logsum = attend_forward(query, keys, values)
    mixed_rows = mixed_heads.transpose(1, 0, 2).reshape(length, local_width)
    pre_act = jnp.dot(seq_rows, full_up, preferred_element_type=jnp.float32) + up_bias.astype(
        jnp.float32
    )
    act_float, gelu_pull = jax.vjp(gelu_tanh, pre_act)
    activ = act_float.astype(jnp.bfloat16)
    partial_sum = jnp.dot(mixed_rows, full_dense, preferred_element_type=jnp.float32) + jnp.dot(
        activ, full_down, preferred_element_type=jnp.float32
    )
    summed = lax.psum_scatter(
        partial_sum.astype(jnp.bfloat16), "mp", scatter_dimension=0, tiled=True
    ).astype(jnp.float32)
    output = (
        local_inputs + summed + dense_bias.astype(jnp.float32) + down_bias.astype(jnp.float32)
    ).astype(jnp.bfloat16)
    grad_rows = lax.all_gather(cotangent, "mp", axis=0, tiled=True)
    back_qkv, back_dense, back_up, back_down = (
        lax.all_gather(qkv_weight, "dp", axis=1, tiled=True),
        lax.all_gather(dense_weight, "dp", axis=1, tiled=True),
        lax.all_gather(up_weight, "dp", axis=0, tiled=True),
        lax.all_gather(down_weight, "dp", axis=1, tiled=True),
    )
    grad_dense = jnp.einsum("tf,td->fd", mixed_rows, grad_rows, preferred_element_type=jnp.float32)
    grad_down = jnp.einsum("tf,td->fd", activ, grad_rows, preferred_element_type=jnp.float32)
    grad_mixed = jnp.einsum(
        "td,fd->tf", grad_rows, back_dense, preferred_element_type=jnp.float32
    ).astype(jnp.bfloat16)
    grad_act = jnp.einsum("td,fd->tf", grad_rows, back_down, preferred_element_type=jnp.float32)
    grad_pre = gelu_pull(grad_act)[0].astype(jnp.bfloat16)
    grad_up = jnp.einsum("td,tf->df", seq_rows, grad_pre, preferred_element_type=jnp.float32)
    grad_heads = grad_mixed.reshape(length, local_heads, HEAD_DIM).transpose(1, 0, 2)
    grad_query, grad_keys, grad_values = attend_backward(query, keys, values, logsum, grad_heads)
    grad_split = jnp.stack(
        [
            rotate_back(grad_query, cosine_table, sine_table),
            rotate_back(grad_keys, cosine_table, sine_table),
            grad_values,
        ]
    )
    grad_proj = (
        grad_split.transpose(0, 2, 1, 3).reshape(3, length, local_width).astype(jnp.bfloat16)
    )
    grad_qkv = jnp.einsum("td,cte->cde", seq_rows, grad_proj, preferred_element_type=jnp.float32)
    grad_normed = jnp.einsum(
        "cte,cde->td", grad_proj, back_qkv, preferred_element_type=jnp.float32
    ) + jnp.einsum("tf,df->td", grad_pre, back_up, preferred_element_type=jnp.float32)
    grad_local = lax.psum_scatter(
        grad_normed.astype(jnp.bfloat16), "mp", scatter_dimension=0, tiled=True
    ).astype(jnp.float32)
    scaled_grad = grad_local * gain_values
    first_mean = jnp.mean(scaled_grad, axis=1, keepdims=True)
    second_mean = jnp.mean(scaled_grad * normal_rows, axis=1, keepdims=True)
    local_cot = cotangent.astype(jnp.float32)
    grad_tokens = (
        local_cot + (scaled_grad - first_mean - normal_rows * second_mean) * inverse_std
    ).astype(jnp.bfloat16)
    grad_gain, grad_shift, grad_out_bias = lax.psum(
        (
            jnp.sum(grad_local * normal_rows, axis=0),
            jnp.sum(grad_local, axis=0),
            jnp.sum(local_cot, axis=0),
        ),
        ("dp", "mp"),
    )
    grad_qkv_bias, grad_up_bias = lax.psum(
        (
            jnp.sum(grad_proj.astype(jnp.float32), axis=1),
            jnp.sum(grad_pre.astype(jnp.float32), axis=0),
        ),
        "dp",
    )
    owned_qkv, owned_dense, owned_up, owned_down = (
        lax.psum_scatter(
            grad_qkv.astype(jnp.bfloat16), "dp", scatter_dimension=1, tiled=True
        ).astype(jnp.float32),
        lax.psum_scatter(
            grad_dense.astype(jnp.bfloat16), "dp", scatter_dimension=1, tiled=True
        ).astype(jnp.float32),
        lax.psum_scatter(
            grad_up.astype(jnp.bfloat16), "dp", scatter_dimension=0, tiled=True
        ).astype(jnp.float32),
        lax.psum_scatter(
            grad_down.astype(jnp.bfloat16), "dp", scatter_dimension=1, tiled=True
        ).astype(jnp.float32),
    )
    return (
        output,
        grad_tokens,
        grad_gain,
        grad_shift,
        owned_qkv,
        grad_qkv_bias,
        owned_dense,
        grad_out_bias,
        owned_up,
        grad_up_bias,
        owned_down,
        grad_out_bias,
    )


def solution(mesh):
    return jax.shard_map(
        on_device,
        mesh=mesh,
        in_specs=(
            P(("dp", "mp"), None),
            P(),
            P(),
            P(None, "dp", "mp"),
            P(None, "mp"),
            P("mp", "dp"),
            P(),
            P("dp", "mp"),
            P("mp"),
            P("mp", "dp"),
            P(),
            P(("dp", "mp"), None),
        ),
        out_specs=(
            P(("dp", "mp"), None),
            P(("dp", "mp"), None),
            P(),
            P(),
            P(None, "dp", "mp"),
            P(None, "mp"),
            P("mp", "dp"),
            P(),
            P("dp", "mp"),
            P("mp"),
            P("mp", "dp"),
            P(),
        ),
        check_vma=False,
    )
```

profile of v0, /device:TPU:0, one launch (start us, length us, event | category | flops | bytes accessed | tf_op | source)
XLA Modules:
  0.0 806.1 jit_solution(12715615152622769470)
XLA Ops:
  8.0 0.7 all-gather.17.cloned.1.call-update
  9.4 0.7 convert_element_type.138
  10.1 1.4 convert_reduce_fusion.3
  11.6 1.6 fusion.50
  13.8 2.7 fusion.47
  16.6 1.2 copy.29
  19.4 21.4 %all-gather.11.cloned.1.call-done = bf16[512,2048]{1,0:T(8,128)(2,1)} async-done(((bf16[512,256]{1,0:T(8,128)(2,1)}), bf16[512,2048]{1,0:T(8,128)(2,1)}) %all-gather.11.cloned.1.call-update) | async-done | bytes 2097168 | tf_op jit(solution)/shard_map/all_gather | solution.py:143
  40.8 82.4 %all-gather.17.cloned.1.call-done = bf16[1024,2048]{1,0:T(8,128)(2,1)} async-done(((bf16[256,2048]{1,0:T(8,128)(2,1)}), bf16[1024,2048]{1,0:T(8,128)(2,1)}) %all-gather.17.cloned.1.call-update) | async-done | bytes 4194320 | tf_op jit(solution)/shard_map/all_gather | solution.py:174
  123.2 6.2 convolution_convert_fusion.3
  129.4 75.3 %all-gather.7.cloned.1.call-done = bf16[1024,2048]{1,0:T(8,128)(2,1)} async-done(((bf16[256,2048]{1,0:T(8,128)(2,1)}), bf16[1024,2048]{1,0:T(8,128)(2,1)}) %all-gather.7.cloned.1.call-update) | async-done | bytes 4194320 | tf_op jit(solution)/shard_map/all_gather | solution.py:139
  204.7 47.5 %all-gather.9.cloned.1.call-done = bf16[3,2048,512]{1,2,0:T(8,128)(2,1)} async-done(((bf16[3,256,512]{1,2,0:T(8,128)(2,1)}), bf16[3,2048,512]{1,2,0:T(8,128)(2,1)}) %all-gather.9.cloned.1.call-update) | async-done | bytes 6291472 | tf_op jit(solution)/shard_map/all_gather | solution.py:142
  252.2 10.2 %broadcast_add_fusion = f32[1024,3,512]{0,2,1:T(8,128)S(1)} fusion(f32[3,512]{1,0:T(4,128)S(1)} %convert_element_type.140, bf16[3,2048,512]{1,2,0:T(8,128)(2,1)} %all-gather.9.cloned.1.call-done, bf16[1024,2048]{1,0:T(8,128)(2,1)} %all-gather.7.cloned.1.call-done), kind=kOutput, calls=%fused_computation.64 | convolution fusion | flops 6444023808 | bytes 16783360 | tf_op jit(solution)/shard_map/td,cde->cte/dot_general | solution.py:148
  264.1 1.1 pad_maximum_fusion
  265.2 1.1 fusion.57
  266.3 33.0 %while.27 = (s32[]{:T(128)}, bf16[2,8,512,64]{2,3,1,0:T(8,128)(2,1)S(1)}, f32[2,8,512]{2,1,0:T(8,128)}, s32[2]{0:T(128)S(1)}, bf16[8,1024,64]{1,2,0:T(8,128)(2,1...) while((s32[]{:T(128)}, ...), condition=%wide.region_5.6_spmd, body=%wide.region_2.5_spmd.sunk | while | flops 1124856320 | bytes 55710388 | solution.py:65
  268.0 4.1 fusion.114
  272.1 4.2 fusion.115
  277.0 5.9 fusion.116
  284.5 4.1 fusion.114
  288.6 4.2 fusion.115
  293.5 5.9 fusion.116
  299.5 1.1 copy-done.12
  300.6 6.0 convolution_convert_fusion.2
  306.7 101.8 %while.28 = (s32[]{:T(128)}, f32[8,1024,64]{1,2,0:T(8,128)}, f32[8,1024,64]{1,2,0:T(8,128)}, f32[2,8,512,64]{2,3,1,0:T(8,128)}, s32[2]{0:T(128)S(1)}, /*index=5*...) while((s32[]{:T(128)}, f32[8,1024,64]{1,2,0:T(8,128)}, ...), condition=%wide.region_9.10_spmd.clone, body=%wide.region_7.9_spmd.clone.sunk | while | flops 2725507584 | bytes 296833920 | solution.py:108
  308.3 0.7 constant_dynamic-slice_fusion.2
  309.4 5.8 subtract_exponential_fusion.3
  315.2 11.6 %multiply_reduce_fusion.2 = (f32[8,512]{1,0:T(8,128)}, f32[8,512,1024]{2,1,0:T(8,128)}) fusion(f32[8,512,1024]{2,1,0:T(8,128)S(1)} %subtract_exponential_fusion.3, bf16[8,1024,64]{1,2,0:T(8,128)(2,1)} %get-tuple-element.426, bf16[8,1024,64]{1,2,0:T(8,128)(2,1)} %get-tuple-element.425, s32[]{:T(128)S(6)} %select_n.45), kind=kOutput, calls=%fused_computation.18.clone.1 | convolution fusion | flops 545255424 | bytes 35143684 | tf_op jit(solution)/shard_map/while/body/eval_jaxpr/hqd,hkd->hqk/dot_general | solution.py:89
  327.1 9.5 %multiply_convert_fusion.5 = bf16[8,512,1024]{2,1,0:T(8,128)(2,1)} fusion(f32[8,512,1024]{2,1,0:T(8,128)S(1)} %subtract_exponential_fusion.3, f32[8,512,1024]{2,1,0:T(8,128)} %get-tuple-element.354, f32[8,512]{1,0:T(8,128)} %get-tuple-element.355), kind=kLoop, calls=%fused_computation.17.clone.1 | loop fusion | flops 12582912 | bytes 41959424 | tf_op jit(solution)/shard_map/while/body/eval_jaxpr/convert_element_type | solution.py:93
  336.6 8.3 %fusion.126 = f32[2,8,512,64]{2,3,1,0:T(8,128)} fusion(f32[2,8,512,64]{2,3,1,0:T(8,128)} %get-tuple-element.406, s32[]{:T(128)} %get-tuple-element.403, bf16[8,512,1024]{2,1,0:T(8,128)(2,1)} %multiply_convert_fusion.5, bf16[8,1024,64]{1,2,0:T(8,128)(2,1)S(1)} %get-tuple-element.423), kind=kOutput, calls=%fused_computation.27.clone.1 | convolution fusion | flops 537133056 | bytes 10486272 | tf_op jit(solution)/shard_map/while/body/eval_jaxpr/hqk,hkd->hqd/dot_general | solution.py:95
  344.9 5.5 select_add_fusion.4
  350.4 3.8 copy-done.1
  354.4 2.9 select_add_fusion.5
  358.5 0.7 constant_dynamic-slice_fusion.2
  359.6 5.8 subtract_exponential_fusion.3
  365.4 11.7 %multiply_reduce_fusion.2 = (f32[8,512]{1,0:T(8,128)}, f32[8,512,1024]{2,1,0:T(8,128)}) fusion(f32[8,512,1024]{2,1,0:T(8,128)S(1)} %subtract_exponential_fusion.3, bf16[8,1024,64]{1,2,0:T(8,128)(2,1)} %get-tuple-element.426, bf16[8,1024,64]{1,2,0:T(8,128)(2,1)} %get-tuple-element.425, s32[]{:T(128)S(6)} %select_n.45), kind=kOutput, calls=%fused_computation.18.clone.1 | convolution fusion | flops 545255424 | bytes 35143684 | tf_op jit(solution)/shard_map/while/body/eval_jaxpr/hqd,hkd->hqk/dot_general | solution.py:89
  377.2 9.7 %multiply_convert_fusion.5 = bf16[8,512,1024]{2,1,0:T(8,128)(2,1)} fusion(f32[8,512,1024]{2,1,0:T(8,128)S(1)} %subtract_exponential_fusion.3, f32[8,512,1024]{2,1,0:T(8,128)} %get-tuple-element.354, f32[8,512]{1,0:T(8,128)} %get-tuple-element.355), kind=kLoop, calls=%fused_computation.17.clone.1 | loop fusion | flops 12582912 | bytes 41959424 | tf_op jit(solution)/shard_map/while/body/eval_jaxpr/convert_element_type | solution.py:93
  386.9 7.2 fusion.126
  394.2 5.6 select_add_fusion.4
  399.8 3.7 copy-done.1
  403.7 4.7 select_add_fusion.5
  408.4 2.0 copy.38
  411.6 0.7 maximum_add_fusion
  412.6 2.6 convert_reduce_fusion.1
  415.4 8.8 %convert_bitcast_fusion = bf16[3,2048,512]{1,2,0:T(8,128)(2,1)} fusion(bf16[3,1024,512]{1,2,0:T(8,128)(2,1)S(1)} %bitcast.116, bf16[1024,2048]{1,0:T(8,128)(2,1)S(1)} %copy-done.28), kind=kOutput, calls=%fused_computation.57 | convolution fusion | flops 6445596672 | bytes 13631488 | tf_op jit(solution)/shard_map/td,cte->cde/dot_general | solution.py:201
  424.9 14.4 %fusion.68 = f32[1024,2048]{1,0:T(8,128)} fusion(bf16[1024,2048]{1,0:T(8,128)(2,1)} %all-gather.7.cloned.1.call-done, bf16[2048,2048]{1,0:T(8,128)(2,1)} %all-gather.13.cloned.1.call-done), kind=kOutput, calls=%fused_computation.129 | convolution fusion | flops 8589934592 | bytes 20971520 | tf_op jit(solution)/shard_map/dot_general | solution.py:160
  439.3 18.9 %convert_reduce_fusion = (f32[2048]{0:T(1024)S(1)}, bf16[1024,2048]{1,0:T(8,128)(2,1)S(1)}) fusion(f32[1024,2048]{1,0:T(8,128)} %fusion.68, f32[2048]{0:T(1024)S(1)} %convert_element_type.144, bf16[1024,2048]{1,0:T(8,128)(2,1)} %all-gather.17.cloned.1.call-done, bf16[2048,2048]{1,0:T(8,128)(2,1)} %all-gather.15.cloned.1.call-done), kind=kOutput, calls=%fused_computation.50 | convolution fusion | flops 8638167040 | bytes 25182208 | tf_op jit(solution)/shard_map/td,fd->tf/dot_general | solution.py:186
  458.2 11.2 %fusion.69 = f32[1024,2048]{1,0:T(8,128)} fusion(bf16[1024,2048]{1,0:T(8,128)(2,1)S(1)} %get-tuple-element.210, bf16[2048,2048]{1,0:T(8,128)(2,1)S(1)} %copy-done.27), kind=kOutput, calls=%fused_computation.130 | convolution fusion | flops 8589934592 | bytes 20971520 | tf_op jit(solution)/shard_map/tf,df->td/dot_general | solution.py:204
  469.4 12.4 %fusion.33 = bf16[1024,2048]{1,0:T(8,128)(2,1)} fusion(f32[1024,2048]{1,0:T(8,128)} %fusion.69, bf16[3,1024,512]{1,2,0:T(8,128)(2,1)S(1)} %bitcast.117, bf16[3,2048,512]{1,2,0:T(8,128)(2,1)} %all-gather.9.cloned.1.call-done), kind=kOutput, calls=%fused_computation.49 | convolution fusion | flops 6446645248 | bytes 22020096 | tf_op jit(solution)/shard_map/cte,cde->td/dot_general | solution.py:202
  482.0 16.2 %fusion.64 = f32[1024,2048]{1,0:T(8,128)S(1)} fusion(bf16[2048,2048]{1,0:T(8,128)(2,1)} %all-gather.15.cloned.1.call-done, f32[1024,2048]{1,0:T(8,128)} %fusion.68, f32[2048]{0:T(1024)S(1)} %convert_element_type.144), kind=kOutput, calls=%fused_computation.126 | convolution fusion | flops 8610906112 | bytes 25174016 | tf_op jit(solution)/shard_map/dot_general | solution.py:165
  498.2 4.3 add_convert_fusion
  502.6 14.1 %convolution_convert_fusion.1 = bf16[2048,2048]{1,0:T(8,128)(2,1)} fusion(bf16[1024,2048]{1,0:T(8,128)(2,1)} %all-gather.7.cloned.1.call-done, bf16[1024,2048]{1,0:T(8,128)(2,1)} %copy-done.30), kind=kOutput, calls=%fused_computation.54 | convolution fusion | flops 8594128896 | bytes 16777216 | tf_op jit(solution)/shard_map/td,tf->df/dot_general | solution.py:188
  516.8 16.1 %convolution_convert_fusion = bf16[2048,2048]{1,0:T(8,128)(2,1)} fusion(bf16[1024,2048]{1,0:T(8,128)(2,1)} %all-gather.17.cloned.1.call-done, f32[1024,2048]{1,0:T(8,128)} %fusion.68, f32[2048]{0:T(1024)S(1)} %convert_element_type.144), kind=kOutput, calls=%fused_computation.53 | convolution fusion | flops 8615100416 | bytes 20979712 | tf_op jit(solution)/shard_map/tf,td->fd/dot_general | solution.py:182
  533.7 1.9 convert_element_type.165
  535.5 25.8 %all-reduce.1 = (f32[3,512]{1,0:T(4,128)}, f32[2048]{0:T(1024)}) all-reduce(f32[3,512]{1,0:T(4,128)S(1)} %reduce_sum.108, f32[2048]{0:T(1024)S(1)} %get-tuple-element.209), channel_id=1, replica_groups=mesh['dp'=8,'mp'=4] {'dp'}, use_global_device_ids=true, to_apply=%region_19.20 | all-reduce | flops 3584 | bytes 28672 | tf_op jit(solution)/shard_map/psum | solution.py:223
  561.4 2.6 copy.34
  563.9 1.3 reduce-scatter.9.cloned.1.call-done
  565.3 2.3 fusion.56
  567.6 77.2 %reduce-scatter.7.cloned.1.call-done = bf16[256,2048]{1,0:T(8,128)(2,1)} async-done(((bf16[1024,2048]{1,0:T(8,128)(2,1)}), bf16[256,2048]{1,0:T(8,128)(2,1)}) %reduce-scatter.7.cloned.1.call-update) | async-done | bytes 1048592 | tf_op jit(solution)/shard_map/reduce_scatter | solution.py:168
  644.8 4.5 convert_reduce_fusion.4
  649.4 41.2 %all-reduce = (f32[2048]{0:T(1024)}, f32[2048]{0:T(1024)}, f32[2048]{0:T(1024)S(1)}) all-reduce(f32[2048]{0:T(1024)S(1)} %get-tuple-element.166, f32[2048]{0:T(1024)S(1)} %get-tuple-element.169, f32[2048]{0:T(1024)S(1)} %get-tuple-element.227), channel_id=1, replica_groups=mesh['dp'=8,'mp'=4] {'dp','mp'}, use_global_device_ids=true, to_apply=%region_14.15 | all-reduce | flops 6144 | bytes 49152 | tf_op jit(solution)/shard_map/psum | solution.py:215
  690.6 30.1 %reduce-scatter.15.cloned.1.call-done = bf16[256,2048]{1,0:T(8,128)(2,1)} async-done(((bf16[2048,2048]{1,0:T(8,128)(2,1)}), bf16[256,2048]{1,0:T(8,128)(2,1)}) %reduce-scatter.15.cloned.1.call-update) | async-done | bytes 1048592 | tf_op jit(solution)/shard_map/reduce_scatter | solution.py:237
  720.7 2.8 convert_element_type.167
  723.5 72.2 %reduce-scatter.17.cloned.1.call-done = bf16[2048,256]{1,0:T(8,128)(2,1)} async-done(((bf16[2048,2048]{1,0:T(8,128)(2,1)}), bf16[2048,256]{1,0:T(8,128)(2,1)}) %reduce-scatter.17.cloned.1.call-update) | async-done | bytes 1048592 | tf_op jit(solution)/shard_map/reduce_scatter | solution.py:240
  795.7 2.7 convert_element_type.170
  (144 shorter events, 15.1 us)
Async XLA Ops:
  7.2 9.4 %copy-start.14 = (bf16[3,256,512]{2,1,0:T(8,128)(2,1)S(1)}, bf16[3,256,512]{2,1,0:T(8,128)(2,1)}, u32[]{:S(2)}) copy-start(bf16[3,256,512]{2,1,0:T(8,128)(2,1)} %param.19) | copy-start | bytes 2359300
  7.2 33.6 %all-gather.11.cloned.1.call-start = ((), (), s32[]{:S(2)}) async-start(), calls=%async_computation.8 | async-start | bytes 2359296 | tf_op jit(solution)/shard_map/all_gather | solution.py:143
  7.9 115.3 %all-gather.17.cloned.1.call-start = ((), (), s32[]{:S(2)}) async-start(), calls=%async_computation.12 | async-start | bytes 5242880 | tf_op jit(solution)/shard_map/all_gather | solution.py:174
  8.7 196.0 %all-gather.7.cloned.1.call-start = ((), (), s32[]{:S(2)}) async-start(), calls=%async_computation.6 | async-start | bytes 5242880 | tf_op jit(solution)/shard_map/all_gather | solution.py:139
  9.4 3.8 copy-start.15
  11.6 1.7 copy-start.18
  11.6 7.5 copy-start.23
  13.3 0.6 copy-start.20
  16.5 235.7 %all-gather.9.cloned.1.call-start = ((), (), s32[]{:S(2)}) async-start(), calls=%async_computation.7 | async-start | bytes 7077888 | tf_op jit(solution)/shard_map/all_gather | solution.py:142
  17.7 407.1 %all-gather.13.cloned.1.call-start = ((), (), s32[]{:S(2)}) async-start(), calls=%async_computation.9 | async-start | bytes 9437184 | tf_op jit(solution)/shard_map/all_gather | solution.py:144
  18.3 421.0 %all-gather.15.cloned.1.call-start = ((), (), s32[]{:S(2)}) async-start(), calls=%async_computation.10 | async-start | bytes 9437184 | tf_op jit(solution)/shard_map/all_gather | solution.py:145
  18.9 514.8 %reduce-scatter.13.cloned.1.call-start = ((), (), s32[]{:S(2)}) async-start(), calls=%async_computation.15 | async-start | bytes 2359296 | tf_op jit(solution)/shard_map/reduce_scatter | solution.py:234
  19.4 244.1 %copy-start.8 = (f32[1024,32]{0,1:T(8,128)}, f32[1024,32]{0,1:T(8,128)S(1)}, u32[]{:S(2)}) copy-start(f32[1024,32]{0,1:T(8,128)S(1)} %get-tuple-element.240) | copy-start | bytes 393220
  19.4 244.1 %copy-start.10 = (f32[1024,32]{0,1:T(8,128)}, f32[1024,32]{0,1:T(8,128)S(1)}, u32[]{:S(2)}) copy-start(f32[1024,32]{0,1:T(8,128)S(1)} %get-tuple-element.241) | copy-start | bytes 393220
  299.5 1.1 copy-start.12
  306.6 254.8 %reduce-scatter.11.cloned.1.call-start = ((), (), s32[]{:S(2)}) async-start(), calls=%async_computation.14 | async-start | bytes 7077888 | tf_op jit(solution)/shard_map/reduce_scatter | solution.py:231
  315.2 11.9 %copy-start = (f32[8,512,1024]{2,1,0:T(8,128)}, f32[8,512,1024]{2,1,0:T(8,128)S(1)}, u32[]{:S(2)}) copy-start(f32[8,512,1024]{2,1,0:T(8,128)S(1)} %subtract_exponential_fusion.3) | copy-start | bytes 50331652 | tf_op jit(solution)/shard_map/while
  336.6 8.3 %copy-start.2 = (f32[8,1024,64]{1,2,0:T(8,128)S(1)}, f32[8,1024,64]{1,2,0:T(8,128)}, u32[]{:S(2)}) copy-start(f32[8,1024,64]{1,2,0:T(8,128)} %get-tuple-element.404) | copy-start | bytes 6291460 | tf_op jit(solution)/shard_map/while
  344.9 9.2 %copy-start.1 = (f32[8,512,1024]{2,1,0:T(8,128)S(1)}, f32[8,512,1024]{2,1,0:T(8,128)}, u32[]{:S(2)}) copy-start(f32[8,512,1024]{2,1,0:T(8,128)} %copy-done) | copy-start | bytes 50331652 | tf_op jit(solution)/shard_map/while
  344.9 9.5 %copy-start.5 = (bf16[8,1024,64]{1,2,0:T(8,128)(2,1)S(1)}, bf16[8,1024,64]{1,2,0:T(8,128)(2,1)}, u32[]{:S(2)}) copy-start(bf16[8,1024,64]{1,2,0:T(8,128)(2,1)} %get-tuple-element.425) | copy-start | bytes 3145732 | tf_op jit(solution)/shard_map/while
  350.4 6.9 copy-start.3
  365.4 11.8 %copy-start = (f32[8,512,1024]{2,1,0:T(8,128)}, f32[8,512,1024]{2,1,0:T(8,128)S(1)}, u32[]{:S(2)}) copy-start(f32[8,512,1024]{2,1,0:T(8,128)S(1)} %subtract_exponential_fusion.3) | copy-start | bytes 50331652 | tf_op jit(solution)/shard_map/while
  386.9 7.3 copy-start.2
  394.2 9.3 %copy-start.1 = (f32[8,512,1024]{2,1,0:T(8,128)S(1)}, f32[8,512,1024]{2,1,0:T(8,128)}, u32[]{:S(2)}) copy-start(f32[8,512,1024]{2,1,0:T(8,128)} %copy-done) | copy-start | bytes 50331652 | tf_op jit(solution)/shard_map/while
  394.2 9.5 %copy-start.5 = (bf16[8,1024,64]{1,2,0:T(8,128)(2,1)S(1)}, bf16[8,1024,64]{1,2,0:T(8,128)(2,1)}, u32[]{:S(2)}) copy-start(bf16[8,1024,64]{1,2,0:T(8,128)(2,1)} %get-tuple-element.425) | copy-start | bytes 3145732 | tf_op jit(solution)/shard_map/while
  399.8 8.6 %copy-start.3 = (f32[8,1024,64]{1,2,0:T(8,128)}, f32[8,1024,64]{1,2,0:T(8,128)S(1)}, u32[]{:S(2)}) copy-start(f32[8,1024,64]{1,2,0:T(8,128)S(1)} %select_add_fusion.4) | copy-start | bytes 6291460 | tf_op jit(solution)/shard_map/while
  408.4 2.3 copy-start.4
  408.4 2.3 copy-start.11
  410.7 0.9 copy-start.9
  412.5 2.8 copy-start.28
  424.2 0.7 copy-start.24
  424.2 141.1 %reduce-scatter.9.cloned.1.call-start = ((), (), s32[]{:S(2)}) async-start(), calls=%async_computation.13 | async-start | bytes 5242880 | tf_op jit(solution)/shard_map/reduce_scatter | solution.py:205
  439.3 18.9 %copy-start.27 = (bf16[2048,2048]{1,0:T(8,128)(2,1)S(1)}, bf16[2048,2048]{1,0:T(8,128)(2,1)}, u32[]{:S(2)}) copy-start(bf16[2048,2048]{1,0:T(8,128)(2,1)} %all-gather.13.cloned.1.call-done) | copy-start | bytes 25165828
  458.2 11.3 %copy-start.30 = (bf16[1024,2048]{1,0:T(8,128)(2,1)}, bf16[1024,2048]{1,0:T(8,128)(2,1)S(1)}, u32[]{:S(2)}) copy-start(bf16[1024,2048]{1,0:T(8,128)(2,1)S(1)} %get-tuple-element.210) | copy-start | bytes 12582916
  481.9 16.3 %copy-start.13 = (bf16[2,8,8,8,512]{4,3,0,2,1:T(8,128)(2,1)S(1)}, bf16[2,8,8,8,512]{4,3,0,2,1:T(8,128)(2,1)}, u32[]{:S(2)}) copy-start(bf16[2,8,8,8,512]{4,3,0,2,1:T(8,128)(2,1)} %copy-done.12) | copy-start | bytes 3145732
  481.9 16.3 %copy-start.29 = (bf16[512,2048]{1,0:T(8,128)(2,1)S(1)}, bf16[512,2048]{1,0:T(8,128)(2,1)}, u32[]{:S(2)}) copy-start(bf16[512,2048]{1,0:T(8,128)(2,1)} %all-gather.11.cloned.1.call-done) | copy-start | bytes 6291460
  481.9 162.9 %reduce-scatter.7.cloned.1.call-start = ((), (), s32[]{:S(2)}) async-start(), calls=%async_computation.11 | async-start | bytes 5242880 | tf_op jit(solution)/shard_map/reduce_scatter | solution.py:168
  502.6 218.1 %reduce-scatter.15.cloned.1.call-start = ((), (), s32[]{:S(2)}) async-start(), calls=%async_computation.16 | async-start | bytes 9437184 | tf_op jit(solution)/shard_map/reduce_scatter | solution.py:237
  516.7 279.0 %reduce-scatter.17.cloned.1.call-start = ((), (), s32[]{:S(2)}) async-start(), calls=%async_computation.17 | async-start | bytes 9437184 | tf_op jit(solution)/shard_map/reduce_scatter | solution.py:240
  532.9 0.7 copy-start.25
  532.9 0.7 copy-start.26
  532.9 0.7 copy-start.17
  532.9 32.4 %copy-start.6 = (bf16[256,2048]{1,0:T(8,128)(2,1)S(1)}, bf16[256,2048]{1,0:T(8,128)(2,1)}, u32[]{:S(2)}) copy-start(bf16[256,2048]{1,0:T(8,128)(2,1)} %param.16) | copy-start | bytes 3145732
  532.9 32.4 %copy-start.16 = (f32[2048]{0:T(1024)S(1)}, f32[2048]{0:T(1024)}, u32[]{:S(2)}) copy-start(f32[2048]{0:T(1024)} %copy-done.15) | copy-start | bytes 24580
  532.9 32.4 %copy-start.19 = (f32[256]{0:T(256)S(1)}, f32[256]{0:T(256)}, u32[]{:S(2)}) copy-start(f32[256]{0:T(256)} %copy-done.18) | copy-start | bytes 3076
  532.9 32.4 %copy-start.21 = (f32[256]{0:T(256)S(1)}, f32[256]{0:T(256)}, u32[]{:S(2)}) copy-start(f32[256]{0:T(256)} %copy-done.20) | copy-start | bytes 3076
  533.6 111.3 %copy-start.7 = (bf16[256,2048]{1,0:T(8,128)(2,1)S(1)}, bf16[256,2048]{1,0:T(8,128)(2,1)}, u32[]{:S(2)}) copy-start(bf16[256,2048]{1,0:T(8,128)(2,1)} %param.27) | copy-start | bytes 3145732
  690.6 108.4 %copy-start.22 = (f32[2048]{0:T(1024)}, f32[2048]{0:T(1024)S(1)}, u32[]{:S(2)}) copy-start(f32[2048]{0:T(1024)S(1)} %get-tuple-element.454) | copy-start | bytes 24580
Sparse Core Ops, SparseCore 0:
  9.9 30.8 all-gather.10
  42.4 80.7 all-gather.16
  125.3 79.2 all-gather.6
  207.0 45.1 all-gather.8
  253.9 54.3 all-gather.12
  310.1 55.9 all-gather.14
  369.4 41.2 reduce-scatter.12
  424.3 61.8 reduce-scatter.10
  488.5 76.7 reduce-scatter.8
  567.5 77.2 reduce-scatter.6
  648.3 72.3 reduce-scatter.14
  724.4 71.2 reduce-scatter.16
where the time goes:
time: 811 us; the launch traced here: 806 us
  waiting for transfers between devices  410 us (51%)
  matrix products  228 us (28%)
  blocking collectives  67.1 us (8%)
  other arithmetic  58.1 us (7%)
  local copies, waits for them, and re-layouts  24.1 us (3%)
  between operations  14.9 us (2%)
    all_gather x1, waiting for transfers between devices, on_device(): grad_rows = lax.all_gather(cotangent, 'mp', axis=0, tiled=True)  82.4 us
    reduce_scatter x1, waiting for transfers between devices, on_device(): lax.psum_scatter(partial_sum.astype(jnp.bfloat16), 'mp', scatter_dimensio...  77.2 us
    all_gather x1, waiting for transfers between devices, on_device(): seq_rows = lax.all_gather(normed, 'mp', axis=0, tiled=True)  75.3 us
    reduce_scatter x1, waiting for transfers between devices, on_device(): lax.psum_scatter(grad_down.astype(jnp.bfloat16), 'dp', scatter_dimension=...  72.2 us
    all_gather x1, waiting for transfers between devices, on_device(): lax.all_gather(qkv_weight, 'dp', axis=1, tiled=True)  47.5 us
    psum x1, blocking collectives, on_device(): lax.psum((jnp.sum(grad_local * normal_rows, axis=0), jnp.sum(grad_local,...  41.2 us
    reduce_scatter x1, waiting for transfers between devices, on_device(): lax.psum_scatter(grad_up.astype(jnp.bfloat16), 'dp', scatter_dimension=0,...  30.1 us
    psum x1, blocking collectives, on_device(): lax.psum((jnp.sum(grad_proj.astype(jnp.float32), axis=1), jnp.sum(grad_pr...  25.8 us
  transfers between devices with their start and end apart: 12, of which 8 were waited for; matrix products, arithmetic and copies ran while one was open for 37% of the time, Pallas kernels for 0%

commit v1 on v0

v1 whole, which is shorter than its diff:
```python
import functools

import jax
import jax.numpy as jnp
from jax import lax
from jax.experimental import pallas as pl
from jax.experimental.pallas import tpu as pltpu
from jax.sharding import PartitionSpec as P

HEAD_DIM = 64
ROT = 32
EPS = 1e-05
LANES = 128
VMEM_LIMIT = 56 << 20
F32 = jnp.float32
BF16 = jnp.bfloat16


def dot(lhs, rhs, lhs_dim, rhs_dim):
    return lax.dot_general(
        lhs, rhs, (((lhs_dim,), (rhs_dim,)), ((), ())), preferred_element_type=F32
    )


def params():
    return pltpu.CompilerParams(vmem_limit_bytes=VMEM_LIMIT)


def cost(flops, transcendentals=0, bytes_accessed=0):
    return pl.CostEstimate(
        flops=int(flops), transcendentals=int(transcendentals), bytes_accessed=int(bytes_accessed)
    )


def rotary_tables(length):
    positions = jnp.arange(length).astype(F32)
    frequency = 10000.0 ** (-jnp.arange(ROT // 2).astype(F32) * 2.0 / ROT)
    angles = positions[:, None] * frequency[None, :]
    cosine, sine = jnp.cos(angles), jnp.sin(angles)
    rest = HEAD_DIM - ROT
    none = jnp.zeros((length, ROT // 2), F32)
    ones, zeros = jnp.ones((length, rest), F32), jnp.zeros((length, rest), F32)
    straight = jnp.concatenate([cosine, cosine, ones], axis=1)
    left = jnp.concatenate([-sine, none, zeros], axis=1)
    right = jnp.concatenate([none, sine, zeros], axis=1)
    return [jnp.concatenate([t, t], axis=1) for t in (straight, left, right)]


def rotated(u, straight, left, right, sign):
    half = ROT // 2
    turned = pltpu.roll(u, LANES - half, 1) * left + pltpu.roll(u, half, 1) * right
    return u * straight + sign * turned


def load_blocks(blocks, place, sems):
    me = lax.axis_index("dp")
    copies = [
        pltpu.make_async_copy(block, place(lax.bitwise_xor(me, j)), sems.at[j])
        for j, block in enumerate(blocks)
    ]
    for copy in copies:
        copy.start()
    for copy in copies:
        copy.wait()


def rows_at(ref, size, lead=()):
    return lambda owner: ref.at[(*lead, pl.ds(pl.multiple_of(owner * size, size), size))]


def columns_at(ref, size):
    return lambda owner: ref.at[:, pl.ds(pl.multiple_of(owner * size, size), size)]


def qkv_kernel(count, x_ref, bias_ref, cos_ref, left_ref, right_ref, *rest):
    blocks, (out_ref, held, sems) = rest[:count], rest[count:]
    width = held.shape[2]

    @pl.when(pl.program_id(0) == 0)
    def _():
        load_blocks(blocks, rows_at(held, blocks[0].shape[1], (slice(None),)), sems)

    for c in range(3):
        y = dot(x_ref[...], held[c], 1, 0) + bias_ref[c : c + 1, :]
        for g in range(width // LANES):
            part = y[:, g * LANES : (g + 1) * LANES]
            if c < 2:
                part = rotated(part, cos_ref[...], left_ref[...], right_ref[...], 1.0)
            if c == 0:
                part = part * HEAD_DIM**-0.5
            start = c * width + g * LANES
            out_ref[:, start : start + LANES] = part.astype(BF16)


def project_qkv(rows, blocks, bias, tables, tile):
    length, model = rows.shape
    width = blocks[0].shape[2]
    count = len(blocks)
    table = pl.BlockSpec((tile, LANES), lambda i: (i, 0))
    return pl.pallas_call(
        functools.partial(qkv_kernel, count),
        grid=(length // tile,),
        in_specs=[
            pl.BlockSpec((tile, model), lambda i: (i, 0)),
            pl.BlockSpec(bias.shape, lambda i: (0, 0)),
            table,
            table,
            table,
        ]
        + [pl.BlockSpec(memory_space=pl.ANY)] * count,
        out_specs=pl.BlockSpec((tile, 3 * width), lambda i: (i, 0)),
        out_shape=jax.ShapeDtypeStruct((length, 3 * width), BF16),
        scratch_shapes=[
            pltpu.VMEM((3, model, width), BF16),
            pltpu.SemaphoreType.DMA((count,)),
        ],
        compiler_params=params(),
        cost_estimate=cost(2 * length * model * 3 * width, 0, 2 * model * (length + 3 * width)),
        name="project_qkv",
    )(rows, bias, *tables, *blocks)


def up_kernel(count, step, x_ref, bias_ref, *rest):
    blocks, (act_ref, slope_ref, held, sems) = rest[:count], rest[count:]

    @pl.when(pl.program_id(0) == 0)
    def _():
        load_blocks(blocks, rows_at(held, blocks[0].shape[0]), sems)

    root = 0.7978845608028654
    for start in range(0, held.shape[1], step):
        part = slice(start, start + step)
        pre = dot(x_ref[...], held[:, part], 1, 0) + bias_ref[:, part]
        square = pre * pre
        turn = jnp.tanh(root * pre * (1.0 + 0.044715 * square))
        half = 0.5 * (1.0 + turn)
        act_ref[:, part] = (pre * half).astype(BF16)
        slope_ref[:, part] = (
            half
            + 0.5 * pre * (1.0 - turn * turn) * (root + (3.0 * 0.044715 * root) * square)
        ).astype(BF16)


def project_up(rows, blocks, bias, tile):
    length, model = rows.shape
    width = blocks[0].shape[1]
    count = len(blocks)
    out = pl.BlockSpec((tile, width), lambda i: (i, 0))
    return pl.pallas_call(
        functools.partial(up_kernel, count, min(256, width)),
        grid=(length // tile,),
        in_specs=[
            pl.BlockSpec((tile, model), lambda i: (i, 0)),
            pl.BlockSpec(bias.shape, lambda i: (0, 0)),
        ]
        + [pl.BlockSpec(memory_space=pl.ANY)] * count,
        out_specs=[out, out],
        out_shape=[jax.ShapeDtypeStruct((length, width), BF16)] * 2,
        scratch_shapes=[pltpu.VMEM((model, width), BF16), pltpu.SemaphoreType.DMA((count,))],
        compiler_params=params(),
        cost_estimate=cost(2 * length * model * width, 0, 2 * model * (length + width)),
        name="project_up",
    )(rows, bias, *blocks)


def attend_kernel(block, q_ref, k_ref, v_ref, out_ref, lse_ref):
    length = q_ref.shape[0]
    lane = lax.broadcasted_iota(jnp.int32, (1, LANES), 1)
    key = lax.broadcasted_iota(jnp.int32, (block, block), 0)
    causal = key <= lax.broadcasted_iota(jnp.int32, (block, block), 1)
    for i in range(length // block):
        rows, before = pl.ds(i * block, block), pl.ds(0, i * block)
        results = []
        for h in range(2):
            mine = (lane < HEAD_DIM) if h == 0 else (lane >= HEAD_DIM)
            query = jnp.where(mine, q_ref[rows, :], 0)
            near = jnp.where(causal, dot(k_ref[rows, :], query, 1, 1), -1e30)
            highest = jnp.max(near, axis=0, keepdims=True)
            if i:
                far = dot(k_ref[before, :], query, 1, 1)
                highest = jnp.maximum(highest, jnp.max(far, axis=0, keepdims=True))
            near = jnp.exp(near - highest)
            total = jnp.sum(near, axis=0, keepdims=True)
            if i:
                far = jnp.exp(far - highest)
                total = total + jnp.sum(far, axis=0, keepdims=True)
            inverse = 1.0 / total
            result = dot((near * inverse).astype(BF16), v_ref[rows, :], 0, 0)
            if i:
                result = result + dot((far * inverse).astype(BF16), v_ref[before, :], 0, 0)
            results.append(result)
            lse_ref[0, h : h + 1, rows] = highest + jnp.log(total)
        out_ref[rows, :] = jnp.where(lane < HEAD_DIM, results[0], results[1]).astype(BF16)


def attend(qkv, block):
    length, width = qkv.shape[0], qkv.shape[1] // 3
    pairs = width // LANES
    at = lambda off: pl.BlockSpec((length, LANES), lambda p, off=off: (0, off * pairs + p))
    return pl.pallas_call(
        functools.partial(attend_kernel, block),
        grid=(pairs,),
        in_specs=[at(0), at(1), at(2)],
        out_specs=[at(0), pl.BlockSpec((1, 8, length), lambda p: (p, 0, 0))],
        out_shape=[
            jax.ShapeDtypeStruct((length, width), BF16),
            jax.ShapeDtypeStruct((pairs, 8, length), F32),
        ],
        compiler_params=params(),
        cost_estimate=cost(16 * length * length * width, pairs * 2 * length * length, 0),
        name="attend",
    )(qkv, qkv, qkv)


def attend_back_kernel(
    block,
    q_ref,
    k_ref,
    v_ref,
    grad_ref,
    mixed_ref,
    lse_ref,
    cos_ref,
    left_ref,
    right_ref,
    gq_ref,
    gk_ref,
    gv_ref,
    sum_ref,
    gk_sum,
    gv_sum,
):
    length = q_ref.shape[0]
    lane = lax.broadcasted_iota(jnp.int32, (1, LANES), 1)
    key = lax.broadcasted_iota(jnp.int32, (block, block), 0)
    causal = key <= lax.broadcasted_iota(jnp.int32, (block, block), 1)
    count = length // block
    sum_ref[...] = jnp.zeros_like(sum_ref)

    def put(ref, which, rows, value):
        value = value.astype(BF16)
        ref[rows, :] = value
        sum_ref[0, which : which + 1, :] += jnp.sum(value.astype(F32), axis=0, keepdims=True)

    def unrotated(value, rows):
        return rotated(value, cos_ref[rows, :], left_ref[rows, :], right_ref[rows, :], -1.0)

    for i in reversed(range(count)):
        rows = pl.ds(i * block, block)
        product = grad_ref[rows, :].astype(F32) * mixed_ref[rows, :].astype(F32)
        gq = None
        for h in range(2):
            mine = (lane < HEAD_DIM) if h == 0 else (lane >= HEAD_DIM)
            query = jnp.where(mine, q_ref[rows, :], 0)
            grad = jnp.where(mine, grad_ref[rows, :], 0)
            ones = jnp.where(mine, jnp.ones((8, LANES), F32), 0.0)
            delta = lax.dot_general(
                ones,
                product,
                (((1,), (1,)), ((), ())),
                precision=lax.Precision.HIGHEST,
                preferred_element_type=F32,
            )[0:1, :]
            lse = lse_ref[0, h : h + 1, rows]
            for j in range(i + 1):
                keys = pl.ds(j * block, block)
                key_rows = k_ref[keys, :]
                probs = jnp.exp(dot(key_rows, query, 1, 1) - lse)
                if j == i:
                    probs = jnp.where(causal, probs, 0.0)
                gprobs = dot(v_ref[keys, :], grad, 1, 1)
                gscores = (probs * (gprobs - delta)).astype(BF16)
                gv, gk = dot(probs.astype(BF16), grad, 1, 0), dot(gscores, query, 1, 0)
                if i == count - 1 and h == 0:
                    gv_sum[keys, :] = gv
                    gk_sum[keys, :] = gk
                else:
                    gv_sum[keys, :] += gv
                    gk_sum[keys, :] += gk
                part = dot(gscores, jnp.where(mine, key_rows, 0), 0, 0)
                gq = part if gq is None else gq + part
        put(gq_ref, 0, rows, unrotated(gq * HEAD_DIM**-0.5, rows))
    for i in range(count):
        rows = pl.ds(i * block, block)
        put(gk_ref, 1, rows, unrotated(gk_sum[rows, :], rows))
        put(gv_ref, 2, rows, gv_sum[rows, :])


def attend_back(qkv, grad, mixed, lse, tables, block):
    length, width = qkv.shape[0], qkv.shape[1] // 3
    pairs = width // LANES
    at = lambda off: pl.BlockSpec((length, LANES), lambda p, off=off: (0, off * pairs + p))
    table = pl.BlockSpec((length, LANES), lambda p: (0, 0))
    return pl.pallas_call(
        functools.partial(attend_back_kernel, block),
        grid=(pairs,),
        in_specs=[at(0), at(1), at(2), at(0), at(0)]
        + [pl.BlockSpec((1, 8, length), lambda p: (p, 0, 0)), table, table, table],
        out_specs=[at(0)] * 3 + [pl.BlockSpec((1, 8, LANES), lambda p: (p, 0, 0))],
        out_shape=[jax.ShapeDtypeStruct((length, width), BF16)] * 3
        + [jax.ShapeDtypeStruct((pairs, 8, LANES), F32)],
        scratch_shapes=[pltpu.VMEM((length, LANES), F32)] * 2,
        compiler_params=params(),
        cost_estimate=cost(40 * length * length * width, pairs * 2 * length * length, 0),
        name="attend_back",
    )(qkv, qkv, qkv, grad, mixed, lse, *tables)


def branch_kernel(count, parts, mixed_ref, act_ref, *rest):
    dense, down = rest[:count], rest[count : 2 * count]
    outs, (dense_held, down_held, sems) = rest[2 * count : 2 * count + parts], rest[-3:]

    @pl.when(pl.program_id(0) == 0)
    def _():
        size = dense[0].shape[1]
        load_blocks(dense, columns_at(dense_held, size), sems.at[0])
        load_blocks(down, columns_at(down_held, size), sems.at[1])

    result = dot(mixed_ref[...], dense_held[...], 1, 0) + dot(act_ref[...], down_held[...], 1, 0)
    for part, out_ref in enumerate(outs):

        @pl.when(pl.program_id(0) == part)
        def _(out_ref=out_ref):
            out_ref[...] = result.astype(BF16)


def quarter_specs(parts, rows, widths):
    return [pl.BlockSpec((rows, w), lambda k, at: ((at[0] + k) % parts, 0)) for w in widths]


def branch_sums(at, mixed, act, dense, down, parts):
    length, width = mixed.shape
    hidden = act.shape[1]
    count, rows = len(dense), length // parts
    model = count * dense[0].shape[1]
    return pl.pallas_call(
        lambda at_ref, *refs: branch_kernel(count, parts, *refs),
        grid_spec=pltpu.PrefetchScalarGridSpec(
            num_scalar_prefetch=1,
            grid=(parts,),
            in_specs=quarter_specs(parts, rows, (width, hidden))
            + [pl.BlockSpec(memory_space=pl.ANY)] * (2 * count),
            out_specs=[pl.BlockSpec((rows, model), lambda k, at: (0, 0))] * parts,
            scratch_shapes=[
                pltpu.VMEM((width, model), BF16),
                pltpu.VMEM((hidden, model), BF16),
                pltpu.SemaphoreType.DMA((2, count)),
            ],
        ),
        out_shape=[jax.ShapeDtypeStruct((rows, model), BF16)] * parts,
        compiler_params=params(),
        cost_estimate=cost(2 * length * model * (width + hidden), 0, 2 * length * model),
        name="branch_sums",
    )(at, mixed, act, *dense, *down)


def grad_in_kernel(count, step, dy_ref, slope_ref, *rest):
    dense, down = rest[:count], rest[count : 2 * count]
    gmixed_ref, gpre_ref, gsum_ref, dsum_ref, dense_held, down_held, sems = rest[2 * count :]

    @pl.when(pl.program_id(0) == 0)
    def _():
        size = dense[0].shape[1]
        load_blocks(dense, columns_at(dense_held, size), sems.at[0])
        load_blocks(down, columns_at(down_held, size), sems.at[1])
        gsum_ref[...] = jnp.zeros_like(gsum_ref)
        dsum_ref[...] = jnp.zeros_like(dsum_ref)

    gmixed_ref[...] = dot(dy_ref[...], dense_held[...], 1, 1).astype(BF16)
    for start in range(0, down_held.shape[0], step):
        part = slice(start, start + step)
        gact = dot(dy_ref[...], down_held[part, :], 1, 1)
        gpre = (gact * slope_ref[:, part].astype(F32)).astype(BF16)
        gpre_ref[:, part] = gpre
        gsum_ref[0:1, part] += jnp.sum(gpre.astype(F32), axis=0, keepdims=True)
    dsum_ref[0:1, :] += jnp.sum(dy_ref[...].astype(F32), axis=0, keepdims=True)


def grad_in(dy, slope, dense, down, tile):
    length, model = dy.shape
    hidden, width = slope.shape[1], dense[0].shape[0]
    count = len(dense)
    return pl.pallas_call(
        functools.partial(grad_in_kernel, count, min(256, hidden)),
        grid=(length // tile,),
        in_specs=[
            pl.BlockSpec((tile, model), lambda i: (i, 0)),
            pl.BlockSpec((tile, hidden), lambda i: (i, 0)),
        ]
        + [pl.BlockSpec(memory_space=pl.ANY)] * (2 * count),
        out_specs=[
            pl.BlockSpec((tile, width), lambda i: (i, 0)),
            pl.BlockSpec((tile, hidden), lambda i: (i, 0)),
            pl.BlockSpec((8, hidden), lambda i: (0, 0)),
            pl.BlockSpec((8, model), lambda i: (0, 0)),
        ],
        out_shape=[
            jax.ShapeDtypeStruct((length, width), BF16),
            jax.ShapeDtypeStruct((length, hidden), BF16),
            jax.ShapeDtypeStruct((8, hidden), F32),
            jax.ShapeDtypeStruct((8, model), F32),
        ],
        scratch_shapes=[
            pltpu.VMEM((width, model), BF16),
            pltpu.VMEM((hidden, model), BF16),
            pltpu.SemaphoreType.DMA((2, count)),
        ],
        compiler_params=params(),
        cost_estimate=cost(2 * length * model * (width + hidden), 0, 2 * length * model),
        name="grad_in",
    )(dy, slope, *dense, *down)


def grad_normed_kernel(count, parts, gq_ref, gk_ref, gv_ref, gpre_ref, *rest):
    qkv, up = rest[:count], rest[count : 2 * count]
    outs, (qkv_held, up_held, sems) = rest[2 * count : 2 * count + parts], rest[-3:]

    @pl.when(pl.program_id(0) == 0)
    def _():
        size = up[0].shape[0]
        load_blocks(qkv, rows_at(qkv_held, size, (slice(None),)), sems.at[0])
        load_blocks(up, rows_at(up_held, size), sems.at[1])

    result = dot(gpre_ref[...], up_held[...], 1, 1)
    for c, ref in enumerate((gq_ref, gk_ref, gv_ref)):
        result = result + dot(ref[...], qkv_held[c], 1, 1)
    for part, out_ref in enumerate(outs):

        @pl.when(pl.program_id(0) == part)
        def _(out_ref=out_ref):
            out_ref[...] = result.astype(BF16)


def grad_normed_sums(at, gqkv, gpre, qkv, up, parts):
    length, hidden = gpre.shape
    width = gqkv[0].shape[1]
    count, rows = len(up), length // parts
    model = count * up[0].shape[0]
    return pl.pallas_call(
        lambda at_ref, *refs: grad_normed_kernel(count, parts, *refs),
        grid_spec=pltpu.PrefetchScalarGridSpec(
            num_scalar_prefetch=1,
            grid=(parts,),
            in_specs=quarter_specs(parts, rows, (width, width, width, hidden))
            + [pl.BlockSpec(memory_space=pl.ANY)] * (2 * count),
            out_specs=[pl.BlockSpec((rows, model), lambda k, at: (0, 0))] * parts,
            scratch_shapes=[
                pltpu.VMEM((3, model, width), BF16),
                pltpu.VMEM((model, hidden), BF16),
                pltpu.SemaphoreType.DMA((2, count)),
            ],
        ),
        out_shape=[jax.ShapeDtypeStruct((rows, model), BF16)] * parts,
        compiler_params=params(),
        cost_estimate=cost(2 * length * model * (3 * width + hidden), 0, 2 * length * model),
        name="grad_normed_sums",
    )(at, *gqkv, gpre, *qkv, *up)


def row_block_kernel(count, terms, x0_ref, x1_ref, *rest):
    first, second, outs = rest[:terms], rest[terms : 2 * terms], rest[2 * terms :]
    for j, out_ref in enumerate(outs):

        @pl.when(pl.program_id(0) == j)
        def _(out_ref=out_ref):
            for c in range(terms):
                grad = dot(x0_ref[...], first[c][...], 0, 0) + dot(x1_ref[...], second[c][...], 0, 0)
                if terms == 1:
                    out_ref[...] = grad.astype(BF16)
                else:
                    out_ref[c] = grad.astype(BF16)


def row_block_grads(me, rows, grads, count):
    length, model = rows[0].shape
    terms, width, size = len(grads[0]), grads[0][0].shape[1], model // count
    shape = (size, width) if terms == 1 else (terms, size, width)
    x = pl.BlockSpec((length, size), lambda j, at: (0, lax.bitwise_xor(at[0], j)))
    whole = pl.BlockSpec((length, width), lambda j, at: (0, 0))
    return pl.pallas_call(
        lambda at_ref, *refs: row_block_kernel(count, terms, *refs),
        grid_spec=pltpu.PrefetchScalarGridSpec(
            num_scalar_prefetch=1,
            grid=(count,),
            in_specs=[x, x] + [whole] * (2 * terms),
            out_specs=[pl.BlockSpec(shape, lambda j, at: (0,) * len(shape))] * count,
        ),
        out_shape=[jax.ShapeDtypeStruct(shape, BF16)] * count,
        compiler_params=params(),
        cost_estimate=cost(4 * length * model * terms * width, 0, 4 * length * model),
        name="row_block_grads",
    )(me, *rows, *grads[0], *grads[1])


def column_block_kernel(x0_ref, x1_ref, g0_ref, g1_ref, *outs):
    for j, out_ref in enumerate(outs):

        @pl.when(pl.program_id(0) == j)
        def _(out_ref=out_ref):
            grad = dot(x0_ref[...], g0_ref[...], 0, 0) + dot(x1_ref[...], g1_ref[...], 0, 0)
            out_ref[...] = grad.astype(BF16)


def column_block_grads(me, inner, outer, count):
    length, width = inner[0].shape
    model = outer[0].shape[1]
    size = model // count
    whole = pl.BlockSpec((length, width), lambda j, at: (0, 0))
    g = pl.BlockSpec((length, size), lambda j, at: (0, lax.bitwise_xor(at[0], j)))
    return pl.pallas_call(
        lambda at_ref, *refs: column_block_kernel(*refs),
        grid_spec=pltpu.PrefetchScalarGridSpec(
            num_scalar_prefetch=1,
            grid=(count,),
            in_specs=[whole, whole, g, g],
            out_specs=[pl.BlockSpec((width, size), lambda j, at: (0, 0))] * count,
        ),
        out_shape=[jax.ShapeDtypeStruct((width, size), BF16)] * count,
        compiler_params=params(),
        cost_estimate=cost(4 * length * model * width, 0, 4 * length * model),
        name="column_block_grads",
    )(me, *inner, *outer)


def assemble_kernel(parts, *refs):
    own, below, above = refs[0], refs[1:parts], refs[parts : 2 * parts - 1]
    out_ref, sems = refs[-2:]
    rows = own.shape[0]
    z = lax.axis_index("mp")
    for wait in (False, True):
        for t in range(parts):
            target = out_ref.at[pl.ds(t * rows, rows)]
            sources = [(z == t, own)]
            sources += [(z == t + k, below[k - 1]) for k in range(1, parts - t)]
            sources += [(z == t - k, above[k - 1]) for k in range(1, t + 1)]
            for here, source in sources:

                @pl.when(here)
                def _(source=source, target=target, t=t):
                    copy = pltpu.make_async_copy(source, target, sems.at[t])
                    if wait:
                        copy.wait()
                    else:
                        copy.start()


def assemble(own, below, above):
    parts = len(below) + 1
    rows, width = own.shape
    return pl.pallas_call(
        functools.partial(assemble_kernel, parts),
        in_specs=[pl.BlockSpec(memory_space=pl.ANY)] * (2 * parts - 1),
        out_specs=pl.BlockSpec(memory_space=pl.ANY),
        out_shape=jax.ShapeDtypeStruct((parts * rows, width), own.dtype),
        scratch_shapes=[pltpu.SemaphoreType.DMA((parts,))],
        compiler_params=params(),
        cost_estimate=cost(0, 0, 4 * parts * rows * width),
        name="assemble",
    )(own, *below, *above)


def after(value, *earlier):
    return lax.optimization_barrier((value, *earlier))[0]


def across(value, bit, count):
    return lax.ppermute(value, "dp", [(i, i ^ bit) for i in range(count)])


def line_gather(own, parts):
    below, above, up, down = [], [], own, own
    for k in range(1, parts):
        up = lax.ppermute(up, "mp", [(i, i + 1) for i in range(k - 1, parts - 1)])
        down = lax.ppermute(down, "mp", [(i + 1, i) for i in range(parts - k)])
        below.append(up)
        above.append(down)
    return below, above


def line_scatter(sums):
    parts = len(sums)
    sums = [list(s) for s in sums]

    def total(k):
        if len(sums[k]) > 1:
            sums[k] = [sum(s.astype(F32) for s in sums[k]).astype(BF16)]
        return sums[k][0]

    for s in range(1, parts):
        up = lax.ppermute(total(parts - s), "mp", [(i, i + 1) for i in range(s)])
        down = lax.ppermute(total(s), "mp", [(i, i - 1) for i in range(parts - s, parts)])
        sums[(parts - s - 1) % parts].append(up)
        sums[(s + 1) % parts].append(down)
    return sums[0]


def chip_bits(count):
    bits, bit = [], 2
    while bit < count:
        bits.append(bit)
        bit *= 2
    return bits


def gather_blocks(own, sibling, count, gate):
    held = {0: own, 1: sibling}
    orders = (chip_bits(count), chip_bits(count)[::-1])
    first = None
    for s in range(len(orders[0])):
        moved = {}
        for half in range(2):
            bit = orders[half][s]
            for j in [j for j in held if j % 2 == half]:
                block = held[j] if s or gate is None else after(held[j], gate)
                moved[j ^ bit] = across(block, bit, count)
        held.update(moved)
        first = first if s else moved
    return [held[j] for j in range(count)], first


def scatter_blocks(blocks, count):
    held = {j: [b] for j, b in enumerate(blocks)}
    orders = (chip_bits(count)[::-1], chip_bits(count))

    def total(j):
        if len(held[j]) > 1:
            held[j] = [sum(b.astype(F32) for b in held[j]).astype(BF16)]
        return held[j][0]

    for s in range(len(orders[0])):
        moved = []
        for half in range(2):
            bit = orders[half][s]
            for j in [j for j in held if j % 2 == half and j & bit]:
                moved.append((j ^ bit, across(total(j), bit, count)))
                del held[j]
        for j, block in moved:
            held[j].append(block)
    mine = sum(b.astype(F32) for b in held[0])
    return mine, total(1)


def all_reduce_small(value, axis, count):
    parts = [value] + [
        lax.ppermute(value, axis, [(i, i ^ j) for i in range(count)]) for j in range(1, count)
    ]
    while len(parts) > 1:
        parts = [a + b for a, b in zip(parts[::2], parts[1::2])]
    return parts[0]


def on_device(
    tokens,
    norm_gain,
    norm_bias,
    qkv_weight,
    qkv_bias,
    dense_weight,
    dense_bias,
    up_weight,
    up_bias,
    down_weight,
    down_bias,
    cotangent,
    *,
    ndp,
    nmp,
):
    me, z = lax.axis_index("dp"), lax.axis_index("mp")
    core = me % 2
    at_dp, at_mp = me.astype(jnp.int32)[None], z.astype(jnp.int32)[None]
    length = tokens.shape[0] * nmp
    tile = min(256, length)
    block = min(512, length)
    width, hidden = qkv_weight.shape[2] // 2, up_weight.shape[1] // 2
    rank = lambda array, axis, which, size: lax.dynamic_slice_in_dim(
        array, which * size, size, axis
    )

    local_inputs = tokens.astype(F32)
    row_mean = jnp.mean(local_inputs, axis=1, keepdims=True)
    centered = local_inputs - row_mean
    row_var = jnp.mean(centered * centered, axis=1, keepdims=True)
    inverse_std = lax.rsqrt(row_var + EPS)
    normal_rows = centered * inverse_std
    gain_values = norm_gain.astype(F32)
    normed = (normal_rows * gain_values + norm_bias.astype(F32)).astype(BF16)

    def halves(weight, axis, size):
        own = rank(weight, axis, core, size)
        return own, across(rank(weight, axis, 1 - core, size), 1, ndp)

    pieces = {
        "qkv": halves(qkv_weight, 2, width),
        "up": halves(up_weight, 1, hidden),
        "dense": halves(dense_weight, 0, width),
        "down": halves(down_weight, 0, hidden),
    }
    gate, gathered = None, {}
    for name in ("qkv", "up", "dense", "down"):
        gathered[name], first = gather_blocks(*pieces[name], ndp, gate)
        gate = next(iter(first.values()))

    below, above = line_gather(normed, nmp)
    rows_own = assemble(normed, below, above)
    rows_other = across(rows_own, 1, ndp)
    late_cotangent = after(cotangent, below[-1], above[-1])
    grad_below, grad_above = line_gather(late_cotangent, nmp)
    dy_own = assemble(cotangent, grad_below, grad_above)
    dy_other = across(dy_own, 1, ndp)
    rows, dy = (rows_own, rows_other), (dy_own, dy_other)

    tables = rotary_tables(length)
    qkv_bias_here = rank(qkv_bias, 1, core, width).astype(F32)
    up_bias_here = rank(up_bias[None, :], 1, core, hidden).astype(F32)
    qkv = [project_qkv(r, gathered["qkv"], qkv_bias_here, tables, tile) for r in rows]
    act, slope = zip(*[project_up(r, gathered["up"], up_bias_here, tile) for r in rows])
    mixed, lse = zip(*[attend(p, block) for p in qkv])
    sums = [
        branch_sums(at_mp, m, a, gathered["dense"], gathered["down"], nmp)
        for m, a in zip(mixed, act)
    ]
    shares = [[mine, across(theirs, 1, ndp)] for mine, theirs in zip(*sums)]
    branches = sum(s.astype(F32) for s in line_scatter(shares))
    output = (local_inputs + branches + dense_bias.astype(F32) + down_bias.astype(F32)).astype(BF16)

    grad_down = column_block_grads(at_dp, act, dy, ndp)
    gmixed, gpre, gpre_sum, dy_sum = zip(
        *[grad_in(d, s, gathered["dense"], gathered["down"], tile) for d, s in zip(dy, slope)]
    )
    grad_up = row_block_grads(at_dp, rows, [[g] for g in gpre], ndp)
    back = [
        attend_back(p, g, m, e, tables, block) for p, g, m, e in zip(qkv, gmixed, mixed, lse)
    ]
    gqkv = [b[:3] for b in back]
    normed_sums = [
        grad_normed_sums(at_mp, g, p, gathered["qkv"], gathered["up"], nmp)
        for g, p in zip(gqkv, gpre)
    ]
    grad_dense = column_block_grads(at_dp, mixed, dy, ndp)
    grad_qkv = row_block_grads(at_dp, rows, gqkv, ndp)

    def owned(blocks, axis):
        mine, theirs = scatter_blocks(blocks, ndp)
        other = across(theirs, 1, ndp).astype(F32)
        return jnp.where(
            core == 0,
            jnp.concatenate([mine, other], axis=axis),
            jnp.concatenate([other, mine], axis=axis),
        )

    owned_down = owned(grad_down, 0)
    owned_up = owned(grad_up, 1)
    owned_dense = owned(grad_dense, 0)
    owned_qkv = owned(grad_qkv, 2)

    pairs = width // LANES
    qkv_sum = sum(b[3] for b in back)[:, :3, :].transpose(1, 0, 2).reshape(3 * width)
    small = jnp.concatenate(
        [sum(s[0] for s in gpre_sum), qkv_sum, sum(s[0] for s in dy_sum)]
    )
    for bit in chip_bits(ndp):
        small = small + across(small, bit, ndp)
    here, grad_out_bias = small[: hidden + 3 * width], small[hidden + 3 * width :]
    there = across(here, 1, ndp)
    even, odd = jnp.where(core == 0, here, there), jnp.where(core == 0, there, here)
    grad_up_bias = jnp.concatenate([even[:hidden], odd[:hidden]])
    grad_qkv_bias = jnp.concatenate(
        [even[hidden:].reshape(3, width), odd[hidden:].reshape(3, width)], axis=1
    )

    shares = [[mine, across(theirs, 1, ndp)] for mine, theirs in zip(*normed_sums)]
    grad_local = sum(s.astype(F32) for s in line_scatter(shares))
    scaled_grad = grad_local * gain_values
    first_mean = jnp.mean(scaled_grad, axis=1, keepdims=True)
    second_mean = jnp.mean(scaled_grad * normal_rows, axis=1, keepdims=True)
    grad_tokens = (
        cotangent.astype(F32)
        + (scaled_grad - first_mean - normal_rows * second_mean) * inverse_std
    ).astype(BF16)
    norm_sums = jnp.concatenate(
        [jnp.sum(grad_local * normal_rows, axis=0), jnp.sum(grad_local, axis=0)]
    )
    norm_sums = all_reduce_small(all_reduce_small(norm_sums, "dp", ndp), "mp", nmp)
    model = norm_gain.shape[0]
    return (
        output,
        grad_tokens,
        norm_sums[:model],
        norm_sums[model:],
        owned_qkv,
        grad_qkv_bias,
        owned_dense,
        grad_out_bias,
        owned_up,
        grad_up_bias,
        owned_down,
        grad_out_bias,
    )


def solution(mesh):
    return jax.shard_map(
        functools.partial(on_device, ndp=mesh.shape["dp"], nmp=mesh.shape["mp"]),
        mesh=mesh,
        in_specs=(
            P(("dp", "mp"), None),
            P(),
            P(),
            P(None, "dp", "mp"),
            P(None, "mp"),
            P("mp", "dp"),
            P(),
            P("dp", "mp"),
            P("mp"),
            P("mp", "dp"),
            P(),
            P(("dp", "mp"), None),
        ),
        out_specs=(
            P(("dp", "mp"), None),
            P(("dp", "mp"), None),
            P(),
            P(),
            P(None, "dp", "mp"),
            P(None, "mp"),
            P("mp", "dp"),
            P(),
            P("dp", "mp"),
            P("mp"),
            P("mp", "dp"),
            P(),
        ),
        check_vma=False,
    )
```

time: 811 us -> 920 us (1.13)
  Pallas kernels: 0 us -> 483 us
  matrix products: 228 us -> 0 us
  waiting for transfers between devices: 410 us -> 241 us
  starting transfers between devices: 0.48 us -> 127 us
  blocking collectives: 67.1 us -> 0 us
  other arithmetic: 58.1 us -> 39.7 us
  between operations: 14.9 us -> 2.66 us
    pallas_call x0 -> x20, Pallas kernels: none -> 483 us  [the longest x2 256 us: assemble(): pl.pallas_call(functools.partial(assemble_kernel, parts), in_specs=[pl.Bl...]
    ppermute x0 -> x103, waiting for transfers between devices: none -> 241 us  [the longest x69 132 us: across(): return lax.ppermute(value, 'dp', [(i, i ^ bit) for i in range(count)])]
    dot_general x26 -> x0, matrix products: 228 us -> none  [the longest x2 23.4 us: one_block(): jnp.einsum('hqd,hkd->hqk', block_grad, values, preferred_element_type=jnp...]
    all_gather x6 -> x0, waiting for transfers between devices: 227 us -> none  [the longest x1 82.4 us: on_device(): grad_rows = lax.all_gather(cotangent, 'mp', axis=0, tiled=True)]
    reduce_scatter x6 -> x0, waiting for transfers between devices: 181 us -> none  [the longest x1 77.2 us: on_device(): lax.psum_scatter(partial_sum.astype(jnp.bfloat16), 'mp', scatter_dimensio...]
    ppermute x0 -> x103, starting transfers between devices: none -> 127 us  [the longest x69 51.7 us: across(): return lax.ppermute(value, 'dp', [(i, i ^ bit) for i in range(count)])]
    psum x2 -> x0, blocking collectives: 67.1 us -> none  [the longest x1 41.2 us: on_device(): lax.psum((jnp.sum(grad_local * normal_rows, axis=0), jnp.sum(grad_local,...]
    reduce_sum x4 -> x0, other arithmetic: 15.7 us -> none  [the longest x2 8.48 us: one_block(): totals = jnp.sum(expon, axis=-1)]
  transfers between devices with their start and end apart: 12 -> 103, of which waited for: 8 -> 38; matrix products, arithmetic and copies ran while one was open for 37% -> 5% of each run, Pallas kernels for 0% -> 37%
where the time goes in v1:
time: 920 us; the launch traced here: 912 us
  Pallas kernels  483 us (52%)
  waiting for transfers between devices  241 us (26%)
  starting transfers between devices  127 us (14%)
  other arithmetic  39.7 us (4%)
  local copies, waits for them, and re-layouts  18.7 us (2%)
    pallas_call x2, Pallas kernels, assemble(): pl.pallas_call(functools.partial(assemble_kernel, parts), in_specs=[pl.Bl...  256 us
    ppermute x69, waiting for transfers between devices, across(): return lax.ppermute(value, 'dp', [(i, i ^ bit) for i in range(count)])  132 us
    ppermute x6, waiting for transfers between devices, line_gather(): down = lax.ppermute(down, 'mp', [(i + 1, i) for i in range(parts - k)])  66.8 us
    ppermute x69, starting transfers between devices, across(): return lax.ppermute(value, 'dp', [(i, i ^ bit) for i in range(count)])  51.7 us
    ppermute x6, starting transfers between devices, line_scatter(): up = lax.ppermute(total(parts - s), 'mp', [(i, i + 1) for i in range(s)])  39.9 us
    pallas_call x2, Pallas kernels, grad_normed_sums(): pl.pallas_call(lambda at_ref, *refs: grad_normed_kernel(count, parts, *re...  32.7 us
    pallas_call x2, Pallas kernels, row_block_grads(): pl.pallas_call(lambda at_ref, *refs: row_block_kernel(count, terms, *refs...  29 us
    pallas_call x2, Pallas kernels, attend_back(): pl.pallas_call(functools.partial(attend_back_kernel, block), grid=(pairs,...  28 us
  transfers between devices with their start and end apart: 103, of which 38 were waited for; matrix products, arithmetic and copies ran while one was open for 5% of the time, Pallas kernels for 37%

profile of v1, /device:TPU:0, one launch (start us, length us, event | category | flops | bytes accessed | tf_op | source)
XLA Modules:
  0.0 911.8 jit_solution(7118477761439887767)
XLA Ops:
  5.0 5.0 collective-permute-start
  11.3 21.0 %collective-permute-done.refs_1_ = bf16[256,2048]{1,0:T(8,128)(2,1)S(1)} collective-permute-done((bf16[256,2048]{1,0:T(8,128)(2,1)S(1)}, bf16[256,2048]{1,0:T(8,128)(2,1)S(1)}, u32[]{:S(2)}, u32[]{:S(2)}) %collective-permute-start) | collective-permute-done | bytes 1048608 | tf_op jit(solution)/shard_map/ppermute | solution.py:573
  33.0 3.5 collective-permute-done.3.refs_4_
  38.5 23.7 %collective-permute-done.4.refs_5_ = bf16[256,2048]{1,0:T(8,128)(2,1)S(1)} collective-permute-done((bf16[256,2048]{1,0:T(8,128)(2,1)S(1)}, bf16[256,2048]{1,0:T(8,128)(2,1)S(1)}, u32[]{:S(2)}, u32[]{:S(2)}) %collective-permute-start.4) | collective-permute-done | bytes 1048608 | tf_op jit(solution)/shard_map/ppermute | solution.py:574
  63.6 23.6 %collective-permute-done.5.refs_6_ = bf16[256,2048]{1,0:T(8,128)(2,1)} collective-permute-done((bf16[256,2048]{1,0:T(8,128)(2,1)S(1)}, bf16[256,2048]{1,0:T(8,128)(2,1)}, u32[]{:S(2)}, u32[]{:S(2)}) %collective-permute-start.5) | collective-permute-done | bytes 1048608 | tf_op jit(solution)/shard_map/ppermute | solution.py:574
  87.3 128.2 %assemble.2.x_ref.refs_0_ = bf16[1024,2048]{1,0:T(8,128)(2,1)} custom-call(bf16[256,2048]{1,0:T(8,128)(2,1)} %copy-done.1, bf16[256,2048]{1,0:T(8,128)(2,1)} %copy-done.17, bf16[256,2048]{1,0:T(8,128)(2,1)} %copy-done.19, bf16[256,2048]{1,0:T(8,128)(2,1)} %copy-done.21, bf16[256,2048]{1,0:T(8,128)(2,1)} %copy-done.18, bf16[256,2048]{1,0:T(8,128)(2,1)} %copy-done.20, ...), custom_call_target="tpu_custom_call" | custom-call | bytes 8388608 | tf_op jit(solution)/shard_map/assemble/pallas_call | solution.py:550
  215.6 2.0 constant_dynamic-slice_fusion.6
  224.7 2.9 collective-permute-done.23.refs_6_.rest_4_
  227.7 5.1 collective-permute-done.22.refs_5_.rest_3_
  237.4 10.8 %collective-permute-done.16.rest_4_.refs_16_ = bf16[256,1024]{1,0:T(8,128)(2,1)S(1)} collective-permute-done((bf16[256,1024]{1,0:T(8,128)(2,1)S(1)}, bf16[256,1024]{1,0:T(8,128)(2,1)S(1)}, u32[]{:S(2)}, u32[]{:S(2)}) %collective-permute-start.16) | collective-permute-done | bytes 524320 | tf_op jit(solution)/shard_map/ppermute | solution.py:567
  250.4 9.1 collective-permute-done.30.refs_14_.rest_12_
  261.0 6.9 collective-permute-done.10.rest_5_.refs_9_
  268.5 7.8 collective-permute-done.11.rest_6_.refs_10_
  279.8 6.6 collective-permute-done.17.rest_5_.refs_17_
  287.1 2.9 multiply_sine_fusion
  290.0 1.9 collective-permute-done.15.rest_3_.refs_15_
  293.5 17.8 %collective-permute-done.21.refs_4_.rest_2_ = bf16[256,256]{1,0:T(8,128)(2,1)S(1)} collective-permute-done((bf16[256,256]{1,0:T(8,128)(2,1)}, bf16[256,256]{1,0:T(8,128)(2,1)S(1)}, u32[]{:S(2)}, u32[]{:S(2)}) %collective-permute-start.21) | collective-permute-done | bytes 131104 | tf_op jit(solution)/shard_map/ppermute | solution.py:567
  313.6 2.8 concatenate.52.left_ref
  316.3 1.7 concatenate.53.right_ref
  318.1 1.7 concatenate.51.cos_ref
  323.0 9.2 %project_qkv.2.q_ref.k_ref.v_ref = bf16[1024,768]{1,0:T(8,128)(2,1)} custom-call(bf16[1024,2048]{1,0:T(8,128)(2,1)} %assemble.2.x_ref.refs_0_, f32[3,256]{1,0:T(4,128)} %fusion.20.bias_ref, f32[1024,128]{1,0:T(8,128)} %concatenate.51.cos_ref, f32[1024,128]{1,0:T(8,128)} %concatenate.52.left_ref, f32[1024,128]{1,0:T(8,128)} %concatenate.53.right_ref, ...), custom_call_target="tpu_custom_call" | custom-call | flops 3221225472 | bytes 7340032 | tf_op jit(solution)/shard_map/project_qkv/pallas_call | solution.py:100
  332.2 3.7 collective-permute-done.26.refs_9_.rest_7_
  339.4 9.2 %project_qkv.3.q_ref.k_ref.v_ref = bf16[1024,768]{1,0:T(8,128)(2,1)} custom-call(bf16[1024,2048]{1,0:T(8,128)(2,1)} %collective-permute-done.34.x_ref.refs_1_, f32[3,256]{1,0:T(4,128)} %fusion.20.bias_ref, f32[1024,128]{1,0:T(8,128)} %concatenate.51.cos_ref, f32[1024,128]{1,0:T(8,128)} %concatenate.52.left_ref, f32[1024,128]{1,0:T(8,128)} %concatenate.53.right_ref, ...), custom_call_target="tpu_custom_call" | custom-call | flops 3221225472 | bytes 7340032 | tf_op jit(solution)/shard_map/project_qkv/pallas_call | solution.py:100
  351.6 8.4 attend.3
  360.8 11.8 %project_up.3 = (bf16[1024,1024]{1,0:T(8,128)(2,1)}, bf16[1024,1024]{1,0:T(8,128)(2,1)}) custom-call(bf16[1024,2048]{1,0:T(8,128)(2,1)} %collective-permute-done.34.x_ref.refs_1_, f32[1,1024]{1,0:T(1,128)} %bitcast.13, bf16[256,1024]{1,0:T(8,128)(2,1)} %copy-done.28, bf16[256,1024]{1,0:T(8,128)(2,1)} %copy-done.59, ...), custom_call_target="tpu_custom_call" | custom-call | flops 4294967296 | bytes 8388608 | tf_op jit(solution)/shard_map/project_up/pallas_call | solution.py:149
  376.9 13.3 %branch_sums.3 = (bf16[256,2048]{1,0:T(8,128)(2,1)}, bf16[256,2048]{1,0:T(8,128)(2,1)}, bf16[256,2048]{1,0:T(8,128)(2,1)}, bf16[256,2048]{1,0:T(8,128)(2,1)}) custom-call(s32[1]{0:T(128)} %bitcast.at_ref, bf16[1024,256]{1,0:T(8,128)(2,1)} %get-tuple-element.100.refs_0_.mixed_ref.refs_1_, bf16[1024,1024]{1,0:T(8,128)(2,1)} %get-tuple-element.101.refs_1_, ...), custom_call_target="tpu_custom_call" | custom-call | flops 5368709120 | bytes 4194304 | tf_op jit(solution)/shard_map/branch_sums/pallas_call | solution.py:336
  390.3 8.4 attend.2
  399.2 11.9 %project_up.2 = (bf16[1024,1024]{1,0:T(8,128)(2,1)}, bf16[1024,1024]{1,0:T(8,128)(2,1)}) custom-call(bf16[1024,2048]{1,0:T(8,128)(2,1)} %assemble.2.x_ref.refs_0_, f32[1,1024]{1,0:T(1,128)} %bitcast.14, bf16[256,1024]{1,0:T(8,128)(2,1)} %copy-done.28, bf16[256,1024]{1,0:T(8,128)(2,1)} %copy-done.59, ...), custom_call_target="tpu_custom_call" | custom-call | flops 4294967296 | bytes 8388608 | tf_op jit(solution)/shard_map/project_up/pallas_call | solution.py:149
  411.1 13.3 %branch_sums.2 = (bf16[256,2048]{1,0:T(8,128)(2,1)}, bf16[256,2048]{1,0:T(8,128)(2,1)}, bf16[256,2048]{1,0:T(8,128)(2,1)}, bf16[256,2048]{1,0:T(8,128)(2,1)}) custom-call(s32[1]{0:T(128)} %bitcast.at_ref, bf16[1024,256]{1,0:T(8,128)(2,1)} %get-tuple-element.91.refs_0_.mixed_ref, bf16[1024,1024]{1,0:T(8,128)(2,1)} %get-tuple-element.94.refs_1_.refs_0_, ...), custom_call_target="tpu_custom_call" | custom-call | flops 5368709120 | bytes 4194304 | tf_op jit(solution)/shard_map/branch_sums/pallas_call | solution.py:336
  428.4 9.4 %collective-permute-start.39 = (bf16[256,2048]{1,0:T(8,128)(2,1)S(1)}, bf16[256,2048]{1,0:T(8,128)(2,1)}, u32[]{:S(2)}, u32[]{:S(2)}) collective-permute-start(bf16[256,2048]{1,0:T(8,128)(2,1)S(1)} %add_convert_fusion.8), channel_id=1, source_target_pairs={{0,1},{4,5},{8,9},{12,13},{16,17},{20,21},{24,25},{28,29}} | collective-permute-start | bytes 3145736 | tf_op jit(solution)/shard_map/ppermute | solution.py:590
  439.9 16.0 %collective-permute-done.50.refs_6_ = bf16[256,2048]{1,0:T(8,128)(2,1)} collective-permute-done((bf16[256,2048]{1,0:T(8,128)(2,1)}, bf16[256,2048]{1,0:T(8,128)(2,1)}, u32[]{:S(2)}, u32[]{:S(2)}) %collective-permute-start.50) | collective-permute-done | bytes 1048608 | tf_op jit(solution)/shard_map/ppermute | solution.py:574
  455.9 128.2 %assemble.3.dy_ref.refs_2_ = bf16[1024,2048]{1,0:T(8,128)(2,1)} custom-call(bf16[256,2048]{1,0:T(8,128)(2,1)} %refs_0_.1, bf16[256,2048]{1,0:T(8,128)(2,1)} %copy-done.14, bf16[256,2048]{1,0:T(8,128)(2,1)} %collective-permute-done.46.refs_2_, bf16[256,2048]{1,0:T(8,128)(2,1)} %copy-done.16, bf16[256,2048]{1,0:T(8,128)(2,1)} %copy-done.15, ...), custom_call_target="tpu_custom_call" | custom-call | bytes 8388608 | tf_op jit(solution)/shard_map/assemble/pallas_call | solution.py:550
  585.4 12.9 %grad_in.2 = (bf16[1024,256]{1,0:T(8,128)(2,1)}, bf16[1024,1024]{1,0:T(8,128)(2,1)}, f32[8,1024]{1,0:T(8,128)}, f32[8,2048]{1,0:T(8,128)}) custom-call(bf16[1024,2048]{1,0:T(8,128)(2,1)} %assemble.3.dy_ref.refs_2_, bf16[1024,1024]{1,0:T(8,128)(2,1)} %get-tuple-element.110.slope_ref, bf16[256,256]{1,0:T(8,128)(2,1)} %get-tuple-element.95.refs_2_.rest_0_, ...), custom_call_target="tpu_custom_call" | custom-call | flops 5368709120 | bytes 4194304 | tf_op jit(solution)/shard_map/grad_in/pallas_call | solution.py:383
  598.4 2.6 add_convert_fusion.7
  601.0 1.9 collective-permute-start.41
  602.9 14.0 %attend_back.2 = (bf16[1024,256]{1,0:T(8,128)(2,1)}, bf16[1024,256]{1,0:T(8,128)(2,1)}, bf16[1024,256]{1,0:T(8,128)(2,1)}, f32[2,8,128]{2,1,0:T(8,128)}) custom-call(bf16[1024,768]{1,0:T(8,128)(2,1)} %project_qkv.2.q_ref.k_ref.v_ref, bf16[1024,768]{1,0:T(8,128)(2,1)} %project_qkv.2.q_ref.k_ref.v_ref, bf16[1024,768]{1,0:T(8,128)(2,1)} %project_qkv.2.q_ref.k_ref.v_ref, ...), custom_call_target="tpu_custom_call" | custom-call | flops 10737418240 | tf_op jit(solution)/shard_map/attend_back/pallas_call | solution.py:294
  617.6 16.4 %grad_normed_sums.2 = (bf16[256,2048]{1,0:T(8,128)(2,1)}, bf16[256,2048]{1,0:T(8,128)(2,1)}, bf16[256,2048]{1,0:T(8,128)(2,1)}, bf16[256,2048]{1,0:T(8,128)(2,1)}) custom-call(s32[1]{0:T(128)} %bitcast.at_ref, bf16[1024,256]{1,0:T(8,128)(2,1)} %get-tuple-element.113.refs_0_.refs_2_, bf16[1024,256]{1,0:T(8,128)(2,1)} %get-tuple-element.114.refs_1_.refs_3_, ...), custom_call_target="tpu_custom_call" | custom-call | flops 7516192768 | bytes 4194304 | tf_op jit(solution)/shard_map/grad_normed_sums/pallas_call | solution.py:439
  635.9 16.0 %column_block_grads.3 = (bf16[1024,256]{1,0:T(8,128)(2,1)}, bf16[1024,256]{1,0:T(8,128)(2,1)}, bf16[1024,256]{1,0:T(8,128)(2,1)}, bf16[1024,256]{1,0:T(8,128)(2,...) custom-call(s32[1]{0:T(128)} %bitcast.2.at_ref, ...), custom_call_target="tpu_custom_call" | custom-call | flops 8589934592 | bytes 8388608 | tf_op jit(solution)/shard_map/column_block_grads/pallas_call | solution.py:510
  653.2 13.0 %grad_in.3 = (bf16[1024,256]{1,0:T(8,128)(2,1)}, bf16[1024,1024]{1,0:T(8,128)(2,1)}, f32[8,1024]{1,0:T(8,128)}, f32[8,2048]{1,0:T(8,128)}) custom-call(bf16[1024,2048]{1,0:T(8,128)(2,1)} %collective-permute-done.51.dy_ref.refs_3_, bf16[1024,1024]{1,0:T(8,128)(2,1)} %get-tuple-element.118.slope_ref, bf16[256,256]{1,0:T(8,128)(2,1)} %get-tuple-element.95.refs_2_.rest_0_, ...), custom_call_target="tpu_custom_call" | custom-call | flops 5368709120 | bytes 4194304 | tf_op jit(solution)/shard_map/grad_in/pallas_call | solution.py:383
  666.2 14.0 %attend_back.3 = (bf16[1024,256]{1,0:T(8,128)(2,1)}, bf16[1024,256]{1,0:T(8,128)(2,1)}, bf16[1024,256]{1,0:T(8,128)(2,1)}, f32[2,8,128]{2,1,0:T(8,128)}) custom-call(bf16[1024,768]{1,0:T(8,128)(2,1)} %project_qkv.3.q_ref.k_ref.v_ref, bf16[1024,768]{1,0:T(8,128)(2,1)} %project_qkv.3.q_ref.k_ref.v_ref, bf16[1024,768]{1,0:T(8,128)(2,1)} %project_qkv.3.q_ref.k_ref.v_ref, ...), custom_call_target="tpu_custom_call" | custom-call | flops 10737418240 | tf_op jit(solution)/shard_map/attend_back/pallas_call | solution.py:294
  683.3 9.1 column_block_grads.2
  695.1 15.9 %row_block_grads.3 = (bf16[256,1024]{1,0:T(8,128)(2,1)}, bf16[256,1024]{1,0:T(8,128)(2,1)}, bf16[256,1024]{1,0:T(8,128)(2,1)}, bf16[256,1024]{1,0:T(8,128)(2,1)}...) custom-call(s32[1]{0:T(128)} %bitcast.2.at_ref, ...), custom_call_target="tpu_custom_call" | custom-call | flops 8589934592 | bytes 8388608 | tf_op jit(solution)/shard_map/row_block_grads/pallas_call | solution.py:480
  712.4 16.4 %grad_normed_sums.3 = (bf16[256,2048]{1,0:T(8,128)(2,1)}, bf16[256,2048]{1,0:T(8,128)(2,1)}, bf16[256,2048]{1,0:T(8,128)(2,1)}, bf16[256,2048]{1,0:T(8,128)(2,1)}) custom-call(s32[1]{0:T(128)} %bitcast.at_ref, bf16[1024,256]{1,0:T(8,128)(2,1)} %get-tuple-element.121.refs_0_.refs_5_, bf16[1024,256]{1,0:T(8,128)(2,1)} %get-tuple-element.122.refs_1_.refs_6_, ...), custom_call_target="tpu_custom_call" | custom-call | flops 7516192768 | bytes 4194304 | tf_op jit(solution)/shard_map/grad_normed_sums/pallas_call | solution.py:439
  728.9 13.1 %row_block_grads.2 = (bf16[3,256,256]{2,1,0:T(8,128)(2,1)}, bf16[3,256,256]{2,1,0:T(8,128)(2,1)}, bf16[3,256,256]{2,1,0:T(8,128)(2,1)}, bf16[3,256,256]{2,1,0:T(...) custom-call(s32[1]{0:T(128)} %bitcast.2.at_ref, ...), custom_call_target="tpu_custom_call" | custom-call | flops 6442450944 | bytes 8388608 | tf_op jit(solution)/shard_map/row_block_grads/pallas_call | solution.py:480
  752.5 3.3 collective-permute-done.87
  765.3 13.9 %collective-permute-start.56 = (bf16[256,2048]{1,0:T(8,128)(2,1)S(1)}, bf16[256,2048]{1,0:T(8,128)(2,1)S(1)}, u32[]{:S(2)}, u32[]{:S(2)}) collective-permute-start(bf16[256,2048]{1,0:T(8,128)(2,1)S(1)} %add_convert_fusion.3), channel_id=1, source_target_pairs={{0,1},{4,5},{8,9},{12,13},{16,17},{20,21},{24,25},{28,29}} | collective-permute-start | bytes 3145736 | tf_op jit(solution)/shard_map/ppermute | solution.py:590
  784.3 10.5 %collective-permute-done.100 = bf16[1024,256]{1,0:T(8,128)(2,1)S(1)} collective-permute-done((bf16[1024,256]{1,0:T(8,128)(2,1)S(1)}, bf16[1024,256]{1,0:T(8,128)(2,1)S(1)}, u32[]{:S(2)}, u32[]{:S(2)}) %collective-permute-start.100) | collective-permute-done | bytes 524320 | tf_op jit(solution)/shard_map/ppermute | solution.py:567
  796.3 5.8 collective-permute-done.56
  804.3 4.8 collective-permute-start.58
  811.1 7.0 collective-permute-done.75
  820.4 6.1 collective-permute-done.74
  827.4 3.2 collective-permute-done.58
  834.8 3.0 collective-permute-done.99
  837.7 5.0 collective-permute-done.89
  843.4 5.5 collective-permute-done.92
  849.0 5.6 collective-permute-start.59
  854.5 4.0 collective-permute-done.98
  862.7 9.7 %collective-permute-done.91 = bf16[256,1024]{1,0:T(8,128)(2,1)S(1)} collective-permute-done((bf16[256,1024]{1,0:T(8,128)(2,1)S(1)}, bf16[256,1024]{1,0:T(8,128)(2,1)S(1)}, u32[]{:S(2)}, u32[]{:S(2)}) %collective-permute-start.91) | collective-permute-done | bytes 524320 | tf_op jit(solution)/shard_map/ppermute | solution.py:567
  872.8 4.3 collective-permute-start.42
  878.8 7.2 collective-permute-done.61
  899.3 2.4 collective-permute-done.67
  902.7 2.0 collective-permute-start.69
  904.7 2.5 collective-permute-start.71
  907.2 3.1 fusion.12
  (423 shorter events, 127.0 us)
Async XLA Ops:
  5.0 27.3 %collective-permute-start = (bf16[256,2048]{1,0:T(8,128)(2,1)S(1)}, bf16[256,2048]{1,0:T(8,128)(2,1)S(1)}, u32[]{:S(2)}, u32[]{:S(2)}) collective-permute-start(bf16[256,2048]{1,0:T(8,128)(2,1)S(1)} %fusion.7.refs_0_), channel_id=1, source_target_pairs={{0,1},{1,2},{2,3},{4,5},{5,6},{6,7},{8,9},{9,10},{10,11},{12,13},{... | collective-permute-start | bytes 3145736 | tf_op jit(solution)/shard_map/ppermute | solution.py:573
  10.0 26.5 %collective-permute-start.3 = (bf16[256,2048]{1,0:T(8,128)(2,1)S(1)}, bf16[256,2048]{1,0:T(8,128)(2,1)S(1)}, u32[]{:S(2)}, u32[]{:S(2)}) collective-permute-start(bf16[256,2048]{1,0:T(8,128)(2,1)S(1)} %fusion.7.refs_0_), channel_id=1, source_target_pairs={{1,0},{2,1},{3,2},{5,4},{6,5},{7,6},{9,8},{10,9},{11,10},{13,12},{... | collective-permute-start | bytes 3145736 | tf_op jit(solution)/shard_map/ppermute | solution.py:574
  36.5 25.8 %collective-permute-start.4 = (bf16[256,2048]{1,0:T(8,128)(2,1)S(1)}, bf16[256,2048]{1,0:T(8,128)(2,1)S(1)}, u32[]{:S(2)}, u32[]{:S(2)}) collective-permute-start(bf16[256,2048]{1,0:T(8,128)(2,1)S(1)} %collective-permute-done.3.refs_4_), channel_id=1, source_target_pairs={{1,0},{2,1},{5,4},{6,5},{9,8},{10,9},{13,12},{14,13},{17,16},{18,1... | collective-permute-start | bytes 3145736 | tf_op jit(solution)/shard_map/ppermute | solution.py:574
  37.8 25.8 %collective-permute-start.2 = (bf16[256,2048]{1,0:T(8,128)(2,1)S(1)}, bf16[256,2048]{1,0:T(8,128)(2,1)S(1)}, u32[]{:S(2)}, u32[]{:S(2)}) collective-permute-start(bf16[256,2048]{1,0:T(8,128)(2,1)S(1)} %collective-permute-done.1.refs_2_), channel_id=1, source_target_pairs={{2,3},{6,7},{10,11},{14,15},{18,19},{22,23},{26,27},{30,31}} | collective-permute-start | bytes 3145736 | tf_op jit(solution)/shard_map/ppermute | solution.py:573
  62.3 25.0 %collective-permute-start.5 = (bf16[256,2048]{1,0:T(8,128)(2,1)S(1)}, bf16[256,2048]{1,0:T(8,128)(2,1)}, u32[]{:S(2)}, u32[]{:S(2)}) collective-permute-start(bf16[256,2048]{1,0:T(8,128)(2,1)S(1)} %collective-permute-done.4.refs_5_), channel_id=1, source_target_pairs={{1,0},{5,4},{9,8},{13,12},{17,16},{21,20},{25,24},{29,28}} | collective-permute-start | bytes 3145736 | tf_op jit(solution)/shard_map/ppermute | solution.py:574
  215.5 122.4 %collective-permute-start.34 = (bf16[1024,2048]{1,0:T(8,128)(2,1)}, bf16[1024,2048]{1,0:T(8,128)(2,1)}, u32[]{:S(2)}, u32[]{:S(2)}) collective-permute-start(bf16[1024,2048]{1,0:T(8,128)(2,1)} %assemble.2.x_ref.refs_0_), channel_id=1, source_target_pairs={{0,4},{4,0},{8,12},{12,8},{16,20},{20,16},{24,28},{28,24},{1,5},{5... | collective-permute-start | bytes 12582920 | tf_op jit(solution)/shard_map/ppermute | solution.py:567
  235.4 24.1 %collective-permute-start.30 = (bf16[1024,256]{1,0:T(8,128)(2,1)S(1)}, bf16[1024,256]{1,0:T(8,128)(2,1)S(1)}, u32[]{:S(2)}, u32[]{:S(2)}) collective-permute-start(bf16[1024,256]{1,0:T(8,128)(2,1)S(1)} %get-tuple-element.97.refs_10_.rest_8_), channel_id=1, source_target_pairs={{0,16},{4,20},{8,24},{12,28},{16,0},{20,4},{24,8},{28,12},{1,17},{... | collective-permute-start | bytes 1572872 | tf_op jit(solution)/shard_map/ppermute | solution.py:567
  236.9 31.0 %collective-permute-start.10 = (bf16[3,256,256]{2,1,0:T(8,128)(2,1)}, bf16[3,256,256]{2,1,0:T(8,128)(2,1)S(1)}, u32[]{:S(2)}, u32[]{:S(2)}) collective-permute-start(bf16[3,256,256]{2,1,0:T(8,128)(2,1)} %collective-permute-done.6.rest_1_.refs_5_), channel_id=1, source_target_pairs={{0,16},{4,20},{8,24},{12,28},{16,0},{20,4},{24,8},{28,12},{1,17},{... | collective-permute-start | bytes 1179656 | tf_op jit(solution)/shard_map/ppermute | solution.py:567
  248.2 28.1 %collective-permute-start.11 = (bf16[3,256,256]{2,1,0:T(8,128)(2,1)}, bf16[3,256,256]{2,1,0:T(8,128)(2,1)S(1)}, u32[]{:S(2)}, u32[]{:S(2)}) collective-permute-start(bf16[3,256,256]{2,1,0:T(8,128)(2,1)} %collective-permute-done.7.rest_2_.refs_6_), channel_id=1, source_target_pairs={{0,16},{4,20},{8,24},{12,28},{16,0},{20,4},{24,8},{28,12},{1,17},{... | collective-permute-start | bytes 1179656 | tf_op jit(solution)/shard_map/ppermute | solution.py:567
  249.8 27.9 %collective-permute-start.14 = (bf16[256,1024]{1,0:T(8,128)(2,1)S(1)}, bf16[256,1024]{1,0:T(8,128)(2,1)}, u32[]{:S(2)}, u32[]{:S(2)}) collective-permute-start(bf16[256,1024]{1,0:T(8,128)(2,1)S(1)} %get-tuple-element.92.rest_0_.refs_12_), channel_id=1, source_target_pairs={{0,8},{4,12},{8,0},{12,4},{16,24},{20,28},{24,16},{28,20},{1,9},{5... | collective-permute-start | bytes 1572872 | tf_op jit(solution)/shard_map/ppermute | solution.py:567
  259.5 27.0 %collective-permute-start.17 = (bf16[256,1024]{1,0:T(8,128)(2,1)S(1)}, bf16[256,1024]{1,0:T(8,128)(2,1)S(1)}, u32[]{:S(2)}, u32[]{:S(2)}) collective-permute-start(bf16[256,1024]{1,0:T(8,128)(2,1)S(1)} %collective-permute-done.13.rest_1_.refs_13_), channel_id=1, source_target_pairs={{0,16},{4,20},{8,24},{12,28},{16,0},{20,4},{24,8},{28,12},{1,17},{... | collective-permute-start | bytes 1572872 | tf_op jit(solution)/shard_map/ppermute | solution.py:567
  277.7 43.3 %collective-permute-start.29 = (bf16[1024,256]{1,0:T(8,128)(2,1)}, bf16[1024,256]{1,0:T(8,128)(2,1)}, u32[]{:S(2)}, u32[]{:S(2)}) collective-permute-start(bf16[1024,256]{1,0:T(8,128)(2,1)} %collective-permute-done.27.refs_11_.rest_9_), channel_id=1, source_target_pairs={{0,8},{4,12},{8,0},{12,4},{16,24},{20,28},{24,16},{28,20},{1,9},{5... | collective-permute-start | bytes 1572872 | tf_op jit(solution)/shard_map/ppermute | solution.py:567
  279.2 42.4 %collective-permute-start.12 = (bf16[3,256,256]{2,1,0:T(8,128)(2,1)S(1)}, bf16[3,256,256]{2,1,0:T(8,128)(2,1)}, u32[]{:S(2)}, u32[]{:S(2)}) collective-permute-start(bf16[3,256,256]{2,1,0:T(8,128)(2,1)S(1)} %collective-permute-done.10.rest_5_.refs_9_), channel_id=1, source_target_pairs={{0,8},{4,12},{8,0},{12,4},{16,24},{20,28},{24,16},{28,20},{1,9},{5... | collective-permute-start | bytes 1179656 | tf_op jit(solution)/shard_map/ppermute | solution.py:567
  286.5 24.8 %collective-permute-start.21 = (bf16[256,256]{1,0:T(8,128)(2,1)}, bf16[256,256]{1,0:T(8,128)(2,1)S(1)}, u32[]{:S(2)}, u32[]{:S(2)}) collective-permute-start(bf16[256,256]{1,0:T(8,128)(2,1)} %get-tuple-element.95.refs_2_.rest_0_), channel_id=1, source_target_pairs={{0,8},{4,12},{8,0},{12,4},{16,24},{20,28},{24,16},{28,20},{1,9},{5... | collective-permute-start | bytes 393224 | tf_op jit(solution)/shard_map/ppermute | solution.py:567
  292.0 28.5 %collective-permute-start.24 = (bf16[256,256]{1,0:T(8,128)(2,1)}, bf16[256,256]{1,0:T(8,128)(2,1)}, u32[]{:S(2)}, u32[]{:S(2)}) collective-permute-start(bf16[256,256]{1,0:T(8,128)(2,1)} %collective-permute-done.20.refs_3_.rest_1_), channel_id=1, source_target_pairs={{0,16},{4,20},{8,24},{12,28},{16,0},{20,4},{24,8},{28,12},{1,17},{... | collective-permute-start | bytes 393224 | tf_op jit(solution)/shard_map/ppermute | solution.py:567
  311.3 25.2 %collective-permute-start.18 = (bf16[256,1024]{1,0:T(8,128)(2,1)}, bf16[256,1024]{1,0:T(8,128)(2,1)}, u32[]{:S(2)}, u32[]{:S(2)}) collective-permute-start(bf16[256,1024]{1,0:T(8,128)(2,1)} %collective-permute-done.14.rest_2_.refs_14_), channel_id=1, source_target_pairs={{0,16},{4,20},{8,24},{12,28},{16,0},{20,4},{24,8},{28,12},{1,17},{... | collective-permute-start | bytes 1572872 | tf_op jit(solution)/shard_map/ppermute | solution.py:567
  320.5 28.1 %collective-permute-start.31 = (bf16[1024,256]{1,0:T(8,128)(2,1)}, bf16[1024,256]{1,0:T(8,128)(2,1)S(1)}, u32[]{:S(2)}, u32[]{:S(2)}) collective-permute-start(bf16[1024,256]{1,0:T(8,128)(2,1)} %collective-permute-done.27.refs_11_.rest_9_), channel_id=1, source_target_pairs={{0,16},{4,20},{8,24},{12,28},{16,0},{20,4},{24,8},{28,12},{1,17},{... | collective-permute-start | bytes 1572872 | tf_op jit(solution)/shard_map/ppermute | solution.py:567
  321.0 29.1 %collective-permute-start.28 = (bf16[1024,256]{1,0:T(8,128)(2,1)S(1)}, bf16[1024,256]{1,0:T(8,128)(2,1)S(1)}, u32[]{:S(2)}, u32[]{:S(2)}) collective-permute-start(bf16[1024,256]{1,0:T(8,128)(2,1)S(1)} %copy-done.32), channel_id=1, source_target_pairs={{0,8},{4,12},{8,0},{12,4},{16,24},{20,28},{24,16},{28,20},{1,9},{5... | collective-permute-start | bytes 1572872 | tf_op jit(solution)/shard_map/ppermute | solution.py:567
  335.9 24.1 %collective-permute-start.19 = (bf16[256,1024]{1,0:T(8,128)(2,1)S(1)}, bf16[256,1024]{1,0:T(8,128)(2,1)S(1)}, u32[]{:S(2)}, u32[]{:S(2)}) collective-permute-start(bf16[256,1024]{1,0:T(8,128)(2,1)S(1)} %copy-done.62), channel_id=1, source_target_pairs={{0,8},{4,12},{8,0},{12,4},{16,24},{20,28},{24,16},{28,20},{1,9},{5... | collective-permute-start | bytes 1572872 | tf_op jit(solution)/shard_map/ppermute | solution.py:567
  336.5 36.2 %collective-permute-start.45 = (bf16[256,2048]{1,0:T(8,128)(2,1)S(1)}, bf16[256,2048]{1,0:T(8,128)(2,1)S(1)}, u32[]{:S(2)}, u32[]{:S(2)}) collective-permute-start(bf16[256,2048]{1,0:T(8,128)(2,1)S(1)} %copy-done.2), channel_id=1, source_target_pairs={{0,1},{1,2},{2,3},{4,5},{5,6},{6,7},{8,9},{9,10},{10,11},{12,13},{... | collective-permute-start | bytes 3145736 | tf_op jit(solution)/shard_map/ppermute | solution.py:573
  337.9 36.4 %collective-permute-start.48 = (bf16[256,2048]{1,0:T(8,128)(2,1)S(1)}, bf16[256,2048]{1,0:T(8,128)(2,1)S(1)}, u32[]{:S(2)}, u32[]{:S(2)}) collective-permute-start(bf16[256,2048]{1,0:T(8,128)(2,1)S(1)} %copy-done.2), channel_id=1, source_target_pairs={{1,0},{2,1},{3,2},{5,4},{6,5},{7,6},{9,8},{10,9},{11,10},{13,12},{... | collective-permute-start | bytes 3145736 | tf_op jit(solution)/shard_map/ppermute | solution.py:574
  348.6 27.3 %collective-permute-start.33 = (bf16[1024,256]{1,0:T(8,128)(2,1)S(1)}, bf16[1024,256]{1,0:T(8,128)(2,1)S(1)}, u32[]{:S(2)}, u32[]{:S(2)}) collective-permute-start(bf16[1024,256]{1,0:T(8,128)(2,1)S(1)} %collective-permute-done.31.refs_15_.rest_13_), channel_id=1, source_target_pairs={{0,8},{4,12},{8,0},{12,4},{16,24},{20,28},{24,16},{28,20},{1,9},{5... | collective-permute-start | bytes 1572872 | tf_op jit(solution)/shard_map/ppermute | solution.py:567
  350.1 25.8 %collective-permute-start.32 = (bf16[1024,256]{1,0:T(8,128)(2,1)S(1)}, bf16[1024,256]{1,0:T(8,128)(2,1)S(1)}, u32[]{:S(2)}, u32[]{:S(2)}) collective-permute-start(bf16[1024,256]{1,0:T(8,128)(2,1)S(1)} %collective-permute-done.28.refs_12_.rest_10_), channel_id=1, source_target_pairs={{0,16},{4,20},{8,24},{12,28},{16,0},{20,4},{24,8},{28,12},{1,17},{... | collective-permute-start | bytes 1572872 | tf_op jit(solution)/shard_map/ppermute | solution.py:567
  372.7 51.8 %collective-permute-start.46 = (bf16[256,2048]{1,0:T(8,128)(2,1)S(1)}, bf16[256,2048]{1,0:T(8,128)(2,1)}, u32[]{:S(2)}, u32[]{:S(2)}) collective-permute-start(bf16[256,2048]{1,0:T(8,128)(2,1)S(1)} %collective-permute-done.45.refs_1_), channel_id=1, source_target_pairs={{1,2},{2,3},{5,6},{6,7},{9,10},{10,11},{13,14},{14,15},{17,18},{18... | collective-permute-start | bytes 3145736 | tf_op jit(solution)/shard_map/ppermute | solution.py:573
  374.3 51.0 %collective-permute-start.49 = (bf16[256,2048]{1,0:T(8,128)(2,1)S(1)}, bf16[256,2048]{1,0:T(8,128)(2,1)}, u32[]{:S(2)}, u32[]{:S(2)}) collective-permute-start(bf16[256,2048]{1,0:T(8,128)(2,1)S(1)} %collective-permute-done.48.refs_4_), channel_id=1, source_target_pairs={{1,0},{2,1},{5,4},{6,5},{9,8},{10,9},{13,12},{14,13},{17,16},{18,1... | collective-permute-start | bytes 3145736 | tf_op jit(solution)/shard_map/ppermute | solution.py:574
  390.3 36.5 %collective-permute-start.38 = (bf16[256,2048]{1,0:T(8,128)(2,1)}, bf16[256,2048]{1,0:T(8,128)(2,1)S(1)}, u32[]{:S(2)}, u32[]{:S(2)}) collective-permute-start(bf16[256,2048]{1,0:T(8,128)(2,1)} %get-tuple-element.108), channel_id=1, source_target_pairs={{0,4},{4,0},{8,12},{12,8},{16,20},{20,16},{24,28},{28,24},{1,5},{5... | collective-permute-start | bytes 3145736 | tf_op jit(solution)/shard_map/ppermute | solution.py:567
  398.8 39.0 %collective-permute-start.36 = (bf16[256,2048]{1,0:T(8,128)(2,1)S(1)}, bf16[256,2048]{1,0:T(8,128)(2,1)S(1)}, u32[]{:S(2)}, u32[]{:S(2)}) collective-permute-start(bf16[256,2048]{1,0:T(8,128)(2,1)S(1)} %copy-done.58), channel_id=1, source_target_pairs={{0,4},{4,0},{8,12},{12,8},{16,20},{20,16},{24,28},{28,24},{1,5},{5... | collective-permute-start | bytes 3145736 | tf_op jit(solution)/shard_map/ppermute | solution.py:567
  425.3 30.6 %collective-permute-start.50 = (bf16[256,2048]{1,0:T(8,128)(2,1)}, bf16[256,2048]{1,0:T(8,128)(2,1)}, u32[]{:S(2)}, u32[]{:S(2)}) collective-permute-start(bf16[256,2048]{1,0:T(8,128)(2,1)} %collective-permute-done.49.refs_5_), channel_id=1, source_target_pairs={{1,0},{5,4},{9,8},{13,12},{17,16},{21,20},{25,24},{29,28}} | collective-permute-start | bytes 3145736 | tf_op jit(solution)/shard_map/ppermute | solution.py:574
  426.6 171.7 %collective-permute-start.37 = (bf16[256,2048]{1,0:T(8,128)(2,1)}, bf16[256,2048]{1,0:T(8,128)(2,1)}, u32[]{:S(2)}, u32[]{:S(2)}) collective-permute-start(bf16[256,2048]{1,0:T(8,128)(2,1)} %get-tuple-element.106), channel_id=1, source_target_pairs={{0,4},{4,0},{8,12},{12,8},{16,20},{20,16},{24,28},{28,24},{1,5},{5... | collective-permute-start | bytes 3145736 | tf_op jit(solution)/shard_map/ppermute | solution.py:567
  428.4 169.9 %collective-permute-start.39 = (bf16[256,2048]{1,0:T(8,128)(2,1)S(1)}, bf16[256,2048]{1,0:T(8,128)(2,1)}, u32[]{:S(2)}, u32[]{:S(2)}) collective-permute-start(bf16[256,2048]{1,0:T(8,128)(2,1)S(1)} %add_convert_fusion.8), channel_id=1, source_target_pairs={{0,1},{4,5},{8,9},{12,13},{16,17},{20,21},{24,25},{28,29}} | collective-permute-start | bytes 3145736 | tf_op jit(solution)/shard_map/ppermute | solution.py:590
  438.2 160.1 %collective-permute-start.40 = (bf16[256,2048]{1,0:T(8,128)(2,1)S(1)}, bf16[256,2048]{1,0:T(8,128)(2,1)}, u32[]{:S(2)}, u32[]{:S(2)}) collective-permute-start(bf16[256,2048]{1,0:T(8,128)(2,1)S(1)} %add_convert_fusion.9), channel_id=1, source_target_pairs={{3,2},{7,6},{11,10},{15,14},{19,18},{23,22},{27,26},{31,30}} | collective-permute-start | bytes 3145736 | tf_op jit(solution)/shard_map/ppermute | solution.py:591
  584.1 51.8 %collective-permute-start.51 = (bf16[1024,2048]{1,0:T(8,128)(2,1)}, bf16[1024,2048]{1,0:T(8,128)(2,1)}, u32[]{:S(2)}, u32[]{:S(2)}) collective-permute-start(bf16[1024,2048]{1,0:T(8,128)(2,1)} %assemble.3.dy_ref.refs_2_), channel_id=1, source_target_pairs={{0,4},{4,0},{8,12},{12,8},{16,20},{20,16},{24,28},{28,24},{1,5},{5... | collective-permute-start | bytes 12582920 | tf_op jit(solution)/shard_map/ppermute | solution.py:567
  601.0 33.0 %collective-permute-start.41 = (bf16[256,2048]{1,0:T(8,128)(2,1)S(1)}, bf16[256,2048]{1,0:T(8,128)(2,1)S(1)}, u32[]{:S(2)}, u32[]{:S(2)}) collective-permute-start(bf16[256,2048]{1,0:T(8,128)(2,1)S(1)} %add_convert_fusion.7), channel_id=1, source_target_pairs={{0,1},{1,2},{4,5},{5,6},{8,9},{9,10},{12,13},{13,14},{16,17},{17,1... | collective-permute-start | bytes 3145736 | tf_op jit(solution)/shard_map/ppermute | solution.py:590
  616.9 18.5 %collective-permute-start.43 = (bf16[256,2048]{1,0:T(8,128)(2,1)S(1)}, bf16[256,2048]{1,0:T(8,128)(2,1)S(1)}, u32[]{:S(2)}, u32[]{:S(2)}) collective-permute-start(bf16[256,2048]{1,0:T(8,128)(2,1)S(1)} %add_convert_fusion.7), channel_id=1, source_target_pairs={{2,1},{3,2},{6,5},{7,6},{10,9},{11,10},{14,13},{15,14},{18,17},{19... | collective-permute-start | bytes 3145736 | tf_op jit(solution)/shard_map/ppermute | solution.py:591
  651.9 130.4 %collective-permute-start.97 = (bf16[1024,256]{1,0:T(8,128)(2,1)}, bf16[1024,256]{1,0:T(8,128)(2,1)}, u32[]{:S(2)}, u32[]{:S(2)}) collective-permute-start(bf16[1024,256]{1,0:T(8,128)(2,1)} %get-tuple-element.165), channel_id=1, source_target_pairs={{0,16},{4,20},{8,24},{12,28},{16,0},{20,4},{24,8},{28,12},{1,17},{... | collective-permute-start | bytes 1572872 | tf_op jit(solution)/shard_map/ppermute | solution.py:567
  682.6 28.3 %collective-permute-start.79 = (f32[3840]{0:T(1024)S(1)}, f32[3840]{0:T(1024)S(1)}, u32[]{:S(2)}, u32[]{:S(2)}) collective-permute-start(f32[3840]{0:T(1024)S(1)} %pad_maximum_fusion.1), channel_id=1, source_target_pairs={{0,8},{4,12},{8,0},{12,4},{16,24},{20,28},{24,16},{28,20},{1,9},{5... | collective-permute-start | bytes 46088 | tf_op jit(solution)/shard_map/ppermute | solution.py:567
  692.4 57.0 %collective-permute-start.83 = (bf16[256,256]{1,0:T(8,128)(2,1)}, bf16[256,256]{1,0:T(8,128)(2,1)}, u32[]{:S(2)}, u32[]{:S(2)}) collective-permute-start(bf16[256,256]{1,0:T(8,128)(2,1)} %get-tuple-element.149), channel_id=1, source_target_pairs={{0,16},{4,20},{8,24},{12,28},{16,0},{20,4},{24,8},{28,12},{1,17},{... | collective-permute-start | bytes 393224 | tf_op jit(solution)/shard_map/ppermute | solution.py:567
  693.1 55.3 %collective-permute-start.86 = (bf16[256,256]{1,0:T(8,128)(2,1)}, bf16[256,256]{1,0:T(8,128)(2,1)}, u32[]{:S(2)}, u32[]{:S(2)}) collective-permute-start(bf16[256,256]{1,0:T(8,128)(2,1)} %get-tuple-element.153), channel_id=1, source_target_pairs={{0,8},{4,12},{8,0},{12,4},{16,24},{20,28},{24,16},{28,20},{1,9},{5... | collective-permute-start | bytes 393224 | tf_op jit(solution)/shard_map/ppermute | solution.py:567
  694.5 56.6 %collective-permute-start.85 = (bf16[256,256]{1,0:T(8,128)(2,1)}, bf16[256,256]{1,0:T(8,128)(2,1)}, u32[]{:S(2)}, u32[]{:S(2)}) collective-permute-start(bf16[256,256]{1,0:T(8,128)(2,1)} %get-tuple-element.151), channel_id=1, source_target_pairs={{0,8},{4,12},{8,0},{12,4},{16,24},{20,28},{24,16},{28,20},{1,9},{5... | collective-permute-start | bytes 393224 | tf_op jit(solution)/shard_map/ppermute | solution.py:567
  711.0 17.8 %collective-permute-start.80 = (f32[3840]{0:T(1024)S(1)}, f32[3840]{0:T(1024)S(1)}, u32[]{:S(2)}, u32[]{:S(2)}) collective-permute-start(f32[3840]{0:T(1024)S(1)} %fusion.21), channel_id=1, source_target_pairs={{0,16},{4,20},{8,24},{12,28},{16,0},{20,4},{24,8},{28,12},{1,17},{... | collective-permute-start | bytes 46088 | tf_op jit(solution)/shard_map/ppermute | solution.py:567
  742.1 21.4 %collective-permute-start.55 = (bf16[256,2048]{1,0:T(8,128)(2,1)}, bf16[256,2048]{1,0:T(8,128)(2,1)}, u32[]{:S(2)}, u32[]{:S(2)}) collective-permute-start(bf16[256,2048]{1,0:T(8,128)(2,1)} %get-tuple-element.131), channel_id=1, source_target_pairs={{0,4},{4,0},{8,12},{12,8},{16,20},{20,16},{24,28},{28,24},{1,5},{5... | collective-permute-start | bytes 3145736 | tf_op jit(solution)/shard_map/ppermute | solution.py:567
  748.4 16.9 %collective-permute-start.53 = (bf16[256,2048]{1,0:T(8,128)(2,1)}, bf16[256,2048]{1,0:T(8,128)(2,1)S(1)}, u32[]{:S(2)}, u32[]{:S(2)}) collective-permute-start(bf16[256,2048]{1,0:T(8,128)(2,1)} %get-tuple-element.127), channel_id=1, source_target_pairs={{0,4},{4,0},{8,12},{12,8},{16,20},{20,16},{24,28},{28,24},{1,5},{5... | collective-permute-start | bytes 3145736 | tf_op jit(solution)/shard_map/ppermute | solution.py:567
  758.2 21.4 %collective-permute-start.73 = (bf16[3,256,256]{2,1,0:T(8,128)(2,1)}, bf16[3,256,256]{2,1,0:T(8,128)(2,1)S(1)}, u32[]{:S(2)}, u32[]{:S(2)}) collective-permute-start(bf16[3,256,256]{2,1,0:T(8,128)(2,1)} %get-tuple-element.135), channel_id=1, source_target_pairs={{0,16},{4,20},{8,24},{12,28},{16,0},{20,4},{24,8},{28,12},{1,17},{... | collective-permute-start | bytes 1179656 | tf_op jit(solution)/shard_map/ppermute | solution.py:567
  762.1 18.6 %collective-permute-start.76 = (bf16[3,256,256]{2,1,0:T(8,128)(2,1)}, bf16[3,256,256]{2,1,0:T(8,128)(2,1)S(1)}, u32[]{:S(2)}, u32[]{:S(2)}) collective-permute-start(bf16[3,256,256]{2,1,0:T(8,128)(2,1)} %get-tuple-element.139), channel_id=1, source_target_pairs={{0,8},{4,12},{8,0},{12,4},{16,24},{20,28},{24,16},{28,20},{1,9},{5... | collective-permute-start | bytes 1179656 | tf_op jit(solution)/shard_map/ppermute | solution.py:567
  763.5 32.0 %collective-permute-start.54 = (bf16[256,2048]{1,0:T(8,128)(2,1)S(1)}, bf16[256,2048]{1,0:T(8,128)(2,1)S(1)}, u32[]{:S(2)}, u32[]{:S(2)}) collective-permute-start(bf16[256,2048]{1,0:T(8,128)(2,1)S(1)} %copy-done.57), channel_id=1, source_target_pairs={{0,4},{4,0},{8,12},{12,8},{16,20},{20,16},{24,28},{28,24},{1,5},{5... | collective-permute-start | bytes 3145736 | tf_op jit(solution)/shard_map/ppermute | solution.py:567
  765.3 36.9 %collective-permute-start.56 = (bf16[256,2048]{1,0:T(8,128)(2,1)S(1)}, bf16[256,2048]{1,0:T(8,128)(2,1)S(1)}, u32[]{:S(2)}, u32[]{:S(2)}) collective-permute-start(bf16[256,2048]{1,0:T(8,128)(2,1)S(1)} %add_convert_fusion.3), channel_id=1, source_target_pairs={{0,1},{4,5},{8,9},{12,13},{16,17},{20,21},{24,25},{28,29}} | collective-permute-start | bytes 3145736 | tf_op jit(solution)/shard_map/ppermute | solution.py:590
  779.6 23.1 %collective-permute-start.57 = (bf16[256,2048]{1,0:T(8,128)(2,1)S(1)}, bf16[256,2048]{1,0:T(8,128)(2,1)S(1)}, u32[]{:S(2)}, u32[]{:S(2)}) collective-permute-start(bf16[256,2048]{1,0:T(8,128)(2,1)S(1)} %add_convert_fusion.4), channel_id=1, source_target_pairs={{3,2},{7,6},{11,10},{15,14},{19,18},{23,22},{27,26},{31,30}} | collective-permute-start | bytes 3145736 | tf_op jit(solution)/shard_map/ppermute | solution.py:591
  782.3 22.0 %collective-permute-start.90 = (bf16[256,1024]{1,0:T(8,128)(2,1)S(1)}, bf16[256,1024]{1,0:T(8,128)(2,1)S(1)}, u32[]{:S(2)}, u32[]{:S(2)}) collective-permute-start(bf16[256,1024]{1,0:T(8,128)(2,1)S(1)} %copy-done.72), channel_id=1, source_target_pairs={{0,16},{4,20},{8,24},{12,28},{16,0},{20,4},{24,8},{28,12},{1,17},{... | collective-permute-start | bytes 1572872 | tf_op jit(solution)/shard_map/ppermute | solution.py:567
  795.5 24.2 %collective-permute-start.72 = (bf16[3,256,256]{2,1,0:T(8,128)(2,1)S(1)}, bf16[3,256,256]{2,1,0:T(8,128)(2,1)S(1)}, u32[]{:S(2)}, u32[]{:S(2)}) collective-permute-start(bf16[3,256,256]{2,1,0:T(8,128)(2,1)S(1)} %copy-done.81), channel_id=1, source_target_pairs={{0,16},{4,20},{8,24},{12,28},{16,0},{20,4},{24,8},{28,12},{1,17},{... | collective-permute-start | bytes 1179656 | tf_op jit(solution)/shard_map/ppermute | solution.py:567
  802.7 16.1 %collective-permute-start.77 = (bf16[3,256,256]{2,1,0:T(8,128)(2,1)S(1)}, bf16[3,256,256]{2,1,0:T(8,128)(2,1)S(1)}, u32[]{:S(2)}, u32[]{:S(2)}) collective-permute-start(bf16[3,256,256]{2,1,0:T(8,128)(2,1)S(1)} %add_convert_fusion.17), channel_id=1, source_target_pairs={{0,16},{4,20},{8,24},{12,28},{16,0},{20,4},{24,8},{28,12},{1,17},{... | collective-permute-start | bytes 1179656 | tf_op jit(solution)/shard_map/ppermute | solution.py:567
  804.3 26.2 %collective-permute-start.58 = (bf16[256,2048]{1,0:T(8,128)(2,1)S(1)}, bf16[256,2048]{1,0:T(8,128)(2,1)S(1)}, u32[]{:S(2)}, u32[]{:S(2)}) collective-permute-start(bf16[256,2048]{1,0:T(8,128)(2,1)S(1)} %add_convert_fusion.2), channel_id=1, source_target_pairs={{0,1},{1,2},{4,5},{5,6},{8,9},{9,10},{12,13},{13,14},{16,17},{17,1... | collective-permute-start | bytes 3145736 | tf_op jit(solution)/shard_map/ppermute | solution.py:590
  809.6 16.9 %collective-permute-start.74 = (bf16[3,256,256]{2,1,0:T(8,128)(2,1)S(1)}, bf16[3,256,256]{2,1,0:T(8,128)(2,1)S(1)}, u32[]{:S(2)}, u32[]{:S(2)}) collective-permute-start(bf16[3,256,256]{2,1,0:T(8,128)(2,1)S(1)} %add_convert_fusion.18), channel_id=1, source_target_pairs={{0,8},{4,12},{8,0},{12,4},{16,24},{20,28},{24,16},{28,20},{1,9},{5... | collective-permute-start | bytes 1179656 | tf_op jit(solution)/shard_map/ppermute | solution.py:567
  819.7 18.0 %collective-permute-start.99 = (bf16[1024,256]{1,0:T(8,128)(2,1)S(1)}, bf16[1024,256]{1,0:T(8,128)(2,1)S(1)}, u32[]{:S(2)}, u32[]{:S(2)}) collective-permute-start(bf16[1024,256]{1,0:T(8,128)(2,1)S(1)} %copy-done.63), channel_id=1, source_target_pairs={{0,8},{4,12},{8,0},{12,4},{16,24},{20,28},{24,16},{28,20},{1,9},{5... | collective-permute-start | bytes 1572872 | tf_op jit(solution)/shard_map/ppermute | solution.py:567
  826.5 16.2 %collective-permute-start.89 = (bf16[256,1024]{1,0:T(8,128)(2,1)S(1)}, bf16[256,1024]{1,0:T(8,128)(2,1)S(1)}, u32[]{:S(2)}, u32[]{:S(2)}) collective-permute-start(bf16[256,1024]{1,0:T(8,128)(2,1)S(1)} %copy-done.68), channel_id=1, source_target_pairs={{0,16},{4,20},{8,24},{12,28},{16,0},{20,4},{24,8},{28,12},{1,17},{... | collective-permute-start | bytes 1572872 | tf_op jit(solution)/shard_map/ppermute | solution.py:567
  830.5 18.4 %collective-permute-start.92 = (bf16[256,1024]{1,0:T(8,128)(2,1)S(1)}, bf16[256,1024]{1,0:T(8,128)(2,1)S(1)}, u32[]{:S(2)}, u32[]{:S(2)}) collective-permute-start(bf16[256,1024]{1,0:T(8,128)(2,1)S(1)} %copy-done.67), channel_id=1, source_target_pairs={{0,8},{4,12},{8,0},{12,4},{16,24},{20,28},{24,16},{28,20},{1,9},{5... | collective-permute-start | bytes 1572872 | tf_op jit(solution)/shard_map/ppermute | solution.py:567
  832.4 26.1 %collective-permute-start.98 = (bf16[1024,256]{1,0:T(8,128)(2,1)S(1)}, bf16[1024,256]{1,0:T(8,128)(2,1)S(1)}, u32[]{:S(2)}, u32[]{:S(2)}) collective-permute-start(bf16[1024,256]{1,0:T(8,128)(2,1)S(1)} %add_convert_fusion.12), channel_id=1, source_target_pairs={{0,8},{4,12},{8,0},{12,4},{16,24},{20,28},{24,16},{28,20},{1,9},{5... | collective-permute-start | bytes 1572872 | tf_op jit(solution)/shard_map/ppermute | solution.py:567
  833.1 27.0 %collective-permute-start.101 = (bf16[1024,256]{1,0:T(8,128)(2,1)S(1)}, bf16[1024,256]{1,0:T(8,128)(2,1)S(1)}, u32[]{:S(2)}, u32[]{:S(2)}) collective-permute-start(bf16[1024,256]{1,0:T(8,128)(2,1)S(1)} %add_convert_fusion.11), channel_id=1, source_target_pairs={{0,16},{4,20},{8,24},{12,28},{16,0},{20,4},{24,8},{28,12},{1,17},{... | collective-permute-start | bytes 1572872 | tf_op jit(solution)/shard_map/ppermute | solution.py:567
  837.7 39.4 %collective-permute-start.52 = (bf16[256,2048]{1,0:T(8,128)(2,1)S(1)}, bf16[256,2048]{1,0:T(8,128)(2,1)S(1)}, u32[]{:S(2)}, u32[]{:S(2)}) collective-permute-start(bf16[256,2048]{1,0:T(8,128)(2,1)S(1)} %copy-done.56), channel_id=1, source_target_pairs={{0,4},{4,0},{8,12},{12,8},{16,20},{20,16},{24,28},{28,24},{1,5},{5... | collective-permute-start | bytes 3145736 | tf_op jit(solution)/shard_map/ppermute | solution.py:567
  842.7 19.7 %collective-permute-start.94 = (bf16[256,1024]{1,0:T(8,128)(2,1)S(1)}, bf16[256,1024]{1,0:T(8,128)(2,1)S(1)}, u32[]{:S(2)}, u32[]{:S(2)}) collective-permute-start(bf16[256,1024]{1,0:T(8,128)(2,1)S(1)} %add_convert_fusion.14), channel_id=1, source_target_pairs={{0,16},{4,20},{8,24},{12,28},{16,0},{20,4},{24,8},{28,12},{1,17},{... | collective-permute-start | bytes 1572872 | tf_op jit(solution)/shard_map/ppermute | solution.py:567
  849.0 29.5 %collective-permute-start.59 = (bf16[256,2048]{1,0:T(8,128)(2,1)S(1)}, bf16[256,2048]{1,0:T(8,128)(2,1)S(1)}, u32[]{:S(2)}, u32[]{:S(2)}) collective-permute-start(bf16[256,2048]{1,0:T(8,128)(2,1)S(1)} %add_convert_fusion.1), channel_id=1, source_target_pairs={{0,1},{1,2},{2,3},{4,5},{5,6},{6,7},{8,9},{9,10},{10,11},{12,13},{... | collective-permute-start | bytes 3145736 | tf_op jit(solution)/shard_map/ppermute | solution.py:590
  858.5 27.4 %collective-permute-start.61 = (bf16[256,2048]{1,0:T(8,128)(2,1)S(1)}, bf16[256,2048]{1,0:T(8,128)(2,1)S(1)}, u32[]{:S(2)}, u32[]{:S(2)}) collective-permute-start(bf16[256,2048]{1,0:T(8,128)(2,1)S(1)} %add_convert_fusion), channel_id=1, source_target_pairs={{1,0},{2,1},{3,2},{5,4},{6,5},{7,6},{9,8},{10,9},{11,10},{13,12},{... | collective-permute-start | bytes 3145736 | tf_op jit(solution)/shard_map/ppermute | solution.py:591
  872.5 32.2 %collective-permute-start.35 = (bf16[256,2048]{1,0:T(8,128)(2,1)S(1)}, bf16[256,2048]{1,0:T(8,128)(2,1)S(1)}, u32[]{:S(2)}, u32[]{:S(2)}) collective-permute-start(bf16[256,2048]{1,0:T(8,128)(2,1)S(1)} %copy-done.55), channel_id=1, source_target_pairs={{0,4},{4,0},{8,12},{12,8},{16,20},{20,16},{24,28},{28,24},{1,5},{5... | collective-permute-start | bytes 3145736 | tf_op jit(solution)/shard_map/ppermute | solution.py:567
  872.8 34.4 %collective-permute-start.42 = (bf16[256,2048]{1,0:T(8,128)(2,1)S(1)}, bf16[256,2048]{1,0:T(8,128)(2,1)S(1)}, u32[]{:S(2)}, u32[]{:S(2)}) collective-permute-start(bf16[256,2048]{1,0:T(8,128)(2,1)S(1)} %copy-done.4), channel_id=1, source_target_pairs={{0,1},{1,2},{2,3},{4,5},{5,6},{6,7},{8,9},{9,10},{10,11},{12,13},{... | collective-permute-start | bytes 3145736 | tf_op jit(solution)/shard_map/ppermute | solution.py:590
  877.2 30.0 %collective-permute-start.44 = (bf16[256,2048]{1,0:T(8,128)(2,1)S(1)}, bf16[256,2048]{1,0:T(8,128)(2,1)S(1)}, u32[]{:S(2)}, u32[]{:S(2)}) collective-permute-start(bf16[256,2048]{1,0:T(8,128)(2,1)S(1)} %add_convert_fusion.5), channel_id=1, source_target_pairs={{1,0},{2,1},{3,2},{5,4},{6,5},{7,6},{9,8},{10,9},{11,10},{13,12},{... | collective-permute-start | bytes 3145736 | tf_op jit(solution)/shard_map/ppermute | solution.py:591
  (127 other events, 2539.4 us)

commit v2 on v0

v2 whole, which is shorter than its diff:
```python
import functools

import jax
import jax.numpy as jnp
from jax import lax
from jax.experimental import pallas as pl
from jax.experimental.pallas import tpu as pltpu
from jax.sharding import PartitionSpec as P

HEAD_DIM = 64
ROT = 32
EPS = 1e-05
LANES = 128
VMEM_LIMIT = 56 << 20
F32 = jnp.float32
BF16 = jnp.bfloat16
ANY = pl.BlockSpec(memory_space=pl.ANY)


def dot(lhs, rhs, lhs_dim, rhs_dim):
    return lax.dot_general(
        lhs, rhs, (((lhs_dim,), (rhs_dim,)), ((), ())), preferred_element_type=F32
    )


def call(kernel, name, operands, deps=(), scalars=(), **spec):
    deps, many, lead = tuple(deps), len(operands), len(scalars)

    def body(*refs):
        kernel(*refs[: lead + many], *refs[lead + many + len(deps) :])

    in_specs = list(spec.pop("in_specs")) + [ANY] * len(deps)
    out_shape, aliases = spec.pop("out_shape"), spec.pop("input_output_aliases", {})
    if scalars:
        grid_spec = pltpu.PrefetchScalarGridSpec(
            num_scalar_prefetch=lead, in_specs=in_specs, **spec
        )
        spec = {"grid_spec": grid_spec}
    else:
        spec["in_specs"] = in_specs
    return pl.pallas_call(
        body,
        out_shape=out_shape,
        input_output_aliases=aliases,
        compiler_params=pltpu.CompilerParams(vmem_limit_bytes=VMEM_LIMIT),
        cost_estimate=pl.CostEstimate(flops=0, transcendentals=0, bytes_accessed=0),
        name=name,
        **spec,
    )(*scalars, *operands, *deps)


def tie(value, *deps):
    return call(
        lambda *refs: None,
        "tie",
        [value],
        deps,
        in_specs=[ANY],
        out_specs=ANY,
        out_shape=jax.ShapeDtypeStruct(value.shape, value.dtype),
        input_output_aliases={0: 0},
    )


def rotary_tables(length):
    positions = jnp.arange(length).astype(F32)
    frequency = 10000.0 ** (-jnp.arange(ROT // 2).astype(F32) * 2.0 / ROT)
    angles = positions[:, None] * frequency[None, :]
    cosine, sine = jnp.cos(angles), jnp.sin(angles)
    rest = HEAD_DIM - ROT
    none = jnp.zeros((length, ROT // 2), F32)
    ones, zeros = jnp.ones((length, rest), F32), jnp.zeros((length, rest), F32)
    straight = jnp.concatenate([cosine, cosine, ones], axis=1)
    left = jnp.concatenate([-sine, none, zeros], axis=1)
    right = jnp.concatenate([none, sine, zeros], axis=1)
    return [jnp.concatenate([t, t], axis=1) for t in (straight, left, right)]


def rotated(u, straight, left, right, sign):
    half = ROT // 2
    turned = pltpu.roll(u, LANES - half, 1) * left + pltpu.roll(u, half, 1) * right
    return u * straight + sign * turned


def normalized(x):
    x = x.astype(F32)
    centered = x - jnp.mean(x, axis=1, keepdims=True)
    variance = jnp.mean(centered * centered, axis=1, keepdims=True)
    return centered * lax.rsqrt(variance + EPS)


def block_copies(blocks, place, sems):
    me = lax.axis_index("dp")
    return [
        pltpu.make_async_copy(block, place(lax.bitwise_xor(me, j)), sems.at[j])
        for j, block in enumerate(blocks)
    ]


def rows_at(ref, size):
    return lambda owner: ref.at[pl.ds(pl.multiple_of(owner * size, size), size)]


def columns_at(ref, size):
    return lambda owner: ref.at[:, pl.ds(pl.multiple_of(owner * size, size), size)]


class Chunks:
    def __init__(self, own, below, above):
        self.own, self.below, self.above = own, list(below), list(above)

    def flat(self):
        return [self.own, *self.below, *self.above]

    @staticmethod
    def of(refs):
        half = len(refs) // 2
        return Chunks(refs[0], refs[1 : 1 + half], refs[1 + half :])


def chunk_copies(chunks, places, parts, held, sems):
    z = lax.axis_index("mp")
    found = []
    for s, sequence in enumerate(chunks):
        for i, m in enumerate(places):
            slot = s * len(places) + i
            options = []
            if m == 0:
                options.append((None, sequence.own))
            else:
                moves = {(at ^ m) - at for at in range(parts)}
                for move in sorted(moves):
                    source = sequence.above[move - 1] if move > 0 else sequence.below[-move - 1]
                    options.append((lax.bitwise_xor(z, m) - z == move, source))
            found.append(
                [
                    (here, pltpu.make_async_copy(source, held.at[slot], sems.at[slot]))
                    for here, source in options
                ]
            )
    return found


def start_all(found):
    for options in found:
        for here, copy in options:
            if here is None:
                copy.start()
            else:
                pl.when(here)(copy.start)


def wait_for(options):
    options[0][1].wait()


def project_kernel(setup, at_ref, bias_ref, gain_ref, shift_ref, cos_ref, left_ref, right_ref, *rest):
    count, parts, places, width, hidden = setup
    refs = 2 * parts - 1
    chunks = [Chunks.of(rest[:refs]), Chunks.of(rest[refs : 2 * refs])]
    blocks, rest = rest[2 * refs : 2 * refs + count], rest[2 * refs + count :]
    qkv_ref, act_ref, slope_ref, normed_ref, tokens_ref, held, x_held, ready, sems, x_sems = rest
    step, steps = pl.program_id(0), 2 * len(places)
    found = chunk_copies(chunks, places, parts, x_held, x_sems)
    loads = block_copies(blocks, rows_at(held, blocks[0].shape[0]), sems)

    def norm(slot):
        return (normalized(x_held[slot]) * gain_ref[...] + shift_ref[...]).astype(BF16)

    @pl.when(step == 0)
    def _():
        for copy in loads:
            copy.start()
        start_all(found)
        wait_for(found[0])
        ready[0] = norm(0)
        for copy in loads:
            copy.wait()

    for slot in range(1, steps):

        @pl.when(step == slot - 1)
        def _(slot=slot):
            wait_for(found[slot])

    x = ready[step % 2]
    normed_ref[...] = x
    tokens_ref[...] = x_held[step]
    ready[(step + 1) % 2] = norm((step + 1) % steps)
    root = 0.7978845608028654
    for t in range((3 * width + hidden) // width):
        columns = slice(t * width, (t + 1) * width)
        y = dot(x, held[:, columns], 1, 0) + bias_ref[:, columns]
        if t < 3:
            for g in range(width // LANES):
                part = y[:, g * LANES : (g + 1) * LANES]
                if t < 2:
                    part = rotated(part, cos_ref[...], left_ref[...], right_ref[...], 1.0)
                if t == 0:
                    part = part * HEAD_DIM**-0.5
                start = t * width + g * LANES
                qkv_ref[:, start : start + LANES] = part.astype(BF16)
        else:
            columns = slice((t - 3) * width, (t - 2) * width)
            square = y * y
            turn = jnp.tanh(root * y * (1.0 + 0.044715 * square))
            half = 0.5 * (1.0 + turn)
            act_ref[:, columns] = (y * half).astype(BF16)
            slope = half * (1.0 + y * (1.0 - turn) * (root + (3.0 * 0.044715 * root) * square))
            slope_ref[:, columns] = slope.astype(BF16)


def project(at_mp, chunks, blocks, bias, gain, shift, tables, width, deps):
    parts, places = len(chunks[0].below) + 1, tuple(range(len(chunks[0].below) + 1))
    rows, model = chunks[0].own.shape
    total, hidden = blocks[0].shape[1], blocks[0].shape[1] - 3 * width
    count, length = len(blocks), 2 * parts * rows
    table = pl.BlockSpec((rows, LANES), lambda i, at: (at[0] ^ (i % parts), 0))
    out = lambda w: pl.BlockSpec((rows, w), lambda i, at: (i - i % parts + (at[0] ^ (i % parts)), 0))
    line = lambda a: pl.BlockSpec(a.shape, lambda i, at: (0, 0))
    widths = (3 * width, hidden, hidden, model, model)
    setup = (count, parts, places, width, hidden)
    return call(
        functools.partial(project_kernel, setup),
        "project",
        [bias, gain, shift, *tables, *chunks[0].flat(), *chunks[1].flat(), *blocks],
        deps,
        (at_mp,),
        grid=(2 * parts,),
        in_specs=[line(bias), line(gain), line(shift), table, table, table]
        + [ANY] * (2 * (2 * parts - 1) + count),
        out_specs=[out(w) for w in widths],
        out_shape=[jax.ShapeDtypeStruct((length, w), BF16) for w in widths],
        scratch_shapes=[
            pltpu.VMEM((model, total), BF16),
            pltpu.VMEM((2 * parts, rows, model), BF16),
            pltpu.VMEM((2, rows, model), BF16),
            pltpu.SemaphoreType.DMA((count,)),
            pltpu.SemaphoreType.DMA((2 * parts,)),
        ],
    )


def attend_kernel(block, q_ref, k_ref, v_ref, out_ref, lse_ref):
    length = q_ref.shape[0]
    lane = lax.broadcasted_iota(jnp.int32, (1, LANES), 1)
    key = lax.broadcasted_iota(jnp.int32, (block, block), 0)
    causal = key <= lax.broadcasted_iota(jnp.int32, (block, block), 1)
    for i in range(length // block):
        rows, before = pl.ds(i * block, block), pl.ds(0, i * block)
        results = []
        for h in range(2):
            mine = (lane < HEAD_DIM) if h == 0 else (lane >= HEAD_DIM)
            query = jnp.where(mine, q_ref[rows, :], 0)
            near = jnp.where(causal, dot(k_ref[rows, :], query, 1, 1), -1e30)
            highest = jnp.max(near, axis=0, keepdims=True)
            if i:
                far = dot(k_ref[before, :], query, 1, 1)
                highest = jnp.maximum(highest, jnp.max(far, axis=0, keepdims=True))
            near = jnp.exp(near - highest)
            total = jnp.sum(near, axis=0, keepdims=True)
            if i:
                far = jnp.exp(far - highest)
                total = total + jnp.sum(far, axis=0, keepdims=True)
            inverse = 1.0 / total
            result = dot((near * inverse).astype(BF16), v_ref[rows, :], 0, 0)
            if i:
                result = result + dot((far * inverse).astype(BF16), v_ref[before, :], 0, 0)
            results.append(result)
            lse_ref[0, h : h + 1, rows] = highest + jnp.log(total)
        out_ref[rows, :] = jnp.where(lane < HEAD_DIM, results[0], results[1]).astype(BF16)


def pair_specs(length, pairs):
    return lambda off: pl.BlockSpec(
        (length, LANES), lambda g: (g // pairs, off * pairs + g % pairs)
    )


def attend(qkv, length, block, deps):
    width, sequences = qkv.shape[1] // 3, qkv.shape[0] // length
    pairs = width // LANES
    at = pair_specs(length, pairs)
    return call(
        functools.partial(attend_kernel, block),
        "attend",
        [qkv, qkv, qkv],
        deps,
        grid=(sequences * pairs,),
        in_specs=[at(0), at(1), at(2)],
        out_specs=[at(0), pl.BlockSpec((1, 8, length), lambda g: (g, 0, 0))],
        out_shape=[
            jax.ShapeDtypeStruct((qkv.shape[0], width), BF16),
            jax.ShapeDtypeStruct((sequences * pairs, 8, length), F32),
        ],
    )


def attend_back_kernel(
    block,
    q_ref,
    k_ref,
    v_ref,
    grad_ref,
    mixed_ref,
    lse_ref,
    cos_ref,
    left_ref,
    right_ref,
    gq_ref,
    gk_ref,
    gv_ref,
    sum_ref,
    gk_sum,
    gv_sum,
):
    length = q_ref.shape[0]
    lane = lax.broadcasted_iota(jnp.int32, (1, LANES), 1)
    key = lax.broadcasted_iota(jnp.int32, (block, block), 0)
    causal = key <= lax.broadcasted_iota(jnp.int32, (block, block), 1)
    count = length // block
    sum_ref[...] = jnp.zeros_like(sum_ref)

    def put(ref, which, rows, value):
        value = value.astype(BF16)
        ref[rows, :] = value
        sum_ref[0, which : which + 1, :] += jnp.sum(value.astype(F32), axis=0, keepdims=True)

    def unrotated(value, rows):
        return rotated(value, cos_ref[rows, :], left_ref[rows, :], right_ref[rows, :], -1.0)

    for i in reversed(range(count)):
        rows = pl.ds(i * block, block)
        product = grad_ref[rows, :].astype(F32) * mixed_ref[rows, :].astype(F32)
        gq = None
        for h in range(2):
            mine = (lane < HEAD_DIM) if h == 0 else (lane >= HEAD_DIM)
            query = jnp.where(mine, q_ref[rows, :], 0)
            grad = jnp.where(mine, grad_ref[rows, :], 0)
            ones = jnp.where(mine, jnp.ones((8, LANES), F32), 0.0)
            delta = lax.dot_general(
                ones,
                product,
                (((1,), (1,)), ((), ())),
                precision=lax.Precision.HIGHEST,
                preferred_element_type=F32,
            )[0:1, :]
            lse = lse_ref[0, h : h + 1, rows]
            for j in range(i + 1):
                keys = pl.ds(j * block, block)
                key_rows = k_ref[keys, :]
                probs = jnp.exp(dot(key_rows, query, 1, 1) - lse)
                if j == i:
                    probs = jnp.where(causal, probs, 0.0)
                gprobs = dot(v_ref[keys, :], grad, 1, 1)
                gscores = (probs * (gprobs - delta)).astype(BF16)
                gv, gk = dot(probs.astype(BF16), grad, 1, 0), dot(gscores, query, 1, 0)
                if i == count - 1 and h == 0:
                    gv_sum[keys, :] = gv
                    gk_sum[keys, :] = gk
                else:
                    gv_sum[keys, :] += gv
                    gk_sum[keys, :] += gk
                part = dot(gscores, jnp.where(mine, key_rows, 0), 0, 0)
                gq = part if gq is None else gq + part
        put(gq_ref, 0, rows, unrotated(gq * HEAD_DIM**-0.5, rows))
    for i in range(count):
        rows = pl.ds(i * block, block)
        put(gk_ref, 1, rows, unrotated(gk_sum[rows, :], rows))
        put(gv_ref, 2, rows, gv_sum[rows, :])


def attend_back(qkv, grad, mixed, lse, tables, length, block, deps):
    width, sequences = qkv.shape[1] // 3, qkv.shape[0] // length
    pairs = width // LANES
    at = pair_specs(length, pairs)
    table = pl.BlockSpec((length, LANES), lambda g: (0, 0))
    small = pl.BlockSpec((1, 8, length), lambda g: (g, 0, 0))
    return call(
        functools.partial(attend_back_kernel, block),
        "attend_back",
        [qkv, qkv, qkv, grad, mixed, lse, *tables],
        deps,
        grid=(sequences * pairs,),
        in_specs=[at(0), at(1), at(2), at(0), at(0), small, table, table, table],
        out_specs=[at(0)] * 3 + [pl.BlockSpec((1, 8, LANES), lambda g: (g, 0, 0))],
        out_shape=[jax.ShapeDtypeStruct((qkv.shape[0], width), BF16)] * 3
        + [jax.ShapeDtypeStruct((sequences * pairs, 8, LANES), F32)],
        scratch_shapes=[pltpu.VMEM((length, LANES), F32)] * 2,
    )


def quarter_map(places, parts):
    turns = len(places)

    def rows_of(i, at):
        offset = jnp.int32(places[0])
        for n in range(1, turns):
            offset = jnp.where(i % turns == n, places[n], offset)
        return jnp.where(i < turns, parts, 0) + (at[0] + offset) % parts

    return rows_of


def split_outputs(step, turns, result, other_ref, own_ref):
    @pl.when(step < turns)
    def _():
        other_ref[0] = result

    @pl.when(step >= turns)
    def _():
        own_ref[0] = result


def split_specs(rows, model, turns):
    return [
        pl.BlockSpec((1, rows, model), lambda i, at: (jnp.minimum(i, turns - 1), 0, 0)),
        pl.BlockSpec((1, rows, model), lambda i, at: (jnp.maximum(i - turns, 0), 0, 0)),
    ]


def branch_kernel(count, turns, at_ref, mixed_ref, act_ref, *rest):
    blocks, (other_ref, own_ref, held, sems) = rest[:count], rest[count:]
    step = pl.program_id(0)

    @pl.when(step == 0)
    def _():
        loads = block_copies(blocks, columns_at(held, blocks[0].shape[1]), sems)
        for copy in loads:
            copy.start()
        for copy in loads:
            copy.wait()

    x = jnp.concatenate([mixed_ref[...], act_ref[...]], axis=1)
    split_outputs(step, turns, dot(x, held[...], 1, 0).astype(BF16), other_ref, own_ref)


def branch_sums(at_mp, mixed, act, blocks, parts, places, deps):
    rows, count, turns = mixed.shape[0] // (2 * parts), len(blocks), len(places)
    inner, model = blocks[0].shape[0], count * blocks[0].shape[1]
    where = quarter_map(places, parts)
    return call(
        functools.partial(branch_kernel, count, turns),
        "branch_sums",
        [mixed, act, *blocks],
        deps,
        (at_mp,),
        grid=(2 * turns,),
        in_specs=[
            pl.BlockSpec((rows, a.shape[1]), lambda i, at: (where(i, at), 0)) for a in (mixed, act)
        ]
        + [ANY] * count,
        out_specs=split_specs(rows, model, turns),
        out_shape=[jax.ShapeDtypeStruct((turns, rows, model), BF16)] * 2,
        scratch_shapes=[pltpu.VMEM((inner, model), BF16), pltpu.SemaphoreType.DMA((count,))],
    )


def grad_in_kernel(setup, at_ref, slope_ref, *rest):
    count, parts, places, width, hidden, many = setup
    refs = many // 2
    chunks = [Chunks.of(rest[:refs]), Chunks.of(rest[refs:many])]
    blocks, rest = rest[many : many + count], rest[many + count :]
    gmixed_ref, gpre_ref, dy_ref, gsum_ref, dsum_ref, held, dy_held, sems, dy_sems = rest[-9:]
    step, steps = pl.program_id(0), 2 * len(places)
    found = chunk_copies(chunks, places, parts, dy_held, dy_sems)
    loads = block_copies(blocks, columns_at(held, blocks[0].shape[1]), sems)

    @pl.when(step == 0)
    def _():
        for copy in loads:
            copy.start()
        start_all(found)
        gsum_ref[...] = jnp.zeros_like(gsum_ref)
        dsum_ref[...] = jnp.zeros_like(dsum_ref)
        for copy in loads:
            copy.wait()

    for slot in range(steps):

        @pl.when(step == slot)
        def _(slot=slot):
            wait_for(found[slot])

    dy = dy_held[step]
    dy_ref[...] = dy
    gmixed_ref[...] = dot(dy, held[:width, :], 1, 1).astype(BF16)
    for start in range(0, hidden, width):
        part = slice(start, start + width)
        gact = dot(dy, held[width + start : 2 * width + start, :], 1, 1)
        gpre = (gact * slope_ref[:, part].astype(F32)).astype(BF16)
        gpre_ref[:, part] = gpre
        gsum_ref[0:1, part] += jnp.sum(gpre.astype(F32), axis=0, keepdims=True)
    dsum_ref[0:1, :] += jnp.sum(dy.astype(F32), axis=0, keepdims=True)


def grad_in(at_mp, chunks, slope, blocks, width, parts, places, earlier, deps):
    rows, model = chunks[0].own.shape
    hidden, length = slope.shape[1], slope.shape[0]
    count, many = len(blocks), len(chunks[0].flat()) * 2
    turns = len(places)

    def where(i, at):
        m = jnp.int32(places[0])
        for n in range(1, turns):
            m = jnp.where(i % turns == n, places[n], m)
        return i // turns * parts + (at[0] ^ m)

    out = lambda w: pl.BlockSpec((rows, w), lambda i, at: (where(i, at), 0))
    total = lambda w: pl.BlockSpec((8, w), lambda i, at: (0, 0))
    setup = (count, parts, places, width, hidden, many)
    operands = [slope, *chunks[0].flat(), *chunks[1].flat(), *blocks]
    aliases = {1 + len(operands) + n: n for n in range(len(earlier))}
    return call(
        functools.partial(grad_in_kernel, setup),
        "grad_in",
        operands + list(earlier),
        deps,
        (at_mp,),
        grid=(2 * turns,),
        in_specs=[out(hidden)] + [ANY] * (many + count + len(earlier)),
        out_specs=[out(width), out(hidden), out(model), total(hidden), total(model)],
        out_shape=[jax.ShapeDtypeStruct((length, w), BF16) for w in (width, hidden, model)]
        + [jax.ShapeDtypeStruct((8, w), F32) for w in (hidden, model)],
        input_output_aliases=aliases,
        scratch_shapes=[
            pltpu.VMEM((width + hidden, model), BF16),
            pltpu.VMEM((2 * turns, rows, model), BF16),
            pltpu.SemaphoreType.DMA((count,)),
            pltpu.SemaphoreType.DMA((2 * turns,)),
        ],
    )


def grad_normed_kernel(
    count, turns, at_ref, gq_ref, gk_ref, gv_ref, gpre_ref, tokens_ref, *rest
):
    blocks, (other_ref, own_ref, sum_ref, held, sems) = rest[:count], rest[count:]
    step = pl.program_id(0)

    @pl.when(step == 0)
    def _():
        loads = block_copies(blocks, rows_at(held, blocks[0].shape[0]), sems)
        for copy in loads:
            copy.start()
        sum_ref[...] = jnp.zeros_like(sum_ref)
        for copy in loads:
            copy.wait()

    g = jnp.concatenate([gq_ref[...], gk_ref[...], gv_ref[...], gpre_ref[...]], axis=1)
    result = dot(g, held[...], 1, 1)
    sum_ref[0:1, :] += jnp.sum(result * normalized(tokens_ref[...]), axis=0, keepdims=True)
    sum_ref[1:2, :] += jnp.sum(result, axis=0, keepdims=True)
    split_outputs(step, turns, result.astype(BF16), other_ref, own_ref)


def grad_normed_sums(at_mp, gqkv, gpre, tokens, blocks, parts, places, deps):
    rows, count, turns = tokens.shape[0] // (2 * parts), len(blocks), len(places)
    model, total = tokens.shape[1], blocks[0].shape[1]
    where = quarter_map(places, parts)
    operands = [*gqkv, gpre, tokens]
    return call(
        functools.partial(grad_normed_kernel, count, turns),
        "grad_normed_sums",
        operands + list(blocks),
        deps,
        (at_mp,),
        grid=(2 * turns,),
        in_specs=[
            pl.BlockSpec((rows, a.shape[1]), lambda i, at: (where(i, at), 0)) for a in operands
        ]
        + [ANY] * count,
        out_specs=split_specs(rows, model, turns)
        + [pl.BlockSpec((8, model), lambda i, at: (0, 0))],
        out_shape=[jax.ShapeDtypeStruct((turns, rows, model), BF16)] * 2
        + [jax.ShapeDtypeStruct((8, model), F32)],
        scratch_shapes=[pltpu.VMEM((model, total), BF16), pltpu.SemaphoreType.DMA((count,))],
    )


def weight_grad_kernel(sizes, left, at_ref, *refs):
    ins, outs = refs[: len(refs) - len(sizes)], refs[len(refs) - len(sizes) :]
    if left:
        grad = jnp.concatenate([dot(ins[0][...], g[...], 0, 0) for g in ins[1:]], axis=1)
    else:
        grad = jnp.concatenate([dot(x[...], ins[-1][...], 0, 0) for x in ins[:-1]], axis=0)
    grad = grad.astype(BF16)
    first = 0
    for size, out_ref in zip(sizes, outs):

        @pl.when((pl.program_id(0) >= first) & (pl.program_id(0) < first + size))
        def _(out_ref=out_ref):
            out_ref[0] = grad

        first += size


def weight_grads(me, xs, gs, count, deps, left):
    plan = scatter_plan(count)
    sets = [(half, s) for s in range(len(plan[0])) for half in range(2)]
    sizes = [len(plan[half][s]) for half, s in sets]
    order = [j for half, s in sets for j in plan[half][s]]
    owners = lax.bitwise_xor(me, jnp.array(order, jnp.int32))
    length, (cut, whole) = xs[0].shape[0], ((xs, gs) if left else (gs, xs))
    size = cut[0].shape[1] // count
    cut_spec = pl.BlockSpec((length, size), lambda i, at: (0, at[i]))
    whole_specs = [pl.BlockSpec(a.shape, lambda i, at: (0, 0)) for a in whole]
    full = sum(a.shape[1] for a in whole)
    shape = (size, full) if left else (full, size)

    def out(first, many):
        return pl.BlockSpec(
            (1, *shape), lambda i, at: (jnp.clip(i - first, 0, many - 1), 0, 0)
        )

    firsts = [sum(sizes[:n]) for n in range(len(sizes))]
    outs = call(
        functools.partial(weight_grad_kernel, sizes, left),
        "weight_grads",
        [*xs, *gs],
        deps,
        (owners,),
        grid=(count,),
        in_specs=[cut_spec] + whole_specs if left else whole_specs + [cut_spec],
        out_specs=[out(first, many) for first, many in zip(firsts, sizes)],
        out_shape=[jax.ShapeDtypeStruct((many, *shape), BF16) for many in sizes],
    )
    return [[o for o, (half, _) in zip(outs, sets) if half == h] for h in range(2)]


def across(value, bit, count):
    return lax.ppermute(value, "dp", [(i, i ^ bit) for i in range(count)])


def line_step(below, above, k, parts):
    up = lax.ppermute(below, "mp", [(i, i + 1) for i in range(k - 1, parts - 1)])
    down = lax.ppermute(above, "mp", [(i + 1, i) for i in range(parts - k)])
    return up, down


class LineScatter:
    def __init__(self, sums):
        self.sums, self.parts = [list(s) for s in sums], len(sums)

    def total(self, k):
        if len(self.sums[k]) > 1:
            self.sums[k] = [sum(s.astype(F32) for s in self.sums[k]).astype(BF16)]
        return self.sums[k][0]

    def ready(self, s):
        return [self.total(k) for k in sorted({self.parts - s, s})]

    def step(self, s):
        parts = self.parts
        up = lax.ppermute(self.total(parts - s), "mp", [(i, i + 1) for i in range(s)])
        down = lax.ppermute(self.total(s), "mp", [(i, i - 1) for i in range(parts - s, parts)])
        self.sums[(parts - s - 1) % parts].append(up)
        self.sums[(s + 1) % parts].append(down)

    def result(self):
        return sum(s.astype(F32) for s in self.sums[0])


def chip_bits(count):
    bits, bit = [], 2
    while bit < count:
        bits.append(bit)
        bit *= 2
    return bits


def gather_blocks(own, sibling, count):
    held = {0: own, 1: sibling}
    orders = (chip_bits(count), chip_bits(count)[::-1])
    for s in range(len(orders[0])):
        moved = {}
        for half in range(2):
            bit = orders[half][s]
            for j in [j for j in held if j % 2 == half]:
                moved[j ^ bit] = across(held[j], bit, count)
        held.update(moved)
    return [held[j] for j in range(count)]


def scatter_orders(count):
    return (chip_bits(count)[::-1], chip_bits(count))


def scatter_plan(count):
    plan = []
    for half, order in enumerate(scatter_orders(count)):
        sets, rest = [[half]], [half]
        for bit in reversed(order):
            sets.insert(0, [j ^ bit for j in rest])
            rest = sets[0] + rest
        plan.append(sets)
    return plan


class BlockScatter:
    def __init__(self, halves, count):
        self.count, self.orders = count, scatter_orders(count)
        self.held = [[[a] for a in arrays] for arrays in halves]

    def total(self, half, s):
        addends = self.held[half][s]
        if len(addends) > 1:
            addends = [sum(a.astype(F32) for a in addends).astype(BF16)]
            self.held[half][s] = addends
        return addends[0]

    def ready(self, s):
        return [self.total(half, s) for half in range(2)]

    def step(self, s):
        for half in range(2):
            came = across(self.total(half, s), self.orders[half][s], self.count)
            first = 0
            for later in self.held[half][s + 1 :]:
                many = later[0].shape[0]
                later.append(came[first : first + many])
                first += many

    def finish(self):
        mine = sum(a[0].astype(F32) for a in self.held[0][-1])
        theirs = across(self.total(1, -1)[0], 1, self.count)
        return mine, theirs.astype(F32)


def on_device(
    tokens,
    norm_gain,
    norm_bias,
    qkv_weight,
    qkv_bias,
    dense_weight,
    dense_bias,
    up_weight,
    up_bias,
    down_weight,
    down_bias,
    cotangent,
    *,
    ndp,
    nmp,
):
    me, z = lax.axis_index("dp"), lax.axis_index("mp")
    core = me % 2
    at_mp = z.astype(jnp.int32)[None]
    length, model = tokens.shape[0] * nmp, tokens.shape[1]
    block = min(512, length)
    width, hidden = qkv_weight.shape[2] // 2, up_weight.shape[1] // 2
    chip_steps = len(chip_bits(ndp))
    rank = lambda array, axis, which, size: lax.dynamic_slice_in_dim(
        array, which * size, size, axis
    )

    def row_pack(which):
        qkv = rank(qkv_weight, 2, which, width)
        return jnp.concatenate([qkv[0], qkv[1], qkv[2], rank(up_weight, 1, which, hidden)], axis=1)

    def column_pack(which):
        return jnp.concatenate(
            [rank(dense_weight, 0, which, width), rank(down_weight, 0, which, hidden)], axis=0
        )

    below, above = [], []
    up, down = tokens, tokens
    for k in range(1, nmp):
        up, down = line_step(up, down, k, nmp)
        below.append(up)
        above.append(down)
    own = Chunks(tokens, below, above)
    other = Chunks.of([across(c, 1, ndp) for c in own.flat()])

    row_blocks = gather_blocks(row_pack(core), across(row_pack(1 - core), 1, ndp), ndp)
    late = tie(column_pack(core), row_blocks[2])
    late_other = tie(across(column_pack(1 - core), 1, ndp), row_blocks[2])
    column_blocks = gather_blocks(late, late_other, ndp)

    tables = rotary_tables(length)
    bias = jnp.concatenate(
        [
            rank(qkv_bias, 1, core, width).astype(F32).reshape(1, 3 * width),
            rank(up_bias[None, :], 1, core, hidden).astype(F32),
        ],
        axis=1,
    )
    gain, shift = norm_gain.astype(F32)[None, :], norm_bias.astype(F32)[None, :]
    cot = tie(cotangent, below[-1], above[-1])
    dy_below, dy_above = [], []
    up, down = line_step(cot, cot, 1, nmp)
    qkv, act, slope, normed, token_rows = project(
        at_mp, (own, other), row_blocks, bias, gain, shift, tables, width, [cot]
    )
    up, down = tie(up, qkv), tie(down, qkv)
    dy_below.append(up)
    dy_above.append(down)
    mixed, lse = attend(qkv, length, block, [up, down])
    anchor = mixed
    for k in range(2, nmp):
        up, down = line_step(up, down, k, nmp)
        if k < nmp - 1:
            up, down = tie(up, anchor), tie(down, anchor)
        dy_below.append(up)
        dy_above.append(down)
    places = list(range(nmp))
    other_sums, own_sums = branch_sums(
        at_mp, mixed, act, column_blocks, nmp, places, [dy_below[-2], dy_above[-2]]
    )
    came = across(other_sums, 1, ndp)
    branches = LineScatter([[own_sums[k], came[k]] for k in range(nmp)])

    dy_own = Chunks(cot, dy_below, dy_above)
    dy_other = Chunks.of([across(c, 1, ndp) for c in dy_own.flat()])
    near = lambda c: Chunks(c.own, c.below[:1], c.above[:1])
    first = grad_in(
        at_mp,
        (near(dy_own), near(dy_other)),
        slope,
        column_blocks,
        width,
        nmp,
        (0, 1),
        (),
        [other_sums],
    )
    second = grad_in(
        at_mp,
        (dy_own, dy_other),
        slope,
        column_blocks,
        width,
        nmp,
        tuple(range(2, nmp)),
        first[:3],
        branches.ready(1),
    )
    branches.step(1)
    gmixed, gpre, dy = second[:3]
    column_grads = BlockScatter(
        weight_grads(me, [mixed, act], [dy], ndp, [second[3]], left=False), ndp
    )
    column_grads.step(0)
    gq, gk, gv, qkv_sums = attend_back(
        qkv, gmixed, mixed, lse, tables, length, block, [column_grads.held[0][0][0], *branches.ready(2)]
    )
    for s in range(2, nmp - 1):
        branches.step(s)
    for s in range(1, chip_steps - 1):
        column_grads.step(s)
    early = [k for k in places if k % 2] if nmp > 2 else places
    late_places = [k for k in places if k not in early]
    grads_a = grad_normed_sums(
        at_mp,
        (gq, gk, gv),
        gpre,
        token_rows,
        row_blocks,
        nmp,
        early,
        [*branches.ready(nmp - 1), *column_grads.ready(chip_steps - 1)],
    )
    branches.step(nmp - 1)
    column_grads.step(chip_steps - 1)
    came_a = across(grads_a[0], 1, ndp)
    grads_b = grad_normed_sums(
        at_mp, (gq, gk, gv), gpre, token_rows, row_blocks, nmp, late_places, [grads_a[2]]
    )
    came_b = across(grads_b[0], 1, ndp)
    shares = {}
    for part, got, kept in ((early, came_a, grads_a[1]), (late_places, came_b, grads_b[1])):
        for n, k in enumerate(part):
            shares[k] = [kept[n], got[n]]
    grad_rows = LineScatter([shares[k] for k in places])
    up_grads = BlockScatter(
        weight_grads(me, [normed], [gpre], ndp, [grads_b[2], *grad_rows.ready(1)], left=True), ndp
    )
    grad_rows.step(1)
    up_grads.step(0)
    qkv_grads = BlockScatter(
        weight_grads(me, [normed], [gq, gk, gv], ndp, [up_grads.held[0][0][0]], left=True), ndp
    )
    for s in range(2, nmp):
        grad_rows.step(s)
    for s in range(1, chip_steps):
        up_grads.step(s)
    for s in range(chip_steps):
        qkv_grads.step(s)

    local_inputs = tokens.astype(F32)
    output = (
        local_inputs
        + branches.result()
        + (dense_bias.astype(F32) + down_bias.astype(F32))[None, :]
    ).astype(BF16)

    pairs = width // LANES
    qkv_sum = (
        qkv_sums.reshape(2, pairs, 8, LANES).sum(0)[:, :3, :].transpose(1, 0, 2).reshape(3 * width)
    )
    small = jnp.concatenate(
        [
            qkv_sum,
            first[3][0] + second[3][0],
            (grads_a[2][:2] + grads_b[2][:2]).reshape(2 * model),
            first[4][0] + second[4][0],
        ]
    )
    for bit in chip_bits(ndp):
        small = small + across(small, bit, ndp)
    inner = 3 * width + hidden
    here, grad_out_bias = small[: inner + 2 * model], small[inner + 2 * model :]
    there = across(here, 1, ndp)
    norm_sums = here[inner:] + there[inner:]
    sums = [norm_sums] + [
        lax.ppermute(norm_sums, "mp", [(i, i ^ j) for i in range(nmp)]) for j in range(1, nmp)
    ]
    while len(sums) > 1:
        sums = [a + b for a, b in zip(sums[::2], sums[1::2])]
    even, odd = jnp.where(core == 0, here, there), jnp.where(core == 0, there, here)
    grad_qkv_bias = jnp.concatenate(
        [even[: 3 * width].reshape(3, width), odd[: 3 * width].reshape(3, width)], axis=1
    )
    grad_up_bias = jnp.concatenate([even[3 * width : inner], odd[3 * width : inner]])

    def both(mine, theirs, axis):
        return jnp.where(
            core == 0,
            jnp.concatenate([mine, theirs], axis=axis),
            jnp.concatenate([theirs, mine], axis=axis),
        )

    mine, theirs = column_grads.finish()
    owned_dense = both(mine[:width], theirs[:width], 0)
    owned_down = both(mine[width:], theirs[width:], 0)
    owned_up = both(*up_grads.finish(), 1)
    mine, theirs = qkv_grads.finish()
    owned_qkv = jnp.stack(
        [
            both(mine[:, c * width : (c + 1) * width], theirs[:, c * width : (c + 1) * width], 1)
            for c in range(3)
        ]
    )

    row_mean = jnp.mean(local_inputs, axis=1, keepdims=True)
    centered = local_inputs - row_mean
    row_var = jnp.mean(centered * centered, axis=1, keepdims=True)
    inverse_std = lax.rsqrt(row_var + EPS)
    normal_rows = centered * inverse_std
    scaled_grad = grad_rows.result() * gain
    first_mean = jnp.mean(scaled_grad, axis=1, keepdims=True)
    second_mean = jnp.mean(scaled_grad * normal_rows, axis=1, keepdims=True)
    grad_tokens = (
        cotangent.astype(F32)
        + (scaled_grad - first_mean - normal_rows * second_mean) * inverse_std
    ).astype(BF16)
    return (
        output,
        grad_tokens,
        sums[0][:model],
        sums[0][model:],
        owned_qkv,
        grad_qkv_bias,
        owned_dense,
        grad_out_bias,
        owned_up,
        grad_up_bias,
        owned_down,
        grad_out_bias,
    )


def solution(mesh):
    return jax.shard_map(
        functools.partial(on_device, ndp=mesh.shape["dp"], nmp=mesh.shape["mp"]),
        mesh=mesh,
        in_specs=(
            P(("dp", "mp"), None),
            P(),
            P(),
            P(None, "dp", "mp"),
            P(None, "mp"),
            P("mp", "dp"),
            P(),
            P("dp", "mp"),
            P("mp"),
            P("mp", "dp"),
            P(),
            P(("dp", "mp"), None),
        ),
        out_specs=(
            P(("dp", "mp"), None),
            P(("dp", "mp"), None),
            P(),
            P(),
            P(None, "dp", "mp"),
            P(None, "mp"),
            P("mp", "dp"),
            P(),
            P("dp", "mp"),
            P("mp"),
            P("mp", "dp"),
            P(),
        ),
        check_vma=False,
    )
```

time: 811 us -> 586 us (0.72)
  matrix products: 228 us -> 0 us
  Pallas kernels: 0 us -> 202 us
  waiting for transfers between devices: 410 us -> 210 us
  starting transfers between devices: 0.48 us -> 86.3 us
  blocking collectives: 67.1 us -> 0 us
  between operations: 14.9 us -> 2.15 us
    dot_general x26 -> x0, matrix products: 228 us -> none  [the longest x2 23.4 us: one_block(): jnp.einsum('hqd,hkd->hqk', block_grad, values, preferred_element_type=jnp...]
    all_gather x6 -> x0, waiting for transfers between devices: 227 us -> none  [the longest x1 82.4 us: on_device(): grad_rows = lax.all_gather(cotangent, 'mp', axis=0, tiled=True)]
    ppermute x0 -> x76, waiting for transfers between devices: none -> 210 us  [the longest x49 106 us: across(): return lax.ppermute(value, 'dp', [(i, i ^ bit) for i in range(count)])]
    pallas_call x0 -> x18, Pallas kernels: none -> 202 us  [call(): pl.pallas_call(body, out_shape=out_shape, input_output_aliases=aliases, c...]
    reduce_scatter x6 -> x0, waiting for transfers between devices: 181 us -> none  [the longest x1 77.2 us: on_device(): lax.psum_scatter(partial_sum.astype(jnp.bfloat16), 'mp', scatter_dimensio...]
    ppermute x0 -> x76, starting transfers between devices: none -> 86.3 us  [the longest x49 32.1 us: across(): return lax.ppermute(value, 'dp', [(i, i ^ bit) for i in range(count)])]
    psum x2 -> x0, blocking collectives: 67.1 us -> none  [the longest x1 41.2 us: on_device(): lax.psum((jnp.sum(grad_local * normal_rows, axis=0), jnp.sum(grad_local,...]
    reduce_sum x5 -> x2, other arithmetic: 17.9 us -> 3.09 us  [the longest x1 2.3 us: on_device(): first_mean = jnp.mean(scaled_grad, axis=1, keepdims=True)]
  transfers between devices with their start and end apart: 12 -> 76, of which waited for: 8 -> 31; matrix products, arithmetic and copies ran while one was open for 37% -> 11% of each run, Pallas kernels for 0% -> 32%
where the time goes in v2:
time: 586 us; the launch traced here: 578 us
  waiting for transfers between devices  210 us (36%)
  Pallas kernels  202 us (34%)
  starting transfers between devices  86.3 us (15%)
  other arithmetic  52.6 us (9%)
  local copies, waits for them, and re-layouts  24.3 us (4%)
    pallas_call x18, Pallas kernels, call(): pl.pallas_call(body, out_shape=out_shape, input_output_aliases=aliases, c...  202 us
    ppermute x49, waiting for transfers between devices, across(): return lax.ppermute(value, 'dp', [(i, i ^ bit) for i in range(count)])  106 us
    ppermute x6, waiting for transfers between devices, line_step(): down = lax.ppermute(above, 'mp', [(i + 1, i) for i in range(parts - k)])  55.8 us
    ppermute x49, starting transfers between devices, across(): return lax.ppermute(value, 'dp', [(i, i ^ bit) for i in range(count)])  32.1 us
    ppermute x6, waiting for transfers between devices, step(): lax.ppermute(self.total(parts - s), 'mp', [(i, i + 1) for i in range(s)])  31 us
    convert_element_type x8, other arithmetic, total(): self.sums[k] = [sum((s.astype(F32) for s in self.sums[k])).astype(BF16)]  19.4 us
    ppermute x6, starting transfers between devices, step(): lax.ppermute(self.total(parts - s), 'mp', [(i, i + 1) for i in range(s)])  18.2 us
    ppermute x6, waiting for transfers between devices, line_step(): lax.ppermute(below, 'mp', [(i, i + 1) for i in range(k - 1, parts - 1)])  17 us
  transfers between devices with their start and end apart: 76, of which 31 were waited for; matrix products, arithmetic and copies ran while one was open for 11% of the time, Pallas kernels for 32%

profile of v2, /device:TPU:0, one launch (start us, length us, event | category | flops | bytes accessed | tf_op | source)
XLA Modules:
  0.0 577.6 jit_solution(8730570419183781911)
XLA Ops:
  3.3 5.9 %collective-permute-start = (bf16[256,2048]{1,0:T(8,128)(2,1)S(1)}, bf16[256,2048]{1,0:T(8,128)(2,1)}, u32[]{:S(2)}, u32[]{:S(2)}) collective-permute-start(bf16[256,2048]{1,0:T(8,128)(2,1)S(1)} %copy-done.2), channel_id=1, source_target_pairs={{0,1},{1,2},{2,3},{4,5},{5,6},{6,7},{8,9},{9,10},{10,11},{12,13},{... | collective-permute-start | bytes 3145736 | tf_op jit(solution)/shard_map/ppermute | solution.py:636
  13.7 17.0 %collective-permute-done.refs_8_ = bf16[256,2048]{1,0:T(8,128)(2,1)} collective-permute-done((bf16[256,2048]{1,0:T(8,128)(2,1)S(1)}, bf16[256,2048]{1,0:T(8,128)(2,1)}, u32[]{:S(2)}, u32[]{:S(2)}) %collective-permute-start) | collective-permute-done | bytes 1048608 | tf_op jit(solution)/shard_map/ppermute | solution.py:636
  30.7 1.6 collective-permute-start.1
  32.3 3.4 collective-permute-done.3.refs_11_
  37.0 1.6 collective-permute-start.17
  41.4 20.4 %collective-permute-done.4.refs_12_ = bf16[256,2048]{1,0:T(8,128)(2,1)} collective-permute-done((bf16[256,2048]{1,0:T(8,128)(2,1)S(1)}, bf16[256,2048]{1,0:T(8,128)(2,1)}, u32[]{:S(2)}, u32[]{:S(2)}) %collective-permute-start.4) | collective-permute-done | bytes 1048608 | tf_op jit(solution)/shard_map/ppermute | solution.py:637
  63.6 14.0 %collective-permute-done.18.refs_27_.refs_12_ = bf16[256,1792]{1,0:T(8,128)(2,1)S(1)} collective-permute-done((bf16[256,1792]{1,0:T(8,128)(2,1)S(1)}, bf16[256,1792]{1,0:T(8,128)(2,1)S(1)}, u32[]{:S(2)}, u32[]{:S(2)}) %collective-permute-start.18) | collective-permute-done | bytes 917536 | tf_op jit(solution)/shard_map/ppermute | solution.py:632
  79.3 7.6 %collective-permute-done.5.refs_2_.refs_13_ = bf16[256,2048]{1,0:T(8,128)(2,1)S(1)} collective-permute-done((bf16[256,2048]{1,0:T(8,128)(2,1)}, bf16[256,2048]{1,0:T(8,128)(2,1)S(1)}, u32[]{:S(2)}, u32[]{:S(2)}) %collective-permute-start.5) | collective-permute-done | bytes 1048608 | tf_op jit(solution)/shard_map/ppermute | solution.py:637
  90.0 7.6 %collective-permute-done.19.refs_28_.refs_13_ = bf16[256,1792]{1,0:T(8,128)(2,1)S(1)} collective-permute-done((bf16[256,1792]{1,0:T(8,128)(2,1)S(1)}, bf16[256,1792]{1,0:T(8,128)(2,1)S(1)}, u32[]{:S(2)}, u32[]{:S(2)}) %collective-permute-start.19) | collective-permute-done | bytes 917536 | tf_op jit(solution)/shard_map/ppermute | solution.py:632
  97.7 2.4 constant_dynamic-slice_fusion
  100.1 3.1 multiply_sine_fusion
  103.2 4.6 collective-permute-start.20
  110.6 3.5 concatenate.134.refs_5_.refs_7_
  114.0 3.5 concatenate.135.refs_6_.refs_8_
  119.5 3.5 concatenate.133.refs_4_.refs_6_
  123.6 33.6 %project.1 = (bf16[2048,768]{1,0:T(8,128)(2,1)}, bf16[2048,1024]{1,0:T(8,128)(2,1)}, bf16[2048,1024]{1,0:T(8,128)(2,1)}, bf16[2048,2048]{1,0:T(8,128)(2,1)}, bf16[2048,2048]{1,0:T(8,128)(2,1)}) custom-call(s32[1]{0:T(128)} %bitcast.refs_0_, f32[1,1792]{1,0:T(1,128)} %maximum_convert_fusion.refs_1_, f32[1,2048]{1,0:T(1,128)} %bitcast.92, f32[1,2048]{1,0:T(1,128)} %bitcast.95, ...), custom_call_target="tpu_custom_call" | custom-call | tf_op jit(solution)/shard_map/project/pallas_call | solution.py:41
  166.1 11.8 %collective-permute-done.26.refs_8_.refs_13_.refs_21_ = bf16[1280,256]{1,0:T(8,128)(2,1)S(1)} collective-permute-done((bf16[1280,256]{1,0:T(8,128)(2,1)}, bf16[1280,256]{1,0:T(8,128)(2,1)S(1)}, u32[]{:S(2)}, u32[]{:S(2)}) %collective-permute-start.26) | collective-permute-done | bytes 655392 | tf_op jit(solution)/shard_map/ppermute | solution.py:632
  181.4 5.5 collective-permute-done.30.refs_0_
  188.4 14.9 %attend.1 = (bf16[2048,256]{1,0:T(8,128)(2,1)}, f32[4,8,1024]{2,1,0:T(8,128)}) custom-call(bf16[2048,768]{1,0:T(8,128)(2,1)} %get-tuple-element.59.refs_1_.refs_0_.refs_2_, bf16[2048,768]{1,0:T(8,128)(2,1)} %get-tuple-element.59.refs_1_.refs_0_.refs_2_, bf16[2048,768]{1,0:T(8,128)(2,1)} %get-tuple-element.59.refs_1_.refs_0_.refs_2_, ...), custom_call_target="tpu_custom_call" | custom-call | tf_op jit(solution)/shard_map/attend/pallas_call | solution.py:41
  204.4 2.8 collective-permute-done.28.refs_10_.refs_15_.refs_23_
  209.2 19.7 %branch_sums.1 = (bf16[4,256,2048]{2,1,0:T(8,128)(2,1)}, bf16[4,256,2048]{2,1,0:T(8,128)(2,1)}) custom-call(s32[1]{0:T(128)} %bitcast.refs_0_, bf16[2048,256]{1,0:T(8,128)(2,1)} %get-tuple-element.60.refs_1_.refs_4_, bf16[2048,1024]{1,0:T(8,128)(2,1)} %get-tuple-element.61.refs_2_, bf16[1280,256]{1,0:T(8,128)(2,1)} %tie.10.refs_3_.refs_8_.refs_16_, ...), custom_call_target="tpu_custom_call" | custom-call | tf_op jit(solution)/shard_map/branch_sums/pallas_call | solution.py:41
  230.9 1.7 collective-permute-start.38
  232.8 4.5 collective-permute-done.40.refs_5_.refs_9_
  239.2 18.8 %collective-permute-done.39.refs_8_ = bf16[256,2048]{1,0:T(8,128)(2,1)} collective-permute-done((bf16[256,2048]{1,0:T(8,128)(2,1)S(1)}, bf16[256,2048]{1,0:T(8,128)(2,1)}, u32[]{:S(2)}, u32[]{:S(2)}) %collective-permute-start.39) | collective-permute-done | bytes 1048608 | tf_op jit(solution)/shard_map/ppermute | solution.py:637
  259.2 3.9 fusion.20
  263.1 2.4 collective-permute-start.32
  265.5 1.6 collective-permute-start.33
  267.6 12.9 %grad_in.2 = (bf16[2048,256]{1,0:T(8,128)(2,1)}, bf16[2048,1024]{1,0:T(8,128)(2,1)}, bf16[2048,2048]{1,0:T(8,128)(2,1)}, f32[8,1024]{1,0:T(8,128)}, f32[8,2048]{1,0:T(8,128)}) custom-call(s32[1]{0:T(128)} %bitcast.refs_0_, bf16[2048,1024]{1,0:T(8,128)(2,1)} %get-tuple-element.64.refs_1_, bf16[256,2048]{1,0:T(8,128)(2,1)} %tie.7.refs_29_.refs_2_, ...), custom_call_target="tpu_custom_call" | custom-call | tf_op jit(solution)/shard_map/grad_in/pallas_call | solution.py:41
  280.6 12.9 %grad_in.3 = (bf16[2048,256]{1,0:T(8,128)(2,1)}, bf16[2048,1024]{1,0:T(8,128)(2,1)}, bf16[2048,2048]{1,0:T(8,128)(2,1)}, f32[8,1024]{1,0:T(8,128)}, f32[8,2048]{1,0:T(8,128)}) custom-call(s32[1]{0:T(128)} %bitcast.refs_0_, bf16[2048,1024]{1,0:T(8,128)(2,1)} %get-tuple-element.64.refs_1_, ...), custom_call_target="tpu_custom_call", output_to_operand_aliasing={{0}: (24, {}), {1}: (25, {}), {2}: (26, {})} | custom-call | tf_op jit(solution)/shard_map/grad_in/pallas_call | solution.py:41
  293.5 19.3 %weight_grads.3 = (bf16[2,1280,256]{2,1,0:T(8,128)(2,1)}, bf16[2,1280,256]{2,1,0:T(8,128)(2,1)}, bf16[1,1280,256]{2,1,0:T(8,128)(2,1)}, bf16[1,1280,256]{2,1,0:T...) custom-call(s32[8]{0:T(128)} %broadcast_xor_fusion.refs_0_, ...), custom_call_target="tpu_custom_call" | custom-call | tf_op jit(solution)/shard_map/weight_grads/pallas_call | solution.py:41
  317.5 2.9 fusion.17.refs_10_
  320.4 1.6 collective-permute-start.36
  322.1 2.4 collective-permute-start.34
  324.5 25.2 %attend_back.1 = (bf16[2048,256]{1,0:T(8,128)(2,1)}, bf16[2048,256]{1,0:T(8,128)(2,1)}, bf16[2048,256]{1,0:T(8,128)(2,1)}, f32[4,8,128]{2,1,0:T(8,128)}) custom-call(bf16[2048,768]{1,0:T(8,128)(2,1)} %get-tuple-element.59.refs_1_.refs_0_.refs_2_, bf16[2048,768]{1,0:T(8,128)(2,1)} %get-tuple-element.59.refs_1_.refs_0_.refs_2_, ...), custom_call_target="tpu_custom_call" | custom-call | tf_op jit(solution)/shard_map/attend_back/pallas_call | solution.py:41
  354.7 13.5 %collective-permute-done.68 = bf16[1,1280,256]{2,1,0:T(8,128)(2,1)} collective-permute-done((bf16[1,1280,256]{2,1,0:T(8,128)(2,1)S(1)}, bf16[1,1280,256]{2,1,0:T(8,128)(2,1)}, u32[]{:S(2)}, u32[]{:S(2)}) %collective-permute-start.68) | collective-permute-done | bytes 655392 | tf_op jit(solution)/shard_map/ppermute | solution.py:632
  369.7 3.0 add_convert_fusion.4.refs_15_
  372.7 2.5 add_convert_fusion.5.refs_14_
  375.1 16.4 %grad_normed_sums.2 = (bf16[2,256,2048]{2,1,0:T(8,128)(2,1)}, bf16[2,256,2048]{2,1,0:T(8,128)(2,1)}, f32[8,2048]{1,0:T(8,128)}) custom-call(s32[1]{0:T(128)} %bitcast.refs_0_, bf16[2048,256]{1,0:T(8,128)(2,1)} %get-tuple-element.73.refs_1_.refs_2_, bf16[2048,256]{1,0:T(8,128)(2,1)} %get-tuple-element.74.refs_2_.refs_3_, ...), custom_call_target="tpu_custom_call" | custom-call | tf_op jit(solution)/shard_map/grad_normed_sums/pallas_call | solution.py:41
  391.6 16.9 %grad_normed_sums.3 = (bf16[2,256,2048]{2,1,0:T(8,128)(2,1)}, bf16[2,256,2048]{2,1,0:T(8,128)(2,1)}, f32[8,2048]{1,0:T(8,128)}) custom-call(s32[1]{0:T(128)} %bitcast.refs_0_, bf16[2048,256]{1,0:T(8,128)(2,1)} %get-tuple-element.73.refs_1_.refs_2_, bf16[2048,256]{1,0:T(8,128)(2,1)} %get-tuple-element.74.refs_2_.refs_3_, ...), custom_call_target="tpu_custom_call" | custom-call | tf_op jit(solution)/shard_map/grad_normed_sums/pallas_call | solution.py:41
  410.1 2.2 fusion.23
  414.1 3.3 collective-permute-done.58
  418.8 1.8 collective-permute-start.60
  420.6 3.4 collective-permute-start.61
  425.3 4.4 fusion.22
  429.7 16.1 %weight_grads.4 = (bf16[2,256,1024]{2,1,0:T(8,128)(2,1)}, bf16[2,256,1024]{2,1,0:T(8,128)(2,1)}, bf16[1,256,1024]{2,1,0:T(8,128)(2,1)}, bf16[1,256,1024]{2,1,0:T...) custom-call(s32[8]{0:T(128)} %broadcast_xor_fusion.refs_0_, ...), custom_call_target="tpu_custom_call" | custom-call | tf_op jit(solution)/shard_map/weight_grads/pallas_call | solution.py:41
  445.8 14.0 %weight_grads.5 = (bf16[2,256,768]{2,1,0:T(8,128)(2,1)}, bf16[2,256,768]{2,1,0:T(8,128)(2,1)}, bf16[1,256,768]{2,1,0:T(8,128)(2,1)}, bf16[1,256,768]{2,1,0:T(8,1...) custom-call(s32[8]{0:T(128)} %broadcast_xor_fusion.refs_0_, ...), custom_call_target="tpu_custom_call" | custom-call | tf_op jit(solution)/shard_map/weight_grads/pallas_call | solution.py:41
  460.4 2.5 collective-permute-start.51
  465.9 1.6 maximum_select_fusion.1
  467.5 11.6 %collective-permute-done.63 = bf16[2,256,768]{2,1,0:T(8,128)(2,1)S(1)} collective-permute-done((bf16[2,256,768]{2,1,0:T(8,128)(2,1)}, bf16[2,256,768]{2,1,0:T(8,128)(2,1)S(1)}, u32[]{:S(2)}, u32[]{:S(2)}) %collective-permute-start.63) | collective-permute-done | bytes 786464 | tf_op jit(solution)/shard_map/ppermute | solution.py:632
  479.8 2.7 collective-permute-done.65
  487.5 2.0 fusion.13
  489.5 15.7 %collective-permute-done.71 = bf16[2,256,1024]{2,1,0:T(8,128)(2,1)S(1)} collective-permute-done((bf16[2,256,1024]{2,1,0:T(8,128)(2,1)S(1)}, bf16[2,256,1024]{2,1,0:T(8,128)(2,1)S(1)}, u32[]{:S(2)}, u32[]{:S(2)}) %collective-permute-start.71) | collective-permute-done | bytes 1048608 | tf_op jit(solution)/shard_map/ppermute | solution.py:632
  505.2 2.5 collective-permute-start.53
  509.6 1.8 collective-permute-done.66
  512.2 2.0 collective-permute-done.64
  514.4 8.6 %collective-permute-done.74 = bf16[1,256,1024]{2,1,0:T(8,128)(2,1)S(1)} collective-permute-done((bf16[1,256,1024]{2,1,0:T(8,128)(2,1)S(1)}, bf16[1,256,1024]{2,1,0:T(8,128)(2,1)S(1)}, u32[]{:S(2)}, u32[]{:S(2)}) %collective-permute-start.74) | collective-permute-done | bytes 524320 | tf_op jit(solution)/shard_map/ppermute | solution.py:632
  523.8 1.9 collective-permute-done.53
  526.1 4.5 collective-permute-start.54
  533.7 3.8 collective-permute-start.35
  539.2 1.6 maximum_select_fusion
  540.8 13.3 %collective-permute-done.54 = bf16[256,2048]{1,0:T(8,128)(2,1)S(1)} collective-permute-done((bf16[256,2048]{1,0:T(8,128)(2,1)S(1)}, bf16[256,2048]{1,0:T(8,128)(2,1)S(1)}, u32[]{:S(2)}, u32[]{:S(2)}) %collective-permute-start.54) | collective-permute-done | bytes 1048608 | tf_op jit(solution)/shard_map/ppermute | solution.py:655
  554.5 2.3 fusion.29
  556.9 15.4 %collective-permute-done.35 = bf16[256,2048]{1,0:T(8,128)(2,1)S(1)} collective-permute-done((bf16[256,2048]{1,0:T(8,128)(2,1)S(1)}, bf16[256,2048]{1,0:T(8,128)(2,1)S(1)}, u32[]{:S(2)}, u32[]{:S(2)}) %collective-permute-start.35) | collective-permute-done | bytes 1048608 | tf_op jit(solution)/shard_map/ppermute | solution.py:655
  572.3 4.5 fusion.8
  (343 shorter events, 81.2 us)
Async XLA Ops:
  3.3 27.3 %collective-permute-start = (bf16[256,2048]{1,0:T(8,128)(2,1)S(1)}, bf16[256,2048]{1,0:T(8,128)(2,1)}, u32[]{:S(2)}, u32[]{:S(2)}) collective-permute-start(bf16[256,2048]{1,0:T(8,128)(2,1)S(1)} %copy-done.2), channel_id=1, source_target_pairs={{0,1},{1,2},{2,3},{4,5},{5,6},{6,7},{8,9},{9,10},{10,11},{12,13},{... | collective-permute-start | bytes 3145736 | tf_op jit(solution)/shard_map/ppermute | solution.py:636
  9.2 26.5 %collective-permute-start.3 = (bf16[256,2048]{1,0:T(8,128)(2,1)S(1)}, bf16[256,2048]{1,0:T(8,128)(2,1)S(1)}, u32[]{:S(2)}, u32[]{:S(2)}) collective-permute-start(bf16[256,2048]{1,0:T(8,128)(2,1)S(1)} %copy-done.2), channel_id=1, source_target_pairs={{1,0},{2,1},{3,2},{5,4},{6,5},{7,6},{9,8},{10,9},{11,10},{13,12},{... | collective-permute-start | bytes 3145736 | tf_op jit(solution)/shard_map/ppermute | solution.py:637
  10.6 26.4 %collective-permute-start.14 = (bf16[256,1792]{1,0:T(8,128)(2,1)S(1)}, bf16[256,1792]{1,0:T(8,128)(2,1)S(1)}, u32[]{:S(2)}, u32[]{:S(2)}) collective-permute-start(bf16[256,1792]{1,0:T(8,128)(2,1)S(1)} %pad_maximum_fusion.1.refs_21_.refs_6_), channel_id=1, source_target_pairs={{0,8},{4,12},{8,0},{12,4},{16,24},{20,28},{24,16},{28,20},{1,9},{5... | collective-permute-start | bytes 2752520 | tf_op jit(solution)/shard_map/ppermute | solution.py:632
  12.1 26.5 %collective-permute-start.16 = (bf16[256,1792]{1,0:T(8,128)(2,1)S(1)}, bf16[256,1792]{1,0:T(8,128)(2,1)S(1)}, u32[]{:S(2)}, u32[]{:S(2)}) collective-permute-start(bf16[256,1792]{1,0:T(8,128)(2,1)S(1)} %pad_maximum_fusion.1.refs_21_.refs_6_), channel_id=1, source_target_pairs={{0,16},{4,20},{8,24},{12,28},{16,0},{20,4},{24,8},{28,12},{1,17},{... | collective-permute-start | bytes 2752520 | tf_op jit(solution)/shard_map/ppermute | solution.py:632
  13.7 26.4 %collective-permute-start.6 = (bf16[256,2048]{1,0:T(8,128)(2,1)S(1)}, bf16[256,2048]{1,0:T(8,128)(2,1)}, u32[]{:S(2)}, u32[]{:S(2)}) collective-permute-start(bf16[256,2048]{1,0:T(8,128)(2,1)S(1)} %copy-done.2), channel_id=1, source_target_pairs={{0,4},{4,0},{8,12},{12,8},{16,20},{20,16},{24,28},{28,24},{1,5},{5... | collective-permute-start | bytes 3145736 | tf_op jit(solution)/shard_map/ppermute | solution.py:632
  35.7 26.0 %collective-permute-start.4 = (bf16[256,2048]{1,0:T(8,128)(2,1)S(1)}, bf16[256,2048]{1,0:T(8,128)(2,1)}, u32[]{:S(2)}, u32[]{:S(2)}) collective-permute-start(bf16[256,2048]{1,0:T(8,128)(2,1)S(1)} %collective-permute-done.3.refs_11_), channel_id=1, source_target_pairs={{1,0},{2,1},{5,4},{6,5},{9,8},{10,9},{13,12},{14,13},{17,16},{18,1... | collective-permute-start | bytes 3145736 | tf_op jit(solution)/shard_map/ppermute | solution.py:637
  37.0 26.0 %collective-permute-start.17 = (bf16[256,1792]{1,0:T(8,128)(2,1)S(1)}, bf16[256,1792]{1,0:T(8,128)(2,1)S(1)}, u32[]{:S(2)}, u32[]{:S(2)}) collective-permute-start(bf16[256,1792]{1,0:T(8,128)(2,1)S(1)} %collective-permute-done.13.refs_22_.refs_7_), channel_id=1, source_target_pairs={{0,16},{4,20},{8,24},{12,28},{16,0},{20,4},{24,8},{28,12},{1,17},{... | collective-permute-start | bytes 2752520 | tf_op jit(solution)/shard_map/ppermute | solution.py:632
  38.6 24.5 %collective-permute-start.15 = (bf16[256,1792]{1,0:T(8,128)(2,1)S(1)}, bf16[256,1792]{1,0:T(8,128)(2,1)S(1)}, u32[]{:S(2)}, u32[]{:S(2)}) collective-permute-start(bf16[256,1792]{1,0:T(8,128)(2,1)S(1)} %collective-permute-done.13.refs_22_.refs_7_), channel_id=1, source_target_pairs={{0,8},{4,12},{8,0},{12,4},{16,24},{20,28},{24,16},{28,20},{1,9},{5... | collective-permute-start | bytes 2752520 | tf_op jit(solution)/shard_map/ppermute | solution.py:632
  40.1 37.5 %collective-permute-start.18 = (bf16[256,1792]{1,0:T(8,128)(2,1)S(1)}, bf16[256,1792]{1,0:T(8,128)(2,1)S(1)}, u32[]{:S(2)}, u32[]{:S(2)}) collective-permute-start(bf16[256,1792]{1,0:T(8,128)(2,1)S(1)} %collective-permute-done.14.refs_23_.refs_1_.refs_8_), channel_id=1, source_target_pairs={{0,16},{4,20},{8,24},{12,28},{16,0},{20,4},{24,8},{28,12},{1,17},{... | collective-permute-start | bytes 2752520 | tf_op jit(solution)/shard_map/ppermute | solution.py:632
  40.6 38.5 %collective-permute-start.2 = (bf16[256,2048]{1,0:T(8,128)(2,1)}, bf16[256,2048]{1,0:T(8,128)(2,1)S(1)}, u32[]{:S(2)}, u32[]{:S(2)}) collective-permute-start(bf16[256,2048]{1,0:T(8,128)(2,1)} %collective-permute-done.1.refs_9_), channel_id=1, source_target_pairs={{2,3},{6,7},{10,11},{14,15},{18,19},{22,23},{26,27},{30,31}} | collective-permute-start | bytes 3145736 | tf_op jit(solution)/shard_map/ppermute | solution.py:636
  61.7 25.2 %collective-permute-start.5 = (bf16[256,2048]{1,0:T(8,128)(2,1)}, bf16[256,2048]{1,0:T(8,128)(2,1)S(1)}, u32[]{:S(2)}, u32[]{:S(2)}) collective-permute-start(bf16[256,2048]{1,0:T(8,128)(2,1)} %collective-permute-done.4.refs_12_), channel_id=1, source_target_pairs={{1,0},{5,4},{9,8},{13,12},{17,16},{21,20},{25,24},{29,28}} | collective-permute-start | bytes 3145736 | tf_op jit(solution)/shard_map/ppermute | solution.py:637
  63.0 25.2 %collective-permute-start.10 = (bf16[256,2048]{1,0:T(8,128)(2,1)S(1)}, bf16[256,2048]{1,0:T(8,128)(2,1)}, u32[]{:S(2)}, u32[]{:S(2)}) collective-permute-start(bf16[256,2048]{1,0:T(8,128)(2,1)S(1)} %collective-permute-done.3.refs_11_), channel_id=1, source_target_pairs={{0,4},{4,0},{8,12},{12,8},{16,20},{20,16},{24,28},{28,24},{1,5},{5... | collective-permute-start | bytes 3145736 | tf_op jit(solution)/shard_map/ppermute | solution.py:632
  63.1 26.6 %collective-permute-start.7 = (bf16[256,2048]{1,0:T(8,128)(2,1)}, bf16[256,2048]{1,0:T(8,128)(2,1)}, u32[]{:S(2)}, u32[]{:S(2)}) collective-permute-start(bf16[256,2048]{1,0:T(8,128)(2,1)} %collective-permute-done.refs_8_), channel_id=1, source_target_pairs={{0,4},{4,0},{8,12},{12,8},{16,20},{20,16},{24,28},{28,24},{1,5},{5... | collective-permute-start | bytes 3145736 | tf_op jit(solution)/shard_map/ppermute | solution.py:632
  77.7 20.0 %collective-permute-start.19 = (bf16[256,1792]{1,0:T(8,128)(2,1)S(1)}, bf16[256,1792]{1,0:T(8,128)(2,1)S(1)}, u32[]{:S(2)}, u32[]{:S(2)}) collective-permute-start(bf16[256,1792]{1,0:T(8,128)(2,1)S(1)} %collective-permute-done.17.refs_26_.refs_11_), channel_id=1, source_target_pairs={{0,8},{4,12},{8,0},{12,4},{16,24},{20,28},{24,16},{28,20},{1,9},{5... | collective-permute-start | bytes 2752520 | tf_op jit(solution)/shard_map/ppermute | solution.py:632
  79.2 24.0 %collective-permute-start.11 = (bf16[256,2048]{1,0:T(8,128)(2,1)}, bf16[256,2048]{1,0:T(8,128)(2,1)}, u32[]{:S(2)}, u32[]{:S(2)}) collective-permute-start(bf16[256,2048]{1,0:T(8,128)(2,1)} %collective-permute-done.4.refs_12_), channel_id=1, source_target_pairs={{0,4},{4,0},{8,12},{12,8},{16,20},{20,16},{24,28},{28,24},{1,5},{5... | collective-permute-start | bytes 3145736 | tf_op jit(solution)/shard_map/ppermute | solution.py:632
  86.9 21.8 %collective-permute-start.8 = (bf16[256,2048]{1,0:T(8,128)(2,1)}, bf16[256,2048]{1,0:T(8,128)(2,1)}, u32[]{:S(2)}, u32[]{:S(2)}) collective-permute-start(bf16[256,2048]{1,0:T(8,128)(2,1)} %collective-permute-done.1.refs_9_), channel_id=1, source_target_pairs={{0,4},{4,0},{8,12},{12,8},{16,20},{20,16},{24,28},{28,24},{1,5},{5... | collective-permute-start | bytes 3145736 | tf_op jit(solution)/shard_map/ppermute | solution.py:632
  88.3 69.0 %collective-permute-start.21 = (bf16[256,2048]{1,0:T(8,128)(2,1)}, bf16[256,2048]{1,0:T(8,128)(2,1)S(1)}, u32[]{:S(2)}, u32[]{:S(2)}) collective-permute-start(bf16[256,2048]{1,0:T(8,128)(2,1)} %tie.7.refs_29_.refs_2_), channel_id=1, source_target_pairs={{1,0},{2,1},{3,2},{5,4},{6,5},{7,6},{9,8},{10,9},{11,10},{13,12},{... | collective-permute-start | bytes 3145736 | tf_op jit(solution)/shard_map/ppermute | solution.py:637
  89.7 33.9 %collective-permute-start.12 = (bf16[256,2048]{1,0:T(8,128)(2,1)}, bf16[256,2048]{1,0:T(8,128)(2,1)}, u32[]{:S(2)}, u32[]{:S(2)}) collective-permute-start(bf16[256,2048]{1,0:T(8,128)(2,1)} %copy-done.37), channel_id=1, source_target_pairs={{0,4},{4,0},{8,12},{12,8},{16,20},{20,16},{24,28},{28,24},{1,5},{5... | collective-permute-start | bytes 3145736 | tf_op jit(solution)/shard_map/ppermute | solution.py:632
  97.6 25.9 %collective-permute-start.9 = (bf16[256,2048]{1,0:T(8,128)(2,1)}, bf16[256,2048]{1,0:T(8,128)(2,1)}, u32[]{:S(2)}, u32[]{:S(2)}) collective-permute-start(bf16[256,2048]{1,0:T(8,128)(2,1)} %copy-done.36), channel_id=1, source_target_pairs={{0,4},{4,0},{8,12},{12,8},{16,20},{20,16},{24,28},{28,24},{1,5},{5... | collective-permute-start | bytes 3145736 | tf_op jit(solution)/shard_map/ppermute | solution.py:632
  103.2 60.4 %collective-permute-start.20 = (bf16[256,2048]{1,0:T(8,128)(2,1)S(1)}, bf16[256,2048]{1,0:T(8,128)(2,1)S(1)}, u32[]{:S(2)}, u32[]{:S(2)}) collective-permute-start(bf16[256,2048]{1,0:T(8,128)(2,1)S(1)} %copy-done.4), channel_id=1, source_target_pairs={{0,1},{1,2},{2,3},{4,5},{5,6},{6,7},{8,9},{9,10},{10,11},{12,13},{... | collective-permute-start | bytes 3145736 | tf_op jit(solution)/shard_map/ppermute | solution.py:636
  108.7 51.8 %collective-permute-start.22 = (bf16[1280,256]{1,0:T(8,128)(2,1)}, bf16[1280,256]{1,0:T(8,128)(2,1)}, u32[]{:S(2)}, u32[]{:S(2)}) collective-permute-start(bf16[1280,256]{1,0:T(8,128)(2,1)} %pad_maximum_fusion.4), channel_id=1, source_target_pairs={{0,4},{4,0},{8,12},{12,8},{16,20},{20,16},{24,28},{28,24},{1,5},{5... | collective-permute-start | bytes 1966088 | tf_op jit(solution)/shard_map/ppermute | solution.py:632
  158.2 28.7 %collective-permute-start.30 = (bf16[256,2048]{1,0:T(8,128)(2,1)}, bf16[256,2048]{1,0:T(8,128)(2,1)S(1)}, u32[]{:S(2)}, u32[]{:S(2)}) collective-permute-start(bf16[256,2048]{1,0:T(8,128)(2,1)} %tie.9.refs_4_.refs_6_), channel_id=1, source_target_pairs={{1,0},{2,1},{5,4},{6,5},{9,8},{10,9},{13,12},{14,13},{17,16},{18,1... | collective-permute-start | bytes 3145736 | tf_op jit(solution)/shard_map/ppermute | solution.py:637
  160.6 17.3 %collective-permute-start.26 = (bf16[1280,256]{1,0:T(8,128)(2,1)}, bf16[1280,256]{1,0:T(8,128)(2,1)S(1)}, u32[]{:S(2)}, u32[]{:S(2)}) collective-permute-start(bf16[1280,256]{1,0:T(8,128)(2,1)} %tie.11.refs_4_.refs_9_.refs_17_), channel_id=1, source_target_pairs={{0,16},{4,20},{8,24},{12,28},{16,0},{20,4},{24,8},{28,12},{1,17},{... | collective-permute-start | bytes 1966088 | tf_op jit(solution)/shard_map/ppermute | solution.py:632
  162.1 17.8 %collective-permute-start.23 = (bf16[1280,256]{1,0:T(8,128)(2,1)}, bf16[1280,256]{1,0:T(8,128)(2,1)S(1)}, u32[]{:S(2)}, u32[]{:S(2)}) collective-permute-start(bf16[1280,256]{1,0:T(8,128)(2,1)} %tie.10.refs_3_.refs_8_.refs_16_), channel_id=1, source_target_pairs={{0,8},{4,12},{8,0},{12,4},{16,24},{20,28},{24,16},{28,20},{1,9},{5... | collective-permute-start | bytes 1966088 | tf_op jit(solution)/shard_map/ppermute | solution.py:632
  164.6 38.8 %collective-permute-start.29 = (bf16[256,2048]{1,0:T(8,128)(2,1)}, bf16[256,2048]{1,0:T(8,128)(2,1)S(1)}, u32[]{:S(2)}, u32[]{:S(2)}) collective-permute-start(bf16[256,2048]{1,0:T(8,128)(2,1)} %tie.8.refs_3_), channel_id=1, source_target_pairs={{1,2},{2,3},{5,6},{6,7},{9,10},{10,11},{13,14},{14,15},{17,18},{18... | collective-permute-start | bytes 3145736 | tf_op jit(solution)/shard_map/ppermute | solution.py:636
  165.5 38.9 %collective-permute-start.24 = (bf16[1280,256]{1,0:T(8,128)(2,1)}, bf16[1280,256]{1,0:T(8,128)(2,1)S(1)}, u32[]{:S(2)}, u32[]{:S(2)}) collective-permute-start(bf16[1280,256]{1,0:T(8,128)(2,1)} %tie.11.refs_4_.refs_9_.refs_17_), channel_id=1, source_target_pairs={{0,8},{4,12},{8,0},{12,4},{16,24},{20,28},{24,16},{28,20},{1,9},{5... | collective-permute-start | bytes 1966088 | tf_op jit(solution)/shard_map/ppermute | solution.py:632
  177.9 26.5 %collective-permute-start.25 = (bf16[1280,256]{1,0:T(8,128)(2,1)S(1)}, bf16[1280,256]{1,0:T(8,128)(2,1)S(1)}, u32[]{:S(2)}, u32[]{:S(2)}) collective-permute-start(bf16[1280,256]{1,0:T(8,128)(2,1)S(1)} %copy-done.11), channel_id=1, source_target_pairs={{0,16},{4,20},{8,24},{12,28},{16,0},{20,4},{24,8},{28,12},{1,17},{... | collective-permute-start | bytes 1966088 | tf_op jit(solution)/shard_map/ppermute | solution.py:632
  179.9 27.3 %collective-permute-start.28 = (bf16[1280,256]{1,0:T(8,128)(2,1)S(1)}, bf16[1280,256]{1,0:T(8,128)(2,1)S(1)}, u32[]{:S(2)}, u32[]{:S(2)}) collective-permute-start(bf16[1280,256]{1,0:T(8,128)(2,1)S(1)} %collective-permute-done.26.refs_8_.refs_13_.refs_21_), channel_id=1, source_target_pairs={{0,8},{4,12},{8,0},{12,4},{16,24},{20,28},{24,16},{28,20},{1,9},{5... | collective-permute-start | bytes 1966088 | tf_op jit(solution)/shard_map/ppermute | solution.py:632
  186.9 21.4 %collective-permute-start.27 = (bf16[1280,256]{1,0:T(8,128)(2,1)S(1)}, bf16[1280,256]{1,0:T(8,128)(2,1)S(1)}, u32[]{:S(2)}, u32[]{:S(2)}) collective-permute-start(bf16[1280,256]{1,0:T(8,128)(2,1)S(1)} %collective-permute-done.23.refs_5_.refs_10_.refs_18_), channel_id=1, source_target_pairs={{0,16},{4,20},{8,24},{12,28},{16,0},{20,4},{24,8},{28,12},{1,17},{... | collective-permute-start | bytes 1966088 | tf_op jit(solution)/shard_map/ppermute | solution.py:632
  228.9 29.6 %collective-permute-start.31 = (bf16[4,256,2048]{2,1,0:T(8,128)(2,1)}, bf16[4,256,2048]{2,1,0:T(8,128)(2,1)S(1)}, u32[]{:S(2)}, u32[]{:S(2)}) collective-permute-start(bf16[4,256,2048]{2,1,0:T(8,128)(2,1)} %get-tuple-element.63.refs_16_), channel_id=1, source_target_pairs={{0,4},{4,0},{8,12},{12,8},{16,20},{20,16},{24,28},{28,24},{1,5},{5... | collective-permute-start | bytes 12582920 | tf_op jit(solution)/shard_map/ppermute | solution.py:632
  229.6 28.4 %collective-permute-start.39 = (bf16[256,2048]{1,0:T(8,128)(2,1)S(1)}, bf16[256,2048]{1,0:T(8,128)(2,1)}, u32[]{:S(2)}, u32[]{:S(2)}) collective-permute-start(bf16[256,2048]{1,0:T(8,128)(2,1)S(1)} %copy-done.16), channel_id=1, source_target_pairs={{1,0},{5,4},{9,8},{13,12},{17,16},{21,20},{25,24},{29,28}} | collective-permute-start | bytes 3145736 | tf_op jit(solution)/shard_map/ppermute | solution.py:637
  230.9 27.1 %collective-permute-start.38 = (bf16[256,2048]{1,0:T(8,128)(2,1)S(1)}, bf16[256,2048]{1,0:T(8,128)(2,1)}, u32[]{:S(2)}, u32[]{:S(2)}) collective-permute-start(bf16[256,2048]{1,0:T(8,128)(2,1)S(1)} %copy-done.18), channel_id=1, source_target_pairs={{2,3},{6,7},{10,11},{14,15},{18,19},{22,23},{26,27},{30,31}} | collective-permute-start | bytes 3145736 | tf_op jit(solution)/shard_map/ppermute | solution.py:636
  237.3 25.8 %collective-permute-start.41 = (bf16[256,2048]{1,0:T(8,128)(2,1)S(1)}, bf16[256,2048]{1,0:T(8,128)(2,1)S(1)}, u32[]{:S(2)}, u32[]{:S(2)}) collective-permute-start(bf16[256,2048]{1,0:T(8,128)(2,1)S(1)} %copy-done.10), channel_id=1, source_target_pairs={{0,4},{4,0},{8,12},{12,8},{16,20},{20,16},{24,28},{28,24},{1,5},{5... | collective-permute-start | bytes 3145736 | tf_op jit(solution)/shard_map/ppermute | solution.py:632
  238.8 26.7 %collective-permute-start.45 = (bf16[256,2048]{1,0:T(8,128)(2,1)S(1)}, bf16[256,2048]{1,0:T(8,128)(2,1)S(1)}, u32[]{:S(2)}, u32[]{:S(2)}) collective-permute-start(bf16[256,2048]{1,0:T(8,128)(2,1)S(1)} %copy-done.16), channel_id=1, source_target_pairs={{0,4},{4,0},{8,12},{12,8},{16,20},{20,16},{24,28},{28,24},{1,5},{5... | collective-permute-start | bytes 3145736 | tf_op jit(solution)/shard_map/ppermute | solution.py:632
  258.0 22.5 %collective-permute-start.42 = (bf16[256,2048]{1,0:T(8,128)(2,1)S(1)}, bf16[256,2048]{1,0:T(8,128)(2,1)}, u32[]{:S(2)}, u32[]{:S(2)}) collective-permute-start(bf16[256,2048]{1,0:T(8,128)(2,1)S(1)} %copy-done.18), channel_id=1, source_target_pairs={{0,4},{4,0},{8,12},{12,8},{16,20},{20,16},{24,28},{28,24},{1,5},{5... | collective-permute-start | bytes 3145736 | tf_op jit(solution)/shard_map/ppermute | solution.py:632
  258.0 22.5 %collective-permute-start.46 = (bf16[256,2048]{1,0:T(8,128)(2,1)}, bf16[256,2048]{1,0:T(8,128)(2,1)}, u32[]{:S(2)}, u32[]{:S(2)}) collective-permute-start(bf16[256,2048]{1,0:T(8,128)(2,1)} %collective-permute-done.39.refs_8_), channel_id=1, source_target_pairs={{0,4},{4,0},{8,12},{12,8},{16,20},{20,16},{24,28},{28,24},{1,5},{5... | collective-permute-start | bytes 3145736 | tf_op jit(solution)/shard_map/ppermute | solution.py:632
  258.5 22.0 %collective-permute-start.43 = (bf16[256,2048]{1,0:T(8,128)(2,1)}, bf16[256,2048]{1,0:T(8,128)(2,1)}, u32[]{:S(2)}, u32[]{:S(2)}) collective-permute-start(bf16[256,2048]{1,0:T(8,128)(2,1)} %collective-permute-done.38.refs_5_), channel_id=1, source_target_pairs={{0,4},{4,0},{8,12},{12,8},{16,20},{20,16},{24,28},{28,24},{1,5},{5... | collective-permute-start | bytes 3145736 | tf_op jit(solution)/shard_map/ppermute | solution.py:632
  263.1 54.4 %collective-permute-start.32 = (bf16[256,2048]{1,0:T(8,128)(2,1)}, bf16[256,2048]{1,0:T(8,128)(2,1)}, u32[]{:S(2)}, u32[]{:S(2)}) collective-permute-start(bf16[256,2048]{1,0:T(8,128)(2,1)} %get-tuple-element.109.refs_28_), channel_id=1, source_target_pairs={{0,1},{4,5},{8,9},{12,13},{16,17},{20,21},{24,25},{28,29}} | collective-permute-start | bytes 3145736 | tf_op jit(solution)/shard_map/ppermute | solution.py:655
  265.5 52.0 %collective-permute-start.33 = (bf16[256,2048]{1,0:T(8,128)(2,1)S(1)}, bf16[256,2048]{1,0:T(8,128)(2,1)}, u32[]{:S(2)}, u32[]{:S(2)}) collective-permute-start(bf16[256,2048]{1,0:T(8,128)(2,1)S(1)} %get-tuple-element.110.refs_27_), channel_id=1, source_target_pairs={{3,2},{7,6},{11,10},{15,14},{19,18},{23,22},{27,26},{31,30}} | collective-permute-start | bytes 3145736 | tf_op jit(solution)/shard_map/ppermute | solution.py:656
  312.8 37.7 %collective-permute-start.47 = (bf16[2,1280,256]{2,1,0:T(8,128)(2,1)}, bf16[2,1280,256]{2,1,0:T(8,128)(2,1)}, u32[]{:S(2)}, u32[]{:S(2)}) collective-permute-start(bf16[2,1280,256]{2,1,0:T(8,128)(2,1)} %get-tuple-element.72.refs_9_), channel_id=1, source_target_pairs={{0,16},{4,20},{8,24},{12,28},{16,0},{20,4},{24,8},{28,12},{1,17},{... | collective-permute-start | bytes 3932168 | tf_op jit(solution)/shard_map/ppermute | solution.py:632
  314.4 38.3 %collective-permute-start.48 = (bf16[2,1280,256]{2,1,0:T(8,128)(2,1)}, bf16[2,1280,256]{2,1,0:T(8,128)(2,1)}, u32[]{:S(2)}, u32[]{:S(2)}) collective-permute-start(bf16[2,1280,256]{2,1,0:T(8,128)(2,1)} %get-tuple-element.80), channel_id=1, source_target_pairs={{0,8},{4,12},{8,0},{12,4},{16,24},{20,28},{24,16},{28,20},{1,9},{5... | collective-permute-start | bytes 3932168 | tf_op jit(solution)/shard_map/ppermute | solution.py:632
  320.4 49.2 %collective-permute-start.36 = (bf16[256,2048]{1,0:T(8,128)(2,1)S(1)}, bf16[256,2048]{1,0:T(8,128)(2,1)}, u32[]{:S(2)}, u32[]{:S(2)}) collective-permute-start(bf16[256,2048]{1,0:T(8,128)(2,1)S(1)} %fusion.17.refs_10_), channel_id=1, source_target_pairs={{2,1},{3,2},{6,5},{7,6},{10,9},{11,10},{14,13},{15,14},{18,17},{19... | collective-permute-start | bytes 3145736 | tf_op jit(solution)/shard_map/ppermute | solution.py:656
  322.1 50.6 %collective-permute-start.34 = (bf16[256,2048]{1,0:T(8,128)(2,1)S(1)}, bf16[256,2048]{1,0:T(8,128)(2,1)}, u32[]{:S(2)}, u32[]{:S(2)}) collective-permute-start(bf16[256,2048]{1,0:T(8,128)(2,1)S(1)} %fusion.17.refs_10_), channel_id=1, source_target_pairs={{0,1},{1,2},{4,5},{5,6},{8,9},{9,10},{12,13},{13,14},{16,17},{17,1... | collective-permute-start | bytes 3145736 | tf_op jit(solution)/shard_map/ppermute | solution.py:655
  354.1 56.0 %collective-permute-start.69 = (bf16[1,1280,256]{2,1,0:T(8,128)(2,1)S(1)}, bf16[1,1280,256]{2,1,0:T(8,128)(2,1)S(1)}, u32[]{:S(2)}, u32[]{:S(2)}) collective-permute-start(bf16[1,1280,256]{2,1,0:T(8,128)(2,1)S(1)} %add_convert_fusion.9.refs_17_), channel_id=1, source_target_pairs={{0,16},{4,20},{8,24},{12,28},{16,0},{20,4},{24,8},{28,12},{1,17},{... | collective-permute-start | bytes 1966088 | tf_op jit(solution)/shard_map/ppermute | solution.py:632
  391.5 33.7 %collective-permute-start.50 = (bf16[2,256,2048]{2,1,0:T(8,128)(2,1)}, bf16[2,256,2048]{2,1,0:T(8,128)(2,1)}, u32[]{:S(2)}, u32[]{:S(2)}) collective-permute-start(bf16[2,256,2048]{2,1,0:T(8,128)(2,1)} %get-tuple-element.85), channel_id=1, source_target_pairs={{0,4},{4,0},{8,12},{12,8},{16,20},{20,16},{24,28},{28,24},{1,5},{5... | collective-permute-start | bytes 6291464 | tf_op jit(solution)/shard_map/ppermute | solution.py:632
  417.6 46.2 %collective-permute-start.70 = (bf16[1280,256]{1,0:T(8,128)(2,1)}, bf16[1280,256]{1,0:T(8,128)(2,1)S(1)}, u32[]{:S(2)}, u32[]{:S(2)}) collective-permute-start(bf16[1280,256]{1,0:T(8,128)(2,1)} %fusion.23), channel_id=1, source_target_pairs={{0,4},{4,0},{8,12},{12,8},{16,20},{20,16},{24,28},{28,24},{1,5},{5... | collective-permute-start | bytes 1966088 | tf_op jit(solution)/shard_map/ppermute | solution.py:632
  418.1 65.1 %collective-permute-start.49 = (bf16[2,256,2048]{2,1,0:T(8,128)(2,1)}, bf16[2,256,2048]{2,1,0:T(8,128)(2,1)}, u32[]{:S(2)}, u32[]{:S(2)}) collective-permute-start(bf16[2,256,2048]{2,1,0:T(8,128)(2,1)} %get-tuple-element.83), channel_id=1, source_target_pairs={{0,4},{4,0},{8,12},{12,8},{16,20},{20,16},{24,28},{28,24},{1,5},{5... | collective-permute-start | bytes 6291464 | tf_op jit(solution)/shard_map/ppermute | solution.py:632
  418.8 41.0 %collective-permute-start.60 = (f32[4096]{0:T(1024)S(1)}, f32[4096]{0:T(1024)S(1)}, u32[]{:S(2)}, u32[]{:S(2)}) collective-permute-start(f32[4096]{0:T(1024)S(1)} %slice_add_fusion), channel_id=1, source_target_pairs={{0,1},{1,0},{2,3},{3,2},{4,5},{5,4},{6,7},{7,6},{8,9},{9,8},{10,11... | collective-permute-start | bytes 49160 | tf_op jit(solution)/shard_map/ppermute | solution.py:917
  420.6 39.8 %collective-permute-start.61 = (f32[4096]{0:T(1024)S(1)}, f32[4096]{0:T(1024)S(1)}, u32[]{:S(2)}, u32[]{:S(2)}) collective-permute-start(f32[4096]{0:T(1024)S(1)} %slice_add_fusion), channel_id=1, source_target_pairs={{0,2},{1,3},{2,0},{3,1},{4,6},{5,7},{6,4},{7,5},{8,10},{9,11},{10,... | collective-permute-start | bytes 49160 | tf_op jit(solution)/shard_map/ppermute | solution.py:917
  425.3 35.2 %collective-permute-start.62 = (f32[4096]{0:T(1024)S(1)}, f32[4096]{0:T(1024)S(1)}, u32[]{:S(2)}, u32[]{:S(2)}) collective-permute-start(f32[4096]{0:T(1024)S(1)} %slice_add_fusion), channel_id=1, source_target_pairs={{0,3},{1,2},{2,1},{3,0},{4,7},{5,6},{6,5},{7,4},{8,11},{9,10},{10,... | collective-permute-start | bytes 49160 | tf_op jit(solution)/shard_map/ppermute | solution.py:917
  459.7 19.4 %collective-permute-start.63 = (bf16[2,256,768]{2,1,0:T(8,128)(2,1)}, bf16[2,256,768]{2,1,0:T(8,128)(2,1)S(1)}, u32[]{:S(2)}, u32[]{:S(2)}) collective-permute-start(bf16[2,256,768]{2,1,0:T(8,128)(2,1)} %get-tuple-element.94), channel_id=1, source_target_pairs={{0,16},{4,20},{8,24},{12,28},{16,0},{20,4},{24,8},{28,12},{1,17},{... | collective-permute-start | bytes 2359304 | tf_op jit(solution)/shard_map/ppermute | solution.py:632
  460.4 24.4 %collective-permute-start.51 = (bf16[256,2048]{1,0:T(8,128)(2,1)S(1)}, bf16[256,2048]{1,0:T(8,128)(2,1)S(1)}, u32[]{:S(2)}, u32[]{:S(2)}) collective-permute-start(bf16[256,2048]{1,0:T(8,128)(2,1)S(1)} %copy-done.13), channel_id=1, source_target_pairs={{0,1},{4,5},{8,9},{12,13},{16,17},{20,21},{24,25},{28,29}} | collective-permute-start | bytes 3145736 | tf_op jit(solution)/shard_map/ppermute | solution.py:655
  463.0 23.1 %collective-permute-start.52 = (bf16[256,2048]{1,0:T(8,128)(2,1)S(1)}, bf16[256,2048]{1,0:T(8,128)(2,1)S(1)}, u32[]{:S(2)}, u32[]{:S(2)}) collective-permute-start(bf16[256,2048]{1,0:T(8,128)(2,1)S(1)} %copy-done.14), channel_id=1, source_target_pairs={{3,2},{7,6},{11,10},{15,14},{19,18},{23,22},{27,26},{31,30}} | collective-permute-start | bytes 3145736 | tf_op jit(solution)/shard_map/ppermute | solution.py:656
  463.7 18.8 %collective-permute-start.65 = (bf16[2,256,768]{2,1,0:T(8,128)(2,1)}, bf16[2,256,768]{2,1,0:T(8,128)(2,1)S(1)}, u32[]{:S(2)}, u32[]{:S(2)}) collective-permute-start(bf16[2,256,768]{2,1,0:T(8,128)(2,1)} %get-tuple-element.97), channel_id=1, source_target_pairs={{0,8},{4,12},{8,0},{12,4},{16,24},{20,28},{24,16},{28,20},{1,9},{5... | collective-permute-start | bytes 2359304 | tf_op jit(solution)/shard_map/ppermute | solution.py:632
  479.1 26.1 %collective-permute-start.71 = (bf16[2,256,1024]{2,1,0:T(8,128)(2,1)S(1)}, bf16[2,256,1024]{2,1,0:T(8,128)(2,1)S(1)}, u32[]{:S(2)}, u32[]{:S(2)}) collective-permute-start(bf16[2,256,1024]{2,1,0:T(8,128)(2,1)S(1)} %copy-done.49), channel_id=1, source_target_pairs={{0,16},{4,20},{8,24},{12,28},{16,0},{20,4},{24,8},{28,12},{1,17},{... | collective-permute-start | bytes 3145736 | tf_op jit(solution)/shard_map/ppermute | solution.py:632
  482.5 26.1 %collective-permute-start.73 = (bf16[2,256,1024]{2,1,0:T(8,128)(2,1)S(1)}, bf16[2,256,1024]{2,1,0:T(8,128)(2,1)S(1)}, u32[]{:S(2)}, u32[]{:S(2)}) collective-permute-start(bf16[2,256,1024]{2,1,0:T(8,128)(2,1)S(1)} %copy-done.69), channel_id=1, source_target_pairs={{0,8},{4,12},{8,0},{12,4},{16,24},{20,28},{24,16},{28,20},{1,9},{5... | collective-permute-start | bytes 3145736 | tf_op jit(solution)/shard_map/ppermute | solution.py:632
  483.2 73.7 %collective-permute-start.37 = (bf16[256,2048]{1,0:T(8,128)(2,1)S(1)}, bf16[256,2048]{1,0:T(8,128)(2,1)S(1)}, u32[]{:S(2)}, u32[]{:S(2)}) collective-permute-start(bf16[256,2048]{1,0:T(8,128)(2,1)S(1)} %copy-done.33), channel_id=1, source_target_pairs={{1,0},{2,1},{3,2},{5,4},{6,5},{7,6},{9,8},{10,9},{11,10},{13,12},{... | collective-permute-start | bytes 3145736 | tf_op jit(solution)/shard_map/ppermute | solution.py:656
  484.8 29.3 %collective-permute-start.64 = (bf16[1,256,768]{2,1,0:T(8,128)(2,1)S(1)}, bf16[1,256,768]{2,1,0:T(8,128)(2,1)S(1)}, u32[]{:S(2)}, u32[]{:S(2)}) collective-permute-start(bf16[1,256,768]{2,1,0:T(8,128)(2,1)S(1)} %add_convert_fusion.16), channel_id=1, source_target_pairs={{0,8},{4,12},{8,0},{12,4},{16,24},{20,28},{24,16},{28,20},{1,9},{5... | collective-permute-start | bytes 1179656 | tf_op jit(solution)/shard_map/ppermute | solution.py:632
  486.1 25.3 %collective-permute-start.66 = (bf16[1,256,768]{2,1,0:T(8,128)(2,1)S(1)}, bf16[1,256,768]{2,1,0:T(8,128)(2,1)S(1)}, u32[]{:S(2)}, u32[]{:S(2)}) collective-permute-start(bf16[1,256,768]{2,1,0:T(8,128)(2,1)S(1)} %add_convert_fusion.15), channel_id=1, source_target_pairs={{0,16},{4,20},{8,24},{12,28},{16,0},{20,4},{24,8},{28,12},{1,17},{... | collective-permute-start | bytes 1179656 | tf_op jit(solution)/shard_map/ppermute | solution.py:632
  505.2 20.5 %collective-permute-start.53 = (bf16[256,2048]{1,0:T(8,128)(2,1)S(1)}, bf16[256,2048]{1,0:T(8,128)(2,1)S(1)}, u32[]{:S(2)}, u32[]{:S(2)}) collective-permute-start(bf16[256,2048]{1,0:T(8,128)(2,1)S(1)} %fusion.13), channel_id=1, source_target_pairs={{0,1},{1,2},{4,5},{5,6},{8,9},{9,10},{12,13},{13,14},{16,17},{17,1... | collective-permute-start | bytes 3145736 | tf_op jit(solution)/shard_map/ppermute | solution.py:655
  508.6 22.0 %collective-permute-start.55 = (bf16[256,2048]{1,0:T(8,128)(2,1)S(1)}, bf16[256,2048]{1,0:T(8,128)(2,1)S(1)}, u32[]{:S(2)}, u32[]{:S(2)}) collective-permute-start(bf16[256,2048]{1,0:T(8,128)(2,1)S(1)} %fusion.13), channel_id=1, source_target_pairs={{2,1},{3,2},{6,5},{7,6},{10,9},{11,10},{14,13},{15,14},{18,17},{19... | collective-permute-start | bytes 3145736 | tf_op jit(solution)/shard_map/ppermute | solution.py:656
  526.1 28.0 %collective-permute-start.54 = (bf16[256,2048]{1,0:T(8,128)(2,1)S(1)}, bf16[256,2048]{1,0:T(8,128)(2,1)S(1)}, u32[]{:S(2)}, u32[]{:S(2)}) collective-permute-start(bf16[256,2048]{1,0:T(8,128)(2,1)S(1)} %add_convert_fusion.1), channel_id=1, source_target_pairs={{0,1},{1,2},{2,3},{4,5},{5,6},{6,7},{8,9},{9,10},{10,11},{12,13},{... | collective-permute-start | bytes 3145736 | tf_op jit(solution)/shard_map/ppermute | solution.py:655
  531.0 23.5 %collective-permute-start.56 = (bf16[256,2048]{1,0:T(8,128)(2,1)S(1)}, bf16[256,2048]{1,0:T(8,128)(2,1)S(1)}, u32[]{:S(2)}, u32[]{:S(2)}) collective-permute-start(bf16[256,2048]{1,0:T(8,128)(2,1)S(1)} %add_convert_fusion), channel_id=1, source_target_pairs={{1,0},{2,1},{3,2},{5,4},{6,5},{7,6},{9,8},{10,9},{11,10},{13,12},{... | collective-permute-start | bytes 3145736 | tf_op jit(solution)/shard_map/ppermute | solution.py:656
  533.7 38.6 %collective-permute-start.35 = (bf16[256,2048]{1,0:T(8,128)(2,1)S(1)}, bf16[256,2048]{1,0:T(8,128)(2,1)S(1)}, u32[]{:S(2)}, u32[]{:S(2)}) collective-permute-start(bf16[256,2048]{1,0:T(8,128)(2,1)S(1)} %copy-done.34), channel_id=1, source_target_pairs={{0,1},{1,2},{2,3},{4,5},{5,6},{6,7},{8,9},{9,10},{10,11},{12,13},{... | collective-permute-start | bytes 3145736 | tf_op jit(solution)/shard_map/ppermute | solution.py:655
  (84 other events, 1760.2 us)

commit v3 on v2

--- a/solution.py
+++ b/solution.py
@@ -2,6 +2,7 @@
 
 import jax
 import jax.numpy as jnp
+import numpy as np
 from jax import lax
 from jax.experimental import pallas as pl
 from jax.experimental.pallas import tpu as pltpu
@@ -49,31 +50,34 @@
     )(*scalars, *operands, *deps)
 
 
-def tie(value, *deps):
+def fence(values, deps=()):
     return call(
         lambda *refs: None,
-        "tie",
-        [value],
+        "fence",
+        values,
         deps,
-        in_specs=[ANY],
-        out_specs=ANY,
-        out_shape=jax.ShapeDtypeStruct(value.shape, value.dtype),
-        input_output_aliases={0: 0},
+        in_specs=[ANY] * len(values),
+        out_specs=[ANY] * len(values),
+        out_shape=[jax.ShapeDtypeStruct(v.shape, v.dtype) for v in values],
+        input_output_aliases={n: n for n in range(len(values))},
     )
 
 
 def rotary_tables(length):
-    positions = jnp.arange(length).astype(F32)
-    frequency = 10000.0 ** (-jnp.arange(ROT // 2).astype(F32) * 2.0 / ROT)
-    angles = positions[:, None] * frequency[None, :]
-    cosine, sine = jnp.cos(angles), jnp.sin(angles)
+    positions = np.arange(length, dtype=np.float32)
+    frequency = 10000.0 ** (-np.arange(ROT // 2, dtype=np.float64) * 2.0 / ROT)
+    angles = positions[:, None] * frequency.astype(np.float32)[None, :]
+    cosine, sine = np.cos(angles.astype(np.float64)), np.sin(angles.astype(np.float64))
     rest = HEAD_DIM - ROT
-    none = jnp.zeros((length, ROT // 2), F32)
-    ones, zeros = jnp.ones((length, rest), F32), jnp.zeros((length, rest), F32)
-    straight = jnp.concatenate([cosine, cosine, ones], axis=1)
-    left = jnp.concatenate([-sine, none, zeros], axis=1)
-    right = jnp.concatenate([none, sine, zeros], axis=1)
-    return [jnp.concatenate([t, t], axis=1) for t in (straight, left, right)]
+    none = np.zeros((length, ROT // 2))
+    ones, zeros = np.ones((length, rest)), np.zeros((length, rest))
+    straight = np.concatenate([cosine, cosine, ones], axis=1)
+    left = np.concatenate([-sine, none, zeros], axis=1)
+    right = np.concatenate([none, sine, zeros], axis=1)
+    return [
+        jnp.asarray(np.concatenate([t, t], axis=1).astype(np.float32))
+        for t in (straight, left, right)
+    ]
 
 
 def rotated(u, straight, left, right, sign):
@@ -105,17 +109,15 @@
     return lambda owner: ref.at[:, pl.ds(pl.multiple_of(owner * size, size), size)]
 
 
-class Chunks:
-    def __init__(self, own, below, above):
-        self.own, self.below, self.above = own, list(below), list(above)
-
-    def flat(self):
-        return [self.own, *self.below, *self.above]
-
-    @staticmethod
-    def of(refs):
-        half = len(refs) // 2
-        return Chunks(refs[0], refs[1 : 1 + half], refs[1 + half :])
+def flat(chunks):
+    return [array for k in sorted(chunks) for array in chunks[k]]
+
+
+def unflat(refs, shifts):
+    refs, chunks = list(refs), {}
+    for k, many in shifts:
+        chunks[k], refs = refs[:many], refs[many:]
+    return chunks
 
 
 def chunk_copies(chunks, places, parts, held, sems):
@@ -123,15 +125,14 @@
     found = []
     for s, sequence in enumerate(chunks):
         for i, m in enumerate(places):
-            slot = s * len(places) + i
-            options = []
-            if m == 0:
-                options.append((None, sequence.own))
-            else:
-                moves = {(at ^ m) - at for at in range(parts)}
-                for move in sorted(moves):
-                    source = sequence.above[move - 1] if move > 0 else sequence.below[-move - 1]
-                    options.append((lax.bitwise_xor(z, m) - z == move, source))
+            slot, options = s * len(places) + i, []
+            for k in sorted({(at - (at ^ m)) % parts for at in range(parts)}):
+                here = lax.rem(z - lax.bitwise_xor(z, m) + parts, parts) == k
+                if len(sequence[k]) == 1:
+                    options.append((None if k == 0 else here, sequence[k][0]))
+                else:
+                    options.append((here & (z >= parts // 2), sequence[k][0]))
+                    options.append((here & (z < parts // 2), sequence[k][1]))
             found.append(
                 [
                     (here, pltpu.make_async_copy(source, held.at[slot], sems.at[slot]))
@@ -155,9 +156,9 @@
 
 
 def project_kernel(setup, at_ref, bias_ref, gain_ref, shift_ref, cos_ref, left_ref, right_ref, *rest):
-    count, parts, places, width, hidden = setup
-    refs = 2 * parts - 1
-    chunks = [Chunks.of(rest[:refs]), Chunks.of(rest[refs : 2 * refs])]
+    count, parts, places, width, hidden, shifts = setup
+    refs = sum(many for _, many in shifts)
+    chunks = [unflat(rest[:refs], shifts), unflat(rest[refs : 2 * refs], shifts)]
     blocks, rest = rest[2 * refs : 2 * refs + count], rest[2 * refs + count :]
     qkv_ref, act_ref, slope_ref, normed_ref, tokens_ref, held, x_held, ready, sems, x_sems = rest
     step, steps = pl.program_id(0), 2 * len(places)
@@ -210,25 +211,25 @@
             slope_ref[:, columns] = slope.astype(BF16)
 
 
-def project(at_mp, chunks, blocks, bias, gain, shift, tables, width, deps):
-    parts, places = len(chunks[0].below) + 1, tuple(range(len(chunks[0].below) + 1))
-    rows, model = chunks[0].own.shape
+def project(at_mp, chunks, blocks, bias, gain, shift, tables, width, parts, deps):
+    places, shifts = tuple(range(parts)), [(k, len(chunks[0][k])) for k in sorted(chunks[0])]
+    rows, model = chunks[0][0][0].shape
     total, hidden = blocks[0].shape[1], blocks[0].shape[1] - 3 * width
     count, length = len(blocks), 2 * parts * rows
     table = pl.BlockSpec((rows, LANES), lambda i, at: (at[0] ^ (i % parts), 0))
     out = lambda w: pl.BlockSpec((rows, w), lambda i, at: (i - i % parts + (at[0] ^ (i % parts)), 0))
     line = lambda a: pl.BlockSpec(a.shape, lambda i, at: (0, 0))
     widths = (3 * width, hidden, hidden, model, model)
-    setup = (count, parts, places, width, hidden)
+    setup = (count, parts, places, width, hidden, shifts)
     return call(
         functools.partial(project_kernel, setup),
         "project",
-        [bias, gain, shift, *tables, *chunks[0].flat(), *chunks[1].flat(), *blocks],
+        [bias, gain, shift, *tables, *flat(chunks[0]), *flat(chunks[1]), *blocks],
         deps,
         (at_mp,),
         grid=(2 * parts,),
         in_specs=[line(bias), line(gain), line(shift), table, table, table]
-        + [ANY] * (2 * (2 * parts - 1) + count),
+        + [ANY] * (2 * len(flat(chunks[0])) + count),
         out_specs=[out(w) for w in widths],
         out_shape=[jax.ShapeDtypeStruct((length, w), BF16) for w in widths],
         scratch_shapes=[
@@ -457,9 +458,10 @@
 
 
 def grad_in_kernel(setup, at_ref, slope_ref, *rest):
-    count, parts, places, width, hidden, many = setup
-    refs = many // 2
-    chunks = [Chunks.of(rest[:refs]), Chunks.of(rest[refs:many])]
+    count, parts, places, width, hidden, shifts = setup
+    refs = sum(many for _, many in shifts)
+    many = 2 * refs
+    chunks = [unflat(rest[:refs], shifts), unflat(rest[refs:many], shifts)]
     blocks, rest = rest[many : many + count], rest[many + count :]
     gmixed_ref, gpre_ref, dy_ref, gsum_ref, dsum_ref, held, dy_held, sems, dy_sems = rest[-9:]
     step, steps = pl.program_id(0), 2 * len(places)
@@ -495,9 +497,10 @@
 
 
 def grad_in(at_mp, chunks, slope, blocks, width, parts, places, earlier, deps):
-    rows, model = chunks[0].own.shape
+    rows, model = chunks[0][0][0].shape
     hidden, length = slope.shape[1], slope.shape[0]
-    count, many = len(blocks), len(chunks[0].flat()) * 2
+    shifts = [(k, len(chunks[0][k])) for k in sorted(chunks[0])]
+    count, many = len(blocks), len(flat(chunks[0])) * 2
     turns = len(places)
 
     def where(i, at):
@@ -508,8 +511,8 @@
 
     out = lambda w: pl.BlockSpec((rows, w), lambda i, at: (where(i, at), 0))
     total = lambda w: pl.BlockSpec((8, w), lambda i, at: (0, 0))
-    setup = (count, parts, places, width, hidden, many)
-    operands = [slope, *chunks[0].flat(), *chunks[1].flat(), *blocks]
+    setup = (count, parts, places, width, hidden, shifts)
+    operands = [slope, *flat(chunks[0]), *flat(chunks[1]), *blocks]
     aliases = {1 + len(operands) + n: n for n in range(len(earlier))}
     return call(
         functools.partial(grad_in_kernel, setup),
@@ -632,10 +635,21 @@
     return lax.ppermute(value, "dp", [(i, i ^ bit) for i in range(count)])
 
 
-def line_step(below, above, k, parts):
-    up = lax.ppermute(below, "mp", [(i, i + 1) for i in range(k - 1, parts - 1)])
-    down = lax.ppermute(above, "mp", [(i + 1, i) for i in range(parts - k)])
-    return up, down
+def ring(value, k, parts):
+    return lax.ppermute(value, "mp", [(i, (i + k) % parts) for i in range(parts)])
+
+
+def gather_near(own, parts):
+    shifts = (1, 3) if parts == 4 else range(1, parts)
+    return {0: [own], **{k: [ring(own, k, parts)] for k in shifts}}
+
+
+def gather_far(chunks, parts):
+    if parts == 4:
+        up = lax.ppermute(chunks[1][0], "mp", [(1, 2), (2, 3)])
+        down = lax.ppermute(chunks[3][0], "mp", [(1, 0), (2, 1)])
+        chunks = {**chunks, 2: [up, down]}
+    return chunks
 
 
 class LineScatter:
@@ -647,15 +661,22 @@
             self.sums[k] = [sum(s.astype(F32) for s in self.sums[k]).astype(BF16)]
         return self.sums[k][0]
 
-    def ready(self, s):
-        return [self.total(k) for k in sorted({self.parts - s, s})]
-
-    def step(self, s):
-        parts = self.parts
-        up = lax.ppermute(self.total(parts - s), "mp", [(i, i + 1) for i in range(s)])
-        down = lax.ppermute(self.total(s), "mp", [(i, i - 1) for i in range(parts - s, parts)])
-        self.sums[(parts - s - 1) % parts].append(up)
-        self.sums[(s + 1) % parts].append(down)
+    def far_ready(self):
+        return [self.total(2)] if self.parts == 4 else []
+
+    def far(self):
+        if self.parts == 4:
+            self.sums[1].append(lax.ppermute(self.total(2), "mp", [(0, 1), (1, 2)]))
+            self.sums[3].append(lax.ppermute(self.total(2), "mp", [(3, 2), (2, 1)]))
+
+    def shifts(self):
+        return (1, 3) if self.parts == 4 else range(1, self.parts)
+
+    def near_ready(self):
+        return [self.total(k) for k in self.shifts()]
+
+    def near(self):
+        self.sums[0] += [ring(self.total(k), k, self.parts) for k in self.shifts()]
 
     def result(self):
         return sum(s.astype(F32) for s in self.sums[0])
@@ -669,17 +690,33 @@
     return bits
 
 
-def gather_blocks(own, sibling, count):
-    held = {0: own, 1: sibling}
-    orders = (chip_bits(count), chip_bits(count)[::-1])
-    for s in range(len(orders[0])):
-        moved = {}
-        for half in range(2):
-            bit = orders[half][s]
-            for j in [j for j in held if j % 2 == half]:
-                moved[j ^ bit] = across(held[j], bit, count)
-        held.update(moved)
-    return [held[j] for j in range(count)]
+class BlockGather:
+    def __init__(self, own, sibling, count):
+        self.held, self.count = {0: own, 1: sibling}, count
+        self.orders = (chip_bits(count), chip_bits(count)[::-1])
+
+    def first(self):
+        start, orders = dict(self.held), self.orders
+        for s in range(min(2, len(orders[0]))):
+            for half in range(2):
+                bit = orders[half][s]
+                self.held[half ^ bit] = across(start[half], bit, self.count)
+
+    def second(self):
+        for s in range(1, len(self.orders[0])):
+            for half in range(2):
+                order = self.orders[half]
+                bit, done = order[s], order[:s]
+                for j in [j for j in self.held if j % 2 == half and not j & bit]:
+                    if j ^ bit not in self.held and not any(j & b for b in order[s:]):
+                        self.held[j ^ bit] = across(self.held[j], bit, self.count)
+
+    def fenced(self, deps=()):
+        keys = sorted(self.held)
+        self.held = dict(zip(keys, fence([self.held[j] for j in keys], deps)))
+
+    def blocks(self):
+        return [self.held[j] for j in range(self.count)]
 
 
 def scatter_orders(count):
@@ -764,19 +801,26 @@
             [rank(dense_weight, 0, which, width), rank(down_weight, 0, which, hidden)], axis=0
         )
 
-    below, above = [], []
-    up, down = tokens, tokens
-    for k in range(1, nmp):
-        up, down = line_step(up, down, k, nmp)
-        below.append(up)
-        above.append(down)
-    own = Chunks(tokens, below, above)
-    other = Chunks.of([across(c, 1, ndp) for c in own.flat()])
-
-    row_blocks = gather_blocks(row_pack(core), across(row_pack(1 - core), 1, ndp), ndp)
-    late = tie(column_pack(core), row_blocks[2])
-    late_other = tie(across(column_pack(1 - core), 1, ndp), row_blocks[2])
-    column_blocks = gather_blocks(late, late_other, ndp)
+    rows = BlockGather(row_pack(core), across(row_pack(1 - core), 1, ndp), ndp)
+    columns = BlockGather(column_pack(core), across(column_pack(1 - core), 1, ndp), ndp)
+    own = gather_near(tokens, nmp)
+    rows.first()
+    keys, moved = sorted(rows.held), [k for k in own if k]
+    fenced = fence(
+        [rows.held[j] for j in keys] + [own[k][0] for k in moved] + [cotangent],
+        columns.held.values(),
+    )
+    rows.held = dict(zip(keys, fenced))
+    own.update({k: [array] for k, array in zip(moved, fenced[len(keys) :])})
+    cot = fenced[-1]
+    other = {k: [across(own[k][0], 1, ndp)] for k in own}
+    rows.second()
+    own = gather_far(own, nmp)
+    far = own.get(2, []) if nmp == 4 else []
+    cot, *held = fence([cot, columns.held[0], columns.held[1]], [*far, *rows.blocks()])
+    columns.held = dict(enumerate(held))
+    if far:
+        other[2] = [across(array, 1, ndp) for array in far]
 
     tables = rotary_tables(length)
     bias = jnp.concatenate(
@@ -787,38 +831,35 @@
         axis=1,
     )
     gain, shift = norm_gain.astype(F32)[None, :], norm_bias.astype(F32)[None, :]
-    cot = tie(cotangent, below[-1], above[-1])
-    dy_below, dy_above = [], []
-    up, down = line_step(cot, cot, 1, nmp)
+    dy_own = gather_near(cot, nmp)
+    columns.first()
     qkv, act, slope, normed, token_rows = project(
-        at_mp, (own, other), row_blocks, bias, gain, shift, tables, width, [cot]
-    )
-    up, down = tie(up, qkv), tie(down, qkv)
-    dy_below.append(up)
-    dy_above.append(down)
-    mixed, lse = attend(qkv, length, block, [up, down])
-    anchor = mixed
-    for k in range(2, nmp):
-        up, down = line_step(up, down, k, nmp)
-        if k < nmp - 1:
-            up, down = tie(up, anchor), tie(down, anchor)
-        dy_below.append(up)
-        dy_above.append(down)
+        at_mp, (own, other), rows.blocks(), bias, gain, shift, tables, width, nmp, [cot]
+    )
+    columns.fenced([qkv])
+    columns.second()
+    mixed, lse = attend(qkv, length, block, [columns.held[0]])
+    moved = [k for k in dy_own if k]
+    dy_own.update(
+        {k: [a] for k, a in zip(moved, fence([dy_own[k][0] for k in moved], [mixed]))}
+    )
+    dy_other = {k: [across(dy_own[k][0], 1, ndp)] for k in dy_own}
+    dy_far = gather_far(dy_own, nmp)
+    if nmp == 4:
+        dy_other[2] = [across(array, 1, ndp) for array in dy_far[2]]
     places = list(range(nmp))
     other_sums, own_sums = branch_sums(
-        at_mp, mixed, act, column_blocks, nmp, places, [dy_below[-2], dy_above[-2]]
+        at_mp, mixed, act, columns.blocks(), nmp, places, [dy_own[1][0]]
     )
     came = across(other_sums, 1, ndp)
     branches = LineScatter([[own_sums[k], came[k]] for k in range(nmp)])
 
-    dy_own = Chunks(cot, dy_below, dy_above)
-    dy_other = Chunks.of([across(c, 1, ndp) for c in dy_own.flat()])
-    near = lambda c: Chunks(c.own, c.below[:1], c.above[:1])
+    near = lambda chunks: {k: chunks[k] for k in (0, 1, nmp - 1)}
     first = grad_in(
         at_mp,
         (near(dy_own), near(dy_other)),
         slope,
-        column_blocks,
+        columns.blocks(),
         width,
         nmp,
         (0, 1),
@@ -827,62 +868,69 @@
     )
     second = grad_in(
         at_mp,
-        (dy_own, dy_other),
+        (dy_far, dy_other),
         slope,
-        column_blocks,
+        columns.blocks(),
         width,
         nmp,
         tuple(range(2, nmp)),
         first[:3],
-        branches.ready(1),
-    )
-    branches.step(1)
+        branches.far_ready(),
+    )
+    branches.far()
     gmixed, gpre, dy = second[:3]
     column_grads = BlockScatter(
         weight_grads(me, [mixed, act], [dy], ndp, [second[3]], left=False), ndp
     )
     column_grads.step(0)
     gq, gk, gv, qkv_sums = attend_back(
-        qkv, gmixed, mixed, lse, tables, length, block, [column_grads.held[0][0][0], *branches.ready(2)]
-    )
-    for s in range(2, nmp - 1):
-        branches.step(s)
+        qkv,
+        gmixed,
+        mixed,
+        lse,
+        tables,
+        length,
+        block,
+        [column_grads.held[0][0][0], *branches.near_ready()],
+    )
+    branches.near()
     for s in range(1, chip_steps - 1):
         column_grads.step(s)
-    early = [k for k in places if k % 2] if nmp > 2 else places
-    late_places = [k for k in places if k not in early]
+    early = [2] if nmp == 4 else places[: nmp // 2]
+    late = [k for k in places if k not in early]
     grads_a = grad_normed_sums(
         at_mp,
         (gq, gk, gv),
         gpre,
         token_rows,
-        row_blocks,
+        rows.blocks(),
         nmp,
         early,
-        [*branches.ready(nmp - 1), *column_grads.ready(chip_steps - 1)],
-    )
-    branches.step(nmp - 1)
+        column_grads.ready(chip_steps - 1),
+    )
     column_grads.step(chip_steps - 1)
     came_a = across(grads_a[0], 1, ndp)
     grads_b = grad_normed_sums(
-        at_mp, (gq, gk, gv), gpre, token_rows, row_blocks, nmp, late_places, [grads_a[2]]
+        at_mp, (gq, gk, gv), gpre, token_rows, rows.blocks(), nmp, late, [grads_a[2]]
     )
     came_b = across(grads_b[0], 1, ndp)
     shares = {}
-    for part, got, kept in ((early, came_a, grads_a[1]), (late_places, came_b, grads_b[1])):
+    for part, got, kept in ((early, came_a, grads_a[1]), (late, came_b, grads_b[1])):
         for n, k in enumerate(part):
             shares[k] = [kept[n], got[n]]
     grad_rows = LineScatter([shares[k] for k in places])
     up_grads = BlockScatter(
-        weight_grads(me, [normed], [gpre], ndp, [grads_b[2], *grad_rows.ready(1)], left=True), ndp
-    )
-    grad_rows.step(1)
+        weight_grads(
+            me, [normed], [gpre], ndp, [grads_b[2], *grad_rows.far_ready()], left=True
+        ),
+        ndp,
+    )
+    grad_rows.far()
     up_grads.step(0)
     qkv_grads = BlockScatter(
         weight_grads(me, [normed], [gq, gk, gv], ndp, [up_grads.held[0][0][0]], left=True), ndp
     )
-    for s in range(2, nmp):
-        grad_rows.step(s)
+    grad_rows.near()
     for s in range(1, chip_steps):
         up_grads.step(s)
     for s in range(chip_steps):

time: 586 us -> 570 us (0.973)
  waiting for transfers between devices: 210 us -> 241 us
  starting transfers between devices: 86.3 us -> 63.6 us
  other arithmetic: 52.6 us -> 37.3 us
  local copies, waits for them, and re-layouts: 24.3 us -> 12.9 us
    ppermute x24 -> x16, starting transfers between devices: 49 us -> 24.5 us  [the longest x8 11.9 us: ring(): lax.ppermute(value, 'mp', [(i, (i + k) % parts) for i in range(parts)])]
    ppermute x49 -> x45, waiting for transfers between devices: 106 us -> 123 us  [across(): return lax.ppermute(value, 'dp', [(i, i ^ bit) for i in range(count)])]
    ppermute x24 -> x16, waiting for transfers between devices: 104 us -> 118 us  [the longest x8 85.8 us: ring(): lax.ppermute(value, 'mp', [(i, (i + k) % parts) for i in range(parts)])]
    concatenate x3 -> x0, local copies, waits for them, and re-layouts: 10.4 us -> none  [rotary_tables(): return [jnp.concatenate([t, t], axis=1) for t in (straight, left, right)]]
    convert_element_type x8 -> x4, other arithmetic: 19.4 us -> 9.06 us  [total(): self.sums[k] = [sum((s.astype(F32) for s in self.sums[k])).astype(BF16)]]
    ppermute x49 -> x45, starting transfers between devices: 32.1 us -> 34.6 us  [across(): return lax.ppermute(value, 'dp', [(i, i ^ bit) for i in range(count)])]
    pallas_call x18 -> x15, Pallas kernels: 202 us -> 203 us  [call(): pl.pallas_call(body, out_shape=out_shape, input_output_aliases=aliases, c...]
  transfers between devices with their start and end apart: 76 -> 64, of which waited for: 31 -> 24; matrix products, arithmetic and copies ran while one was open for 11% -> 6% of each run, Pallas kernels for 32% -> 27%
where the time goes in v3:
time: 570 us; the launch traced here: 560 us
  waiting for transfers between devices  241 us (42%)
  Pallas kernels  203 us (36%)
  starting transfers between devices  63.6 us (11%)
  other arithmetic  37.3 us (7%)
  local copies, waits for them, and re-layouts  12.9 us (2%)
    pallas_call x15, Pallas kernels, call(): pl.pallas_call(body, out_shape=out_shape, input_output_aliases=aliases, c...  203 us
    ppermute x45, waiting for transfers between devices, across(): return lax.ppermute(value, 'dp', [(i, i ^ bit) for i in range(count)])  123 us
    ppermute x8, waiting for transfers between devices, ring(): lax.ppermute(value, 'mp', [(i, (i + k) % parts) for i in range(parts)])  85.8 us
    ppermute x45, starting transfers between devices, across(): return lax.ppermute(value, 'dp', [(i, i ^ bit) for i in range(count)])  34.6 us
    ppermute x2, waiting for transfers between devices, gather_far(): down = lax.ppermute(chunks[3][0], 'mp', [(1, 0), (2, 1)])  32.5 us
    ppermute x8, starting transfers between devices, ring(): lax.ppermute(value, 'mp', [(i, (i + k) % parts) for i in range(parts)])  11.9 us
  transfers between devices with their start and end apart: 64, of which 24 were waited for; matrix products, arithmetic and copies ran while one was open for 6% of the time, Pallas kernels for 27%

profile of v3, /device:TPU:0, one launch (start us, length us, event | category | flops | bytes accessed | tf_op | source)
XLA Modules:
  0.0 559.9 jit_solution(4175204290512439544)
XLA Ops:
  0.7 1.3 constant_dynamic-slice_fusion.4
  2.9 2.6 collective-permute-start.1
  5.9 1.6 collective-permute-start.5
  7.5 2.2 collective-permute-start.6
  9.7 1.5 collective-permute-start.3
  12.4 14.2 %collective-permute-done.1.refs_2_ = bf16[256,1792]{1,0:T(8,128)(2,1)S(1)} collective-permute-done((bf16[256,1792]{1,0:T(8,128)(2,1)S(1)}, bf16[256,1792]{1,0:T(8,128)(2,1)S(1)}, u32[]{:S(2)}, u32[]{:S(2)}) %collective-permute-start.1) | collective-permute-done | bytes 917536 | tf_op jit(solution)/shard_map/ppermute | solution.py:635
  26.7 2.0 collective-permute-start.4
  30.5 2.5 collective-permute-done.3.refs_4_
  33.7 21.3 %collective-permute-done.6.refs_7_ = bf16[256,2048]{1,0:T(8,128)(2,1)S(1)} collective-permute-done((bf16[256,2048]{1,0:T(8,128)(2,1)S(1)}, bf16[256,2048]{1,0:T(8,128)(2,1)S(1)}, u32[]{:S(2)}, u32[]{:S(2)}) %collective-permute-start.6) | collective-permute-done | bytes 1048608 | tf_op jit(solution)/shard_map/ppermute | solution.py:639
  57.9 1.5 collective-permute-start.15
  59.4 1.3 collective-permute-start.16
  61.5 1.3 collective-permute-start.9
  62.8 17.0 %collective-permute-done.15.refs_11_.refs_23_.refs_12_ = bf16[256,1792]{1,0:T(8,128)(2,1)S(1)} collective-permute-done((bf16[256,1792]{1,0:T(8,128)(2,1)}, bf16[256,1792]{1,0:T(8,128)(2,1)S(1)}, u32[]{:S(2)}, u32[]{:S(2)}) %collective-permute-start.15) | collective-permute-done | bytes 917536 | tf_op jit(solution)/shard_map/ppermute | solution.py:635
  81.6 7.1 %collective-permute-done.9.refs_4_.refs_10_ = bf16[256,2048]{1,0:T(8,128)(2,1)S(1)} collective-permute-done((bf16[256,2048]{1,0:T(8,128)(2,1)}, bf16[256,2048]{1,0:T(8,128)(2,1)S(1)}, u32[]{:S(2)}, u32[]{:S(2)}) %collective-permute-start.9) | collective-permute-done | bytes 1048608 | tf_op jit(solution)/shard_map/ppermute | solution.py:650
  92.8 14.9 %collective-permute-done.17.refs_2_ = bf16[1280,256]{1,0:T(8,128)(2,1)S(1)} collective-permute-done((bf16[1280,256]{1,0:T(8,128)(2,1)}, bf16[1280,256]{1,0:T(8,128)(2,1)S(1)}, u32[]{:S(2)}, u32[]{:S(2)}) %collective-permute-start.17) | collective-permute-done | bytes 655392 | tf_op jit(solution)/shard_map/ppermute | solution.py:635
  108.1 1.7 collective-permute-start.23
  109.9 2.1 collective-permute-start.24
  113.8 34.2 %project.1 = (bf16[2048,768]{1,0:T(8,128)(2,1)}, bf16[2048,1024]{1,0:T(8,128)(2,1)}, bf16[2048,1024]{1,0:T(8,128)(2,1)}, bf16[2048,2048]{1,0:T(8,128)(2,1)}, bf16[2048,2048]{1,0:T(8,128)(2,1)}) custom-call(s32[1]{0:T(128)} %bitcast.refs_0_, f32[1,1792]{1,0:T(1,128)} %maximum_convert_fusion.refs_1_, f32[1,2048]{1,0:T(1,128)} %bitcast.92, f32[1,2048]{1,0:T(1,128)} %bitcast.95, ...), custom_call_target="tpu_custom_call" | custom-call | tf_op jit(solution)/shard_map/project/pallas_call | solution.py:42
  149.1 1.5 collective-permute-start.21
  151.2 14.9 %attend.1 = (bf16[2048,256]{1,0:T(8,128)(2,1)}, f32[4,8,1024]{2,1,0:T(8,128)}) custom-call(bf16[2048,768]{1,0:T(8,128)(2,1)} %get-tuple-element.89.refs_6_.refs_0_.refs_1_.refs_2_, bf16[2048,768]{1,0:T(8,128)(2,1)} %get-tuple-element.89.refs_6_.refs_0_.refs_1_.refs_2_, bf16[2048,768]{1,0:T(8,128)(2,1)} %get-tuple-element.89.refs_6_.refs_0_.refs_1_.refs_2_, ...), custom_call_target="tpu_custom_call" | custom-call | tf_op jit(solution)/shard_map/attend/pallas_call | solution.py:42
  168.2 18.9 %branch_sums.1 = (bf16[4,256,2048]{2,1,0:T(8,128)(2,1)}, bf16[4,256,2048]{2,1,0:T(8,128)(2,1)}) custom-call(s32[1]{0:T(128)} %bitcast.refs_0_, bf16[2048,256]{1,0:T(8,128)(2,1)} %get-tuple-element.93.refs_2_.refs_1_.refs_4_, bf16[2048,1024]{1,0:T(8,128)(2,1)} %get-tuple-element.94.refs_2_, bf16[1280,256]{1,0:T(8,128)(2,1)} %get-tuple-element.92.refs_3_.refs_8_.refs_12_, ...), custom_call_target="tpu_custom_call" | custom-call | tf_op jit(solution)/shard_map/branch_sums/pallas_call | solution.py:42
  187.3 1.8 collective-permute-start.30
  189.1 1.3 collective-permute-start.31
  191.3 25.4 %collective-permute-done.31.refs_5_ = bf16[256,2048]{1,0:T(8,128)(2,1)} collective-permute-done((bf16[256,2048]{1,0:T(8,128)(2,1)}, bf16[256,2048]{1,0:T(8,128)(2,1)}, u32[]{:S(2)}, u32[]{:S(2)}) %collective-permute-start.31) | collective-permute-done | bytes 1048608 | tf_op jit(solution)/shard_map/ppermute | solution.py:650
  218.2 1.5 fusion.19.refs_23_
  219.7 3.8 collective-permute-start.26
  223.6 1.6 collective-permute-start.28
  226.5 13.3 %grad_in.2 = (bf16[2048,256]{1,0:T(8,128)(2,1)}, bf16[2048,1024]{1,0:T(8,128)(2,1)}, bf16[2048,2048]{1,0:T(8,128)(2,1)}, f32[8,1024]{1,0:T(8,128)}, f32[8,2048]{1,0:T(8,128)}) custom-call(s32[1]{0:T(128)} %bitcast.refs_0_, bf16[2048,1024]{1,0:T(8,128)(2,1)} %get-tuple-element.103.refs_1_, bf16[256,2048]{1,0:T(8,128)(2,1)} %get-tuple-element.88.refs_25_.refs_2_, ...), custom_call_target="tpu_custom_call" | custom-call | tf_op jit(solution)/shard_map/grad_in/pallas_call | solution.py:42
  239.8 13.2 %grad_in.3 = (bf16[2048,256]{1,0:T(8,128)(2,1)}, bf16[2048,1024]{1,0:T(8,128)(2,1)}, bf16[2048,2048]{1,0:T(8,128)(2,1)}, f32[8,1024]{1,0:T(8,128)}, f32[8,2048]{1,0:T(8,128)}) custom-call(s32[1]{0:T(128)} %bitcast.refs_0_, bf16[2048,1024]{1,0:T(8,128)(2,1)} %get-tuple-element.103.refs_1_, ...), custom_call_target="tpu_custom_call", output_to_operand_aliasing={{0}: (20, {}), {1}: (21, {}), {2}: (22, {})} | custom-call | tf_op jit(solution)/shard_map/grad_in/pallas_call | solution.py:42
  253.0 19.8 %weight_grads.3 = (bf16[2,1280,256]{2,1,0:T(8,128)(2,1)}, bf16[2,1280,256]{2,1,0:T(8,128)(2,1)}, bf16[1,1280,256]{2,1,0:T(8,128)(2,1)}, bf16[1,1280,256]{2,1,0:T...) custom-call(s32[8]{0:T(128)} %broadcast_xor_fusion.refs_0_, ...), custom_call_target="tpu_custom_call" | custom-call | tf_op jit(solution)/shard_map/weight_grads/pallas_call | solution.py:42
  273.3 1.4 collective-permute-start.38
  276.5 4.9 fusion.17
  281.4 25.3 %attend_back.1 = (bf16[2048,256]{1,0:T(8,128)(2,1)}, bf16[2048,256]{1,0:T(8,128)(2,1)}, bf16[2048,256]{1,0:T(8,128)(2,1)}, f32[4,8,128]{2,1,0:T(8,128)}) custom-call(bf16[2048,768]{1,0:T(8,128)(2,1)} %get-tuple-element.89.refs_6_.refs_0_.refs_1_.refs_2_, bf16[2048,768]{1,0:T(8,128)(2,1)} %get-tuple-element.89.refs_6_.refs_0_.refs_1_.refs_2_, ...), custom_call_target="tpu_custom_call" | custom-call | tf_op jit(solution)/shard_map/attend_back/pallas_call | solution.py:42
  307.5 2.3 add_convert_fusion.4.refs_14_
  310.9 11.4 %grad_normed_sums.2 = (bf16[1,256,2048]{2,1,0:T(8,128)(2,1)}, bf16[1,256,2048]{2,1,0:T(8,128)(2,1)}, f32[8,2048]{1,0:T(8,128)}) custom-call(s32[1]{0:T(128)} %bitcast.refs_0_, bf16[2048,256]{1,0:T(8,128)(2,1)} %get-tuple-element.113.refs_1_.refs_2_, bf16[2048,256]{1,0:T(8,128)(2,1)} %get-tuple-element.114.refs_2_.refs_3_, ...), custom_call_target="tpu_custom_call" | custom-call | tf_op jit(solution)/shard_map/grad_normed_sums/pallas_call | solution.py:42
  322.3 21.8 %grad_normed_sums.3 = (bf16[3,256,2048]{2,1,0:T(8,128)(2,1)}, bf16[3,256,2048]{2,1,0:T(8,128)(2,1)}, f32[8,2048]{1,0:T(8,128)}) custom-call(s32[1]{0:T(128)} %bitcast.refs_0_, bf16[2048,256]{1,0:T(8,128)(2,1)} %get-tuple-element.113.refs_1_.refs_2_, bf16[2048,256]{1,0:T(8,128)(2,1)} %get-tuple-element.114.refs_2_.refs_3_, ...), custom_call_target="tpu_custom_call" | custom-call | tf_op jit(solution)/shard_map/grad_normed_sums/pallas_call | solution.py:42
  345.8 3.3 collective-permute-done.45
  349.1 1.6 collective-permute-start.46
  351.1 2.0 collective-permute-done.46
  353.9 1.5 collective-permute-start.57
  356.4 3.5 collective-permute-start.50
  362.6 8.2 %collective-permute-done.57 = bf16[1,1280,256]{2,1,0:T(8,128)(2,1)} collective-permute-done((bf16[1,1280,256]{2,1,0:T(8,128)(2,1)S(1)}, bf16[1,1280,256]{2,1,0:T(8,128)(2,1)}, u32[]{:S(2)}, u32[]{:S(2)}) %collective-permute-start.57) | collective-permute-done | bytes 655392 | tf_op jit(solution)/shard_map/ppermute | solution.py:635
  370.7 1.5 fusion.21
  372.4 1.6 convert_add_fusion.1
  374.0 1.4 fusion.20.refs_4_
  375.3 16.1 %weight_grads.4 = (bf16[2,256,1024]{2,1,0:T(8,128)(2,1)}, bf16[2,256,1024]{2,1,0:T(8,128)(2,1)}, bf16[1,256,1024]{2,1,0:T(8,128)(2,1)}, bf16[1,256,1024]{2,1,0:T...) custom-call(s32[8]{0:T(128)} %broadcast_xor_fusion.refs_0_, ...), custom_call_target="tpu_custom_call" | custom-call | tf_op jit(solution)/shard_map/weight_grads/pallas_call | solution.py:42
  391.5 13.8 %weight_grads.5 = (bf16[2,256,768]{2,1,0:T(8,128)(2,1)}, bf16[2,256,768]{2,1,0:T(8,128)(2,1)}, bf16[1,256,768]{2,1,0:T(8,128)(2,1)}, bf16[1,256,768]{2,1,0:T(8,1...) custom-call(s32[8]{0:T(128)} %broadcast_xor_fusion.refs_0_, ...), custom_call_target="tpu_custom_call" | custom-call | tf_op jit(solution)/shard_map/weight_grads/pallas_call | solution.py:42
  405.3 1.6 collective-permute-start.51
  408.1 1.4 collective-permute-start.53
  411.1 1.6 maximum_select_fusion.1
  412.7 13.2 %collective-permute-done.51 = bf16[2,256,768]{2,1,0:T(8,128)(2,1)S(1)} collective-permute-done((bf16[2,256,768]{2,1,0:T(8,128)(2,1)}, bf16[2,256,768]{2,1,0:T(8,128)(2,1)S(1)}, u32[]{:S(2)}, u32[]{:S(2)}) %collective-permute-start.51) | collective-permute-done | bytes 786464 | tf_op jit(solution)/shard_map/ppermute | solution.py:635
  426.0 1.3 collective-permute-start.41
  429.5 18.4 %collective-permute-done.59 = bf16[2,256,1024]{2,1,0:T(8,128)(2,1)S(1)} collective-permute-done((bf16[2,256,1024]{2,1,0:T(8,128)(2,1)S(1)}, bf16[2,256,1024]{2,1,0:T(8,128)(2,1)S(1)}, u32[]{:S(2)}, u32[]{:S(2)}) %collective-permute-start.59) | collective-permute-done | bytes 1048608 | tf_op jit(solution)/shard_map/ppermute | solution.py:635
  448.0 1.4 collective-permute-start.52
  451.4 7.4 %collective-permute-done.52 = bf16[1,256,768]{2,1,0:T(8,128)(2,1)S(1)} collective-permute-done((bf16[1,256,768]{2,1,0:T(8,128)(2,1)S(1)}, bf16[1,256,768]{2,1,0:T(8,128)(2,1)S(1)}, u32[]{:S(2)}, u32[]{:S(2)}) %collective-permute-start.52) | collective-permute-done | bytes 393248 | tf_op jit(solution)/shard_map/ppermute | solution.py:635
  458.8 1.4 collective-permute-start.60
  460.9 10.6 %collective-permute-done.60 = bf16[1,256,1024]{2,1,0:T(8,128)(2,1)S(1)} collective-permute-done((bf16[1,256,1024]{2,1,0:T(8,128)(2,1)S(1)}, bf16[1,256,1024]{2,1,0:T(8,128)(2,1)S(1)}, u32[]{:S(2)}, u32[]{:S(2)}) %collective-permute-start.60) | collective-permute-done | bytes 524320 | tf_op jit(solution)/shard_map/ppermute | solution.py:635
  474.8 1.9 collective-permute-start.42
  476.6 7.2 %collective-permute-done.62 = bf16[1,256,1024]{2,1,0:T(8,128)(2,1)S(1)} collective-permute-done((bf16[1,256,1024]{2,1,0:T(8,128)(2,1)S(1)}, bf16[1,256,1024]{2,1,0:T(8,128)(2,1)S(1)}, u32[]{:S(2)}, u32[]{:S(2)}) %collective-permute-start.62) | collective-permute-done | bytes 524320 | tf_op jit(solution)/shard_map/ppermute | solution.py:635
  483.8 2.0 collective-permute-start.44
  488.2 1.6 maximum_select_fusion
  489.8 43.9 %collective-permute-done.42 = bf16[256,2048]{1,0:T(8,128)(2,1)S(1)} collective-permute-done((bf16[256,2048]{1,0:T(8,128)(2,1)S(1)}, bf16[256,2048]{1,0:T(8,128)(2,1)S(1)}, u32[]{:S(2)}, u32[]{:S(2)}) %collective-permute-start.42) | collective-permute-done | bytes 1048608 | tf_op jit(solution)/shard_map/ppermute | solution.py:639
  533.6 19.8 %collective-permute-done.44 = bf16[256,2048]{1,0:T(8,128)(2,1)S(1)} collective-permute-done((bf16[256,2048]{1,0:T(8,128)(2,1)S(1)}, bf16[256,2048]{1,0:T(8,128)(2,1)S(1)}, u32[]{:S(2)}, u32[]{:S(2)}) %collective-permute-start.44) | collective-permute-done | bytes 1048608 | tf_op jit(solution)/shard_map/ppermute | solution.py:639
  554.6 4.5 fusion.8
  (293 shorter events, 49.6 us)
Async XLA Ops:
  2.3 9.0 %collective-permute-start = (bf16[256,1792]{1,0:T(8,128)(2,1)S(1)}, bf16[256,1792]{1,0:T(8,128)(2,1)S(1)}, u32[]{:S(2)}, u32[]{:S(2)}) collective-permute-start(bf16[256,1792]{1,0:T(8,128)(2,1)S(1)} %pad_maximum_fusion.2), channel_id=1, source_target_pairs={{0,4},{4,0},{8,12},{12,8},{16,20},{20,16},{24,28},{28,24},{1,5},{5... | collective-permute-start | bytes 2752520 | tf_op jit(solution)/shard_map/ppermute | solution.py:635
  2.9 23.8 %collective-permute-start.1 = (bf16[256,1792]{1,0:T(8,128)(2,1)S(1)}, bf16[256,1792]{1,0:T(8,128)(2,1)S(1)}, u32[]{:S(2)}, u32[]{:S(2)}) collective-permute-start(bf16[256,1792]{1,0:T(8,128)(2,1)S(1)} %pad_maximum_fusion.1.refs_0_), channel_id=1, source_target_pairs={{0,8},{4,12},{8,0},{12,4},{16,24},{20,28},{24,16},{28,20},{1,9},{5... | collective-permute-start | bytes 2752520 | tf_op jit(solution)/shard_map/ppermute | solution.py:635
  5.6 4.1 collective-permute-start.7
  5.9 27.8 %collective-permute-start.5 = (bf16[256,2048]{1,0:T(8,128)(2,1)S(1)}, bf16[256,2048]{1,0:T(8,128)(2,1)S(1)}, u32[]{:S(2)}, u32[]{:S(2)}) collective-permute-start(bf16[256,2048]{1,0:T(8,128)(2,1)S(1)} %copy-done.4), channel_id=1, source_target_pairs={{0,1},{1,2},{2,3},{3,0},{4,5},{5,6},{6,7},{7,4},{8,9},{9,10},{10,1... | collective-permute-start | bytes 3145736 | tf_op jit(solution)/shard_map/ppermute | solution.py:639
  7.5 47.6 %collective-permute-start.6 = (bf16[256,2048]{1,0:T(8,128)(2,1)S(1)}, bf16[256,2048]{1,0:T(8,128)(2,1)S(1)}, u32[]{:S(2)}, u32[]{:S(2)}) collective-permute-start(bf16[256,2048]{1,0:T(8,128)(2,1)S(1)} %copy-done.4), channel_id=1, source_target_pairs={{0,3},{1,0},{2,1},{3,2},{4,7},{5,4},{6,5},{7,6},{8,11},{9,8},{10,9... | collective-permute-start | bytes 3145736 | tf_op jit(solution)/shard_map/ppermute | solution.py:639
  9.7 23.2 %collective-permute-start.3 = (bf16[256,1792]{1,0:T(8,128)(2,1)S(1)}, bf16[256,1792]{1,0:T(8,128)(2,1)S(1)}, u32[]{:S(2)}, u32[]{:S(2)}) collective-permute-start(bf16[256,1792]{1,0:T(8,128)(2,1)S(1)} %pad_maximum_fusion.1.refs_0_), channel_id=1, source_target_pairs={{0,16},{4,20},{8,24},{12,28},{16,0},{20,4},{24,8},{28,12},{1,17},{... | collective-permute-start | bytes 2752520 | tf_op jit(solution)/shard_map/ppermute | solution.py:635
  11.3 43.8 %collective-permute-start.2 = (bf16[256,1792]{1,0:T(8,128)(2,1)S(1)}, bf16[256,1792]{1,0:T(8,128)(2,1)S(1)}, u32[]{:S(2)}, u32[]{:S(2)}) collective-permute-start(bf16[256,1792]{1,0:T(8,128)(2,1)S(1)} %collective-permute-done.refs_1_), channel_id=1, source_target_pairs={{0,8},{4,12},{8,0},{12,4},{16,24},{20,28},{24,16},{28,20},{1,9},{5... | collective-permute-start | bytes 2752520 | tf_op jit(solution)/shard_map/ppermute | solution.py:635
  26.7 29.4 %collective-permute-start.4 = (bf16[256,1792]{1,0:T(8,128)(2,1)S(1)}, bf16[256,1792]{1,0:T(8,128)(2,1)S(1)}, u32[]{:S(2)}, u32[]{:S(2)}) collective-permute-start(bf16[256,1792]{1,0:T(8,128)(2,1)S(1)} %collective-permute-done.refs_1_), channel_id=1, source_target_pairs={{0,16},{4,20},{8,24},{12,28},{16,0},{20,4},{24,8},{28,12},{1,17},{... | collective-permute-start | bytes 2752520 | tf_op jit(solution)/shard_map/ppermute | solution.py:635
  57.9 21.9 %collective-permute-start.15 = (bf16[256,1792]{1,0:T(8,128)(2,1)}, bf16[256,1792]{1,0:T(8,128)(2,1)S(1)}, u32[]{:S(2)}, u32[]{:S(2)}) collective-permute-start(bf16[256,1792]{1,0:T(8,128)(2,1)} %get-tuple-element.83.refs_7_.refs_19_.refs_8_), channel_id=1, source_target_pairs={{0,16},{4,20},{8,24},{12,28},{16,0},{20,4},{24,8},{28,12},{1,17},{... | collective-permute-start | bytes 2752520 | tf_op jit(solution)/shard_map/ppermute | solution.py:635
  59.4 21.6 %collective-permute-start.16 = (bf16[256,1792]{1,0:T(8,128)(2,1)}, bf16[256,1792]{1,0:T(8,128)(2,1)S(1)}, u32[]{:S(2)}, u32[]{:S(2)}) collective-permute-start(bf16[256,1792]{1,0:T(8,128)(2,1)} %get-tuple-element.86.refs_10_.refs_22_.refs_11_), channel_id=1, source_target_pairs={{0,8},{4,12},{8,0},{12,4},{16,24},{20,28},{24,16},{28,20},{1,9},{5... | collective-permute-start | bytes 2752520 | tf_op jit(solution)/shard_map/ppermute | solution.py:635
  60.7 20.3 %collective-permute-start.8 = (bf16[256,2048]{1,0:T(8,128)(2,1)}, bf16[256,2048]{1,0:T(8,128)(2,1)S(1)}, u32[]{:S(2)}, u32[]{:S(2)}) collective-permute-start(bf16[256,2048]{1,0:T(8,128)(2,1)} %get-tuple-element.79.refs_8_), channel_id=1, source_target_pairs={{1,2},{2,3},{5,6},{6,7},{9,10},{10,11},{13,14},{14,15},{17,18},{18... | collective-permute-start | bytes 3145736 | tf_op jit(solution)/shard_map/ppermute | solution.py:649
  61.5 27.2 %collective-permute-start.9 = (bf16[256,2048]{1,0:T(8,128)(2,1)}, bf16[256,2048]{1,0:T(8,128)(2,1)S(1)}, u32[]{:S(2)}, u32[]{:S(2)}) collective-permute-start(bf16[256,2048]{1,0:T(8,128)(2,1)} %get-tuple-element.80.refs_11_), channel_id=1, source_target_pairs={{1,0},{2,1},{5,4},{6,5},{9,8},{10,9},{13,12},{14,13},{17,16},{18,1... | collective-permute-start | bytes 3145736 | tf_op jit(solution)/shard_map/ppermute | solution.py:650
  62.8 26.9 %collective-permute-start.10 = (bf16[256,2048]{1,0:T(8,128)(2,1)S(1)}, bf16[256,2048]{1,0:T(8,128)(2,1)S(1)}, u32[]{:S(2)}, u32[]{:S(2)}) collective-permute-start(bf16[256,2048]{1,0:T(8,128)(2,1)S(1)} %copy-done.4), channel_id=1, source_target_pairs={{0,4},{4,0},{8,12},{12,8},{16,20},{20,16},{24,28},{28,24},{1,5},{5... | collective-permute-start | bytes 3145736 | tf_op jit(solution)/shard_map/ppermute | solution.py:635
  79.8 10.9 %collective-permute-start.11 = (bf16[256,2048]{1,0:T(8,128)(2,1)}, bf16[256,2048]{1,0:T(8,128)(2,1)S(1)}, u32[]{:S(2)}, u32[]{:S(2)}) collective-permute-start(bf16[256,2048]{1,0:T(8,128)(2,1)} %get-tuple-element.79.refs_8_), channel_id=1, source_target_pairs={{0,4},{4,0},{8,12},{12,8},{16,20},{20,16},{24,28},{28,24},{1,5},{5... | collective-permute-start | bytes 3145736 | tf_op jit(solution)/shard_map/ppermute | solution.py:635
  81.1 10.1 %collective-permute-start.14 = (bf16[256,2048]{1,0:T(8,128)(2,1)}, bf16[256,2048]{1,0:T(8,128)(2,1)}, u32[]{:S(2)}, u32[]{:S(2)}) collective-permute-start(bf16[256,2048]{1,0:T(8,128)(2,1)} %get-tuple-element.80.refs_11_), channel_id=1, source_target_pairs={{0,4},{4,0},{8,12},{12,8},{16,20},{20,16},{24,28},{28,24},{1,5},{5... | collective-permute-start | bytes 3145736 | tf_op jit(solution)/shard_map/ppermute | solution.py:635
  81.1 27.1 %collective-permute-start.12 = (bf16[256,2048]{1,0:T(8,128)(2,1)S(1)}, bf16[256,2048]{1,0:T(8,128)(2,1)}, u32[]{:S(2)}, u32[]{:S(2)}) collective-permute-start(bf16[256,2048]{1,0:T(8,128)(2,1)S(1)} %collective-permute-done.8.refs_3_.refs_9_), channel_id=1, source_target_pairs={{0,4},{4,0},{8,12},{12,8},{16,20},{20,16},{24,28},{28,24},{1,5},{5... | collective-permute-start | bytes 3145736 | tf_op jit(solution)/shard_map/ppermute | solution.py:635
  88.7 21.2 %collective-permute-start.13 = (bf16[256,2048]{1,0:T(8,128)(2,1)S(1)}, bf16[256,2048]{1,0:T(8,128)(2,1)}, u32[]{:S(2)}, u32[]{:S(2)}) collective-permute-start(bf16[256,2048]{1,0:T(8,128)(2,1)S(1)} %collective-permute-done.9.refs_4_.refs_10_), channel_id=1, source_target_pairs={{0,4},{4,0},{8,12},{12,8},{16,20},{20,16},{24,28},{28,24},{1,5},{5... | collective-permute-start | bytes 3145736 | tf_op jit(solution)/shard_map/ppermute | solution.py:635
  89.7 17.9 %collective-permute-start.17 = (bf16[1280,256]{1,0:T(8,128)(2,1)}, bf16[1280,256]{1,0:T(8,128)(2,1)S(1)}, u32[]{:S(2)}, u32[]{:S(2)}) collective-permute-start(bf16[1280,256]{1,0:T(8,128)(2,1)} %get-tuple-element.90.refs_0_), channel_id=1, source_target_pairs={{0,8},{4,12},{8,0},{12,4},{16,24},{20,28},{24,16},{28,20},{1,9},{5... | collective-permute-start | bytes 1966088 | tf_op jit(solution)/shard_map/ppermute | solution.py:635
  90.7 57.4 %collective-permute-start.19 = (bf16[1280,256]{1,0:T(8,128)(2,1)}, bf16[1280,256]{1,0:T(8,128)(2,1)S(1)}, u32[]{:S(2)}, u32[]{:S(2)}) collective-permute-start(bf16[1280,256]{1,0:T(8,128)(2,1)} %get-tuple-element.90.refs_0_), channel_id=1, source_target_pairs={{0,16},{4,20},{8,24},{12,28},{16,0},{20,4},{24,8},{28,12},{1,17},{... | collective-permute-start | bytes 1966088 | tf_op jit(solution)/shard_map/ppermute | solution.py:635
  91.7 56.4 %collective-permute-start.18 = (bf16[1280,256]{1,0:T(8,128)(2,1)}, bf16[1280,256]{1,0:T(8,128)(2,1)S(1)}, u32[]{:S(2)}, u32[]{:S(2)}) collective-permute-start(bf16[1280,256]{1,0:T(8,128)(2,1)} %get-tuple-element.91.refs_1_), channel_id=1, source_target_pairs={{0,8},{4,12},{8,0},{12,4},{16,24},{20,28},{24,16},{28,20},{1,9},{5... | collective-permute-start | bytes 1966088 | tf_op jit(solution)/shard_map/ppermute | solution.py:635
  107.6 40.4 %collective-permute-start.20 = (bf16[1280,256]{1,0:T(8,128)(2,1)}, bf16[1280,256]{1,0:T(8,128)(2,1)}, u32[]{:S(2)}, u32[]{:S(2)}) collective-permute-start(bf16[1280,256]{1,0:T(8,128)(2,1)} %get-tuple-element.91.refs_1_), channel_id=1, source_target_pairs={{0,16},{4,20},{8,24},{12,28},{16,0},{20,4},{24,8},{28,12},{1,17},{... | collective-permute-start | bytes 1966088 | tf_op jit(solution)/shard_map/ppermute | solution.py:635
  108.1 58.0 %collective-permute-start.23 = (bf16[256,2048]{1,0:T(8,128)(2,1)}, bf16[256,2048]{1,0:T(8,128)(2,1)S(1)}, u32[]{:S(2)}, u32[]{:S(2)}) collective-permute-start(bf16[256,2048]{1,0:T(8,128)(2,1)} %get-tuple-element.88.refs_25_.refs_2_), channel_id=1, source_target_pairs={{0,1},{1,2},{2,3},{3,0},{4,5},{5,6},{6,7},{7,4},{8,9},{9,10},{10,1... | collective-permute-start | bytes 3145736 | tf_op jit(solution)/shard_map/ppermute | solution.py:639
  109.9 56.3 %collective-permute-start.24 = (bf16[256,2048]{1,0:T(8,128)(2,1)}, bf16[256,2048]{1,0:T(8,128)(2,1)}, u32[]{:S(2)}, u32[]{:S(2)}) collective-permute-start(bf16[256,2048]{1,0:T(8,128)(2,1)} %get-tuple-element.88.refs_25_.refs_2_), channel_id=1, source_target_pairs={{0,3},{1,0},{2,1},{3,2},{4,7},{5,4},{6,5},{7,6},{8,11},{9,8},{10,9... | collective-permute-start | bytes 3145736 | tf_op jit(solution)/shard_map/ppermute | solution.py:639
  149.1 18.0 %collective-permute-start.21 = (bf16[1280,256]{1,0:T(8,128)(2,1)}, bf16[1280,256]{1,0:T(8,128)(2,1)S(1)}, u32[]{:S(2)}, u32[]{:S(2)}) collective-permute-start(bf16[1280,256]{1,0:T(8,128)(2,1)} %get-tuple-element.96.refs_5_.refs_10_.refs_14_), channel_id=1, source_target_pairs={{0,16},{4,20},{8,24},{12,28},{16,0},{20,4},{24,8},{28,12},{1,17},{... | collective-permute-start | bytes 1966088 | tf_op jit(solution)/shard_map/ppermute | solution.py:635
  150.6 16.5 %collective-permute-start.22 = (bf16[1280,256]{1,0:T(8,128)(2,1)}, bf16[1280,256]{1,0:T(8,128)(2,1)S(1)}, u32[]{:S(2)}, u32[]{:S(2)}) collective-permute-start(bf16[1280,256]{1,0:T(8,128)(2,1)} %get-tuple-element.99.refs_8_.refs_13_.refs_17_), channel_id=1, source_target_pairs={{0,8},{4,12},{8,0},{12,4},{16,24},{20,28},{24,16},{28,20},{1,9},{5... | collective-permute-start | bytes 1966088 | tf_op jit(solution)/shard_map/ppermute | solution.py:635
  187.2 29.5 %collective-permute-start.25 = (bf16[4,256,2048]{2,1,0:T(8,128)(2,1)}, bf16[4,256,2048]{2,1,0:T(8,128)(2,1)S(1)}, u32[]{:S(2)}, u32[]{:S(2)}) collective-permute-start(bf16[4,256,2048]{2,1,0:T(8,128)(2,1)} %get-tuple-element.102.refs_16_), channel_id=1, source_target_pairs={{0,4},{4,0},{8,12},{12,8},{16,20},{20,16},{24,28},{28,24},{1,5},{5... | collective-permute-start | bytes 12582920 | tf_op jit(solution)/shard_map/ppermute | solution.py:635
  187.3 3.7 collective-permute-start.30
  189.1 27.6 %collective-permute-start.31 = (bf16[256,2048]{1,0:T(8,128)(2,1)}, bf16[256,2048]{1,0:T(8,128)(2,1)}, u32[]{:S(2)}, u32[]{:S(2)}) collective-permute-start(bf16[256,2048]{1,0:T(8,128)(2,1)} %get-tuple-element.104.refs_4_.refs_6_), channel_id=1, source_target_pairs={{1,0},{2,1},{5,4},{6,5},{9,8},{10,9},{13,12},{14,13},{17,16},{18,1... | collective-permute-start | bytes 3145736 | tf_op jit(solution)/shard_map/ppermute | solution.py:650
  190.4 29.3 %collective-permute-start.32 = (bf16[256,2048]{1,0:T(8,128)(2,1)S(1)}, bf16[256,2048]{1,0:T(8,128)(2,1)S(1)}, u32[]{:S(2)}, u32[]{:S(2)}) collective-permute-start(bf16[256,2048]{1,0:T(8,128)(2,1)S(1)} %copy-done.2), channel_id=1, source_target_pairs={{0,4},{4,0},{8,12},{12,8},{16,20},{20,16},{24,28},{28,24},{1,5},{5... | collective-permute-start | bytes 3145736 | tf_op jit(solution)/shard_map/ppermute | solution.py:635
  190.8 32.7 %collective-permute-start.33 = (bf16[256,2048]{1,0:T(8,128)(2,1)S(1)}, bf16[256,2048]{1,0:T(8,128)(2,1)S(1)}, u32[]{:S(2)}, u32[]{:S(2)}) collective-permute-start(bf16[256,2048]{1,0:T(8,128)(2,1)S(1)} %copy-done.13), channel_id=1, source_target_pairs={{0,4},{4,0},{8,12},{12,8},{16,20},{20,16},{24,28},{28,24},{1,5},{5... | collective-permute-start | bytes 3145736 | tf_op jit(solution)/shard_map/ppermute | solution.py:635
  191.0 34.5 %collective-permute-start.36 = (bf16[256,2048]{1,0:T(8,128)(2,1)}, bf16[256,2048]{1,0:T(8,128)(2,1)S(1)}, u32[]{:S(2)}, u32[]{:S(2)}) collective-permute-start(bf16[256,2048]{1,0:T(8,128)(2,1)} %get-tuple-element.104.refs_4_.refs_6_), channel_id=1, source_target_pairs={{0,4},{4,0},{8,12},{12,8},{16,20},{20,16},{24,28},{28,24},{1,5},{5... | collective-permute-start | bytes 3145736 | tf_op jit(solution)/shard_map/ppermute | solution.py:635
  216.7 23.0 %collective-permute-start.34 = (bf16[256,2048]{1,0:T(8,128)(2,1)}, bf16[256,2048]{1,0:T(8,128)(2,1)}, u32[]{:S(2)}, u32[]{:S(2)}) collective-permute-start(bf16[256,2048]{1,0:T(8,128)(2,1)} %collective-permute-done.30.refs_4_), channel_id=1, source_target_pairs={{0,4},{4,0},{8,12},{12,8},{16,20},{20,16},{24,28},{28,24},{1,5},{5... | collective-permute-start | bytes 3145736 | tf_op jit(solution)/shard_map/ppermute | solution.py:635
  216.7 23.0 %collective-permute-start.35 = (bf16[256,2048]{1,0:T(8,128)(2,1)}, bf16[256,2048]{1,0:T(8,128)(2,1)}, u32[]{:S(2)}, u32[]{:S(2)}) collective-permute-start(bf16[256,2048]{1,0:T(8,128)(2,1)} %collective-permute-done.31.refs_5_), channel_id=1, source_target_pairs={{0,4},{4,0},{8,12},{12,8},{16,20},{20,16},{24,28},{28,24},{1,5},{5... | collective-permute-start | bytes 3145736 | tf_op jit(solution)/shard_map/ppermute | solution.py:635
  219.7 56.7 %collective-permute-start.26 = (bf16[256,2048]{1,0:T(8,128)(2,1)S(1)}, bf16[256,2048]{1,0:T(8,128)(2,1)}, u32[]{:S(2)}, u32[]{:S(2)}) collective-permute-start(bf16[256,2048]{1,0:T(8,128)(2,1)S(1)} %fusion.19.refs_23_), channel_id=1, source_target_pairs={{0,1},{1,2},{4,5},{5,6},{8,9},{9,10},{12,13},{13,14},{16,17},{17,1... | collective-permute-start | bytes 3145736 | tf_op jit(solution)/shard_map/ppermute | solution.py:669
  223.6 52.9 %collective-permute-start.28 = (bf16[256,2048]{1,0:T(8,128)(2,1)S(1)}, bf16[256,2048]{1,0:T(8,128)(2,1)}, u32[]{:S(2)}, u32[]{:S(2)}) collective-permute-start(bf16[256,2048]{1,0:T(8,128)(2,1)S(1)} %fusion.19.refs_23_), channel_id=1, source_target_pairs={{3,2},{2,1},{7,6},{6,5},{11,10},{10,9},{15,14},{14,13},{19,18},{18... | collective-permute-start | bytes 3145736 | tf_op jit(solution)/shard_map/ppermute | solution.py:670
  272.8 34.6 %collective-permute-start.37 = (bf16[2,1280,256]{2,1,0:T(8,128)(2,1)}, bf16[2,1280,256]{2,1,0:T(8,128)(2,1)}, u32[]{:S(2)}, u32[]{:S(2)}) collective-permute-start(bf16[2,1280,256]{2,1,0:T(8,128)(2,1)} %get-tuple-element.112.refs_9_), channel_id=1, source_target_pairs={{0,16},{4,20},{8,24},{12,28},{16,0},{20,4},{24,8},{28,12},{1,17},{... | collective-permute-start | bytes 3932168 | tf_op jit(solution)/shard_map/ppermute | solution.py:635
  273.3 36.4 %collective-permute-start.38 = (bf16[2,1280,256]{2,1,0:T(8,128)(2,1)}, bf16[2,1280,256]{2,1,0:T(8,128)(2,1)S(1)}, u32[]{:S(2)}, u32[]{:S(2)}) collective-permute-start(bf16[2,1280,256]{2,1,0:T(8,128)(2,1)} %get-tuple-element.120), channel_id=1, source_target_pairs={{0,8},{4,12},{8,0},{12,4},{16,24},{20,28},{24,16},{28,20},{1,9},{5... | collective-permute-start | bytes 3932168 | tf_op jit(solution)/shard_map/ppermute | solution.py:635
  345.1 4.0 collective-permute-start.45
  349.1 4.0 collective-permute-start.46
  353.1 2.3 collective-permute-start.47
  353.2 19.2 %collective-permute-start.56 = (bf16[1,1280,256]{2,1,0:T(8,128)(2,1)S(1)}, bf16[1,1280,256]{2,1,0:T(8,128)(2,1)}, u32[]{:S(2)}, u32[]{:S(2)}) collective-permute-start(bf16[1,1280,256]{2,1,0:T(8,128)(2,1)S(1)} %copy-done.37), channel_id=1, source_target_pairs={{0,8},{4,12},{8,0},{12,4},{16,24},{20,28},{24,16},{28,20},{1,9},{5... | collective-permute-start | bytes 1966088 | tf_op jit(solution)/shard_map/ppermute | solution.py:635
  353.9 16.9 %collective-permute-start.57 = (bf16[1,1280,256]{2,1,0:T(8,128)(2,1)S(1)}, bf16[1,1280,256]{2,1,0:T(8,128)(2,1)}, u32[]{:S(2)}, u32[]{:S(2)}) collective-permute-start(bf16[1,1280,256]{2,1,0:T(8,128)(2,1)S(1)} %copy-done.38), channel_id=1, source_target_pairs={{0,16},{4,20},{8,24},{12,28},{16,0},{20,4},{24,8},{28,12},{1,17},{... | collective-permute-start | bytes 1966088 | tf_op jit(solution)/shard_map/ppermute | solution.py:635
  355.5 5.7 %collective-permute-start.48 = (f32[4096]{0:T(1024)S(1)}, f32[4096]{0:T(1024)S(1)}, u32[]{:S(2)}, u32[]{:S(2)}) collective-permute-start(f32[4096]{0:T(1024)S(1)} %slice_add_fusion), channel_id=1, source_target_pairs={{0,1},{1,0},{2,3},{3,2},{4,5},{5,4},{6,7},{7,6},{8,9},{9,8},{10,11... | collective-permute-start | bytes 49160 | tf_op jit(solution)/shard_map/ppermute | solution.py:965
  355.5 5.6 %collective-permute-start.49 = (f32[4096]{0:T(1024)S(1)}, f32[4096]{0:T(1024)S(1)}, u32[]{:S(2)}, u32[]{:S(2)}) collective-permute-start(f32[4096]{0:T(1024)S(1)} %slice_add_fusion), channel_id=1, source_target_pairs={{0,2},{1,3},{2,0},{3,1},{4,6},{5,7},{6,4},{7,5},{8,10},{9,11},{10,... | collective-permute-start | bytes 49160 | tf_op jit(solution)/shard_map/ppermute | solution.py:965
  356.4 5.5 collective-permute-start.50
  361.1 12.8 %collective-permute-start.40 = (bf16[1,256,2048]{2,1,0:T(8,128)(2,1)}, bf16[1,256,2048]{2,1,0:T(8,128)(2,1)S(1)}, u32[]{:S(2)}, u32[]{:S(2)}) collective-permute-start(bf16[1,256,2048]{2,1,0:T(8,128)(2,1)} %get-tuple-element.125), channel_id=1, source_target_pairs={{0,4},{4,0},{8,12},{12,8},{16,20},{20,16},{24,28},{28,24},{1,5},{5... | collective-permute-start | bytes 3145736 | tf_op jit(solution)/shard_map/ppermute | solution.py:635
  361.1 112.3 %collective-permute-start.39 = (bf16[3,256,2048]{2,1,0:T(8,128)(2,1)}, bf16[3,256,2048]{2,1,0:T(8,128)(2,1)S(1)}, u32[]{:S(2)}, u32[]{:S(2)}) collective-permute-start(bf16[3,256,2048]{2,1,0:T(8,128)(2,1)} %get-tuple-element.123), channel_id=1, source_target_pairs={{0,4},{4,0},{8,12},{12,8},{16,20},{20,16},{24,28},{28,24},{1,5},{5... | collective-permute-start | bytes 9437192 | tf_op jit(solution)/shard_map/ppermute | solution.py:635
  372.3 37.2 %collective-permute-start.58 = (bf16[1280,256]{1,0:T(8,128)(2,1)S(1)}, bf16[1280,256]{1,0:T(8,128)(2,1)S(1)}, u32[]{:S(2)}, u32[]{:S(2)}) collective-permute-start(bf16[1280,256]{1,0:T(8,128)(2,1)S(1)} %fusion.21), channel_id=1, source_target_pairs={{0,4},{4,0},{8,12},{12,8},{16,20},{20,16},{24,28},{28,24},{1,5},{5... | collective-permute-start | bytes 1966088 | tf_op jit(solution)/shard_map/ppermute | solution.py:635
  405.3 20.6 %collective-permute-start.51 = (bf16[2,256,768]{2,1,0:T(8,128)(2,1)}, bf16[2,256,768]{2,1,0:T(8,128)(2,1)S(1)}, u32[]{:S(2)}, u32[]{:S(2)}) collective-permute-start(bf16[2,256,768]{2,1,0:T(8,128)(2,1)} %get-tuple-element.134), channel_id=1, source_target_pairs={{0,16},{4,20},{8,24},{12,28},{16,0},{20,4},{24,8},{28,12},{1,17},{... | collective-permute-start | bytes 2359304 | tf_op jit(solution)/shard_map/ppermute | solution.py:635
  407.0 41.0 %collective-permute-start.59 = (bf16[2,256,1024]{2,1,0:T(8,128)(2,1)S(1)}, bf16[2,256,1024]{2,1,0:T(8,128)(2,1)S(1)}, u32[]{:S(2)}, u32[]{:S(2)}) collective-permute-start(bf16[2,256,1024]{2,1,0:T(8,128)(2,1)S(1)} %copy-done.43), channel_id=1, source_target_pairs={{0,16},{4,20},{8,24},{12,28},{16,0},{20,4},{24,8},{28,12},{1,17},{... | collective-permute-start | bytes 3145736 | tf_op jit(solution)/shard_map/ppermute | solution.py:635
  408.1 20.6 %collective-permute-start.53 = (bf16[2,256,768]{2,1,0:T(8,128)(2,1)}, bf16[2,256,768]{2,1,0:T(8,128)(2,1)S(1)}, u32[]{:S(2)}, u32[]{:S(2)}) collective-permute-start(bf16[2,256,768]{2,1,0:T(8,128)(2,1)} %get-tuple-element.137), channel_id=1, source_target_pairs={{0,8},{4,12},{8,0},{12,4},{16,24},{20,28},{24,16},{28,20},{1,9},{5... | collective-permute-start | bytes 2359304 | tf_op jit(solution)/shard_map/ppermute | solution.py:635
  409.5 40.9 %collective-permute-start.61 = (bf16[2,256,1024]{2,1,0:T(8,128)(2,1)S(1)}, bf16[2,256,1024]{2,1,0:T(8,128)(2,1)S(1)}, u32[]{:S(2)}, u32[]{:S(2)}) collective-permute-start(bf16[2,256,1024]{2,1,0:T(8,128)(2,1)S(1)} %copy-done.64), channel_id=1, source_target_pairs={{0,8},{4,12},{8,0},{12,4},{16,24},{20,28},{24,16},{28,20},{1,9},{5... | collective-permute-start | bytes 3145736 | tf_op jit(solution)/shard_map/ppermute | solution.py:635
  426.0 46.2 %collective-permute-start.41 = (bf16[256,2048]{1,0:T(8,128)(2,1)S(1)}, bf16[256,2048]{1,0:T(8,128)(2,1)S(1)}, u32[]{:S(2)}, u32[]{:S(2)}) collective-permute-start(bf16[256,2048]{1,0:T(8,128)(2,1)S(1)} %copy-done.33), channel_id=1, source_target_pairs={{0,1},{1,2},{4,5},{5,6},{8,9},{9,10},{12,13},{13,14},{16,17},{17,1... | collective-permute-start | bytes 3145736 | tf_op jit(solution)/shard_map/ppermute | solution.py:669
  428.7 44.8 %collective-permute-start.43 = (bf16[256,2048]{1,0:T(8,128)(2,1)S(1)}, bf16[256,2048]{1,0:T(8,128)(2,1)S(1)}, u32[]{:S(2)}, u32[]{:S(2)}) collective-permute-start(bf16[256,2048]{1,0:T(8,128)(2,1)S(1)} %copy-done.33), channel_id=1, source_target_pairs={{3,2},{2,1},{7,6},{6,5},{11,10},{10,9},{15,14},{14,13},{19,18},{18... | collective-permute-start | bytes 3145736 | tf_op jit(solution)/shard_map/ppermute | solution.py:670
  448.0 10.8 %collective-permute-start.52 = (bf16[1,256,768]{2,1,0:T(8,128)(2,1)S(1)}, bf16[1,256,768]{2,1,0:T(8,128)(2,1)S(1)}, u32[]{:S(2)}, u32[]{:S(2)}) collective-permute-start(bf16[1,256,768]{2,1,0:T(8,128)(2,1)S(1)} %add_convert_fusion.10), channel_id=1, source_target_pairs={{0,8},{4,12},{8,0},{12,4},{16,24},{20,28},{24,16},{28,20},{1,9},{5... | collective-permute-start | bytes 1179656 | tf_op jit(solution)/shard_map/ppermute | solution.py:635
  450.4 10.3 %collective-permute-start.54 = (bf16[1,256,768]{2,1,0:T(8,128)(2,1)S(1)}, bf16[1,256,768]{2,1,0:T(8,128)(2,1)S(1)}, u32[]{:S(2)}, u32[]{:S(2)}) collective-permute-start(bf16[1,256,768]{2,1,0:T(8,128)(2,1)S(1)} %add_convert_fusion.9), channel_id=1, source_target_pairs={{0,16},{4,20},{8,24},{12,28},{16,0},{20,4},{24,8},{28,12},{1,17},{... | collective-permute-start | bytes 1179656 | tf_op jit(solution)/shard_map/ppermute | solution.py:635
  458.8 12.7 %collective-permute-start.60 = (bf16[1,256,1024]{2,1,0:T(8,128)(2,1)S(1)}, bf16[1,256,1024]{2,1,0:T(8,128)(2,1)S(1)}, u32[]{:S(2)}, u32[]{:S(2)}) collective-permute-start(bf16[1,256,1024]{2,1,0:T(8,128)(2,1)S(1)} %add_convert_fusion.7), channel_id=1, source_target_pairs={{0,8},{4,12},{8,0},{12,4},{16,24},{20,28},{24,16},{28,20},{1,9},{5... | collective-permute-start | bytes 1572872 | tf_op jit(solution)/shard_map/ppermute | solution.py:635
  460.7 93.9 %collective-permute-start.27 = (bf16[256,2048]{1,0:T(8,128)(2,1)S(1)}, bf16[256,2048]{1,0:T(8,128)(2,1)S(1)}, u32[]{:S(2)}, u32[]{:S(2)}) collective-permute-start(bf16[256,2048]{1,0:T(8,128)(2,1)S(1)} %copy-done.32), channel_id=1, source_target_pairs={{0,1},{1,2},{2,3},{3,0},{4,5},{5,6},{6,7},{7,4},{8,9},{9,10},{10,1... | collective-permute-start | bytes 3145736 | tf_op jit(solution)/shard_map/ppermute | solution.py:639
  471.5 83.1 %collective-permute-start.29 = (bf16[256,2048]{1,0:T(8,128)(2,1)S(1)}, bf16[256,2048]{1,0:T(8,128)(2,1)S(1)}, u32[]{:S(2)}, u32[]{:S(2)}) collective-permute-start(bf16[256,2048]{1,0:T(8,128)(2,1)S(1)} %copy-done.31), channel_id=1, source_target_pairs={{0,3},{1,0},{2,1},{3,2},{4,7},{5,4},{6,5},{7,6},{8,11},{9,8},{10,9... | collective-permute-start | bytes 3145736 | tf_op jit(solution)/shard_map/ppermute | solution.py:639
  472.2 11.7 %collective-permute-start.62 = (bf16[1,256,1024]{2,1,0:T(8,128)(2,1)S(1)}, bf16[1,256,1024]{2,1,0:T(8,128)(2,1)S(1)}, u32[]{:S(2)}, u32[]{:S(2)}) collective-permute-start(bf16[1,256,1024]{2,1,0:T(8,128)(2,1)S(1)} %add_convert_fusion.6), channel_id=1, source_target_pairs={{0,16},{4,20},{8,24},{12,28},{16,0},{20,4},{24,8},{28,12},{1,17},{... | collective-permute-start | bytes 1572872 | tf_op jit(solution)/shard_map/ppermute | solution.py:635
  473.5 12.6 %collective-permute-start.55 = (bf16[256,768]{1,0:T(8,128)(2,1)S(1)}, bf16[256,768]{1,0:T(8,128)(2,1)S(1)}, u32[]{:S(2)}, u32[]{:S(2)}) collective-permute-start(bf16[256,768]{1,0:T(8,128)(2,1)S(1)} %fusion.23), channel_id=1, source_target_pairs={{0,4},{4,0},{8,12},{12,8},{16,20},{20,16},{24,28},{28,24},{1,5},{5... | collective-permute-start | bytes 1179656 | tf_op jit(solution)/shard_map/ppermute | solution.py:635
  474.8 58.9 %collective-permute-start.42 = (bf16[256,2048]{1,0:T(8,128)(2,1)S(1)}, bf16[256,2048]{1,0:T(8,128)(2,1)S(1)}, u32[]{:S(2)}, u32[]{:S(2)}) collective-permute-start(bf16[256,2048]{1,0:T(8,128)(2,1)S(1)} %get-tuple-element.151), channel_id=1, source_target_pairs={{0,1},{1,2},{2,3},{3,0},{4,5},{5,6},{6,7},{7,4},{8,9},{9,10},{10,1... | collective-permute-start | bytes 3145736 | tf_op jit(solution)/shard_map/ppermute | solution.py:639
  483.8 69.6 %collective-permute-start.44 = (bf16[256,2048]{1,0:T(8,128)(2,1)S(1)}, bf16[256,2048]{1,0:T(8,128)(2,1)S(1)}, u32[]{:S(2)}, u32[]{:S(2)}) collective-permute-start(bf16[256,2048]{1,0:T(8,128)(2,1)S(1)} %get-tuple-element.152), channel_id=1, source_target_pairs={{0,3},{1,0},{2,1},{3,2},{4,7},{5,4},{6,5},{7,6},{8,11},{9,8},{10,9... | collective-permute-start | bytes 3145736 | tf_op jit(solution)/shard_map/ppermute | solution.py:639
  486.1 2.0 collective-permute-start.63
  (67 other events, 1372.7 us)

commit v4 on v3

--- a/solution.py
+++ b/solution.py
@@ -109,15 +109,20 @@
     return lambda owner: ref.at[:, pl.ds(pl.multiple_of(owner * size, size), size)]
 
 
-def flat(chunks):
-    return [array for k in sorted(chunks) for array in chunks[k]]
-
-
-def unflat(refs, shifts):
-    refs, chunks = list(refs), {}
-    for k, many in shifts:
-        chunks[k], refs = refs[:many], refs[many:]
-    return chunks
+def arrays_of(chunks):
+    return [array for array, _ in chunks]
+
+
+def shifts_of(chunks):
+    return tuple(shifts for _, shifts in chunks)
+
+
+def by_shift(refs, shifts):
+    found = {}
+    for ref, group in zip(refs, shifts):
+        for n, k in enumerate(group):
+            found[k] = ref if len(group) == 1 else ref.at[n]
+    return found
 
 
 def chunk_copies(chunks, places, parts, held, sems):
@@ -128,11 +133,7 @@
             slot, options = s * len(places) + i, []
             for k in sorted({(at - (at ^ m)) % parts for at in range(parts)}):
                 here = lax.rem(z - lax.bitwise_xor(z, m) + parts, parts) == k
-                if len(sequence[k]) == 1:
-                    options.append((None if k == 0 else here, sequence[k][0]))
-                else:
-                    options.append((here & (z >= parts // 2), sequence[k][0]))
-                    options.append((here & (z < parts // 2), sequence[k][1]))
+                options.append((here if k else None, sequence[k]))
             found.append(
                 [
                     (here, pltpu.make_async_copy(source, held.at[slot], sems.at[slot]))
@@ -157,11 +158,10 @@
 
 def project_kernel(setup, at_ref, bias_ref, gain_ref, shift_ref, cos_ref, left_ref, right_ref, *rest):
     count, parts, places, width, hidden, shifts = setup
-    refs = sum(many for _, many in shifts)
-    chunks = [unflat(rest[:refs], shifts), unflat(rest[refs : 2 * refs], shifts)]
-    blocks, rest = rest[2 * refs : 2 * refs + count], rest[2 * refs + count :]
-    qkv_ref, act_ref, slope_ref, normed_ref, tokens_ref, held, x_held, ready, sems, x_sems = rest
-    step, steps = pl.program_id(0), 2 * len(places)
+    chunks = [by_shift(rest, shifts)]
+    blocks = rest[len(shifts) : len(shifts) + count]
+    qkv_ref, act_ref, slope_ref, normed_ref, tokens_ref, held, x_held, ready, sems, x_sems = rest[-10:]
+    step, steps = pl.program_id(0), len(places)
     found = chunk_copies(chunks, places, parts, x_held, x_sems)
     loads = block_copies(blocks, rows_at(held, blocks[0].shape[0]), sems)
 
@@ -211,33 +211,34 @@
             slope_ref[:, columns] = slope.astype(BF16)
 
 
-def project(at_mp, chunks, blocks, bias, gain, shift, tables, width, parts, deps):
-    places, shifts = tuple(range(parts)), [(k, len(chunks[0][k])) for k in sorted(chunks[0])]
-    rows, model = chunks[0][0][0].shape
-    total, hidden = blocks[0].shape[1], blocks[0].shape[1] - 3 * width
-    count, length = len(blocks), 2 * parts * rows
-    table = pl.BlockSpec((rows, LANES), lambda i, at: (at[0] ^ (i % parts), 0))
-    out = lambda w: pl.BlockSpec((rows, w), lambda i, at: (i - i % parts + (at[0] ^ (i % parts)), 0))
+def project(at_mp, sequence, chunks, blocks, bias, gain, shift, tables, width, parts, earlier, deps):
+    places, total = tuple(range(parts)), blocks[0].shape[1]
+    rows, model, count = tables[0].shape[0] // parts, gain.shape[1], len(blocks)
+    hidden = total - 3 * width
+    table = pl.BlockSpec((rows, LANES), lambda i, at: (at[0] ^ i, 0))
+    out = lambda w: pl.BlockSpec((rows, w), lambda i, at: (sequence * parts + (at[0] ^ i), 0))
     line = lambda a: pl.BlockSpec(a.shape, lambda i, at: (0, 0))
     widths = (3 * width, hidden, hidden, model, model)
-    setup = (count, parts, places, width, hidden, shifts)
+    setup = (count, parts, places, width, hidden, shifts_of(chunks))
+    operands = [bias, gain, shift, *tables, *arrays_of(chunks), *blocks]
     return call(
         functools.partial(project_kernel, setup),
         "project",
-        [bias, gain, shift, *tables, *flat(chunks[0]), *flat(chunks[1]), *blocks],
+        operands + list(earlier),
         deps,
         (at_mp,),
-        grid=(2 * parts,),
+        grid=(parts,),
         in_specs=[line(bias), line(gain), line(shift), table, table, table]
-        + [ANY] * (2 * len(flat(chunks[0])) + count),
+        + [ANY] * (len(chunks) + count + len(earlier)),
         out_specs=[out(w) for w in widths],
-        out_shape=[jax.ShapeDtypeStruct((length, w), BF16) for w in widths],
+        out_shape=[jax.ShapeDtypeStruct((2 * parts * rows, w), BF16) for w in widths],
+        input_output_aliases={1 + len(operands) + n: n for n in range(len(earlier))},
         scratch_shapes=[
             pltpu.VMEM((model, total), BF16),
-            pltpu.VMEM((2 * parts, rows, model), BF16),
+            pltpu.VMEM((parts, rows, model), BF16),
             pltpu.VMEM((2, rows, model), BF16),
             pltpu.SemaphoreType.DMA((count,)),
-            pltpu.SemaphoreType.DMA((2 * parts,)),
+            pltpu.SemaphoreType.DMA((parts,)),
         ],
     )
 
@@ -458,11 +459,12 @@
 
 
 def grad_in_kernel(setup, at_ref, slope_ref, *rest):
-    count, parts, places, width, hidden, shifts = setup
-    refs = sum(many for _, many in shifts)
-    many = 2 * refs
-    chunks = [unflat(rest[:refs], shifts), unflat(rest[refs:many], shifts)]
-    blocks, rest = rest[many : many + count], rest[many + count :]
+    count, parts, places, width, hidden, groups = setup
+    chunks, many = [], 0
+    for shifts in groups:
+        chunks.append(by_shift(rest[many:], shifts))
+        many += len(shifts)
+    blocks = rest[many : many + count]
     gmixed_ref, gpre_ref, dy_ref, gsum_ref, dsum_ref, held, dy_held, sems, dy_sems = rest[-9:]
     step, steps = pl.program_id(0), 2 * len(places)
     found = chunk_copies(chunks, places, parts, dy_held, dy_sems)
@@ -497,10 +499,9 @@
 
 
 def grad_in(at_mp, chunks, slope, blocks, width, parts, places, earlier, deps):
-    rows, model = chunks[0][0][0].shape
+    model = len(blocks) * blocks[0].shape[1]
     hidden, length = slope.shape[1], slope.shape[0]
-    shifts = [(k, len(chunks[0][k])) for k in sorted(chunks[0])]
-    count, many = len(blocks), len(flat(chunks[0])) * 2
+    rows, count, many = length // (2 * parts), len(blocks), sum(len(c) for c in chunks)
     turns = len(places)
 
     def where(i, at):
@@ -511,8 +512,8 @@
 
     out = lambda w: pl.BlockSpec((rows, w), lambda i, at: (where(i, at), 0))
     total = lambda w: pl.BlockSpec((8, w), lambda i, at: (0, 0))
-    setup = (count, parts, places, width, hidden, shifts)
-    operands = [slope, *flat(chunks[0]), *flat(chunks[1]), *blocks]
+    setup = (count, parts, places, width, hidden, [shifts_of(c) for c in chunks])
+    operands = [slope, *arrays_of(chunks[0]), *arrays_of(chunks[1]), *blocks]
     aliases = {1 + len(operands) + n: n for n in range(len(earlier))}
     return call(
         functools.partial(grad_in_kernel, setup),
@@ -639,47 +640,26 @@
     return lax.ppermute(value, "mp", [(i, (i + k) % parts) for i in range(parts)])
 
 
-def gather_near(own, parts):
-    shifts = (1, 3) if parts == 4 else range(1, parts)
-    return {0: [own], **{k: [ring(own, k, parts)] for k in shifts}}
+def near_shifts(parts):
+    return (1, 3) if parts == 4 else tuple(range(1, parts))
 
 
 def gather_far(chunks, parts):
-    if parts == 4:
-        up = lax.ppermute(chunks[1][0], "mp", [(1, 2), (2, 3)])
-        down = lax.ppermute(chunks[3][0], "mp", [(1, 0), (2, 1)])
-        chunks = {**chunks, 2: [up, down]}
-    return chunks
-
-
-class LineScatter:
-    def __init__(self, sums):
-        self.sums, self.parts = [list(s) for s in sums], len(sums)
-
-    def total(self, k):
-        if len(self.sums[k]) > 1:
-            self.sums[k] = [sum(s.astype(F32) for s in self.sums[k]).astype(BF16)]
-        return self.sums[k][0]
-
-    def far_ready(self):
-        return [self.total(2)] if self.parts == 4 else []
-
-    def far(self):
-        if self.parts == 4:
-            self.sums[1].append(lax.ppermute(self.total(2), "mp", [(0, 1), (1, 2)]))
-            self.sums[3].append(lax.ppermute(self.total(2), "mp", [(3, 2), (2, 1)]))
-
-    def shifts(self):
-        return (1, 3) if self.parts == 4 else range(1, self.parts)
-
-    def near_ready(self):
-        return [self.total(k) for k in self.shifts()]
-
-    def near(self):
-        self.sums[0] += [ring(self.total(k), k, self.parts) for k in self.shifts()]
-
-    def result(self):
-        return sum(s.astype(F32) for s in self.sums[0])
+    if parts != 4:
+        return None
+    up = lax.ppermute(chunks[1], "mp", [(1, 2), (2, 3)])
+    down = lax.ppermute(chunks[3], "mp", [(1, 0), (2, 1)])
+    return up + down
+
+
+def added(addends):
+    return sum(a.astype(F32) for a in addends).astype(BF16)
+
+
+def send_far(farthest):
+    up = lax.ppermute(farthest, "mp", [(0, 1), (1, 2)])
+    down = lax.ppermute(farthest, "mp", [(3, 2), (2, 1)])
+    return [up, down]
 
 
 def chip_bits(count):
@@ -695,25 +675,25 @@
         self.held, self.count = {0: own, 1: sibling}, count
         self.orders = (chip_bits(count), chip_bits(count)[::-1])
 
-    def first(self):
-        start, orders = dict(self.held), self.orders
-        for s in range(min(2, len(orders[0]))):
+    def own_to(self, s):
+        if s < len(self.orders[0]):
             for half in range(2):
-                bit = orders[half][s]
-                self.held[half ^ bit] = across(start[half], bit, self.count)
-
-    def second(self):
+                bit = self.orders[half][s]
+                self.held[half ^ bit] = across(self.held[half], bit, self.count)
+
+    def rest(self):
         for s in range(1, len(self.orders[0])):
             for half in range(2):
                 order = self.orders[half]
-                bit, done = order[s], order[:s]
-                for j in [j for j in self.held if j % 2 == half and not j & bit]:
-                    if j ^ bit not in self.held and not any(j & b for b in order[s:]):
-                        self.held[j ^ bit] = across(self.held[j], bit, self.count)
-
-    def fenced(self, deps=()):
+                for j in [j for j in self.held if j % 2 == half]:
+                    if j ^ order[s] not in self.held and not any(j & b for b in order[s:]):
+                        self.held[j ^ order[s]] = across(self.held[j], order[s], self.count)
+
+    def fenced(self, others=(), deps=()):
         keys = sorted(self.held)
-        self.held = dict(zip(keys, fence([self.held[j] for j in keys], deps)))
+        values = fence([self.held[j] for j in keys] + list(others), deps)
+        self.held = dict(zip(keys, values))
+        return values[len(keys) :]
 
     def blocks(self):
         return [self.held[j] for j in range(self.count)]
@@ -738,30 +718,36 @@
     def __init__(self, halves, count):
         self.count, self.orders = count, scatter_orders(count)
         self.held = [[[a] for a in arrays] for arrays in halves]
+        self.steps = len(self.orders[0])
 
     def total(self, half, s):
-        addends = self.held[half][s]
-        if len(addends) > 1:
-            addends = [sum(a.astype(F32) for a in addends).astype(BF16)]
-            self.held[half][s] = addends
-        return addends[0]
+        if len(self.held[half][s]) > 1:
+            self.held[half][s] = [added(self.held[half][s])]
+        return self.held[half][s][0]
 
     def ready(self, s):
         return [self.total(half, s) for half in range(2)]
 
-    def step(self, s):
+    def send(self, s):
+        return [across(self.total(h, s), self.orders[h][s], self.count) for h in range(2)]
+
+    def arrive(self, s, came):
         for half in range(2):
-            came = across(self.total(half, s), self.orders[half][s], self.count)
             first = 0
             for later in self.held[half][s + 1 :]:
                 many = later[0].shape[0]
-                later.append(came[first : first + many])
+                later.append(came[half][first : first + many])
                 first += many
 
-    def finish(self):
-        mine = sum(a[0].astype(F32) for a in self.held[0][-1])
-        theirs = across(self.total(1, -1)[0], 1, self.count)
-        return mine, theirs.astype(F32)
+    def between(self):
+        for s in range(1, self.steps - 1):
+            self.arrive(s, self.send(s))
+
+    def last(self):
+        return self.total(1, -1)[0]
+
+    def finish(self, theirs):
+        return sum(a[0].astype(F32) for a in self.held[0][-1]), theirs.astype(F32)
 
 
 def on_device(
@@ -801,26 +787,32 @@
             [rank(dense_weight, 0, which, width), rank(down_weight, 0, which, hidden)], axis=0
         )
 
+    def stage(*arrays):
+        return jnp.stack(arrays), tuple([0, *near])
+
+    near, places, pairs = near_shifts(nmp), list(range(nmp)), width // LANES
     rows = BlockGather(row_pack(core), across(row_pack(1 - core), 1, ndp), ndp)
     columns = BlockGather(column_pack(core), across(column_pack(1 - core), 1, ndp), ndp)
-    own = gather_near(tokens, nmp)
-    rows.first()
-    keys, moved = sorted(rows.held), [k for k in own if k]
-    fenced = fence(
-        [rows.held[j] for j in keys] + [own[k][0] for k in moved] + [cotangent],
-        columns.held.values(),
-    )
-    rows.held = dict(zip(keys, fenced))
-    own.update({k: [array] for k, array in zip(moved, fenced[len(keys) :])})
-    cot = fenced[-1]
-    other = {k: [across(own[k][0], 1, ndp)] for k in own}
-    rows.second()
-    own = gather_far(own, nmp)
-    far = own.get(2, []) if nmp == 4 else []
-    cot, *held = fence([cot, columns.held[0], columns.held[1]], [*far, *rows.blocks()])
-    columns.held = dict(enumerate(held))
-    if far:
-        other[2] = [across(array, 1, ndp) for array in far]
+    head, tail = near[0], near[1:]
+    came = {head: ring(tokens, head, nmp)}
+    rows.own_to(0)
+    came[head], begun = rows.fenced([came[head], tokens], columns.held.values())
+    came.update({k: ring(begun, k, nmp) for k in tail})
+    rows.own_to(1)
+    *held, cot = rows.fenced([*came.values(), cotangent])
+    came = dict(zip(near, held))
+    own = [(tokens, (0,))] + [(came[k], (k,)) for k in near]
+    packed, shifts = stage(tokens, *held)
+    other = [(across(packed, 1, ndp), shifts)]
+    far = gather_far(came, nmp)
+    rows.rest()
+    cot, *held = rows.fenced(
+        [cot, columns.held[0], columns.held[1]] + ([far] if nmp == 4 else []), [other[0][0]]
+    )
+    columns.held = dict(enumerate(held[:2]))
+    if nmp == 4:
+        own.append((held[2], (2,)))
+        other.append((across(held[2], 1, ndp), (2,)))
 
     tables = rotary_tables(length)
     bias = jnp.concatenate(
@@ -831,58 +823,68 @@
         axis=1,
     )
     gain, shift = norm_gain.astype(F32)[None, :], norm_bias.astype(F32)[None, :]
-    dy_own = gather_near(cot, nmp)
-    columns.first()
+    came = {head: ring(cot, head, nmp)}
+    columns.own_to(0)
+    common = (rows.blocks(), bias, gain, shift, tables, width, nmp)
+    first = project(at_mp, 0, own, *common, (), [cot])
+    cot, came[head] = columns.fenced([cot, came[head]], [first[0]])
+    came.update({k: ring(cot, k, nmp) for k in tail})
+    columns.own_to(1)
     qkv, act, slope, normed, token_rows = project(
-        at_mp, (own, other), rows.blocks(), bias, gain, shift, tables, width, nmp, [cot]
-    )
-    columns.fenced([qkv])
-    columns.second()
+        at_mp, 1, other, *common, first, [columns.held[0]]
+    )
+    columns.fenced(deps=[qkv])
+    columns.rest()
     mixed, lse = attend(qkv, length, block, [columns.held[0]])
-    moved = [k for k in dy_own if k]
-    dy_own.update(
-        {k: [a] for k, a in zip(moved, fence([dy_own[k][0] for k in moved], [mixed]))}
-    )
-    dy_other = {k: [across(dy_own[k][0], 1, ndp)] for k in dy_own}
-    dy_far = gather_far(dy_own, nmp)
-    if nmp == 4:
-        dy_other[2] = [across(array, 1, ndp) for array in dy_far[2]]
-    places = list(range(nmp))
+    held = columns.fenced(came.values(), [mixed])
+    came = dict(zip(near, held))
+    dy_own = [(cot, (0,))] + [(came[k], (k,)) for k in near]
+    packed, shifts = stage(cot, *held)
+    dy_packed = across(packed, 1, ndp)
+    far = gather_far(came, nmp)
     other_sums, own_sums = branch_sums(
-        at_mp, mixed, act, columns.blocks(), nmp, places, [dy_own[1][0]]
-    )
-    came = across(other_sums, 1, ndp)
-    branches = LineScatter([[own_sums[k], came[k]] for k in range(nmp)])
-
-    near = lambda chunks: {k: chunks[k] for k in (0, 1, nmp - 1)}
-    first = grad_in(
+        at_mp, mixed, act, columns.blocks(), nmp, places, [packed]
+    )
+    dy_packed, other_sums, *far = fence(
+        [dy_packed, other_sums] + ([far] if nmp == 4 else []), [own_sums]
+    )
+    theirs = across(other_sums, 1, ndp)
+
+    dy_other = [(dy_packed, shifts)]
+    grad_a = grad_in(
+        at_mp, (dy_own, dy_other), slope, columns.blocks(), width, nmp, (0, 1), (), [other_sums]
+    )
+    far_other = [across(a, 1, ndp) for a in far]
+    theirs, *far_other = fence([theirs, *far_other], [grad_a[3]])
+    shares = [[own_sums[k], theirs[k]] for k in places]
+    farthest = [added(shares[2])] if nmp == 4 else []
+    moved = [a for f in farthest for a in send_far(f)]
+    grad_b = grad_in(
         at_mp,
-        (near(dy_own), near(dy_other)),
+        (dy_own + [(a, (2,)) for a in far], dy_other + [(a, (2,)) for a in far_other]),
         slope,
         columns.blocks(),
         width,
         nmp,
-        (0, 1),
-        (),
-        [other_sums],
-    )
-    second = grad_in(
-        at_mp,
-        (dy_far, dy_other),
-        slope,
-        columns.blocks(),
-        width,
-        nmp,
-        tuple(range(2, nmp)),
-        first[:3],
-        branches.far_ready(),
-    )
-    branches.far()
-    gmixed, gpre, dy = second[:3]
+        tuple(places[2:]),
+        grad_a[:3],
+        [grad_a[3], *farthest],
+    )
+    gmixed, gpre, dy = grad_b[:3]
     column_grads = BlockScatter(
-        weight_grads(me, [mixed, act], [dy], ndp, [second[3]], left=False), ndp
-    )
-    column_grads.step(0)
+        weight_grads(me, [mixed, act], [dy], ndp, [grad_b[3]], left=False), ndp
+    )
+
+    def with_far(shares, moved):
+        if moved:
+            shares[1], shares[3] = shares[1] + [moved[0]], shares[3] + [moved[1]]
+        return {k: added(shares[k]) for k in near}
+
+    if moved:
+        moved = fence(moved, [column_grads.held[0][0][0]])
+    sums = with_far(shares, moved)
+    brought = [ring(sums[head], head, nmp)]
+    column_came = column_grads.send(0)
     gq, gk, gv, qkv_sums = attend_back(
         qkv,
         gmixed,
@@ -891,86 +893,100 @@
         tables,
         length,
         block,
-        [column_grads.held[0][0][0], *branches.near_ready()],
-    )
-    branches.near()
-    for s in range(1, chip_steps - 1):
-        column_grads.step(s)
-    early = [2] if nmp == 4 else places[: nmp // 2]
-    late = [k for k in places if k not in early]
-    grads_a = grad_normed_sums(
-        at_mp,
-        (gq, gk, gv),
-        gpre,
-        token_rows,
-        rows.blocks(),
-        nmp,
-        early,
-        column_grads.ready(chip_steps - 1),
-    )
-    column_grads.step(chip_steps - 1)
-    came_a = across(grads_a[0], 1, ndp)
-    grads_b = grad_normed_sums(
-        at_mp, (gq, gk, gv), gpre, token_rows, rows.blocks(), nmp, late, [grads_a[2]]
-    )
-    came_b = across(grads_b[0], 1, ndp)
-    shares = {}
-    for part, got, kept in ((early, came_a, grads_a[1]), (late, came_b, grads_b[1])):
+        [column_grads.held[0][0][0], *sums.values()],
+    )
+    brought[0], *held = fence([brought[0], *(sums[k] for k in tail)], [gq])
+    brought += [ring(a, k, nmp) for k, a in zip(tail, held)]
+
+    def normed_part(part, deps):
+        return grad_normed_sums(
+            at_mp, (gq, gk, gv), gpre, token_rows, rows.blocks(), nmp, part, deps
+        )
+
+    thirds = ([2], [1, 3], [0]) if nmp == 4 else (places[1:2], places[2:], places[:1])
+    other_a, own_a, sums_a = normed_part(thirds[0], [brought[0]])
+    *column_came, other_a = fence([*column_came, other_a], [sums_a])
+    column_grads.arrive(0, column_came)
+    column_grads.between()
+    column_came = column_grads.send(-1 + chip_steps)
+    most = other_a.shape[1] // 2
+    came_a = [across(p, 1, ndp) for p in (other_a[:, :most], other_a[:, most:])]
+    other_b, own_b, sums_b = normed_part(
+        thirds[1], [sums_a, *column_grads.ready(chip_steps - 1)]
+    )
+    brought[1:] = fence(brought[1:], [sums_b])
+    c0, c1, a0, a1, other_b = fence([*column_came, *came_a, other_b], [brought[1]])
+    column_grads.arrive(chip_steps - 1, [c0, c1])
+    came_a = jnp.concatenate([a0, a1], axis=1)
+    came_b = across(other_b, 1, ndp)
+    shares = [[] for _ in places]
+    for part, kept, got in ((thirds[0], own_a, came_a),):
         for n, k in enumerate(part):
             shares[k] = [kept[n], got[n]]
-    grad_rows = LineScatter([shares[k] for k in places])
+    farthest = [added(shares[2])] if nmp == 4 else []
+    moved = [a for f in farthest for a in send_far(f)]
     up_grads = BlockScatter(
         weight_grads(
-            me, [normed], [gpre], ndp, [grads_b[2], *grad_rows.far_ready()], left=True
+            me, [normed], [gpre], ndp, [sums_b, *farthest, column_grads.last()], left=True
         ),
         ndp,
     )
-    grad_rows.far()
-    up_grads.step(0)
+    up_came = up_grads.send(0)
+    other_c, own_c, sums_c = normed_part(thirds[2], [up_grads.held[0][0][0]])
+    qkv_sum = (
+        qkv_sums.reshape(2, pairs, 8, LANES).sum(0)[:, :3, :].transpose(1, 0, 2).reshape(3 * width)
+    )
+    norm_sums = (sums_a + sums_b + sums_c)[:2].reshape(2 * model)
+    small = jnp.concatenate(
+        [norm_sums, qkv_sum, grad_a[3][0] + grad_b[3][0], grad_a[4][0] + grad_b[4][0]]
+    )
+    came_b, other_c, column_last, small, *moved = fence(
+        [came_b, other_c, column_grads.last(), small, *moved], [sums_c]
+    )
+    for n, k in enumerate(thirds[1]):
+        shares[k] = [own_b[n], came_b[n]]
+    sums = with_far(shares, moved)
+    came = {head: ring(sums[head], head, nmp)}
+    column_theirs = across(column_last, 1, ndp)
+    small = lax.all_gather(small, "dp")
     qkv_grads = BlockScatter(
-        weight_grads(me, [normed], [gq, gk, gv], ndp, [up_grads.held[0][0][0]], left=True), ndp
-    )
-    grad_rows.near()
-    for s in range(1, chip_steps):
-        up_grads.step(s)
-    for s in range(chip_steps):
-        qkv_grads.step(s)
+        weight_grads(me, [normed], [gq, gk, gv], ndp, [sums_c, *sums.values()], left=True), ndp
+    )
+    *up_came, q0, q1, column_theirs, small = fence(
+        [*up_came, qkv_grads.held[0][0][0], qkv_grads.held[1][0][0], column_theirs, small]
+    )
+    qkv_grads.held[0][0], qkv_grads.held[1][0] = [q0], [q1]
+    up_grads.arrive(0, up_came)
+    up_grads.between()
+    up_came = up_grads.send(chip_steps - 1)
+    qkv_came = qkv_grads.send(0)
+    small = small.reshape(ndp // 2, 2, -1).sum(axis=0)
+    norm_sums, small = small[:, : 2 * model].sum(axis=0), small[:, 2 * model :]
+    came[head], other_c, norm_sums, *held = fence(
+        [came[head], other_c, norm_sums, *(sums[k] for k in tail)], [q0]
+    )
+    half = held[0].shape[0] // 2
+    early = [ring(a[:half], k, nmp) for k, a in zip(tail, held)]
+    u0, u1, *qkv_came = fence([*up_came, *qkv_came], [came[head]])
+    up_grads.arrive(chip_steps - 1, [u0, u1])
+    up_theirs = across(up_grads.last(), 1, ndp)
+    qkv_grads.arrive(0, qkv_came)
+    qkv_grads.between()
+    late = fence([*early, *(a[half:] for a in held)])
+    early, late = late[: len(tail)], late[len(tail) :]
+    late = [ring(a, k, nmp) for k, a in zip(tail, late)]
+    came.update({k: jnp.concatenate(pair) for k, *pair in zip(tail, early, late)})
+    came_c = across(other_c, 1, ndp)
+    qkv_grads.arrive(chip_steps - 1, qkv_grads.send(chip_steps - 1))
+    qkv_theirs = across(qkv_grads.last(), 1, ndp)
+    norm_sums = lax.all_gather(norm_sums, "mp").sum(axis=0)
 
     local_inputs = tokens.astype(F32)
     output = (
         local_inputs
-        + branches.result()
+        + sum(a.astype(F32) for a in [own_sums[0], theirs[0], *brought])
         + (dense_bias.astype(F32) + down_bias.astype(F32))[None, :]
     ).astype(BF16)
-
-    pairs = width // LANES
-    qkv_sum = (
-        qkv_sums.reshape(2, pairs, 8, LANES).sum(0)[:, :3, :].transpose(1, 0, 2).reshape(3 * width)
-    )
-    small = jnp.concatenate(
-        [
-            qkv_sum,
-            first[3][0] + second[3][0],
-            (grads_a[2][:2] + grads_b[2][:2]).reshape(2 * model),
-            first[4][0] + second[4][0],
-        ]
-    )
-    for bit in chip_bits(ndp):
-        small = small + across(small, bit, ndp)
-    inner = 3 * width + hidden
-    here, grad_out_bias = small[: inner + 2 * model], small[inner + 2 * model :]
-    there = across(here, 1, ndp)
-    norm_sums = here[inner:] + there[inner:]
-    sums = [norm_sums] + [
-        lax.ppermute(norm_sums, "mp", [(i, i ^ j) for i in range(nmp)]) for j in range(1, nmp)
-    ]
-    while len(sums) > 1:
-        sums = [a + b for a, b in zip(sums[::2], sums[1::2])]
-    even, odd = jnp.where(core == 0, here, there), jnp.where(core == 0, there, here)
-    grad_qkv_bias = jnp.concatenate(
-        [even[: 3 * width].reshape(3, width), odd[: 3 * width].reshape(3, width)], axis=1
-    )
-    grad_up_bias = jnp.concatenate([even[3 * width : inner], odd[3 * width : inner]])
 
     def both(mine, theirs, axis):
         return jnp.where(
@@ -979,11 +995,11 @@
             jnp.concatenate([theirs, mine], axis=axis),
         )
 
-    mine, theirs = column_grads.finish()
+    mine, theirs = column_grads.finish(column_theirs)
     owned_dense = both(mine[:width], theirs[:width], 0)
     owned_down = both(mine[width:], theirs[width:], 0)
-    owned_up = both(*up_grads.finish(), 1)
-    mine, theirs = qkv_grads.finish()
+    owned_up = both(*up_grads.finish(up_theirs), 1)
+    mine, theirs = qkv_grads.finish(qkv_theirs)
     owned_qkv = jnp.stack(
         [
             both(mine[:, c * width : (c + 1) * width], theirs[:, c * width : (c + 1) * width], 1)
@@ -991,23 +1007,28 @@
         ]
     )
 
-    row_mean = jnp.mean(local_inputs, axis=1, keepdims=True)
-    centered = local_inputs - row_mean
-    row_var = jnp.mean(centered * centered, axis=1, keepdims=True)
-    inverse_std = lax.rsqrt(row_var + EPS)
+    inner = 3 * width + hidden
+    grad_out_bias = small[0, inner:]
+    grad_qkv_bias = jnp.concatenate(
+        [small[h, : 3 * width].reshape(3, width) for h in range(2)], axis=1
+    )
+    grad_up_bias = small[:, 3 * width : inner].reshape(2 * hidden)
+
+    centered = local_inputs - jnp.mean(local_inputs, axis=1, keepdims=True)
+    inverse_std = lax.rsqrt(jnp.mean(centered * centered, axis=1, keepdims=True) + EPS)
     normal_rows = centered * inverse_std
-    scaled_grad = grad_rows.result() * gain
-    first_mean = jnp.mean(scaled_grad, axis=1, keepdims=True)
-    second_mean = jnp.mean(scaled_grad * normal_rows, axis=1, keepdims=True)
+    grad_rows = sum(a.astype(F32) for a in [own_c[0], came_c[0], *came.values()])
+    scaled = grad_rows * gain
+    first_mean = jnp.mean(scaled, axis=1, keepdims=True)
+    second_mean = jnp.mean(scaled * normal_rows, axis=1, keepdims=True)
     grad_tokens = (
-        cotangent.astype(F32)
-        + (scaled_grad - first_mean - normal_rows * second_mean) * inverse_std
+        cotangent.astype(F32) + (scaled - first_mean - normal_rows * second_mean) * inverse_std
     ).astype(BF16)
     return (
         output,
         grad_tokens,
-        sums[0][:model],
-        sums[0][model:],
+        norm_sums[:model],
+        norm_sums[model:],
         owned_qkv,
         grad_qkv_bias,
         owned_dense,

time: 570 us -> 497 us (0.87)
  waiting for transfers between devices: 241 us -> 84.1 us
  blocking collectives: 0 us -> 30.7 us
  local copies, waits for them, and re-layouts: 12.9 us -> 40.6 us
  other arithmetic: 37.3 us -> 63.1 us
  Pallas kernels: 203 us -> 213 us
  starting transfers between devices: 63.6 us -> 55.8 us
    ppermute x45 -> x38, waiting for transfers between devices: 123 us -> 40.5 us  [across(): return lax.ppermute(value, 'dp', [(i, i ^ bit) for i in range(count)])]
    ppermute x8 -> x9, waiting for transfers between devices: 85.8 us -> 11.2 us  [ring(): lax.ppermute(value, 'mp', [(i, (i + k) % parts) for i in range(parts)])]
    all_gather x0 -> x2, blocking collectives: none -> 30.7 us  [the longest x1 20.9 us: on_device(): norm_sums = lax.all_gather(norm_sums, 'mp').sum(axis=0)]
    unnamed x137 -> x188, local copies, waits for them, and re-layouts: 10.5 us -> 32.5 us
    pallas_call x15 -> x31, Pallas kernels: 203 us -> 213 us  [call(): pl.pallas_call(body, out_shape=out_shape, input_output_aliases=aliases, c...]
    convert_element_type x13, other arithmetic: 17.8 us -> 27.6 us  [the longest x10 23 us: added(): return sum((a.astype(F32) for a in addends)).astype(BF16)]
    ppermute x45 -> x38, starting transfers between devices: 34.6 us -> 27.7 us  [across(): return lax.ppermute(value, 'dp', [(i, i ^ bit) for i in range(count)])]
    ppermute x11 -> x8, starting transfers between devices: 17.1 us -> 10.7 us  [the longest x2 5.03 us: send_far(): up = lax.ppermute(farthest, 'mp', [(0, 1), (1, 2)])]
  transfers between devices with their start and end apart: 64 -> 55, of which waited for: 24 -> 12; matrix products, arithmetic and copies ran while one was open for 6% -> 13% of each run, Pallas kernels for 27% -> 44%
where the time goes in v4:
time: 497 us; the launch traced here: 490 us
  Pallas kernels  213 us (43%)
  waiting for transfers between devices  84.1 us (17%)
  other arithmetic  63.1 us (13%)
  starting transfers between devices  55.8 us (11%)
  local copies, waits for them, and re-layouts  40.6 us (8%)
  blocking collectives  30.7 us (6%)
    pallas_call x31, Pallas kernels, call(): pl.pallas_call(body, out_shape=out_shape, input_output_aliases=aliases, c...  213 us
    ppermute x38, waiting for transfers between devices, across(): return lax.ppermute(value, 'dp', [(i, i ^ bit) for i in range(count)])  40.5 us
    unnamed x188, local copies, waits for them, and re-layouts  32.5 us
    ppermute x2, waiting for transfers between devices, gather_far(): down = lax.ppermute(chunks[3], 'mp', [(1, 0), (2, 1)])  32.5 us
    ppermute x38, starting transfers between devices, across(): return lax.ppermute(value, 'dp', [(i, i ^ bit) for i in range(count)])  27.7 us
    convert_element_type x10, other arithmetic, added(): return sum((a.astype(F32) for a in addends)).astype(BF16)  23 us
    all_gather x1, blocking collectives, on_device(): norm_sums = lax.all_gather(norm_sums, 'mp').sum(axis=0)  20.9 us
    ppermute x9, starting transfers between devices, ring(): lax.ppermute(value, 'mp', [(i, (i + k) % parts) for i in range(parts)])  17.5 us
  transfers between devices with their start and end apart: 55, of which 12 were waited for; matrix products, arithmetic and copies ran while one was open for 13% of the time, Pallas kernels for 44%

profile of v4, /device:TPU:0, one launch (start us, length us, event | category | flops | bytes accessed | tf_op | source)
XLA Modules:
  0.0 489.9 jit_solution(6623882705936279451)
XLA Ops:
  2.9 2.6 collective-permute-start.1
  5.4 1.6 collective-permute-start.3
  7.1 1.6 collective-permute-start.2
  10.9 15.5 %collective-permute-done.1.refs_2_ = bf16[256,1792]{1,0:T(8,128)(2,1)S(1)} collective-permute-done((bf16[256,1792]{1,0:T(8,128)(2,1)S(1)}, bf16[256,1792]{1,0:T(8,128)(2,1)S(1)}, u32[]{:S(2)}, u32[]{:S(2)}) %collective-permute-start.1) | collective-permute-done | bytes 917536 | tf_op jit(solution)/shard_map/ppermute | solution.py:636
  26.4 6.1 %collective-permute-done.3.refs_4_ = bf16[256,2048]{1,0:T(8,128)(2,1)S(1)} collective-permute-done((bf16[256,2048]{1,0:T(8,128)(2,1)S(1)}, bf16[256,2048]{1,0:T(8,128)(2,1)S(1)}, u32[]{:S(2)}, u32[]{:S(2)}) %collective-permute-start.3) | collective-permute-done | bytes 1048608 | tf_op jit(solution)/shard_map/ppermute | solution.py:640
  34.5 1.7 collective-permute-start.7
  36.8 1.5 collective-permute-start.6
  39.3 18.5 %collective-permute-done.5.refs_3_ = bf16[256,1792]{1,0:T(8,128)(2,1)S(1)} collective-permute-done((bf16[256,1792]{1,0:T(8,128)(2,1)}, bf16[256,1792]{1,0:T(8,128)(2,1)S(1)}, u32[]{:S(2)}, u32[]{:S(2)}) %collective-permute-start.5) | collective-permute-done | bytes 917536 | tf_op jit(solution)/shard_map/ppermute | solution.py:636
  60.2 2.0 pad_maximum_fusion
  65.1 1.5 collective-permute-start.9
  66.6 24.4 %collective-permute-done.12 = bf16[256,2048]{1,0:T(8,128)(2,1)S(1)} collective-permute-done((bf16[256,2048]{1,0:T(8,128)(2,1)S(1)}, bf16[256,2048]{1,0:T(8,128)(2,1)S(1)}, u32[]{:S(2)}, u32[]{:S(2)}) %collective-permute-start.12) | collective-permute-done | bytes 1048608 | tf_op jit(solution)/shard_map/ppermute | solution.py:651
  94.6 2.7 collective-permute-start.16
  97.3 1.5 collective-permute-start.15
  100.7 19.7 %project.2 = (bf16[2048,768]{1,0:T(8,128)(2,1)}, bf16[2048,1024]{1,0:T(8,128)(2,1)}, bf16[2048,1024]{1,0:T(8,128)(2,1)}, bf16[2048,2048]{1,0:T(8,128)(2,1)}, bf16[2048,2048]{1,0:T(8,128)(2,1)}) custom-call(s32[1]{0:T(128)} %bitcast.refs_0_, f32[1,1792]{1,0:T(1,128)} %maximum_convert_fusion.refs_1_, f32[1,2048]{1,0:T(1,128)} %bitcast.110, ...), custom_call_target="tpu_custom_call" | custom-call | tf_op jit(solution)/shard_map/project/pallas_call | solution.py:42
  122.4 1.5 collective-permute-start.17
  124.3 1.5 collective-permute-start.21
  126.8 19.6 %project.3 = (bf16[2048,768]{1,0:T(8,128)(2,1)}, bf16[2048,1024]{1,0:T(8,128)(2,1)}, bf16[2048,1024]{1,0:T(8,128)(2,1)}, bf16[2048,2048]{1,0:T(8,128)(2,1)}, bf16[2048,2048]{1,0:T(8,128)(2,1)}) custom-call(s32[1]{0:T(128)} %bitcast.refs_0_, ...), custom_call_target="tpu_custom_call", output_to_operand_aliasing={{0}: (17, {}), {1}: (18, {}), {2}: (19, {}), {3}: (20, {}),... | custom-call | tf_op jit(solution)/shard_map/project/pallas_call | solution.py:42
  147.6 1.5 collective-permute-start.19
  149.3 14.9 %attend.1 = (bf16[2048,256]{1,0:T(8,128)(2,1)}, f32[4,8,1024]{2,1,0:T(8,128)}) custom-call(bf16[2048,768]{1,0:T(8,128)(2,1)} %get-tuple-element.188.refs_6_.refs_0_.refs_1_.refs_2_, bf16[2048,768]{1,0:T(8,128)(2,1)} %get-tuple-element.188.refs_6_.refs_0_.refs_1_.refs_2_, bf16[2048,768]{1,0:T(8,128)(2,1)} %get-tuple-element.188.refs_6_.refs_0_.refs_1_.refs_2_, ...), custom_call_target="tpu_custom_call" | custom-call | tf_op jit(solution)/shard_map/attend/pallas_call | solution.py:42
  167.4 3.7 pad_maximum_fusion.1.refs_11_
  173.1 18.9 %branch_sums.1 = (bf16[4,256,2048]{2,1,0:T(8,128)(2,1)}, bf16[4,256,2048]{2,1,0:T(8,128)(2,1)}) custom-call(s32[1]{0:T(128)} %bitcast.refs_0_, bf16[2048,256]{1,0:T(8,128)(2,1)} %get-tuple-element.193.refs_10_.refs_1_.refs_4_, bf16[2048,1024]{1,0:T(8,128)(2,1)} %get-tuple-element.194.refs_2_, bf16[1280,256]{1,0:T(8,128)(2,1)} %get-tuple-element.202.refs_3_.refs_6_.refs_8_, ...), custom_call_target="tpu_custom_call" | custom-call | tf_op jit(solution)/shard_map/branch_sums/pallas_call | solution.py:42
  192.0 8.1 %collective-permute-done.24 = bf16[256,2048]{1,0:T(8,128)(2,1)S(1)} collective-permute-done((bf16[256,2048]{1,0:T(8,128)(2,1)S(1)}, bf16[256,2048]{1,0:T(8,128)(2,1)S(1)}, u32[]{:S(2)}, u32[]{:S(2)}) %collective-permute-start.24) | collective-permute-done | bytes 1048608 | tf_op jit(solution)/shard_map/ppermute | solution.py:651
  201.5 1.7 copy-done.16
  203.7 13.2 %grad_in.2 = (bf16[2048,256]{1,0:T(8,128)(2,1)}, bf16[2048,1024]{1,0:T(8,128)(2,1)}, bf16[2048,2048]{1,0:T(8,128)(2,1)}, f32[8,1024]{1,0:T(8,128)}, f32[8,2048]{1,0:T(8,128)}) custom-call(s32[1]{0:T(128)} %bitcast.refs_0_, bf16[2048,1024]{1,0:T(8,128)(2,1)} %get-tuple-element.216.refs_1_, bf16[256,2048]{1,0:T(8,128)(2,1)} %get-tuple-element.201.refs_2_, ...), custom_call_target="tpu_custom_call" | custom-call | tf_op jit(solution)/shard_map/grad_in/pallas_call | solution.py:42
  217.0 2.1 copy-done.24
  219.4 2.2 copy-done.23
  221.6 1.6 fusion.19.refs_20_
  223.2 3.6 collective-permute-start.27
  228.2 13.1 %grad_in.3 = (bf16[2048,256]{1,0:T(8,128)(2,1)}, bf16[2048,1024]{1,0:T(8,128)(2,1)}, bf16[2048,2048]{1,0:T(8,128)(2,1)}, f32[8,1024]{1,0:T(8,128)}, f32[8,2048]{1,0:T(8,128)}) custom-call(s32[1]{0:T(128)} %bitcast.refs_0_, bf16[2048,1024]{1,0:T(8,128)(2,1)} %get-tuple-element.216.refs_1_, ...), custom_call_target="tpu_custom_call", output_to_operand_aliasing={{0}: (16, {}), {1}: (17, {}), {2}: (18, {})} | custom-call | tf_op jit(solution)/shard_map/grad_in/pallas_call | solution.py:42
  241.4 19.4 %weight_grads.3 = (bf16[2,1280,256]{2,1,0:T(8,128)(2,1)}, bf16[2,1280,256]{2,1,0:T(8,128)(2,1)}, bf16[1,1280,256]{2,1,0:T(8,128)(2,1)}, bf16[1,1280,256]{2,1,0:T...) custom-call(s32[8]{0:T(128)} %broadcast_xor_fusion.refs_0_, ...), custom_call_target="tpu_custom_call" | custom-call | tf_op jit(solution)/shard_map/weight_grads/pallas_call | solution.py:42
  260.7 1.5 collective-permute-start.31
  264.2 4.5 fusion.16
  270.9 25.2 %attend_back.1 = (bf16[2048,256]{1,0:T(8,128)(2,1)}, bf16[2048,256]{1,0:T(8,128)(2,1)}, bf16[2048,256]{1,0:T(8,128)(2,1)}, f32[4,8,128]{2,1,0:T(8,128)}) custom-call(bf16[2048,768]{1,0:T(8,128)(2,1)} %get-tuple-element.188.refs_6_.refs_0_.refs_1_.refs_2_, bf16[2048,768]{1,0:T(8,128)(2,1)} %get-tuple-element.188.refs_6_.refs_0_.refs_1_.refs_2_, ...), custom_call_target="tpu_custom_call" | custom-call | tf_op jit(solution)/shard_map/attend_back/pallas_call | solution.py:42
  297.1 3.7 collective-permute-start.30
  300.9 11.3 %grad_normed_sums.3 = (bf16[1,256,2048]{2,1,0:T(8,128)(2,1)}, bf16[1,256,2048]{2,1,0:T(8,128)(2,1)}, f32[8,2048]{1,0:T(8,128)}) custom-call(s32[1]{0:T(128)} %bitcast.refs_0_, bf16[2048,256]{1,0:T(8,128)(2,1)} %get-tuple-element.231.refs_2_.refs_1_, bf16[2048,256]{1,0:T(8,128)(2,1)} %get-tuple-element.234.refs_2_.refs_3_, ...), custom_call_target="tpu_custom_call" | custom-call | tf_op jit(solution)/shard_map/grad_normed_sums/pallas_call | solution.py:42
  313.2 2.1 add_convert_fusion.3.refs_16_
  318.0 2.1 add_convert_fusion.4.refs_15_
  320.0 1.4 collective-permute-start.33
  323.2 16.4 %grad_normed_sums.4 = (bf16[2,256,2048]{2,1,0:T(8,128)(2,1)}, bf16[2,256,2048]{2,1,0:T(8,128)(2,1)}, f32[8,2048]{1,0:T(8,128)}) custom-call(s32[1]{0:T(128)} %bitcast.refs_0_, bf16[2048,256]{1,0:T(8,128)(2,1)} %get-tuple-element.231.refs_2_.refs_1_, bf16[2048,256]{1,0:T(8,128)(2,1)} %get-tuple-element.234.refs_2_.refs_3_, ...), custom_call_target="tpu_custom_call" | custom-call | tf_op jit(solution)/shard_map/grad_normed_sums/pallas_call | solution.py:42
  342.9 1.6 fusion.20.refs_4_
  344.5 1.5 collective-permute-start.38
  346.8 2.2 fusion.21.refs_5_.refs_2_
  349.0 16.1 %weight_grads.4 = (bf16[2,256,1024]{2,1,0:T(8,128)(2,1)}, bf16[2,256,1024]{2,1,0:T(8,128)(2,1)}, bf16[1,256,1024]{2,1,0:T(8,128)(2,1)}, bf16[1,256,1024]{2,1,0:T...) custom-call(s32[8]{0:T(128)} %broadcast_xor_fusion.refs_0_, ...), custom_call_target="tpu_custom_call" | custom-call | tf_op jit(solution)/shard_map/weight_grads/pallas_call | solution.py:42
  365.1 11.2 %grad_normed_sums.5 = (bf16[1,256,2048]{2,1,0:T(8,128)(2,1)}, bf16[1,256,2048]{2,1,0:T(8,128)(2,1)}, f32[8,2048]{1,0:T(8,128)}) custom-call(s32[1]{0:T(128)} %bitcast.refs_0_, bf16[2048,256]{1,0:T(8,128)(2,1)} %get-tuple-element.231.refs_2_.refs_1_, bf16[2048,256]{1,0:T(8,128)(2,1)} %get-tuple-element.234.refs_2_.refs_3_, ...), custom_call_target="tpu_custom_call" | custom-call | tf_op jit(solution)/shard_map/grad_normed_sums/pallas_call | solution.py:42
  376.4 1.6 collective-permute-start.41
  378.9 1.7 convert_add_fusion.1
  384.4 5.6 %fusion.14 = (bf16[256,2048]{1,0:T(8,128)(2,1)}, bf16[256,2048]{1,0:T(8,128)(2,1)}) fusion(bf16[256,2048]{1,0:T(8,128)(2,1)} %get-tuple-element.267, bf16[2,256,2048]{2,1,0:T(8,128)(2,1)} %get-tuple-element.263, bf16[2,256,2048]{2,1,0:T(8,128)(2,1)} %get-tuple-element.256, bf16[256,2048]{1,0:T(8,128)(2,1)} %get-tuple-element.264), kind=kLoop, calls=%fused_computation.23 | loop fusion | flops 6291456 | bytes 8388608 | tf_op jit(solution)/shard_map/convert_element_type | solution.py:656
  390.0 2.7 collective-permute-start.40
  392.7 14.0 %weight_grads.5 = (bf16[2,256,768]{2,1,0:T(8,128)(2,1)}, bf16[2,256,768]{2,1,0:T(8,128)(2,1)}, bf16[1,256,768]{2,1,0:T(8,128)(2,1)}, bf16[1,256,768]{2,1,0:T(8,1...) custom-call(s32[8]{0:T(128)} %broadcast_xor_fusion.refs_0_, ...), custom_call_target="tpu_custom_call" | custom-call | tf_op jit(solution)/shard_map/weight_grads/pallas_call | solution.py:42
  406.8 9.8 %all-gather.2 = f32[8,1,7936]{2,1,0:T(1,128)S(1)} all-gather(f32[1,1,7936]{2,1,0:T(1,128)S(1)} %reshape.287), channel_id=2, replica_groups=mesh['dp'=8,'mp'=4] {'dp'}, dimensions={0}, use_global_device_ids=true | all-gather | bytes 285696 | tf_op jit(solution)/shard_map/all_gather | solution.py:951
  419.8 2.2 add_convert_fusion.6
  423.3 1.5 collective-permute-start.49
  426.8 1.6 maximum_select_fusion.1
  429.7 1.5 collective-permute-start.47
  432.8 2.4 fusion.28
  436.6 20.9 %all-gather.1 = f32[16384]{0:T(1024)S(1)} all-gather(f32[4096]{0:T(1024)S(1)} %copy-done.78), channel_id=3, replica_groups=mesh['dp'=8,'mp'=4] {'mp'}, dimensions={0}, use_global_device_ids=true | all-gather | bytes 81920 | tf_op jit(solution)/shard_map/all_gather | solution.py:982
  458.6 1.5 fusion.22
  463.1 1.6 collective-permute-start.51
  466.1 1.8 collective-permute-start.46
  468.0 4.9 %collective-permute-done.52 = bf16[1,256,768]{2,1,0:T(8,128)(2,1)S(1)} collective-permute-done((bf16[1,256,768]{2,1,0:T(8,128)(2,1)S(1)}, bf16[1,256,768]{2,1,0:T(8,128)(2,1)S(1)}, u32[]{:S(2)}, u32[]{:S(2)}) %collective-permute-start.52) | collective-permute-done | bytes 393248 | tf_op jit(solution)/shard_map/ppermute | solution.py:636
  475.6 1.7 maximum_select_fusion
  477.3 2.7 collective-permute-done.46
  480.1 2.6 fusion.26
  482.7 4.5 fusion.8
  (345 shorter events, 72.0 us)
Async XLA Ops:
  0.6 98.2 %copy-start = (bf16[3,512]{1,0:T(4,128)(2,1)S(1)}, bf16[3,512]{1,0:T(4,128)(2,1)}, u32[]{:S(2)}) copy-start(bf16[3,512]{1,0:T(4,128)(2,1)} %param.22) | copy-start | bytes 9220
  2.3 4.8 collective-permute-start
  2.9 23.6 %collective-permute-start.1 = (bf16[256,1792]{1,0:T(8,128)(2,1)S(1)}, bf16[256,1792]{1,0:T(8,128)(2,1)S(1)}, u32[]{:S(2)}, u32[]{:S(2)}) collective-permute-start(bf16[256,1792]{1,0:T(8,128)(2,1)S(1)} %pad_maximum_fusion.3.refs_0_), channel_id=1, source_target_pairs={{0,8},{4,12},{8,0},{12,4},{16,24},{20,28},{24,16},{28,20},{1,9},{5... | collective-permute-start | bytes 2752520 | tf_op jit(solution)/shard_map/ppermute | solution.py:636
  5.4 27.1 %collective-permute-start.3 = (bf16[256,2048]{1,0:T(8,128)(2,1)S(1)}, bf16[256,2048]{1,0:T(8,128)(2,1)S(1)}, u32[]{:S(2)}, u32[]{:S(2)}) collective-permute-start(bf16[256,2048]{1,0:T(8,128)(2,1)S(1)} %copy-done.9), channel_id=1, source_target_pairs={{0,1},{1,2},{2,3},{3,0},{4,5},{5,6},{6,7},{7,4},{8,9},{9,10},{10,1... | collective-permute-start | bytes 3145736 | tf_op jit(solution)/shard_map/ppermute | solution.py:640
  7.1 25.5 %collective-permute-start.2 = (bf16[256,1792]{1,0:T(8,128)(2,1)S(1)}, bf16[256,1792]{1,0:T(8,128)(2,1)S(1)}, u32[]{:S(2)}, u32[]{:S(2)}) collective-permute-start(bf16[256,1792]{1,0:T(8,128)(2,1)S(1)} %collective-permute-done.refs_1_), channel_id=1, source_target_pairs={{0,16},{4,20},{8,24},{12,28},{16,0},{20,4},{24,8},{28,12},{1,17},{... | collective-permute-start | bytes 2752520 | tf_op jit(solution)/shard_map/ppermute | solution.py:636
  8.8 2.2 collective-permute-start.4
  10.7 27.6 %copy-start.52 = (bf16[256,2048]{1,0:T(8,128)(2,1)S(1)}, bf16[256,2048]{1,0:T(8,128)(2,1)}, u32[]{:S(2)}) copy-start(bf16[256,2048]{1,0:T(8,128)(2,1)} %param.29) | copy-start | bytes 3145732
  10.9 21.6 %copy-start.13 = (bf16[1280,256]{1,0:T(8,128)(2,1)}, bf16[1280,256]{1,0:T(8,128)(2,1)S(1)}, u32[]{:S(2)}) copy-start(bf16[1280,256]{1,0:T(8,128)(2,1)S(1)} %collective-permute-done.4.refs_7_.refs_10_) | copy-start | bytes 1966084
  34.5 24.7 %collective-permute-start.7 = (bf16[256,2048]{1,0:T(8,128)(2,1)}, bf16[256,2048]{1,0:T(8,128)(2,1)S(1)}, u32[]{:S(2)}, u32[]{:S(2)}) collective-permute-start(bf16[256,2048]{1,0:T(8,128)(2,1)} %get-tuple-element.160), channel_id=1, source_target_pairs={{0,3},{1,0},{2,1},{3,2},{4,7},{5,4},{6,5},{7,6},{8,11},{9,8},{10,9... | collective-permute-start | bytes 3145736 | tf_op jit(solution)/shard_map/ppermute | solution.py:640
  36.2 21.6 %collective-permute-start.5 = (bf16[256,1792]{1,0:T(8,128)(2,1)}, bf16[256,1792]{1,0:T(8,128)(2,1)S(1)}, u32[]{:S(2)}, u32[]{:S(2)}) collective-permute-start(bf16[256,1792]{1,0:T(8,128)(2,1)} %get-tuple-element.156.refs_1_), channel_id=1, source_target_pairs={{0,8},{4,12},{8,0},{12,4},{16,24},{20,28},{24,16},{28,20},{1,9},{5... | collective-permute-start | bytes 2752520 | tf_op jit(solution)/shard_map/ppermute | solution.py:636
  36.8 21.0 %collective-permute-start.6 = (bf16[256,1792]{1,0:T(8,128)(2,1)}, bf16[256,1792]{1,0:T(8,128)(2,1)S(1)}, u32[]{:S(2)}, u32[]{:S(2)}) collective-permute-start(bf16[256,1792]{1,0:T(8,128)(2,1)} %get-tuple-element.155.refs_0_), channel_id=1, source_target_pairs={{0,16},{4,20},{8,24},{12,28},{16,0},{20,4},{24,8},{28,12},{1,17},{... | collective-permute-start | bytes 2752520 | tf_op jit(solution)/shard_map/ppermute | solution.py:636
  62.2 30.1 %collective-permute-start.8 = (bf16[3,256,2048]{2,1,0:T(8,128)(2,1)S(1)}, bf16[3,256,2048]{2,1,0:T(8,128)(2,1)S(1)}, u32[]{:S(2)}, u32[]{:S(2)}) collective-permute-start(bf16[3,256,2048]{2,1,0:T(8,128)(2,1)S(1)} %pad_maximum_fusion), channel_id=1, source_target_pairs={{0,4},{4,0},{8,12},{12,8},{16,20},{20,16},{24,28},{28,24},{1,5},{5... | collective-permute-start | bytes 9437192 | tf_op jit(solution)/shard_map/ppermute | solution.py:636
  62.3 4.3 collective-permute-start.11
  63.1 27.9 %collective-permute-start.12 = (bf16[256,2048]{1,0:T(8,128)(2,1)S(1)}, bf16[256,2048]{1,0:T(8,128)(2,1)S(1)}, u32[]{:S(2)}, u32[]{:S(2)}) collective-permute-start(bf16[256,2048]{1,0:T(8,128)(2,1)S(1)} %copy-done.33), channel_id=1, source_target_pairs={{1,0},{2,1},{5,4},{6,5},{9,8},{10,9},{13,12},{14,13},{17,16},{18,1... | collective-permute-start | bytes 3145736 | tf_op jit(solution)/shard_map/ppermute | solution.py:651
  64.4 27.9 %collective-permute-start.10 = (bf16[256,1792]{1,0:T(8,128)(2,1)S(1)}, bf16[256,1792]{1,0:T(8,128)(2,1)S(1)}, u32[]{:S(2)}, u32[]{:S(2)}) collective-permute-start(bf16[256,1792]{1,0:T(8,128)(2,1)S(1)} %copy-done.8), channel_id=1, source_target_pairs={{0,8},{4,12},{8,0},{12,4},{16,24},{20,28},{24,16},{28,20},{1,9},{5... | collective-permute-start | bytes 2752520 | tf_op jit(solution)/shard_map/ppermute | solution.py:636
  65.1 27.2 %collective-permute-start.9 = (bf16[256,1792]{1,0:T(8,128)(2,1)S(1)}, bf16[256,1792]{1,0:T(8,128)(2,1)S(1)}, u32[]{:S(2)}, u32[]{:S(2)}) collective-permute-start(bf16[256,1792]{1,0:T(8,128)(2,1)S(1)} %copy-done.6), channel_id=1, source_target_pairs={{0,16},{4,20},{8,24},{12,28},{16,0},{20,4},{24,8},{28,12},{1,17},{... | collective-permute-start | bytes 2752520 | tf_op jit(solution)/shard_map/ppermute | solution.py:636
  94.6 26.8 %collective-permute-start.16 = (bf16[256,2048]{1,0:T(8,128)(2,1)}, bf16[256,2048]{1,0:T(8,128)(2,1)S(1)}, u32[]{:S(2)}, u32[]{:S(2)}) collective-permute-start(bf16[256,2048]{1,0:T(8,128)(2,1)} %get-tuple-element.179.refs_19_.refs_4_), channel_id=1, source_target_pairs={{0,1},{1,2},{2,3},{3,0},{4,5},{5,6},{6,7},{7,4},{8,9},{9,10},{10,1... | collective-permute-start | bytes 3145736 | tf_op jit(solution)/shard_map/ppermute | solution.py:640
  97.3 23.1 %collective-permute-start.14 = (bf16[1280,256]{1,0:T(8,128)(2,1)}, bf16[1280,256]{1,0:T(8,128)(2,1)S(1)}, u32[]{:S(2)}, u32[]{:S(2)}) collective-permute-start(bf16[1280,256]{1,0:T(8,128)(2,1)} %get-tuple-element.185.refs_0_), channel_id=1, source_target_pairs={{0,8},{4,12},{8,0},{12,4},{16,24},{20,28},{24,16},{28,20},{1,9},{5... | collective-permute-start | bytes 1966088 | tf_op jit(solution)/shard_map/ppermute | solution.py:636
  97.3 23.1 %collective-permute-start.15 = (bf16[1280,256]{1,0:T(8,128)(2,1)}, bf16[1280,256]{1,0:T(8,128)(2,1)S(1)}, u32[]{:S(2)}, u32[]{:S(2)}) collective-permute-start(bf16[1280,256]{1,0:T(8,128)(2,1)} %get-tuple-element.186.refs_1_), channel_id=1, source_target_pairs={{0,16},{4,20},{8,24},{12,28},{16,0},{20,4},{24,8},{28,12},{1,17},{... | collective-permute-start | bytes 1966088 | tf_op jit(solution)/shard_map/ppermute | solution.py:636
  98.8 27.0 %collective-permute-start.13 = (bf16[256,2048]{1,0:T(8,128)(2,1)}, bf16[256,2048]{1,0:T(8,128)(2,1)S(1)}, u32[]{:S(2)}, u32[]{:S(2)}) collective-permute-start(bf16[256,2048]{1,0:T(8,128)(2,1)} %get-tuple-element.170.refs_10_), channel_id=1, source_target_pairs={{0,4},{4,0},{8,12},{12,8},{16,20},{20,16},{24,28},{28,24},{1,5},{5... | collective-permute-start | bytes 3145736 | tf_op jit(solution)/shard_map/ppermute | solution.py:636
  122.4 24.1 %collective-permute-start.17 = (bf16[1280,256]{1,0:T(8,128)(2,1)}, bf16[1280,256]{1,0:T(8,128)(2,1)S(1)}, u32[]{:S(2)}, u32[]{:S(2)}) collective-permute-start(bf16[1280,256]{1,0:T(8,128)(2,1)} %get-tuple-element.189.refs_1_), channel_id=1, source_target_pairs={{0,8},{4,12},{8,0},{12,4},{16,24},{20,28},{24,16},{28,20},{1,9},{5... | collective-permute-start | bytes 1966088 | tf_op jit(solution)/shard_map/ppermute | solution.py:636
  123.8 22.6 %collective-permute-start.18 = (bf16[1280,256]{1,0:T(8,128)(2,1)}, bf16[1280,256]{1,0:T(8,128)(2,1)S(1)}, u32[]{:S(2)}, u32[]{:S(2)}) collective-permute-start(bf16[1280,256]{1,0:T(8,128)(2,1)} %get-tuple-element.187.refs_22_.refs_0_), channel_id=1, source_target_pairs={{0,16},{4,20},{8,24},{12,28},{16,0},{20,4},{24,8},{28,12},{1,17},{... | collective-permute-start | bytes 1966088 | tf_op jit(solution)/shard_map/ppermute | solution.py:636
  124.3 39.9 %collective-permute-start.21 = (bf16[256,2048]{1,0:T(8,128)(2,1)}, bf16[256,2048]{1,0:T(8,128)(2,1)S(1)}, u32[]{:S(2)}, u32[]{:S(2)}) collective-permute-start(bf16[256,2048]{1,0:T(8,128)(2,1)} %get-tuple-element.201.refs_2_), channel_id=1, source_target_pairs={{0,3},{1,0},{2,1},{3,2},{4,7},{5,4},{6,5},{7,6},{8,11},{9,8},{10,9... | collective-permute-start | bytes 3145736 | tf_op jit(solution)/shard_map/ppermute | solution.py:640
  147.6 16.7 %collective-permute-start.19 = (bf16[1280,256]{1,0:T(8,128)(2,1)}, bf16[1280,256]{1,0:T(8,128)(2,1)S(1)}, u32[]{:S(2)}, u32[]{:S(2)}) collective-permute-start(bf16[1280,256]{1,0:T(8,128)(2,1)} %get-tuple-element.196.refs_2_), channel_id=1, source_target_pairs={{0,16},{4,20},{8,24},{12,28},{16,0},{20,4},{24,8},{28,12},{1,17},{... | collective-permute-start | bytes 1966088 | tf_op jit(solution)/shard_map/ppermute | solution.py:636
  149.1 16.2 %collective-permute-start.20 = (bf16[1280,256]{1,0:T(8,128)(2,1)}, bf16[1280,256]{1,0:T(8,128)(2,1)S(1)}, u32[]{:S(2)}, u32[]{:S(2)}) collective-permute-start(bf16[1280,256]{1,0:T(8,128)(2,1)} %get-tuple-element.199.refs_5_), channel_id=1, source_target_pairs={{0,8},{4,12},{8,0},{12,4},{16,24},{20,28},{24,16},{28,20},{1,9},{5... | collective-permute-start | bytes 1966088 | tf_op jit(solution)/shard_map/ppermute | solution.py:636
  171.1 30.4 %collective-permute-start.22 = (bf16[3,256,2048]{2,1,0:T(8,128)(2,1)}, bf16[3,256,2048]{2,1,0:T(8,128)(2,1)S(1)}, u32[]{:S(2)}, u32[]{:S(2)}) collective-permute-start(bf16[3,256,2048]{2,1,0:T(8,128)(2,1)} %pad_maximum_fusion.1.refs_11_), channel_id=1, source_target_pairs={{0,4},{4,0},{8,12},{12,8},{16,20},{20,16},{24,28},{28,24},{1,5},{5... | collective-permute-start | bytes 9437192 | tf_op jit(solution)/shard_map/ppermute | solution.py:636
  171.1 20.9 %collective-permute-start.23 = (bf16[256,2048]{1,0:T(8,128)(2,1)S(1)}, bf16[256,2048]{1,0:T(8,128)(2,1)S(1)}, u32[]{:S(2)}, u32[]{:S(2)}) collective-permute-start(bf16[256,2048]{1,0:T(8,128)(2,1)S(1)} %copy-done.18), channel_id=1, source_target_pairs={{1,2},{2,3},{5,6},{6,7},{9,10},{10,11},{13,14},{14,15},{17,18},{18... | collective-permute-start | bytes 3145736 | tf_op jit(solution)/shard_map/ppermute | solution.py:650
  171.8 28.3 %collective-permute-start.24 = (bf16[256,2048]{1,0:T(8,128)(2,1)S(1)}, bf16[256,2048]{1,0:T(8,128)(2,1)S(1)}, u32[]{:S(2)}, u32[]{:S(2)}) collective-permute-start(bf16[256,2048]{1,0:T(8,128)(2,1)S(1)} %copy-done.26), channel_id=1, source_target_pairs={{1,0},{2,1},{5,4},{6,5},{9,8},{10,9},{13,12},{14,13},{17,16},{18,1... | collective-permute-start | bytes 3145736 | tf_op jit(solution)/shard_map/ppermute | solution.py:651
  203.2 13.8 %collective-permute-start.25 = (bf16[4,256,2048]{2,1,0:T(8,128)(2,1)}, bf16[4,256,2048]{2,1,0:T(8,128)(2,1)S(1)}, u32[]{:S(2)}, u32[]{:S(2)}) collective-permute-start(bf16[4,256,2048]{2,1,0:T(8,128)(2,1)} %get-tuple-element.214.refs_14_), channel_id=1, source_target_pairs={{0,4},{4,0},{8,12},{12,8},{16,20},{20,16},{24,28},{28,24},{1,5},{5... | collective-permute-start | bytes 12582920 | tf_op jit(solution)/shard_map/ppermute | solution.py:636
  203.2 13.7 %collective-permute-start.26 = (bf16[256,2048]{1,0:T(8,128)(2,1)}, bf16[256,2048]{1,0:T(8,128)(2,1)S(1)}, u32[]{:S(2)}, u32[]{:S(2)}) collective-permute-start(bf16[256,2048]{1,0:T(8,128)(2,1)} %get-tuple-element.215.refs_5_), channel_id=1, source_target_pairs={{0,4},{4,0},{8,12},{12,8},{16,20},{20,16},{24,28},{28,24},{1,5},{5... | collective-permute-start | bytes 3145736 | tf_op jit(solution)/shard_map/ppermute | solution.py:636
  219.4 8.3 %copy-start.88 = (s32[8]{0:T(128)S(1)}, s32[8]{0:T(128)}, u32[]{:S(2)}) copy-start(s32[8]{0:T(128)} %constant.53.clone) | copy-start | bytes 100
  223.2 39.0 %collective-permute-start.27 = (bf16[256,2048]{1,0:T(8,128)(2,1)S(1)}, bf16[256,2048]{1,0:T(8,128)(2,1)S(1)}, u32[]{:S(2)}, u32[]{:S(2)}) collective-permute-start(bf16[256,2048]{1,0:T(8,128)(2,1)S(1)} %fusion.19.refs_20_), channel_id=1, source_target_pairs={{0,1},{1,2},{4,5},{5,6},{8,9},{9,10},{12,13},{13,14},{16,17},{17,1... | collective-permute-start | bytes 3145736 | tf_op jit(solution)/shard_map/ppermute | solution.py:660
  226.8 35.5 %collective-permute-start.28 = (bf16[256,2048]{1,0:T(8,128)(2,1)S(1)}, bf16[256,2048]{1,0:T(8,128)(2,1)S(1)}, u32[]{:S(2)}, u32[]{:S(2)}) collective-permute-start(bf16[256,2048]{1,0:T(8,128)(2,1)S(1)} %fusion.19.refs_20_), channel_id=1, source_target_pairs={{3,2},{2,1},{7,6},{6,5},{11,10},{10,9},{15,14},{14,13},{19,18},{18... | collective-permute-start | bytes 3145736 | tf_op jit(solution)/shard_map/ppermute | solution.py:661
  260.7 51.4 %collective-permute-start.31 = (bf16[2,1280,256]{2,1,0:T(8,128)(2,1)}, bf16[2,1280,256]{2,1,0:T(8,128)(2,1)}, u32[]{:S(2)}, u32[]{:S(2)}) collective-permute-start(bf16[2,1280,256]{2,1,0:T(8,128)(2,1)} %get-tuple-element.226.refs_2_.refs_9_), channel_id=1, source_target_pairs={{0,16},{4,20},{8,24},{12,28},{16,0},{20,4},{24,8},{28,12},{1,17},{... | collective-permute-start | bytes 3932168 | tf_op jit(solution)/shard_map/ppermute | solution.py:636
  262.2 49.9 %collective-permute-start.32 = (bf16[2,1280,256]{2,1,0:T(8,128)(2,1)}, bf16[2,1280,256]{2,1,0:T(8,128)(2,1)}, u32[]{:S(2)}, u32[]{:S(2)}) collective-permute-start(bf16[2,1280,256]{2,1,0:T(8,128)(2,1)} %get-tuple-element.240), channel_id=1, source_target_pairs={{0,8},{4,12},{8,0},{12,4},{16,24},{20,28},{24,16},{28,20},{1,9},{5... | collective-permute-start | bytes 3932168 | tf_op jit(solution)/shard_map/ppermute | solution.py:636
  268.7 27.4 %collective-permute-start.29 = (bf16[256,2048]{1,0:T(8,128)(2,1)S(1)}, bf16[256,2048]{1,0:T(8,128)(2,1)S(1)}, u32[]{:S(2)}, u32[]{:S(2)}) collective-permute-start(bf16[256,2048]{1,0:T(8,128)(2,1)S(1)} %get-tuple-element.304.refs_10_), channel_id=1, source_target_pairs={{0,1},{1,2},{2,3},{3,0},{4,5},{5,6},{6,7},{7,4},{8,9},{9,10},{10,1... | collective-permute-start | bytes 3145736 | tf_op jit(solution)/shard_map/ppermute | solution.py:640
  297.1 42.5 %collective-permute-start.30 = (bf16[256,2048]{1,0:T(8,128)(2,1)}, bf16[256,2048]{1,0:T(8,128)(2,1)S(1)}, u32[]{:S(2)}, u32[]{:S(2)}) collective-permute-start(bf16[256,2048]{1,0:T(8,128)(2,1)} %get-tuple-element.233), channel_id=1, source_target_pairs={{0,3},{1,0},{2,1},{3,2},{4,7},{5,4},{6,5},{7,6},{8,11},{9,8},{10,9... | collective-permute-start | bytes 3145736 | tf_op jit(solution)/shard_map/ppermute | solution.py:640
  315.3 25.3 %collective-permute-start.34 = (bf16[1,1280,256]{2,1,0:T(8,128)(2,1)}, bf16[1,1280,256]{2,1,0:T(8,128)(2,1)S(1)}, u32[]{:S(2)}, u32[]{:S(2)}) collective-permute-start(bf16[1,1280,256]{2,1,0:T(8,128)(2,1)} %add_convert_fusion.3.refs_16_), channel_id=1, source_target_pairs={{0,16},{4,20},{8,24},{12,28},{16,0},{20,4},{24,8},{28,12},{1,17},{... | collective-permute-start | bytes 1966088 | tf_op jit(solution)/shard_map/ppermute | solution.py:636
  317.4 23.2 %collective-permute-start.35 = (bf16[1,128,2048]{2,1,0:T(8,128)(2,1)}, bf16[1,128,2048]{2,1,0:T(8,128)(2,1)}, u32[]{:S(2)}, u32[]{:S(2)}) collective-permute-start(bf16[1,128,2048]{2,1,0:T(8,128)(2,1)} %get-tuple-element.312), channel_id=1, source_target_pairs={{0,4},{4,0},{8,12},{12,8},{16,20},{20,16},{24,28},{28,24},{1,5},{5... | collective-permute-start | bytes 1572872 | tf_op jit(solution)/shard_map/ppermute | solution.py:636
  317.4 23.2 %collective-permute-start.36 = (bf16[1,128,2048]{2,1,0:T(8,128)(2,1)}, bf16[1,128,2048]{2,1,0:T(8,128)(2,1)}, u32[]{:S(2)}, u32[]{:S(2)}) collective-permute-start(bf16[1,128,2048]{2,1,0:T(8,128)(2,1)} %get-tuple-element.311), channel_id=1, source_target_pairs={{0,4},{4,0},{8,12},{12,8},{16,20},{20,16},{24,28},{28,24},{1,5},{5... | collective-permute-start | bytes 1572872 | tf_op jit(solution)/shard_map/ppermute | solution.py:636
  320.0 20.6 %collective-permute-start.33 = (bf16[1,1280,256]{2,1,0:T(8,128)(2,1)}, bf16[1,1280,256]{2,1,0:T(8,128)(2,1)S(1)}, u32[]{:S(2)}, u32[]{:S(2)}) collective-permute-start(bf16[1,1280,256]{2,1,0:T(8,128)(2,1)} %add_convert_fusion.4.refs_15_), channel_id=1, source_target_pairs={{0,8},{4,12},{8,0},{12,4},{16,24},{20,28},{24,16},{28,20},{1,9},{5... | collective-permute-start | bytes 1966088 | tf_op jit(solution)/shard_map/ppermute | solution.py:636
  341.7 40.7 %collective-permute-start.37 = (bf16[2,256,2048]{2,1,0:T(8,128)(2,1)}, bf16[2,256,2048]{2,1,0:T(8,128)(2,1)S(1)}, u32[]{:S(2)}, u32[]{:S(2)}) collective-permute-start(bf16[2,256,2048]{2,1,0:T(8,128)(2,1)} %get-tuple-element.257), channel_id=1, source_target_pairs={{0,4},{4,0},{8,12},{12,8},{16,20},{20,16},{24,28},{28,24},{1,5},{5... | collective-permute-start | bytes 6291464 | tf_op jit(solution)/shard_map/ppermute | solution.py:636
  344.5 37.8 %collective-permute-start.38 = (bf16[256,2048]{1,0:T(8,128)(2,1)S(1)}, bf16[256,2048]{1,0:T(8,128)(2,1)S(1)}, u32[]{:S(2)}, u32[]{:S(2)}) collective-permute-start(bf16[256,2048]{1,0:T(8,128)(2,1)S(1)} %fusion.20.refs_4_), channel_id=1, source_target_pairs={{0,1},{1,2},{4,5},{5,6},{8,9},{9,10},{12,13},{13,14},{16,17},{17,1... | collective-permute-start | bytes 3145736 | tf_op jit(solution)/shard_map/ppermute | solution.py:660
  346.0 36.4 %collective-permute-start.39 = (bf16[256,2048]{1,0:T(8,128)(2,1)S(1)}, bf16[256,2048]{1,0:T(8,128)(2,1)S(1)}, u32[]{:S(2)}, u32[]{:S(2)}) collective-permute-start(bf16[256,2048]{1,0:T(8,128)(2,1)S(1)} %fusion.20.refs_4_), channel_id=1, source_target_pairs={{3,2},{2,1},{7,6},{6,5},{11,10},{10,9},{15,14},{14,13},{19,18},{18... | collective-permute-start | bytes 3145736 | tf_op jit(solution)/shard_map/ppermute | solution.py:661
  376.4 40.9 %collective-permute-start.41 = (bf16[2,256,1024]{2,1,0:T(8,128)(2,1)}, bf16[2,256,1024]{2,1,0:T(8,128)(2,1)S(1)}, u32[]{:S(2)}, u32[]{:S(2)}) collective-permute-start(bf16[2,256,1024]{2,1,0:T(8,128)(2,1)} %get-tuple-element.254.refs_14_), channel_id=1, source_target_pairs={{0,16},{4,20},{8,24},{12,28},{16,0},{20,4},{24,8},{28,12},{1,17},{... | collective-permute-start | bytes 3145736 | tf_op jit(solution)/shard_map/ppermute | solution.py:636
  378.9 38.4 %collective-permute-start.42 = (bf16[2,256,1024]{2,1,0:T(8,128)(2,1)}, bf16[2,256,1024]{2,1,0:T(8,128)(2,1)}, u32[]{:S(2)}, u32[]{:S(2)}) collective-permute-start(bf16[2,256,1024]{2,1,0:T(8,128)(2,1)} %get-tuple-element.266), channel_id=1, source_target_pairs={{0,8},{4,12},{8,0},{12,4},{16,24},{20,28},{24,16},{28,20},{1,9},{5... | collective-permute-start | bytes 3145736 | tf_op jit(solution)/shard_map/ppermute | solution.py:636
  384.4 32.9 %collective-permute-start.43 = (bf16[1280,256]{1,0:T(8,128)(2,1)}, bf16[1280,256]{1,0:T(8,128)(2,1)S(1)}, u32[]{:S(2)}, u32[]{:S(2)}) collective-permute-start(bf16[1280,256]{1,0:T(8,128)(2,1)} %get-tuple-element.270), channel_id=1, source_target_pairs={{0,4},{4,0},{8,12},{12,8},{16,20},{20,16},{24,28},{28,24},{1,5},{5... | collective-permute-start | bytes 1966088 | tf_op jit(solution)/shard_map/ppermute | solution.py:636
  390.0 41.8 %collective-permute-start.40 = (bf16[256,2048]{1,0:T(8,128)(2,1)}, bf16[256,2048]{1,0:T(8,128)(2,1)S(1)}, u32[]{:S(2)}, u32[]{:S(2)}) collective-permute-start(bf16[256,2048]{1,0:T(8,128)(2,1)} %get-tuple-element.306.refs_6_), channel_id=1, source_target_pairs={{0,1},{1,2},{2,3},{3,0},{4,5},{5,6},{6,7},{7,4},{8,9},{9,10},{10,1... | collective-permute-start | bytes 3145736 | tf_op jit(solution)/shard_map/ppermute | solution.py:640
  392.7 14.0 %copy-start.76 = (f32[7936]{0:T(1024)S(1)}, f32[7936]{0:T(1024)}, u32[]{:S(2)}) copy-start(f32[7936]{0:T(1024)} %get-tuple-element.271) | copy-start | bytes 95236
  422.8 66.1 %copy-start.80 = (f32[1,2048]{1,0:T(1,128)}, f32[1,2048]{1,0:T(1,128)S(1)}, u32[]{:S(2)}) copy-start(f32[1,2048]{1,0:T(1,128)S(1)} %slice.258) | copy-start | bytes 24580
  422.8 35.4 %collective-permute-start.48 = (bf16[1,256,1024]{2,1,0:T(8,128)(2,1)}, bf16[1,256,1024]{2,1,0:T(8,128)(2,1)}, u32[]{:S(2)}, u32[]{:S(2)}) collective-permute-start(bf16[1,256,1024]{2,1,0:T(8,128)(2,1)} %add_convert_fusion.6), channel_id=1, source_target_pairs={{0,16},{4,20},{8,24},{12,28},{16,0},{20,4},{24,8},{28,12},{1,17},{... | collective-permute-start | bytes 1572872 | tf_op jit(solution)/shard_map/ppermute | solution.py:636
  423.3 34.9 %collective-permute-start.49 = (bf16[2,256,768]{2,1,0:T(8,128)(2,1)}, bf16[2,256,768]{2,1,0:T(8,128)(2,1)}, u32[]{:S(2)}, u32[]{:S(2)}) collective-permute-start(bf16[2,256,768]{2,1,0:T(8,128)(2,1)} %get-tuple-element.273.refs_4_), channel_id=1, source_target_pairs={{0,16},{4,20},{8,24},{12,28},{16,0},{20,4},{24,8},{28,12},{1,17},{... | collective-permute-start | bytes 2359304 | tf_op jit(solution)/shard_map/ppermute | solution.py:636
  424.9 33.3 %collective-permute-start.50 = (bf16[2,256,768]{2,1,0:T(8,128)(2,1)}, bf16[2,256,768]{2,1,0:T(8,128)(2,1)}, u32[]{:S(2)}, u32[]{:S(2)}) collective-permute-start(bf16[2,256,768]{2,1,0:T(8,128)(2,1)} %get-tuple-element.285), channel_id=1, source_target_pairs={{0,8},{4,12},{8,0},{12,4},{16,24},{20,28},{24,16},{28,20},{1,9},{5... | collective-permute-start | bytes 2359304 | tf_op jit(solution)/shard_map/ppermute | solution.py:636
  429.7 28.5 %collective-permute-start.47 = (bf16[1,256,1024]{2,1,0:T(8,128)(2,1)}, bf16[1,256,1024]{2,1,0:T(8,128)(2,1)}, u32[]{:S(2)}, u32[]{:S(2)}) collective-permute-start(bf16[1,256,1024]{2,1,0:T(8,128)(2,1)} %add_convert_fusion.7), channel_id=1, source_target_pairs={{0,8},{4,12},{8,0},{12,4},{16,24},{20,28},{24,16},{28,20},{1,9},{5... | collective-permute-start | bytes 1572872 | tf_op jit(solution)/shard_map/ppermute | solution.py:636
  432.8 25.3 %copy-start.50 = (bf16[1,256,2048]{2,1,0:T(8,128)(2,1)S(1)}, bf16[1,256,2048]{2,1,0:T(8,128)(2,1)}, u32[]{:S(2)}) copy-start(bf16[1,256,2048]{2,1,0:T(8,128)(2,1)} %get-tuple-element.274) | copy-start | bytes 3145732
  435.2 30.9 %collective-permute-start.45 = (bf16[128,2048]{1,0:T(8,128)(2,1)}, bf16[128,2048]{1,0:T(8,128)(2,1)}, u32[]{:S(2)}, u32[]{:S(2)}) collective-permute-start(bf16[128,2048]{1,0:T(8,128)(2,1)} %get-tuple-element.310), channel_id=1, source_target_pairs={{0,3},{1,0},{2,1},{3,2},{4,7},{5,4},{6,5},{7,6},{8,11},{9,8},{10,9... | collective-permute-start | bytes 1572872 | tf_op jit(solution)/shard_map/ppermute | solution.py:640
  458.2 21.8 %collective-permute-start.44 = (bf16[1,256,2048]{2,1,0:T(8,128)(2,1)S(1)}, bf16[1,256,2048]{2,1,0:T(8,128)(2,1)}, u32[]{:S(2)}, u32[]{:S(2)}) collective-permute-start(bf16[1,256,2048]{2,1,0:T(8,128)(2,1)S(1)} %copy-done.50), channel_id=1, source_target_pairs={{0,4},{4,0},{8,12},{12,8},{16,20},{20,16},{24,28},{28,24},{1,5},{5... | collective-permute-start | bytes 3145736 | tf_op jit(solution)/shard_map/ppermute | solution.py:636
  460.1 15.3 %collective-permute-start.54 = (bf16[256,1024]{1,0:T(8,128)(2,1)S(1)}, bf16[256,1024]{1,0:T(8,128)(2,1)S(1)}, u32[]{:S(2)}, u32[]{:S(2)}) collective-permute-start(bf16[256,1024]{1,0:T(8,128)(2,1)S(1)} %fusion.22), channel_id=1, source_target_pairs={{0,4},{4,0},{8,12},{12,8},{16,20},{20,16},{24,28},{28,24},{1,5},{5... | collective-permute-start | bytes 1572872 | tf_op jit(solution)/shard_map/ppermute | solution.py:636
  461.5 11.4 %collective-permute-start.52 = (bf16[1,256,768]{2,1,0:T(8,128)(2,1)S(1)}, bf16[1,256,768]{2,1,0:T(8,128)(2,1)S(1)}, u32[]{:S(2)}, u32[]{:S(2)}) collective-permute-start(bf16[1,256,768]{2,1,0:T(8,128)(2,1)S(1)} %add_convert_fusion.9), channel_id=1, source_target_pairs={{0,16},{4,20},{8,24},{12,28},{16,0},{20,4},{24,8},{28,12},{1,17},{... | collective-permute-start | bytes 1179656 | tf_op jit(solution)/shard_map/ppermute | solution.py:636
  463.1 9.8 %copy-start.72 = (bf16[1,256,768]{2,1,0:T(8,128)(2,1)S(1)}, bf16[1,256,768]{2,1,0:T(8,128)(2,1)}, u32[]{:S(2)}) copy-start(bf16[1,256,768]{2,1,0:T(8,128)(2,1)} %get-tuple-element.288) | copy-start | bytes 1179652
  463.1 11.1 %collective-permute-start.51 = (bf16[1,256,768]{2,1,0:T(8,128)(2,1)S(1)}, bf16[1,256,768]{2,1,0:T(8,128)(2,1)S(1)}, u32[]{:S(2)}, u32[]{:S(2)}) collective-permute-start(bf16[1,256,768]{2,1,0:T(8,128)(2,1)S(1)} %add_convert_fusion.10), channel_id=1, source_target_pairs={{0,8},{4,12},{8,0},{12,4},{16,24},{20,28},{24,16},{28,20},{1,9},{5... | collective-permute-start | bytes 1179656 | tf_op jit(solution)/shard_map/ppermute | solution.py:636
  464.8 9.5 %copy-start.75 = (bf16[1,256,768]{2,1,0:T(8,128)(2,1)S(1)}, bf16[1,256,768]{2,1,0:T(8,128)(2,1)}, u32[]{:S(2)}) copy-start(bf16[1,256,768]{2,1,0:T(8,128)(2,1)} %get-tuple-element.280) | copy-start | bytes 1179652
  466.1 13.9 %collective-permute-start.46 = (bf16[128,2048]{1,0:T(8,128)(2,1)}, bf16[128,2048]{1,0:T(8,128)(2,1)S(1)}, u32[]{:S(2)}, u32[]{:S(2)}) collective-permute-start(bf16[128,2048]{1,0:T(8,128)(2,1)} %get-tuple-element.278), channel_id=1, source_target_pairs={{0,3},{1,0},{2,1},{3,2},{4,7},{5,4},{6,5},{7,6},{8,11},{9,8},{10,9... | collective-permute-start | bytes 1572872 | tf_op jit(solution)/shard_map/ppermute | solution.py:640
  474.1 13.2 %collective-permute-start.53 = (bf16[256,768]{1,0:T(8,128)(2,1)S(1)}, bf16[256,768]{1,0:T(8,128)(2,1)S(1)}, u32[]{:S(2)}, u32[]{:S(2)}) collective-permute-start(bf16[256,768]{1,0:T(8,128)(2,1)S(1)} %fusion.23), channel_id=1, source_target_pairs={{0,4},{4,0},{8,12},{12,8},{16,20},{20,16},{24,28},{28,24},{1,5},{5... | collective-permute-start | bytes 1179656 | tf_op jit(solution)/shard_map/ppermute | solution.py:636
  (81 other events, 219.7 us)

commit v5 on v4

--- a/solution.py
+++ b/solution.py
@@ -12,7 +12,6 @@
 ROT = 32
 EPS = 1e-05
 LANES = 128
-VMEM_LIMIT = 56 << 20
 F32 = jnp.float32
 BF16 = jnp.bfloat16
 ANY = pl.BlockSpec(memory_space=pl.ANY)
@@ -24,7 +23,7 @@
     )
 
 
-def call(kernel, name, operands, deps=(), scalars=(), **spec):
+def call(kernel, name, operands, deps=(), scalars=(), vmem=2, **spec):
     deps, many, lead = tuple(deps), len(operands), len(scalars)
 
     def body(*refs):
@@ -43,7 +42,7 @@
         body,
         out_shape=out_shape,
         input_output_aliases=aliases,
-        compiler_params=pltpu.CompilerParams(vmem_limit_bytes=VMEM_LIMIT),
+        compiler_params=pltpu.CompilerParams(vmem_limit_bytes=vmem << 20),
         cost_estimate=pl.CostEstimate(flops=0, transcendentals=0, bytes_accessed=0),
         name=name,
         **spec,
@@ -227,6 +226,7 @@
         operands + list(earlier),
         deps,
         (at_mp,),
+        vmem=32,
         grid=(parts,),
         in_specs=[line(bias), line(gain), line(shift), table, table, table]
         + [ANY] * (len(chunks) + count + len(earlier)),
@@ -288,6 +288,7 @@
         "attend",
         [qkv, qkv, qkv],
         deps,
+        vmem=26,
         grid=(sequences * pairs,),
         in_specs=[at(0), at(1), at(2)],
         out_specs=[at(0), pl.BlockSpec((1, 8, length), lambda g: (g, 0, 0))],
@@ -383,6 +384,7 @@
         "attend_back",
         [qkv, qkv, qkv, grad, mixed, lse, *tables],
         deps,
+        vmem=26,
         grid=(sequences * pairs,),
         in_specs=[at(0), at(1), at(2), at(0), at(0), small, table, table, table],
         out_specs=[at(0)] * 3 + [pl.BlockSpec((1, 8, LANES), lambda g: (g, 0, 0))],
@@ -447,6 +449,7 @@
         [mixed, act, *blocks],
         deps,
         (at_mp,),
+        vmem=22,
         grid=(2 * turns,),
         in_specs=[
             pl.BlockSpec((rows, a.shape[1]), lambda i, at: (where(i, at), 0)) for a in (mixed, act)
@@ -521,6 +524,7 @@
         operands + list(earlier),
         deps,
         (at_mp,),
+        vmem=24,
         grid=(2 * turns,),
         in_specs=[out(hidden)] + [ANY] * (many + count + len(earlier)),
         out_specs=[out(width), out(hidden), out(model), total(hidden), total(model)],
@@ -569,6 +573,7 @@
         operands + list(blocks),
         deps,
         (at_mp,),
+        vmem=28,
         grid=(2 * turns,),
         in_specs=[
             pl.BlockSpec((rows, a.shape[1]), lambda i, at: (where(i, at), 0)) for a in operands
@@ -624,6 +629,7 @@
         [*xs, *gs],
         deps,
         (owners,),
+        vmem=32,
         grid=(count,),
         in_specs=[cut_spec] + whole_specs if left else whole_specs + [cut_spec],
         out_specs=[out(first, many) for first, many in zip(firsts, sizes)],
@@ -925,14 +931,9 @@
             shares[k] = [kept[n], got[n]]
     farthest = [added(shares[2])] if nmp == 4 else []
     moved = [a for f in farthest for a in send_far(f)]
-    up_grads = BlockScatter(
-        weight_grads(
-            me, [normed], [gpre], ndp, [sums_b, *farthest, column_grads.last()], left=True
-        ),
-        ndp,
-    )
-    up_came = up_grads.send(0)
-    other_c, own_c, sums_c = normed_part(thirds[2], [up_grads.held[0][0][0]])
+    other_c, own_c, sums_c = normed_part(
+        thirds[2], [sums_b, *farthest, column_grads.last()]
+    )
     qkv_sum = (
         qkv_sums.reshape(2, pairs, 8, LANES).sum(0)[:, :3, :].transpose(1, 0, 2).reshape(3 * width)
     )
@@ -940,34 +941,43 @@
     small = jnp.concatenate(
         [norm_sums, qkv_sum, grad_a[3][0] + grad_b[3][0], grad_a[4][0] + grad_b[4][0]]
     )
-    came_b, other_c, column_last, small, *moved = fence(
-        [came_b, other_c, column_grads.last(), small, *moved], [sums_c]
-    )
+    bits = chip_bits(ndp)
+    for bit in bits[:-2]:
+        small = small + across(small, bit, ndp)
+    small_came = across(small, bits[-2], ndp)
+    up_grads = BlockScatter(
+        weight_grads(me, [normed], [gpre], ndp, [sums_c, small], left=True), ndp
+    )
+    came_b, other_c, column_last, small_came, *moved = fence(
+        [came_b, other_c, column_grads.last(), small_came, *moved], [up_grads.held[0][0][0]]
+    )
+    small = small + small_came
+    small_came = across(small, bits[-1], ndp)
+    up_came = up_grads.send(0)
     for n, k in enumerate(thirds[1]):
         shares[k] = [own_b[n], came_b[n]]
     sums = with_far(shares, moved)
     came = {head: ring(sums[head], head, nmp)}
     column_theirs = across(column_last, 1, ndp)
-    small = lax.all_gather(small, "dp")
     qkv_grads = BlockScatter(
-        weight_grads(me, [normed], [gq, gk, gv], ndp, [sums_c, *sums.values()], left=True), ndp
-    )
-    *up_came, q0, q1, column_theirs, small = fence(
-        [*up_came, qkv_grads.held[0][0][0], qkv_grads.held[1][0][0], column_theirs, small]
+        weight_grads(me, [normed], [gq, gk, gv], ndp, [small, *sums.values()], left=True), ndp
+    )
+    *up_came, q0, q1, column_theirs, small_came = fence(
+        [*up_came, qkv_grads.held[0][0][0], qkv_grads.held[1][0][0], column_theirs, small_came]
     )
     qkv_grads.held[0][0], qkv_grads.held[1][0] = [q0], [q1]
     up_grads.arrive(0, up_came)
     up_grads.between()
     up_came = up_grads.send(chip_steps - 1)
     qkv_came = qkv_grads.send(0)
-    small = small.reshape(ndp // 2, 2, -1).sum(axis=0)
-    norm_sums, small = small[:, : 2 * model].sum(axis=0), small[:, 2 * model :]
-    came[head], other_c, norm_sums, *held = fence(
-        [came[head], other_c, norm_sums, *(sums[k] for k in tail)], [q0]
+    small = small + small_came
+    came[head], other_c, small, *held = fence(
+        [came[head], other_c, small, *(sums[k] for k in tail)], [q0]
     )
     half = held[0].shape[0] // 2
     early = [ring(a[:half], k, nmp) for k, a in zip(tail, held)]
-    u0, u1, *qkv_came = fence([*up_came, *qkv_came], [came[head]])
+    u0, u1, small, *qkv_came = fence([*up_came, small, *qkv_came], [came[head]])
+    small_other = across(small, 1, ndp)
     up_grads.arrive(chip_steps - 1, [u0, u1])
     up_theirs = across(up_grads.last(), 1, ndp)
     qkv_grads.arrive(0, qkv_came)
@@ -979,7 +989,13 @@
     came_c = across(other_c, 1, ndp)
     qkv_grads.arrive(chip_steps - 1, qkv_grads.send(chip_steps - 1))
     qkv_theirs = across(qkv_grads.last(), 1, ndp)
-    norm_sums = lax.all_gather(norm_sums, "mp").sum(axis=0)
+    norm_sums = small[: 2 * model] + small_other[: 2 * model]
+    norm_sums = [norm_sums] + [
+        lax.ppermute(norm_sums, "mp", [(i, i ^ j) for i in range(nmp)]) for j in range(1, nmp)
+    ]
+    while len(norm_sums) > 1:
+        norm_sums = [a + b for a, b in zip(norm_sums[::2], norm_sums[1::2])]
+    norm_sums = norm_sums[0]
 
     local_inputs = tokens.astype(F32)
     output = (
@@ -1008,11 +1024,13 @@
     )
 
     inner = 3 * width + hidden
-    grad_out_bias = small[0, inner:]
+    grad_out_bias = small[2 * model + inner :]
+    here, there = (a[2 * model : 2 * model + inner] for a in (small, small_other))
+    even, odd = jnp.where(core == 0, here, there), jnp.where(core == 0, there, here)
     grad_qkv_bias = jnp.concatenate(
-        [small[h, : 3 * width].reshape(3, width) for h in range(2)], axis=1
-    )
-    grad_up_bias = small[:, 3 * width : inner].reshape(2 * hidden)
+        [a[: 3 * width].reshape(3, width) for a in (even, odd)], axis=1
+    )
+    grad_up_bias = jnp.concatenate([even[3 * width :], odd[3 * width :]])
 
     centered = local_inputs - jnp.mean(local_inputs, axis=1, keepdims=True)
     inverse_std = lax.rsqrt(jnp.mean(centered * centered, axis=1, keepdims=True) + EPS)

time: 497 us -> 499 us (level)
  Pallas kernels: 213 us -> 175 us
  local copies, waits for them, and re-layouts: 40.6 us -> 78.1 us
  waiting for transfers between devices: 84.1 us -> 116 us
  blocking collectives: 30.7 us -> 0 us
  other arithmetic: 63.1 us -> 52.8 us
  starting transfers between devices: 55.8 us -> 65.9 us
    pallas_call x31, Pallas kernels: 213 us -> 175 us  [call(): pl.pallas_call(body, out_shape=out_shape, input_output_aliases=aliases, c...]
    unnamed x188 -> x276, local copies, waits for them, and re-layouts: 32.5 us -> 68.8 us
    ppermute x38 -> x41, waiting for transfers between devices: 40.5 us -> 71.7 us  [across(): return lax.ppermute(value, 'dp', [(i, i ^ bit) for i in range(count)])]
    all_gather x2 -> x0, blocking collectives: 30.7 us -> none  [the longest x1 20.9 us: on_device(): norm_sums = lax.all_gather(norm_sums, 'mp').sum(axis=0)]
    convert_element_type x10, other arithmetic: 23 us -> 17.3 us  [added(): return sum((a.astype(F32) for a in addends)).astype(BF16)]
    ppermute x38 -> x41, starting transfers between devices: 27.7 us -> 30.5 us  [across(): return lax.ppermute(value, 'dp', [(i, i ^ bit) for i in range(count)])]
  transfers between devices with their start and end apart: 55 -> 61, of which waited for: 12 -> 18; matrix products, arithmetic and copies ran while one was open for 13% -> 11% of each run, Pallas kernels for 44% -> 36%
where the time goes in v5:
time: 499 us; the launch traced here: 491 us
  Pallas kernels  175 us (35%)
  waiting for transfers between devices  116 us (23%)
  local copies, waits for them, and re-layouts  78.1 us (16%)
  starting transfers between devices  65.9 us (13%)
  other arithmetic  52.8 us (11%)
    pallas_call x31, Pallas kernels, call(): pl.pallas_call(body, out_shape=out_shape, input_output_aliases=aliases, c...  175 us
    ppermute x41, waiting for transfers between devices, across(): return lax.ppermute(value, 'dp', [(i, i ^ bit) for i in range(count)])  71.7 us
    unnamed x276, local copies, waits for them, and re-layouts  68.8 us
    ppermute x2, waiting for transfers between devices, gather_far(): down = lax.ppermute(chunks[3], 'mp', [(1, 0), (2, 1)])  35 us
    ppermute x41, starting transfers between devices, across(): return lax.ppermute(value, 'dp', [(i, i ^ bit) for i in range(count)])  30.5 us
    convert_element_type x10, other arithmetic, added(): return sum((a.astype(F32) for a in addends)).astype(BF16)  17.3 us
    ppermute x9, starting transfers between devices, ring(): lax.ppermute(value, 'mp', [(i, (i + k) % parts) for i in range(parts)])  17 us
  transfers between devices with their start and end apart: 61, of which 18 were waited for; matrix products, arithmetic and copies ran while one was open for 11% of the time, Pallas kernels for 36%

profile of v5, /device:TPU:0, one launch (start us, length us, event | category | flops | bytes accessed | tf_op | source)
XLA Modules:
  0.0 491.3 jit_solution(8542583970448856527)
XLA Ops:
  2.9 2.6 collective-permute-start.1
  5.4 1.6 collective-permute-start.3
  7.1 1.6 collective-permute-start.2
  11.1 15.4 %collective-permute-done.1.refs_2_ = bf16[256,1792]{1,0:T(8,128)(2,1)S(1)} collective-permute-done((bf16[256,1792]{1,0:T(8,128)(2,1)S(1)}, bf16[256,1792]{1,0:T(8,128)(2,1)S(1)}, u32[]{:S(2)}, u32[]{:S(2)}) %collective-permute-start.1) | collective-permute-done | bytes 917536 | tf_op jit(solution)/shard_map/ppermute | solution.py:642
  26.4 6.1 %collective-permute-done.3.refs_4_ = bf16[256,2048]{1,0:T(8,128)(2,1)S(1)} collective-permute-done((bf16[256,2048]{1,0:T(8,128)(2,1)S(1)}, bf16[256,2048]{1,0:T(8,128)(2,1)S(1)}, u32[]{:S(2)}, u32[]{:S(2)}) %collective-permute-start.3) | collective-permute-done | bytes 1048608 | tf_op jit(solution)/shard_map/ppermute | solution.py:646
  32.6 1.7 collective-permute-start.7
  34.9 1.5 collective-permute-start.6
  37.3 18.3 %collective-permute-done.5.refs_3_ = bf16[256,1792]{1,0:T(8,128)(2,1)S(1)} collective-permute-done((bf16[256,1792]{1,0:T(8,128)(2,1)S(1)}, bf16[256,1792]{1,0:T(8,128)(2,1)S(1)}, u32[]{:S(2)}, u32[]{:S(2)}) %collective-permute-start.5) | collective-permute-done | bytes 917536 | tf_op jit(solution)/shard_map/ppermute | solution.py:642
  60.5 1.5 collective-permute-start.9
  62.0 24.1 %collective-permute-done.12 = bf16[256,2048]{1,0:T(8,128)(2,1)S(1)} collective-permute-done((bf16[256,2048]{1,0:T(8,128)(2,1)S(1)}, bf16[256,2048]{1,0:T(8,128)(2,1)S(1)}, u32[]{:S(2)}, u32[]{:S(2)}) %collective-permute-start.12) | collective-permute-done | bytes 1048608 | tf_op jit(solution)/shard_map/ppermute | solution.py:657
  87.6 1.7 copy-done.72
  96.8 2.7 collective-permute-start.16
  99.6 1.5 collective-permute-start.15
  117.5 16.8 %project.2 = (bf16[2048,768]{1,0:T(8,128)(2,1)S(1)}, bf16[2048,1024]{1,0:T(8,128)(2,1)S(1)}, bf16[2048,1024]{1,0:T(8,128)(2,1)}, bf16[2048,2048]{1,0:T(8,128)(2,1)}, bf16[2048,2048]{1,0:T(8,128)(2,1)}) custom-call(s32[1]{0:T(128)} %bitcast.refs_0_, f32[1,1792]{1,0:T(1,128)S(1)} %maximum_convert_fusion.refs_1_, f32[1,2048]{1,0:T(1,128)S(1)} %bitcast.98, ...), custom_call_target="tpu_custom_call" | custom-call | tf_op jit(solution)/shard_map/project/pallas_call | solution.py:41
  134.4 2.0 collective-permute-start.17
  136.8 1.6 collective-permute-start.21
  138.6 16.8 %project.3 = (bf16[2048,768]{1,0:T(8,128)(2,1)S(1)}, bf16[2048,1024]{1,0:T(8,128)(2,1)S(1)}, bf16[2048,1024]{1,0:T(8,128)(2,1)}, bf16[2048,2048]{1,0:T(8,128)(2,1)}, bf16[2048,2048]{1,0:T(8,128)(2,1)}) custom-call(s32[1]{0:T(128)} %bitcast.refs_0_, ...), custom_call_target="tpu_custom_call", output_to_operand_aliasing={{0}: (17, {}), {1}: (18, {}), {2}: (19, {}), {3}: (20, {}),... | custom-call | tf_op jit(solution)/shard_map/project/pallas_call | solution.py:41
  155.4 1.6 collective-permute-start.19
  157.1 13.9 %attend.1 = (bf16[2048,256]{1,0:T(8,128)(2,1)S(1)}, f32[4,8,1024]{2,1,0:T(8,128)S(1)}) custom-call(bf16[2048,768]{1,0:T(8,128)(2,1)S(1)} %get-tuple-element.189.refs_6_.refs_0_.refs_1_.refs_2_, bf16[2048,768]{1,0:T(8,128)(2,1)S(1)} %get-tuple-element.189.refs_6_.refs_0_.refs_1_.refs_2_, ...), custom_call_target="tpu_custom_call" | custom-call | tf_op jit(solution)/shard_map/attend/pallas_call | solution.py:41
  173.2 2.4 pad_maximum_fusion.1.refs_11_
  177.9 15.3 %branch_sums.1 = (bf16[4,256,2048]{2,1,0:T(8,128)(2,1)S(1)}, bf16[4,256,2048]{2,1,0:T(8,128)(2,1)S(1)}) custom-call(s32[1]{0:T(128)} %bitcast.refs_0_, bf16[2048,256]{1,0:T(8,128)(2,1)S(1)} %get-tuple-element.194.refs_10_.refs_1_.refs_4_, bf16[2048,1024]{1,0:T(8,128)(2,1)S(1)} %get-tuple-element.195.refs_2_, ...), custom_call_target="tpu_custom_call" | custom-call | tf_op jit(solution)/shard_map/branch_sums/pallas_call | solution.py:41
  193.2 10.8 %collective-permute-done.24 = bf16[256,2048]{1,0:T(8,128)(2,1)S(1)} collective-permute-done((bf16[256,2048]{1,0:T(8,128)(2,1)S(1)}, bf16[256,2048]{1,0:T(8,128)(2,1)S(1)}, u32[]{:S(2)}, u32[]{:S(2)}) %collective-permute-start.24) | collective-permute-done | bytes 1048608 | tf_op jit(solution)/shard_map/ppermute | solution.py:657
  205.0 1.6 copy-done.37
  206.7 10.2 %grad_in.2 = (bf16[2048,256]{1,0:T(8,128)(2,1)S(1)}, bf16[2048,1024]{1,0:T(8,128)(2,1)S(1)}, bf16[2048,2048]{1,0:T(8,128)(2,1)}, f32[8,1024]{1,0:T(8,128)S(1)}, f32[8,2048]{1,0:T(8,128)S(1)}) custom-call(s32[1]{0:T(128)} %bitcast.refs_0_, bf16[2048,1024]{1,0:T(8,128)(2,1)S(1)} %copy-done.37, bf16[256,2048]{1,0:T(8,128)(2,1)} %get-tuple-element.202.refs_2_, ...), custom_call_target="tpu_custom_call" | custom-call | tf_op jit(solution)/shard_map/grad_in/pallas_call | solution.py:41
  219.0 3.5 fusion.19.refs_20_
  222.5 4.7 collective-permute-start.27
  227.2 1.6 collective-permute-start.28
  230.1 9.8 %grad_in.3 = (bf16[2048,256]{1,0:T(8,128)(2,1)S(1)}, bf16[2048,1024]{1,0:T(8,128)(2,1)S(1)}, bf16[2048,2048]{1,0:T(8,128)(2,1)}, f32[8,1024]{1,0:T(8,128)S(1)}, f32[8,2048]{1,0:T(8,128)S(1)}) custom-call(s32[1]{0:T(128)} %bitcast.refs_0_, bf16[2048,1024]{1,0:T(8,128)(2,1)S(1)} %copy-done.37, ...), custom_call_target="tpu_custom_call", output_to_operand_aliasing={{0}: (16, {}), {1}: (17, {}), {2}: (18, {})} | custom-call | tf_op jit(solution)/shard_map/grad_in/pallas_call | solution.py:41
  240.0 2.0 copy-done.4
  242.9 3.4 copy-done.38
  247.5 17.0 %weight_grads.3 = (bf16[2,1280,256]{2,1,0:T(8,128)(2,1)}, bf16[2,1280,256]{2,1,0:T(8,128)(2,1)}, bf16[1,1280,256]{2,1,0:T(8,128)(2,1)S(1)}, bf16[1,1280,256]{2,1...) custom-call(s32[8]{0:T(128)S(1)} %broadcast_xor_fusion.refs_0_, ...), custom_call_target="tpu_custom_call" | custom-call | tf_op jit(solution)/shard_map/weight_grads/pallas_call | solution.py:41
  266.5 4.3 fusion.16
  271.1 1.6 convert_reduce_fusion
  272.8 1.6 fusion.9
  277.9 23.9 %attend_back.1 = (bf16[2048,256]{1,0:T(8,128)(2,1)S(1)}, bf16[2048,256]{1,0:T(8,128)(2,1)S(1)}, bf16[2048,256]{1,0:T(8,128)(2,1)S(1)}, f32[4,8,128]{2,1,0:T(8,128)S(1)}) custom-call(bf16[2048,768]{1,0:T(8,128)(2,1)S(1)} %get-tuple-element.189.refs_6_.refs_0_.refs_1_.refs_2_, bf16[2048,768]{1,0:T(8,128)(2,1)S(1)} %get-tuple-element.189.refs_6_.refs_0_.refs_1_.refs_2_, ...), custom_call_target="tpu_custom_call" | custom-call | tf_op jit(solution)/shard_map/attend_back/pallas_call | solution.py:41
  301.9 3.8 collective-permute-start.30
  305.8 3.4 copy-done.2
  309.2 6.9 %grad_normed_sums.3 = (bf16[1,256,2048]{2,1,0:T(8,128)(2,1)S(1)}, bf16[1,256,2048]{2,1,0:T(8,128)(2,1)S(1)}, f32[8,2048]{1,0:T(8,128)S(1)}) custom-call(s32[1]{0:T(128)} %bitcast.refs_0_, bf16[2048,256]{1,0:T(8,128)(2,1)S(1)} %get-tuple-element.232.refs_2_.refs_1_, bf16[2048,256]{1,0:T(8,128)(2,1)S(1)} %get-tuple-element.235.refs_2_.refs_3_, ...), custom_call_target="tpu_custom_call" | custom-call | tf_op jit(solution)/shard_map/grad_normed_sums/pallas_call | solution.py:41
  317.6 2.1 add_convert_fusion.3.refs_16_
  321.8 2.1 add_convert_fusion.4.refs_15_
  323.9 1.7 collective-permute-start.33
  329.0 2.2 copy-done.6
  340.8 13.5 %grad_normed_sums.4 = (bf16[2,256,2048]{2,1,0:T(8,128)(2,1)S(1)}, bf16[2,256,2048]{2,1,0:T(8,128)(2,1)S(1)}, f32[8,2048]{1,0:T(8,128)S(1)}) custom-call(s32[1]{0:T(128)} %bitcast.refs_0_, bf16[2048,256]{1,0:T(8,128)(2,1)S(1)} %copy-done.52, bf16[2048,256]{1,0:T(8,128)(2,1)S(1)} %copy-done.64, bf16[2048,256]{1,0:T(8,128)(2,1)S(1)} %copy-done.67, ...), custom_call_target="tpu_custom_call" | custom-call | tf_op jit(solution)/shard_map/grad_normed_sums/pallas_call | solution.py:41
  356.3 1.7 fusion.20.refs_15_
  358.0 2.3 collective-permute-start.39
  362.9 3.4 copy-done.3
  366.3 8.1 %grad_normed_sums.5 = (bf16[1,256,2048]{2,1,0:T(8,128)(2,1)}, bf16[1,256,2048]{2,1,0:T(8,128)(2,1)S(1)}, f32[8,2048]{1,0:T(8,128)S(1)}) custom-call(s32[1]{0:T(128)} %bitcast.refs_0_, bf16[2048,256]{1,0:T(8,128)(2,1)S(1)} %copy-done.52, bf16[2048,256]{1,0:T(8,128)(2,1)S(1)} %copy-done.64, bf16[2048,256]{1,0:T(8,128)(2,1)S(1)} %copy-done.67, ...), custom_call_target="tpu_custom_call" | custom-call | tf_op jit(solution)/shard_map/grad_normed_sums/pallas_call | solution.py:41
  377.5 3.4 copy-done.8
  380.9 12.6 %weight_grads.4 = (bf16[2,256,1024]{2,1,0:T(8,128)(2,1)S(1)}, bf16[2,256,1024]{2,1,0:T(8,128)(2,1)S(1)}, bf16[1,256,1024]{2,1,0:T(8,128)(2,1)S(1)}, bf16[1,256,1...) custom-call(s32[8]{0:T(128)S(1)} %broadcast_xor_fusion.refs_0_, ...), custom_call_target="tpu_custom_call" | custom-call | tf_op jit(solution)/shard_map/weight_grads/pallas_call | solution.py:41
  393.6 1.6 collective-permute-start.42
  395.9 1.6 collective-permute-start.45
  400.5 10.6 %weight_grads.5 = (bf16[2,256,768]{2,1,0:T(8,128)(2,1)S(1)}, bf16[2,256,768]{2,1,0:T(8,128)(2,1)S(1)}, bf16[1,256,768]{2,1,0:T(8,128)(2,1)S(1)}, bf16[1,256,768]...) custom-call(s32[8]{0:T(128)S(1)} %broadcast_xor_fusion.refs_0_, ...), custom_call_target="tpu_custom_call" | custom-call | tf_op jit(solution)/shard_map/weight_grads/pallas_call | solution.py:41
  411.1 7.4 %collective-permute-done.42.refs_0_ = bf16[2,256,1024]{2,1,0:T(8,128)(2,1)S(1)} collective-permute-done((bf16[2,256,1024]{2,1,0:T(8,128)(2,1)S(1)}, bf16[2,256,1024]{2,1,0:T(8,128)(2,1)S(1)}, u32[]{:S(2)}, u32[]{:S(2)}) %collective-permute-start.42) | collective-permute-done | bytes 1048608 | tf_op jit(solution)/shard_map/ppermute | solution.py:642
  423.9 1.6 maximum_select_fusion.1
  427.3 2.1 collective-permute-start.47
  429.4 5.1 %collective-permute-done.50.refs_1_ = bf16[1,256,1024]{2,1,0:T(8,128)(2,1)S(1)} collective-permute-done((bf16[1,256,1024]{2,1,0:T(8,128)(2,1)S(1)}, bf16[1,256,1024]{2,1,0:T(8,128)(2,1)S(1)}, u32[]{:S(2)}, u32[]{:S(2)}) %collective-permute-start.50) | collective-permute-done | bytes 524320 | tf_op jit(solution)/shard_map/ppermute | solution.py:642
  435.7 12.7 %collective-permute-done.51.refs_3_ = bf16[2,256,768]{2,1,0:T(8,128)(2,1)S(1)} collective-permute-done((bf16[2,256,768]{2,1,0:T(8,128)(2,1)S(1)}, bf16[2,256,768]{2,1,0:T(8,128)(2,1)S(1)}, u32[]{:S(2)}, u32[]{:S(2)}) %collective-permute-start.51) | collective-permute-done | bytes 786464 | tf_op jit(solution)/shard_map/ppermute | solution.py:642
  457.1 1.9 collective-permute-start.55
  467.3 2.6 collective-permute-start.48
  469.9 6.2 %collective-permute-done.58 = bf16[1,256,768]{2,1,0:T(8,128)(2,1)S(1)} collective-permute-done((bf16[1,256,768]{2,1,0:T(8,128)(2,1)}, bf16[1,256,768]{2,1,0:T(8,128)(2,1)S(1)}, u32[]{:S(2)}, u32[]{:S(2)}) %collective-permute-start.58) | collective-permute-done | bytes 393248 | tf_op jit(solution)/shard_map/ppermute | solution.py:642
  477.6 1.6 maximum_select_fusion
  479.1 2.0 collective-permute-done.48
  481.2 2.5 fusion.27
  483.8 5.1 %fusion.8 = (bf16[256,2048]{1,0:T(8,128)(2,1)}, bf16[256,2048]{1,0:T(8,128)(2,1)}) fusion(bf16[256,2048]{1,0:T(8,128)(2,1)S(1)} %copy-done.24, f32[256,2048]{1,0:T(8,128)S(1)} %get-tuple-element.302, bf16[256,2048]{1,0:T(8,128)(2,1)S(1)} %copy-done.118, f32[256]{0:T(256)S(1)} %get-tuple-element.335, f32[256]{0:T(256)S(1)} %copy-done.129, ...), kind=kLoop, calls=%fused_computation.13 | loop fusion | flops 10485760 | bytes 10498048 | tf_op jit(solution)/shard_map/convert_element_type | solution.py:1044
  (447 shorter events, 110.2 us)
Async XLA Ops:
  0.6 100.5 %copy-start = (bf16[3,512]{1,0:T(4,128)(2,1)S(1)}, bf16[3,512]{1,0:T(4,128)(2,1)}, u32[]{:S(2)}) copy-start(bf16[3,512]{1,0:T(4,128)(2,1)} %param.22) | copy-start | bytes 9220
  2.3 4.8 collective-permute-start
  2.9 23.6 %collective-permute-start.1 = (bf16[256,1792]{1,0:T(8,128)(2,1)S(1)}, bf16[256,1792]{1,0:T(8,128)(2,1)S(1)}, u32[]{:S(2)}, u32[]{:S(2)}) collective-permute-start(bf16[256,1792]{1,0:T(8,128)(2,1)S(1)} %pad_maximum_fusion.3.refs_0_), channel_id=1, source_target_pairs={{0,8},{4,12},{8,0},{12,4},{16,24},{20,28},{24,16},{28,20},{1,9},{5... | collective-permute-start | bytes 2752520 | tf_op jit(solution)/shard_map/ppermute | solution.py:642
  5.4 27.1 %collective-permute-start.3 = (bf16[256,2048]{1,0:T(8,128)(2,1)S(1)}, bf16[256,2048]{1,0:T(8,128)(2,1)S(1)}, u32[]{:S(2)}, u32[]{:S(2)}) collective-permute-start(bf16[256,2048]{1,0:T(8,128)(2,1)S(1)} %copy-done.22), channel_id=1, source_target_pairs={{0,1},{1,2},{2,3},{3,0},{4,5},{5,6},{6,7},{7,4},{8,9},{9,10},{10,1... | collective-permute-start | bytes 3145736 | tf_op jit(solution)/shard_map/ppermute | solution.py:646
  7.1 25.5 %collective-permute-start.2 = (bf16[256,1792]{1,0:T(8,128)(2,1)S(1)}, bf16[256,1792]{1,0:T(8,128)(2,1)S(1)}, u32[]{:S(2)}, u32[]{:S(2)}) collective-permute-start(bf16[256,1792]{1,0:T(8,128)(2,1)S(1)} %collective-permute-done.refs_1_), channel_id=1, source_target_pairs={{0,16},{4,20},{8,24},{12,28},{16,0},{20,4},{24,8},{28,12},{1,17},{... | collective-permute-start | bytes 2752520 | tf_op jit(solution)/shard_map/ppermute | solution.py:642
  8.8 2.3 collective-permute-start.4
  32.6 24.5 %collective-permute-start.7 = (bf16[256,2048]{1,0:T(8,128)(2,1)S(1)}, bf16[256,2048]{1,0:T(8,128)(2,1)S(1)}, u32[]{:S(2)}, u32[]{:S(2)}) collective-permute-start(bf16[256,2048]{1,0:T(8,128)(2,1)S(1)} %get-tuple-element.161), channel_id=1, source_target_pairs={{0,3},{1,0},{2,1},{3,2},{4,7},{5,4},{6,5},{7,6},{8,11},{9,8},{10,9... | collective-permute-start | bytes 3145736 | tf_op jit(solution)/shard_map/ppermute | solution.py:646
  34.3 21.4 %collective-permute-start.5 = (bf16[256,1792]{1,0:T(8,128)(2,1)S(1)}, bf16[256,1792]{1,0:T(8,128)(2,1)S(1)}, u32[]{:S(2)}, u32[]{:S(2)}) collective-permute-start(bf16[256,1792]{1,0:T(8,128)(2,1)S(1)} %get-tuple-element.157.refs_1_), channel_id=1, source_target_pairs={{0,8},{4,12},{8,0},{12,4},{16,24},{20,28},{24,16},{28,20},{1,9},{5... | collective-permute-start | bytes 2752520 | tf_op jit(solution)/shard_map/ppermute | solution.py:642
  34.9 20.8 %collective-permute-start.6 = (bf16[256,1792]{1,0:T(8,128)(2,1)S(1)}, bf16[256,1792]{1,0:T(8,128)(2,1)S(1)}, u32[]{:S(2)}, u32[]{:S(2)}) collective-permute-start(bf16[256,1792]{1,0:T(8,128)(2,1)S(1)} %get-tuple-element.156.refs_0_), channel_id=1, source_target_pairs={{0,16},{4,20},{8,24},{12,28},{16,0},{20,4},{24,8},{28,12},{1,17},{... | collective-permute-start | bytes 2752520 | tf_op jit(solution)/shard_map/ppermute | solution.py:642
  57.4 30.1 %collective-permute-start.8 = (bf16[3,256,2048]{2,1,0:T(8,128)(2,1)S(1)}, bf16[3,256,2048]{2,1,0:T(8,128)(2,1)S(1)}, u32[]{:S(2)}, u32[]{:S(2)}) collective-permute-start(bf16[3,256,2048]{2,1,0:T(8,128)(2,1)S(1)} %pad_maximum_fusion), channel_id=1, source_target_pairs={{0,4},{4,0},{8,12},{12,8},{16,20},{20,16},{24,28},{28,24},{1,5},{5... | collective-permute-start | bytes 9437192 | tf_op jit(solution)/shard_map/ppermute | solution.py:642
  58.1 4.0 collective-permute-start.11
  58.8 27.4 %collective-permute-start.12 = (bf16[256,2048]{1,0:T(8,128)(2,1)S(1)}, bf16[256,2048]{1,0:T(8,128)(2,1)S(1)}, u32[]{:S(2)}, u32[]{:S(2)}) collective-permute-start(bf16[256,2048]{1,0:T(8,128)(2,1)S(1)} %get-tuple-element.163.refs_9_), channel_id=1, source_target_pairs={{1,0},{2,1},{5,4},{6,5},{9,8},{10,9},{13,12},{14,13},{17,16},{18,1... | collective-permute-start | bytes 3145736 | tf_op jit(solution)/shard_map/ppermute | solution.py:657
  60.1 27.4 %collective-permute-start.10 = (bf16[256,1792]{1,0:T(8,128)(2,1)S(1)}, bf16[256,1792]{1,0:T(8,128)(2,1)S(1)}, u32[]{:S(2)}, u32[]{:S(2)}) collective-permute-start(bf16[256,1792]{1,0:T(8,128)(2,1)S(1)} %get-tuple-element.169.refs_5_), channel_id=1, source_target_pairs={{0,8},{4,12},{8,0},{12,4},{16,24},{20,28},{24,16},{28,20},{1,9},{5... | collective-permute-start | bytes 2752520 | tf_op jit(solution)/shard_map/ppermute | solution.py:642
  60.5 27.0 %collective-permute-start.9 = (bf16[256,1792]{1,0:T(8,128)(2,1)S(1)}, bf16[256,1792]{1,0:T(8,128)(2,1)S(1)}, u32[]{:S(2)}, u32[]{:S(2)}) collective-permute-start(bf16[256,1792]{1,0:T(8,128)(2,1)S(1)} %get-tuple-element.166.refs_2_), channel_id=1, source_target_pairs={{0,16},{4,20},{8,24},{12,28},{16,0},{20,4},{24,8},{28,12},{1,17},{... | collective-permute-start | bytes 2752520 | tf_op jit(solution)/shard_map/ppermute | solution.py:642
  96.8 37.5 %collective-permute-start.16 = (bf16[256,2048]{1,0:T(8,128)(2,1)}, bf16[256,2048]{1,0:T(8,128)(2,1)}, u32[]{:S(2)}, u32[]{:S(2)}) collective-permute-start(bf16[256,2048]{1,0:T(8,128)(2,1)} %get-tuple-element.180.refs_19_.refs_4_), channel_id=1, source_target_pairs={{0,1},{1,2},{2,3},{3,0},{4,5},{5,6},{6,7},{7,4},{8,9},{9,10},{10,1... | collective-permute-start | bytes 3145736 | tf_op jit(solution)/shard_map/ppermute | solution.py:646
  99.5 34.8 %collective-permute-start.14 = (bf16[1280,256]{1,0:T(8,128)(2,1)}, bf16[1280,256]{1,0:T(8,128)(2,1)}, u32[]{:S(2)}, u32[]{:S(2)}) collective-permute-start(bf16[1280,256]{1,0:T(8,128)(2,1)} %get-tuple-element.186.refs_0_), channel_id=1, source_target_pairs={{0,8},{4,12},{8,0},{12,4},{16,24},{20,28},{24,16},{28,20},{1,9},{5... | collective-permute-start | bytes 1966088 | tf_op jit(solution)/shard_map/ppermute | solution.py:642
  99.6 34.7 %collective-permute-start.15 = (bf16[1280,256]{1,0:T(8,128)(2,1)}, bf16[1280,256]{1,0:T(8,128)(2,1)}, u32[]{:S(2)}, u32[]{:S(2)}) collective-permute-start(bf16[1280,256]{1,0:T(8,128)(2,1)} %get-tuple-element.187.refs_1_), channel_id=1, source_target_pairs={{0,16},{4,20},{8,24},{12,28},{16,0},{20,4},{24,8},{28,12},{1,17},{... | collective-permute-start | bytes 1966088 | tf_op jit(solution)/shard_map/ppermute | solution.py:642
  101.1 37.4 %collective-permute-start.13 = (bf16[256,2048]{1,0:T(8,128)(2,1)}, bf16[256,2048]{1,0:T(8,128)(2,1)}, u32[]{:S(2)}, u32[]{:S(2)}) collective-permute-start(bf16[256,2048]{1,0:T(8,128)(2,1)} %get-tuple-element.171.refs_10_), channel_id=1, source_target_pairs={{0,4},{4,0},{8,12},{12,8},{16,20},{20,16},{24,28},{28,24},{1,5},{5... | collective-permute-start | bytes 3145736 | tf_op jit(solution)/shard_map/ppermute | solution.py:642
  134.4 21.0 %collective-permute-start.17 = (bf16[1280,256]{1,0:T(8,128)(2,1)}, bf16[1280,256]{1,0:T(8,128)(2,1)S(1)}, u32[]{:S(2)}, u32[]{:S(2)}) collective-permute-start(bf16[1280,256]{1,0:T(8,128)(2,1)} %get-tuple-element.190.refs_1_), channel_id=1, source_target_pairs={{0,8},{4,12},{8,0},{12,4},{16,24},{20,28},{24,16},{28,20},{1,9},{5... | collective-permute-start | bytes 1966088 | tf_op jit(solution)/shard_map/ppermute | solution.py:642
  136.3 19.0 %collective-permute-start.18 = (bf16[1280,256]{1,0:T(8,128)(2,1)}, bf16[1280,256]{1,0:T(8,128)(2,1)S(1)}, u32[]{:S(2)}, u32[]{:S(2)}) collective-permute-start(bf16[1280,256]{1,0:T(8,128)(2,1)} %get-tuple-element.188.refs_22_.refs_0_), channel_id=1, source_target_pairs={{0,16},{4,20},{8,24},{12,28},{16,0},{20,4},{24,8},{28,12},{1,17},{... | collective-permute-start | bytes 1966088 | tf_op jit(solution)/shard_map/ppermute | solution.py:642
  136.8 34.2 %collective-permute-start.21 = (bf16[256,2048]{1,0:T(8,128)(2,1)}, bf16[256,2048]{1,0:T(8,128)(2,1)S(1)}, u32[]{:S(2)}, u32[]{:S(2)}) collective-permute-start(bf16[256,2048]{1,0:T(8,128)(2,1)} %get-tuple-element.202.refs_2_), channel_id=1, source_target_pairs={{0,3},{1,0},{2,1},{3,2},{4,7},{5,4},{6,5},{7,6},{8,11},{9,8},{10,9... | collective-permute-start | bytes 3145736 | tf_op jit(solution)/shard_map/ppermute | solution.py:646
  155.4 16.6 %collective-permute-start.19 = (bf16[1280,256]{1,0:T(8,128)(2,1)}, bf16[1280,256]{1,0:T(8,128)(2,1)S(1)}, u32[]{:S(2)}, u32[]{:S(2)}) collective-permute-start(bf16[1280,256]{1,0:T(8,128)(2,1)} %get-tuple-element.197.refs_2_), channel_id=1, source_target_pairs={{0,16},{4,20},{8,24},{12,28},{16,0},{20,4},{24,8},{28,12},{1,17},{... | collective-permute-start | bytes 1966088 | tf_op jit(solution)/shard_map/ppermute | solution.py:642
  157.0 16.2 %collective-permute-start.20 = (bf16[1280,256]{1,0:T(8,128)(2,1)}, bf16[1280,256]{1,0:T(8,128)(2,1)S(1)}, u32[]{:S(2)}, u32[]{:S(2)}) collective-permute-start(bf16[1280,256]{1,0:T(8,128)(2,1)} %get-tuple-element.200.refs_5_), channel_id=1, source_target_pairs={{0,8},{4,12},{8,0},{12,4},{16,24},{20,28},{24,16},{28,20},{1,9},{5... | collective-permute-start | bytes 1966088 | tf_op jit(solution)/shard_map/ppermute | solution.py:642
  173.2 31.8 %copy-start.74 = (bf16[1280,256]{1,0:T(8,128)(2,1)}, bf16[1280,256]{1,0:T(8,128)(2,1)S(1)}, u32[]{:S(2)}) copy-start(bf16[1280,256]{1,0:T(8,128)(2,1)S(1)} %get-tuple-element.209.refs_9_.refs_12_.refs_14_) | copy-start | bytes 1966084
  175.6 28.8 %collective-permute-start.22 = (bf16[3,256,2048]{2,1,0:T(8,128)(2,1)S(1)}, bf16[3,256,2048]{2,1,0:T(8,128)(2,1)S(1)}, u32[]{:S(2)}, u32[]{:S(2)}) collective-permute-start(bf16[3,256,2048]{2,1,0:T(8,128)(2,1)S(1)} %pad_maximum_fusion.1.refs_11_), channel_id=1, source_target_pairs={{0,4},{4,0},{8,12},{12,8},{16,20},{20,16},{24,28},{28,24},{1,5},{5... | collective-permute-start | bytes 9437192 | tf_op jit(solution)/shard_map/ppermute | solution.py:642
  175.7 17.5 %collective-permute-start.23 = (bf16[256,2048]{1,0:T(8,128)(2,1)}, bf16[256,2048]{1,0:T(8,128)(2,1)S(1)}, u32[]{:S(2)}, u32[]{:S(2)}) collective-permute-start(bf16[256,2048]{1,0:T(8,128)(2,1)} %get-tuple-element.211.refs_3_), channel_id=1, source_target_pairs={{1,2},{2,3},{5,6},{6,7},{9,10},{10,11},{13,14},{14,15},{17,18},{18... | collective-permute-start | bytes 3145736 | tf_op jit(solution)/shard_map/ppermute | solution.py:656
  176.4 27.6 %collective-permute-start.24 = (bf16[256,2048]{1,0:T(8,128)(2,1)S(1)}, bf16[256,2048]{1,0:T(8,128)(2,1)S(1)}, u32[]{:S(2)}, u32[]{:S(2)}) collective-permute-start(bf16[256,2048]{1,0:T(8,128)(2,1)S(1)} %get-tuple-element.212.refs_4_), channel_id=1, source_target_pairs={{1,0},{2,1},{5,4},{6,5},{9,8},{10,9},{13,12},{14,13},{17,16},{18,1... | collective-permute-start | bytes 3145736 | tf_op jit(solution)/shard_map/ppermute | solution.py:657
  204.4 12.6 %collective-permute-start.25 = (bf16[4,256,2048]{2,1,0:T(8,128)(2,1)S(1)}, bf16[4,256,2048]{2,1,0:T(8,128)(2,1)S(1)}, u32[]{:S(2)}, u32[]{:S(2)}) collective-permute-start(bf16[4,256,2048]{2,1,0:T(8,128)(2,1)S(1)} %get-tuple-element.215.refs_14_), channel_id=1, source_target_pairs={{0,4},{4,0},{8,12},{12,8},{16,20},{20,16},{24,28},{28,24},{1,5},{5... | collective-permute-start | bytes 12582920 | tf_op jit(solution)/shard_map/ppermute | solution.py:642
  204.5 12.5 %collective-permute-start.26 = (bf16[256,2048]{1,0:T(8,128)(2,1)S(1)}, bf16[256,2048]{1,0:T(8,128)(2,1)S(1)}, u32[]{:S(2)}, u32[]{:S(2)}) collective-permute-start(bf16[256,2048]{1,0:T(8,128)(2,1)S(1)} %get-tuple-element.216.refs_5_), channel_id=1, source_target_pairs={{0,4},{4,0},{8,12},{12,8},{16,20},{20,16},{24,28},{28,24},{1,5},{5... | collective-permute-start | bytes 3145736 | tf_op jit(solution)/shard_map/ppermute | solution.py:642
  222.5 44.0 %collective-permute-start.27 = (bf16[256,2048]{1,0:T(8,128)(2,1)}, bf16[256,2048]{1,0:T(8,128)(2,1)}, u32[]{:S(2)}, u32[]{:S(2)}) collective-permute-start(bf16[256,2048]{1,0:T(8,128)(2,1)} %fusion.19.refs_20_), channel_id=1, source_target_pairs={{0,1},{1,2},{4,5},{5,6},{8,9},{9,10},{12,13},{13,14},{16,17},{17,1... | collective-permute-start | bytes 3145736 | tf_op jit(solution)/shard_map/ppermute | solution.py:666
  227.2 39.2 %collective-permute-start.28 = (bf16[256,2048]{1,0:T(8,128)(2,1)}, bf16[256,2048]{1,0:T(8,128)(2,1)}, u32[]{:S(2)}, u32[]{:S(2)}) collective-permute-start(bf16[256,2048]{1,0:T(8,128)(2,1)} %fusion.19.refs_20_), channel_id=1, source_target_pairs={{3,2},{2,1},{7,6},{6,5},{11,10},{10,9},{15,14},{14,13},{19,18},{18... | collective-permute-start | bytes 3145736 | tf_op jit(solution)/shard_map/ppermute | solution.py:667
  264.5 51.7 %collective-permute-start.31 = (bf16[2,1280,256]{2,1,0:T(8,128)(2,1)}, bf16[2,1280,256]{2,1,0:T(8,128)(2,1)}, u32[]{:S(2)}, u32[]{:S(2)}) collective-permute-start(bf16[2,1280,256]{2,1,0:T(8,128)(2,1)} %get-tuple-element.227.refs_2_.refs_9_), channel_id=1, source_target_pairs={{0,16},{4,20},{8,24},{12,28},{16,0},{20,4},{24,8},{28,12},{1,17},{... | collective-permute-start | bytes 3932168 | tf_op jit(solution)/shard_map/ppermute | solution.py:642
  265.1 51.1 %collective-permute-start.32 = (bf16[2,1280,256]{2,1,0:T(8,128)(2,1)}, bf16[2,1280,256]{2,1,0:T(8,128)(2,1)}, u32[]{:S(2)}, u32[]{:S(2)}) collective-permute-start(bf16[2,1280,256]{2,1,0:T(8,128)(2,1)} %get-tuple-element.241), channel_id=1, source_target_pairs={{0,8},{4,12},{8,0},{12,4},{16,24},{20,28},{24,16},{28,20},{1,9},{5... | collective-permute-start | bytes 3932168 | tf_op jit(solution)/shard_map/ppermute | solution.py:642
  270.8 31.1 %collective-permute-start.29 = (bf16[256,2048]{1,0:T(8,128)(2,1)}, bf16[256,2048]{1,0:T(8,128)(2,1)}, u32[]{:S(2)}, u32[]{:S(2)}) collective-permute-start(bf16[256,2048]{1,0:T(8,128)(2,1)} %get-tuple-element.304.refs_10_), channel_id=1, source_target_pairs={{0,1},{1,2},{2,3},{3,0},{4,5},{5,6},{6,7},{7,4},{8,9},{9,10},{10,1... | collective-permute-start | bytes 3145736 | tf_op jit(solution)/shard_map/ppermute | solution.py:646
  272.7 29.0 %copy-start.127 = (f32[256]{0:T(256)}, f32[256]{0:T(256)S(1)}, u32[]{:S(2)}) copy-start(f32[256]{0:T(256)S(1)} %broadcast_multiply_fusion.1) | copy-start | bytes 3076
  301.9 52.4 %collective-permute-start.30 = (bf16[256,2048]{1,0:T(8,128)(2,1)}, bf16[256,2048]{1,0:T(8,128)(2,1)}, u32[]{:S(2)}, u32[]{:S(2)}) collective-permute-start(bf16[256,2048]{1,0:T(8,128)(2,1)} %get-tuple-element.234), channel_id=1, source_target_pairs={{0,3},{1,0},{2,1},{3,2},{4,7},{5,4},{6,5},{7,6},{8,11},{9,8},{10,9... | collective-permute-start | bytes 3145736 | tf_op jit(solution)/shard_map/ppermute | solution.py:646
  319.7 34.6 %collective-permute-start.34 = (bf16[1,1280,256]{2,1,0:T(8,128)(2,1)}, bf16[1,1280,256]{2,1,0:T(8,128)(2,1)S(1)}, u32[]{:S(2)}, u32[]{:S(2)}) collective-permute-start(bf16[1,1280,256]{2,1,0:T(8,128)(2,1)} %add_convert_fusion.3.refs_16_), channel_id=1, source_target_pairs={{0,16},{4,20},{8,24},{12,28},{16,0},{20,4},{24,8},{28,12},{1,17},{... | collective-permute-start | bytes 1966088 | tf_op jit(solution)/shard_map/ppermute | solution.py:642
  321.3 33.0 %collective-permute-start.35 = (bf16[1,128,2048]{2,1,0:T(8,128)(2,1)}, bf16[1,128,2048]{2,1,0:T(8,128)(2,1)}, u32[]{:S(2)}, u32[]{:S(2)}) collective-permute-start(bf16[1,128,2048]{2,1,0:T(8,128)(2,1)} %get-tuple-element.312), channel_id=1, source_target_pairs={{0,4},{4,0},{8,12},{12,8},{16,20},{20,16},{24,28},{28,24},{1,5},{5... | collective-permute-start | bytes 1572872 | tf_op jit(solution)/shard_map/ppermute | solution.py:642
  321.3 33.0 %collective-permute-start.36 = (bf16[1,128,2048]{2,1,0:T(8,128)(2,1)}, bf16[1,128,2048]{2,1,0:T(8,128)(2,1)}, u32[]{:S(2)}, u32[]{:S(2)}) collective-permute-start(bf16[1,128,2048]{2,1,0:T(8,128)(2,1)} %get-tuple-element.311), channel_id=1, source_target_pairs={{0,4},{4,0},{8,12},{12,8},{16,20},{20,16},{24,28},{28,24},{1,5},{5... | collective-permute-start | bytes 1572872 | tf_op jit(solution)/shard_map/ppermute | solution.py:642
  323.9 30.4 %collective-permute-start.33 = (bf16[1,1280,256]{2,1,0:T(8,128)(2,1)}, bf16[1,1280,256]{2,1,0:T(8,128)(2,1)}, u32[]{:S(2)}, u32[]{:S(2)}) collective-permute-start(bf16[1,1280,256]{2,1,0:T(8,128)(2,1)} %add_convert_fusion.4.refs_15_), channel_id=1, source_target_pairs={{0,8},{4,12},{8,0},{12,4},{16,24},{20,28},{24,16},{28,20},{1,9},{5... | collective-permute-start | bytes 1966088 | tf_op jit(solution)/shard_map/ppermute | solution.py:642
  355.6 40.2 %collective-permute-start.37 = (bf16[2,256,2048]{2,1,0:T(8,128)(2,1)S(1)}, bf16[2,256,2048]{2,1,0:T(8,128)(2,1)S(1)}, u32[]{:S(2)}, u32[]{:S(2)}) collective-permute-start(bf16[2,256,2048]{2,1,0:T(8,128)(2,1)S(1)} %get-tuple-element.256), channel_id=1, source_target_pairs={{0,4},{4,0},{8,12},{12,8},{16,20},{20,16},{24,28},{28,24},{1,5},{5... | collective-permute-start | bytes 6291464 | tf_op jit(solution)/shard_map/ppermute | solution.py:642
  358.0 37.8 %collective-permute-start.39 = (bf16[256,2048]{1,0:T(8,128)(2,1)S(1)}, bf16[256,2048]{1,0:T(8,128)(2,1)S(1)}, u32[]{:S(2)}, u32[]{:S(2)}) collective-permute-start(bf16[256,2048]{1,0:T(8,128)(2,1)S(1)} %fusion.20.refs_15_), channel_id=1, source_target_pairs={{0,1},{1,2},{4,5},{5,6},{8,9},{9,10},{12,13},{13,14},{16,17},{17,1... | collective-permute-start | bytes 3145736 | tf_op jit(solution)/shard_map/ppermute | solution.py:666
  360.4 35.4 %collective-permute-start.40 = (bf16[256,2048]{1,0:T(8,128)(2,1)S(1)}, bf16[256,2048]{1,0:T(8,128)(2,1)S(1)}, u32[]{:S(2)}, u32[]{:S(2)}) collective-permute-start(bf16[256,2048]{1,0:T(8,128)(2,1)S(1)} %fusion.20.refs_15_), channel_id=1, source_target_pairs={{3,2},{2,1},{7,6},{6,5},{11,10},{10,9},{15,14},{14,13},{19,18},{18... | collective-permute-start | bytes 3145736 | tf_op jit(solution)/shard_map/ppermute | solution.py:667
  374.5 20.7 %collective-permute-start.38 = (f32[7936]{0:T(1024)S(1)}, f32[7936]{0:T(1024)S(1)}, u32[]{:S(2)}, u32[]{:S(2)}) collective-permute-start(f32[7936]{0:T(1024)S(1)} %pad_maximum_fusion.7.refs_4_), channel_id=1, source_target_pairs={{0,8},{4,12},{8,0},{12,4},{16,24},{20,28},{24,16},{28,20},{1,9},{5... | collective-permute-start | bytes 95240 | tf_op jit(solution)/shard_map/ppermute | solution.py:642
  393.6 24.9 %collective-permute-start.42 = (bf16[2,256,1024]{2,1,0:T(8,128)(2,1)S(1)}, bf16[2,256,1024]{2,1,0:T(8,128)(2,1)S(1)}, u32[]{:S(2)}, u32[]{:S(2)}) collective-permute-start(bf16[2,256,1024]{2,1,0:T(8,128)(2,1)S(1)} %get-tuple-element.263.refs_6_), channel_id=1, source_target_pairs={{0,16},{4,20},{8,24},{12,28},{16,0},{20,4},{24,8},{28,12},{1,17},{... | collective-permute-start | bytes 3145736 | tf_op jit(solution)/shard_map/ppermute | solution.py:642
  395.2 24.1 %collective-permute-start.43 = (bf16[2,256,1024]{2,1,0:T(8,128)(2,1)S(1)}, bf16[2,256,1024]{2,1,0:T(8,128)(2,1)S(1)}, u32[]{:S(2)}, u32[]{:S(2)}) collective-permute-start(bf16[2,256,1024]{2,1,0:T(8,128)(2,1)S(1)} %get-tuple-element.268), channel_id=1, source_target_pairs={{0,8},{4,12},{8,0},{12,4},{16,24},{20,28},{24,16},{28,20},{1,9},{5... | collective-permute-start | bytes 3145736 | tf_op jit(solution)/shard_map/ppermute | solution.py:642
  395.9 23.3 %collective-permute-start.45 = (f32[7936]{0:T(1024)S(1)}, f32[7936]{0:T(1024)S(1)}, u32[]{:S(2)}, u32[]{:S(2)}) collective-permute-start(f32[7936]{0:T(1024)S(1)} %fusion.26.refs_5_), channel_id=1, source_target_pairs={{0,16},{4,20},{8,24},{12,28},{16,0},{20,4},{24,8},{28,12},{1,17},{... | collective-permute-start | bytes 95240 | tf_op jit(solution)/shard_map/ppermute | solution.py:642
  397.4 21.8 %collective-permute-start.44 = (bf16[1280,256]{1,0:T(8,128)(2,1)S(1)}, bf16[1280,256]{1,0:T(8,128)(2,1)S(1)}, u32[]{:S(2)}, u32[]{:S(2)}) collective-permute-start(bf16[1280,256]{1,0:T(8,128)(2,1)S(1)} %get-tuple-element.272), channel_id=1, source_target_pairs={{0,4},{4,0},{8,12},{12,8},{16,20},{20,16},{24,28},{28,24},{1,5},{5... | collective-permute-start | bytes 1966088 | tf_op jit(solution)/shard_map/ppermute | solution.py:642
  398.9 27.5 %collective-permute-start.41 = (bf16[256,2048]{1,0:T(8,128)(2,1)S(1)}, bf16[256,2048]{1,0:T(8,128)(2,1)S(1)}, u32[]{:S(2)}, u32[]{:S(2)}) collective-permute-start(bf16[256,2048]{1,0:T(8,128)(2,1)S(1)} %get-tuple-element.306.refs_6_), channel_id=1, source_target_pairs={{0,1},{1,2},{2,3},{3,0},{4,5},{5,6},{6,7},{7,4},{8,9},{9,10},{10,1... | collective-permute-start | bytes 3145736 | tf_op jit(solution)/shard_map/ppermute | solution.py:646
  419.5 14.9 %collective-permute-start.50 = (bf16[1,256,1024]{2,1,0:T(8,128)(2,1)S(1)}, bf16[1,256,1024]{2,1,0:T(8,128)(2,1)S(1)}, u32[]{:S(2)}, u32[]{:S(2)}) collective-permute-start(bf16[1,256,1024]{2,1,0:T(8,128)(2,1)S(1)} %add_convert_fusion.6), channel_id=1, source_target_pairs={{0,16},{4,20},{8,24},{12,28},{16,0},{20,4},{24,8},{28,12},{1,17},{... | collective-permute-start | bytes 1572872 | tf_op jit(solution)/shard_map/ppermute | solution.py:642
  420.8 14.9 %collective-permute-start.49 = (bf16[1,256,1024]{2,1,0:T(8,128)(2,1)S(1)}, bf16[1,256,1024]{2,1,0:T(8,128)(2,1)S(1)}, u32[]{:S(2)}, u32[]{:S(2)}) collective-permute-start(bf16[1,256,1024]{2,1,0:T(8,128)(2,1)S(1)} %add_convert_fusion.7), channel_id=1, source_target_pairs={{0,8},{4,12},{8,0},{12,4},{16,24},{20,28},{24,16},{28,20},{1,9},{5... | collective-permute-start | bytes 1572872 | tf_op jit(solution)/shard_map/ppermute | solution.py:642
  422.1 26.3 %collective-permute-start.51 = (bf16[2,256,768]{2,1,0:T(8,128)(2,1)S(1)}, bf16[2,256,768]{2,1,0:T(8,128)(2,1)S(1)}, u32[]{:S(2)}, u32[]{:S(2)}) collective-permute-start(bf16[2,256,768]{2,1,0:T(8,128)(2,1)S(1)} %get-tuple-element.274.refs_4_), channel_id=1, source_target_pairs={{0,16},{4,20},{8,24},{12,28},{16,0},{20,4},{24,8},{28,12},{1,17},{... | collective-permute-start | bytes 2359304 | tf_op jit(solution)/shard_map/ppermute | solution.py:642
  423.0 26.6 %collective-permute-start.52 = (bf16[2,256,768]{2,1,0:T(8,128)(2,1)S(1)}, bf16[2,256,768]{2,1,0:T(8,128)(2,1)S(1)}, u32[]{:S(2)}, u32[]{:S(2)}) collective-permute-start(bf16[2,256,768]{2,1,0:T(8,128)(2,1)S(1)} %get-tuple-element.285), channel_id=1, source_target_pairs={{0,8},{4,12},{8,0},{12,4},{16,24},{20,28},{24,16},{28,20},{1,9},{5... | collective-permute-start | bytes 2359304 | tf_op jit(solution)/shard_map/ppermute | solution.py:642
  427.3 40.1 %collective-permute-start.47 = (bf16[128,2048]{1,0:T(8,128)(2,1)}, bf16[128,2048]{1,0:T(8,128)(2,1)}, u32[]{:S(2)}, u32[]{:S(2)}) collective-permute-start(bf16[128,2048]{1,0:T(8,128)(2,1)} %get-tuple-element.310), channel_id=1, source_target_pairs={{0,3},{1,0},{2,1},{3,2},{4,7},{5,4},{6,5},{7,6},{8,11},{9,8},{10,9... | collective-permute-start | bytes 1572872 | tf_op jit(solution)/shard_map/ppermute | solution.py:646
  434.5 46.7 %collective-permute-start.46 = (bf16[1,256,2048]{2,1,0:T(8,128)(2,1)}, bf16[1,256,2048]{2,1,0:T(8,128)(2,1)}, u32[]{:S(2)}, u32[]{:S(2)}) collective-permute-start(bf16[1,256,2048]{2,1,0:T(8,128)(2,1)} %get-tuple-element.275), channel_id=1, source_target_pairs={{0,4},{4,0},{8,12},{12,8},{16,20},{20,16},{24,28},{28,24},{1,5},{5... | collective-permute-start | bytes 3145736 | tf_op jit(solution)/shard_map/ppermute | solution.py:642
  449.6 4.6 collective-permute-start.53
  456.0 7.6 %collective-permute-start.54 = (f32[4096]{0:T(1024)}, f32[4096]{0:T(1024)}, u32[]{:S(2)}, u32[]{:S(2)}) collective-permute-start(f32[4096]{0:T(1024)} %slice_add_fusion), channel_id=1, source_target_pairs={{0,1},{1,0},{2,3},{3,2},{4,5},{5,4},{6,7},{7,6},{8,9},{9,8},{10,11... | collective-permute-start | bytes 49160 | tf_op jit(solution)/shard_map/ppermute | solution.py:994
  457.1 6.6 %collective-permute-start.55 = (f32[4096]{0:T(1024)}, f32[4096]{0:T(1024)}, u32[]{:S(2)}, u32[]{:S(2)}) collective-permute-start(f32[4096]{0:T(1024)} %slice_add_fusion), channel_id=1, source_target_pairs={{0,2},{1,3},{2,0},{3,1},{4,6},{5,7},{6,4},{7,5},{8,10},{9,11},{10,... | collective-permute-start | bytes 49160 | tf_op jit(solution)/shard_map/ppermute | solution.py:994
  459.0 5.9 %collective-permute-start.56 = (f32[4096]{0:T(1024)}, f32[4096]{0:T(1024)}, u32[]{:S(2)}, u32[]{:S(2)}) collective-permute-start(f32[4096]{0:T(1024)} %slice_add_fusion), channel_id=1, source_target_pairs={{0,3},{1,2},{2,1},{3,0},{4,7},{5,6},{6,5},{7,4},{8,11},{9,10},{10,... | collective-permute-start | bytes 49160 | tf_op jit(solution)/shard_map/ppermute | solution.py:994
  463.7 12.9 %collective-permute-start.60 = (bf16[256,1024]{1,0:T(8,128)(2,1)}, bf16[256,1024]{1,0:T(8,128)(2,1)S(1)}, u32[]{:S(2)}, u32[]{:S(2)}) collective-permute-start(bf16[256,1024]{1,0:T(8,128)(2,1)} %fusion.22), channel_id=1, source_target_pairs={{0,4},{4,0},{8,12},{12,8},{16,20},{20,16},{24,28},{28,24},{1,5},{5... | collective-permute-start | bytes 1572872 | tf_op jit(solution)/shard_map/ppermute | solution.py:642
  463.7 12.6 %collective-permute-start.57 = (bf16[1,256,768]{2,1,0:T(8,128)(2,1)}, bf16[1,256,768]{2,1,0:T(8,128)(2,1)S(1)}, u32[]{:S(2)}, u32[]{:S(2)}) collective-permute-start(bf16[1,256,768]{2,1,0:T(8,128)(2,1)} %add_convert_fusion.10), channel_id=1, source_target_pairs={{0,8},{4,12},{8,0},{12,4},{16,24},{20,28},{24,16},{28,20},{1,9},{5... | collective-permute-start | bytes 1179656 | tf_op jit(solution)/shard_map/ppermute | solution.py:642
  464.8 11.2 %collective-permute-start.58 = (bf16[1,256,768]{2,1,0:T(8,128)(2,1)}, bf16[1,256,768]{2,1,0:T(8,128)(2,1)S(1)}, u32[]{:S(2)}, u32[]{:S(2)}) collective-permute-start(bf16[1,256,768]{2,1,0:T(8,128)(2,1)} %add_convert_fusion.9), channel_id=1, source_target_pairs={{0,16},{4,20},{8,24},{12,28},{16,0},{20,4},{24,8},{28,12},{1,17},{... | collective-permute-start | bytes 1179656 | tf_op jit(solution)/shard_map/ppermute | solution.py:642
  467.3 13.9 %collective-permute-start.48 = (bf16[128,2048]{1,0:T(8,128)(2,1)S(1)}, bf16[128,2048]{1,0:T(8,128)(2,1)S(1)}, u32[]{:S(2)}, u32[]{:S(2)}) collective-permute-start(bf16[128,2048]{1,0:T(8,128)(2,1)S(1)} %get-tuple-element.279), channel_id=1, source_target_pairs={{0,3},{1,0},{2,1},{3,2},{4,7},{5,4},{6,5},{7,6},{8,11},{9,8},{10,9... | collective-permute-start | bytes 1572872 | tf_op jit(solution)/shard_map/ppermute | solution.py:646
  476.2 12.7 %collective-permute-start.59 = (bf16[256,768]{1,0:T(8,128)(2,1)S(1)}, bf16[256,768]{1,0:T(8,128)(2,1)S(1)}, u32[]{:S(2)}, u32[]{:S(2)}) collective-permute-start(bf16[256,768]{1,0:T(8,128)(2,1)S(1)} %fusion.23), channel_id=1, source_target_pairs={{0,4},{4,0},{8,12},{12,8},{16,20},{20,16},{24,28},{28,24},{1,5},{5... | collective-permute-start | bytes 1179656 | tf_op jit(solution)/shard_map/ppermute | solution.py:642
  (133 other events, 794.0 us)

commit v6 on v5

--- a/solution.py
+++ b/solution.py
@@ -14,7 +14,7 @@
 LANES = 128
 F32 = jnp.float32
 BF16 = jnp.bfloat16
-ANY = pl.BlockSpec(memory_space=pl.ANY)
+HBM = pl.BlockSpec(memory_space=pltpu.HBM)
 
 
 def dot(lhs, rhs, lhs_dim, rhs_dim):
@@ -23,13 +23,13 @@
     )
 
 
-def call(kernel, name, operands, deps=(), scalars=(), vmem=2, **spec):
+def call(kernel, name, operands, deps=(), scalars=(), vmem=63, **spec):
     deps, many, lead = tuple(deps), len(operands), len(scalars)
 
     def body(*refs):
         kernel(*refs[: lead + many], *refs[lead + many + len(deps) :])
 
-    in_specs = list(spec.pop("in_specs")) + [ANY] * len(deps)
+    in_specs = list(spec.pop("in_specs")) + [HBM] * len(deps)
     out_shape, aliases = spec.pop("out_shape"), spec.pop("input_output_aliases", {})
     if scalars:
         grid_spec = pltpu.PrefetchScalarGridSpec(
@@ -55,8 +55,8 @@
         "fence",
         values,
         deps,
-        in_specs=[ANY] * len(values),
-        out_specs=[ANY] * len(values),
+        in_specs=[HBM] * len(values),
+        out_specs=[HBM] * len(values),
         out_shape=[jax.ShapeDtypeStruct(v.shape, v.dtype) for v in values],
         input_output_aliases={n: n for n in range(len(values))},
     )
@@ -92,20 +92,30 @@
     return centered * lax.rsqrt(variance + EPS)
 
 
-def block_copies(blocks, place, sems):
+def block_copies(blocks, place, sems, pieces=None):
     me = lax.axis_index("dp")
-    return [
-        pltpu.make_async_copy(block, place(lax.bitwise_xor(me, j)), sems.at[j])
-        for j, block in enumerate(blocks)
-    ]
-
-
-def rows_at(ref, size):
-    return lambda owner: ref.at[pl.ds(pl.multiple_of(owner * size, size), size)]
-
-
-def columns_at(ref, size):
-    return lambda owner: ref.at[:, pl.ds(pl.multiple_of(owner * size, size), size)]
+    parts = []
+    for j, block in enumerate(blocks):
+        owner = lax.bitwise_xor(me, j)
+        for n, (source, target) in enumerate(pieces(block, owner) if pieces else [(block, place(owner))]):
+            if n == len(parts):
+                parts.append([])
+            parts[n].append(pltpu.make_async_copy(source, target, sems.at[n, j]))
+    return parts
+
+
+def start_copies(copies):
+    for copy in copies:
+        copy.start()
+
+
+def wait_copies(copies):
+    for copy in copies:
+        copy.wait()
+
+
+def span(owner, size):
+    return pl.ds(pl.multiple_of(owner * size, size), size)
 
 
 def arrays_of(chunks):
@@ -162,20 +172,27 @@
     qkv_ref, act_ref, slope_ref, normed_ref, tokens_ref, held, x_held, ready, sems, x_sems = rest[-10:]
     step, steps = pl.program_id(0), len(places)
     found = chunk_copies(chunks, places, parts, x_held, x_sems)
-    loads = block_copies(blocks, rows_at(held, blocks[0].shape[0]), sems)
+    size, tiles = blocks[0].shape[0], (3 * width + hidden) // width
+    column = lambda t: slice(t * width, (t + 1) * width)
+    loads = block_copies(
+        blocks,
+        None,
+        sems,
+        lambda block, owner: [
+            (block.at[:, column(t)], held.at[span(owner, size), column(t)]) for t in range(tiles)
+        ],
+    )
 
     def norm(slot):
         return (normalized(x_held[slot]) * gain_ref[...] + shift_ref[...]).astype(BF16)
 
     @pl.when(step == 0)
     def _():
-        for copy in loads:
-            copy.start()
         start_all(found)
+        for copies in loads:
+            start_copies(copies)
         wait_for(found[0])
         ready[0] = norm(0)
-        for copy in loads:
-            copy.wait()
 
     for slot in range(1, steps):
 
@@ -188,8 +205,9 @@
     tokens_ref[...] = x_held[step]
     ready[(step + 1) % 2] = norm((step + 1) % steps)
     root = 0.7978845608028654
-    for t in range((3 * width + hidden) // width):
-        columns = slice(t * width, (t + 1) * width)
+    for t in range(tiles):
+        columns = column(t)
+        pl.when(step == 0)(functools.partial(wait_copies, loads[t]))
         y = dot(x, held[:, columns], 1, 0) + bias_ref[:, columns]
         if t < 3:
             for g in range(width // LANES):
@@ -226,10 +244,9 @@
         operands + list(earlier),
         deps,
         (at_mp,),
-        vmem=32,
         grid=(parts,),
         in_specs=[line(bias), line(gain), line(shift), table, table, table]
-        + [ANY] * (len(chunks) + count + len(earlier)),
+        + [HBM] * (len(chunks) + count + len(earlier)),
         out_specs=[out(w) for w in widths],
         out_shape=[jax.ShapeDtypeStruct((2 * parts * rows, w), BF16) for w in widths],
         input_output_aliases={1 + len(operands) + n: n for n in range(len(earlier))},
@@ -237,7 +254,7 @@
             pltpu.VMEM((model, total), BF16),
             pltpu.VMEM((parts, rows, model), BF16),
             pltpu.VMEM((2, rows, model), BF16),
-            pltpu.SemaphoreType.DMA((count,)),
+            pltpu.SemaphoreType.DMA((total // width, count)),
             pltpu.SemaphoreType.DMA((parts,)),
         ],
     )
@@ -288,7 +305,6 @@
         "attend",
         [qkv, qkv, qkv],
         deps,
-        vmem=26,
         grid=(sequences * pairs,),
         in_specs=[at(0), at(1), at(2)],
         out_specs=[at(0), pl.BlockSpec((1, 8, length), lambda g: (g, 0, 0))],
@@ -384,7 +400,6 @@
         "attend_back",
         [qkv, qkv, qkv, grad, mixed, lse, *tables],
         deps,
-        vmem=26,
         grid=(sequences * pairs,),
         in_specs=[at(0), at(1), at(2), at(0), at(0), small, table, table, table],
         out_specs=[at(0)] * 3 + [pl.BlockSpec((1, 8, LANES), lambda g: (g, 0, 0))],
@@ -406,16 +421,6 @@
     return rows_of
 
 
-def split_outputs(step, turns, result, other_ref, own_ref):
-    @pl.when(step < turns)
-    def _():
-        other_ref[0] = result
-
-    @pl.when(step >= turns)
-    def _():
-        own_ref[0] = result
-
-
 def split_specs(rows, model, turns):
     return [
         pl.BlockSpec((1, rows, model), lambda i, at: (jnp.minimum(i, turns - 1), 0, 0)),
@@ -425,18 +430,28 @@
 
 def branch_kernel(count, turns, at_ref, mixed_ref, act_ref, *rest):
     blocks, (other_ref, own_ref, held, sems) = rest[:count], rest[count:]
-    step = pl.program_id(0)
+    step, size, me = pl.program_id(0), blocks[0].shape[1], lax.axis_index("dp")
+    (loads,) = block_copies(blocks, lambda owner: held.at[:, span(owner, size)], sems)
+
+    def rows():
+        return jnp.concatenate([mixed_ref[...], act_ref[...]], axis=1)
 
     @pl.when(step == 0)
     def _():
-        loads = block_copies(blocks, columns_at(held, blocks[0].shape[1]), sems)
-        for copy in loads:
-            copy.start()
-        for copy in loads:
+        start_copies(loads)
+        x = rows()
+        for j, copy in enumerate(loads):
             copy.wait()
-
-    x = jnp.concatenate([mixed_ref[...], act_ref[...]], axis=1)
-    split_outputs(step, turns, dot(x, held[...], 1, 0).astype(BF16), other_ref, own_ref)
+            columns = span(lax.bitwise_xor(me, j), size)
+            other_ref[0, :, columns] = dot(x, held[:, columns], 1, 0).astype(BF16)
+
+    @pl.when((step > 0) & (step < turns))
+    def _():
+        other_ref[0] = dot(rows(), held[...], 1, 0).astype(BF16)
+
+    @pl.when(step >= turns)
+    def _():
+        own_ref[0] = dot(rows(), held[...], 1, 0).astype(BF16)
 
 
 def branch_sums(at_mp, mixed, act, blocks, parts, places, deps):
@@ -449,15 +464,14 @@
         [mixed, act, *blocks],
         deps,
         (at_mp,),
-        vmem=22,
         grid=(2 * turns,),
         in_specs=[
             pl.BlockSpec((rows, a.shape[1]), lambda i, at: (where(i, at), 0)) for a in (mixed, act)
         ]
-        + [ANY] * count,
+        + [HBM] * count,
         out_specs=split_specs(rows, model, turns),
         out_shape=[jax.ShapeDtypeStruct((turns, rows, model), BF16)] * 2,
-        scratch_shapes=[pltpu.VMEM((inner, model), BF16), pltpu.SemaphoreType.DMA((count,))],
+        scratch_shapes=[pltpu.VMEM((inner, model), BF16), pltpu.SemaphoreType.DMA((1, count))],
     )
 
 
@@ -471,17 +485,24 @@
     gmixed_ref, gpre_ref, dy_ref, gsum_ref, dsum_ref, held, dy_held, sems, dy_sems = rest[-9:]
     step, steps = pl.program_id(0), 2 * len(places)
     found = chunk_copies(chunks, places, parts, dy_held, dy_sems)
-    loads = block_copies(blocks, columns_at(held, blocks[0].shape[1]), sems)
+    size, tiles = blocks[0].shape[1], (width + hidden) // width
+    row = lambda t: slice(t * width, (t + 1) * width)
+    loads = block_copies(
+        blocks,
+        None,
+        sems,
+        lambda block, owner: [
+            (block.at[row(t)], held.at[row(t), span(owner, size)]) for t in range(tiles)
+        ],
+    )
 
     @pl.when(step == 0)
     def _():
-        for copy in loads:
-            copy.start()
         start_all(found)
+        for copies in loads:
+            start_copies(copies)
         gsum_ref[...] = jnp.zeros_like(gsum_ref)
         dsum_ref[...] = jnp.zeros_like(dsum_ref)
-        for copy in loads:
-            copy.wait()
 
     for slot in range(steps):
 
@@ -491,14 +512,16 @@
 
     dy = dy_held[step]
     dy_ref[...] = dy
+    dsum_ref[0:1, :] += jnp.sum(dy.astype(F32), axis=0, keepdims=True)
+    pl.when(step == 0)(functools.partial(wait_copies, loads[0]))
     gmixed_ref[...] = dot(dy, held[:width, :], 1, 1).astype(BF16)
-    for start in range(0, hidden, width):
-        part = slice(start, start + width)
-        gact = dot(dy, held[width + start : 2 * width + start, :], 1, 1)
+    for t in range(1, tiles):
+        part = row(t - 1)
+        pl.when(step == 0)(functools.partial(wait_copies, loads[t]))
+        gact = dot(dy, held[row(t), :], 1, 1)
         gpre = (gact * slope_ref[:, part].astype(F32)).astype(BF16)
         gpre_ref[:, part] = gpre
         gsum_ref[0:1, part] += jnp.sum(gpre.astype(F32), axis=0, keepdims=True)
-    dsum_ref[0:1, :] += jnp.sum(dy.astype(F32), axis=0, keepdims=True)
 
 
 def grad_in(at_mp, chunks, slope, blocks, width, parts, places, earlier, deps):
@@ -524,9 +547,8 @@
         operands + list(earlier),
         deps,
         (at_mp,),
-        vmem=24,
         grid=(2 * turns,),
-        in_specs=[out(hidden)] + [ANY] * (many + count + len(earlier)),
+        in_specs=[out(hidden)] + [HBM] * (many + count + len(earlier)),
         out_specs=[out(width), out(hidden), out(model), total(hidden), total(model)],
         out_shape=[jax.ShapeDtypeStruct((length, w), BF16) for w in (width, hidden, model)]
         + [jax.ShapeDtypeStruct((8, w), F32) for w in (hidden, model)],
@@ -534,7 +556,7 @@
         scratch_shapes=[
             pltpu.VMEM((width + hidden, model), BF16),
             pltpu.VMEM((2 * turns, rows, model), BF16),
-            pltpu.SemaphoreType.DMA((count,)),
+            pltpu.SemaphoreType.DMA(((width + hidden) // width, count)),
             pltpu.SemaphoreType.DMA((2 * turns,)),
         ],
     )
@@ -543,23 +565,37 @@
 def grad_normed_kernel(
     count, turns, at_ref, gq_ref, gk_ref, gv_ref, gpre_ref, tokens_ref, *rest
 ):
-    blocks, (other_ref, own_ref, sum_ref, held, sems) = rest[:count], rest[count:]
-    step = pl.program_id(0)
+    blocks, (other_ref, own_ref, sum_ref, held, result, sems) = rest[:count], rest[count:]
+    step, size, me = pl.program_id(0), blocks[0].shape[0], lax.axis_index("dp")
+    (loads,) = block_copies(blocks, lambda owner: held.at[span(owner, size)], sems)
+
+    def grads():
+        return jnp.concatenate([gq_ref[...], gk_ref[...], gv_ref[...], gpre_ref[...]], axis=1)
 
     @pl.when(step == 0)
     def _():
-        loads = block_copies(blocks, rows_at(held, blocks[0].shape[0]), sems)
-        for copy in loads:
-            copy.start()
+        start_copies(loads)
         sum_ref[...] = jnp.zeros_like(sum_ref)
-        for copy in loads:
+        g = grads()
+        for j, copy in enumerate(loads):
             copy.wait()
-
-    g = jnp.concatenate([gq_ref[...], gk_ref[...], gv_ref[...], gpre_ref[...]], axis=1)
-    result = dot(g, held[...], 1, 1)
-    sum_ref[0:1, :] += jnp.sum(result * normalized(tokens_ref[...]), axis=0, keepdims=True)
-    sum_ref[1:2, :] += jnp.sum(result, axis=0, keepdims=True)
-    split_outputs(step, turns, result.astype(BF16), other_ref, own_ref)
+            there = span(lax.bitwise_xor(me, j), size)
+            result[:, there] = dot(g, held[there, :], 1, 1)
+
+    @pl.when(step > 0)
+    def _():
+        result[...] = dot(grads(), held[...], 1, 1)
+
+    sum_ref[0:1, :] += jnp.sum(result[...] * normalized(tokens_ref[...]), axis=0, keepdims=True)
+    sum_ref[1:2, :] += jnp.sum(result[...], axis=0, keepdims=True)
+
+    @pl.when(step < turns)
+    def _():
+        other_ref[0] = result[...].astype(BF16)
+
+    @pl.when(step >= turns)
+    def _():
+        own_ref[0] = result[...].astype(BF16)
 
 
 def grad_normed_sums(at_mp, gqkv, gpre, tokens, blocks, parts, places, deps):
@@ -573,33 +609,55 @@
         operands + list(blocks),
         deps,
         (at_mp,),
-        vmem=28,
         grid=(2 * turns,),
         in_specs=[
             pl.BlockSpec((rows, a.shape[1]), lambda i, at: (where(i, at), 0)) for a in operands
         ]
-        + [ANY] * count,
+        + [HBM] * count,
         out_specs=split_specs(rows, model, turns)
         + [pl.BlockSpec((8, model), lambda i, at: (0, 0))],
         out_shape=[jax.ShapeDtypeStruct((turns, rows, model), BF16)] * 2
         + [jax.ShapeDtypeStruct((8, model), F32)],
-        scratch_shapes=[pltpu.VMEM((model, total), BF16), pltpu.SemaphoreType.DMA((count,))],
-    )
-
-
-def weight_grad_kernel(sizes, left, at_ref, *refs):
-    ins, outs = refs[: len(refs) - len(sizes)], refs[len(refs) - len(sizes) :]
-    if left:
-        grad = jnp.concatenate([dot(ins[0][...], g[...], 0, 0) for g in ins[1:]], axis=1)
-    else:
-        grad = jnp.concatenate([dot(x[...], ins[-1][...], 0, 0) for x in ins[:-1]], axis=0)
-    grad = grad.astype(BF16)
+        scratch_shapes=[
+            pltpu.VMEM((model, total), BF16),
+            pltpu.VMEM((rows, model), F32),
+            pltpu.SemaphoreType.DMA((1, count)),
+        ],
+    )
+
+
+def weight_grad_kernel(sizes, left, tile, at_ref, cut_ref, *refs):
+    *refs, held, grad, sems = refs
+    whole, outs = refs[: len(refs) - len(sizes)], refs[len(refs) - len(sizes) :]
+    step = pl.program_id(0)
+    starts = [(ref, start) for ref in whole for start in range(0, ref.shape[1], tile)]
+    place = lambda n: slice(n * tile, (n + 1) * tile)
+    loads = [
+        pltpu.make_async_copy(ref.at[:, start : start + tile], held.at[:, place(n)], sems.at[n])
+        for n, (ref, start) in enumerate(starts)
+    ]
+
+    @pl.when(step == 0)
+    def _():
+        start_copies(loads)
+        for n, copy in enumerate(loads):
+            copy.wait()
+            if left:
+                grad[:, place(n)] = dot(cut_ref[...], held[:, place(n)], 0, 0).astype(BF16)
+            else:
+                grad[place(n), :] = dot(held[:, place(n)], cut_ref[...], 0, 0).astype(BF16)
+
+    @pl.when(step > 0)
+    def _():
+        pair = (cut_ref[...], held[...]) if left else (held[...], cut_ref[...])
+        grad[...] = dot(*pair, 0, 0).astype(BF16)
+
     first = 0
     for size, out_ref in zip(sizes, outs):
 
-        @pl.when((pl.program_id(0) >= first) & (pl.program_id(0) < first + size))
+        @pl.when((step >= first) & (step < first + size))
         def _(out_ref=out_ref):
-            out_ref[0] = grad
+            out_ref[0] = grad[...]
 
         first += size
 
@@ -613,8 +671,7 @@
     length, (cut, whole) = xs[0].shape[0], ((xs, gs) if left else (gs, xs))
     size = cut[0].shape[1] // count
     cut_spec = pl.BlockSpec((length, size), lambda i, at: (0, at[i]))
-    whole_specs = [pl.BlockSpec(a.shape, lambda i, at: (0, 0)) for a in whole]
-    full = sum(a.shape[1] for a in whole)
+    full, tile = sum(a.shape[1] for a in whole), min(a.shape[1] for a in whole)
     shape = (size, full) if left else (full, size)
 
     def out(first, many):
@@ -624,16 +681,20 @@
 
     firsts = [sum(sizes[:n]) for n in range(len(sizes))]
     outs = call(
-        functools.partial(weight_grad_kernel, sizes, left),
+        functools.partial(weight_grad_kernel, sizes, left, min(tile, 256)),
         "weight_grads",
-        [*xs, *gs],
+        [*cut, *whole],
         deps,
         (owners,),
-        vmem=32,
         grid=(count,),
-        in_specs=[cut_spec] + whole_specs if left else whole_specs + [cut_spec],
+        in_specs=[cut_spec] + [HBM] * len(whole),
         out_specs=[out(first, many) for first, many in zip(firsts, sizes)],
         out_shape=[jax.ShapeDtypeStruct((many, *shape), BF16) for many in sizes],
+        scratch_shapes=[
+            pltpu.VMEM((length, full), BF16),
+            pltpu.VMEM(shape, BF16),
+            pltpu.SemaphoreType.DMA((full // min(tile, 256),)),
+        ],
     )
     return [[o for o, (half, _) in zip(outs, sets) if half == h] for h in range(2)]
 

time: 499 us -> 544 us (1.090)
  Pallas kernels: 175 us -> 264 us
  local copies, waits for them, and re-layouts: 78.1 us -> 26.3 us
  other arithmetic: 52.8 us -> 73.7 us
  waiting for transfers between devices: 116 us -> 103 us
    pallas_call x31, Pallas kernels: 175 us -> 264 us  [call(): pl.pallas_call(body, out_shape=out_shape, input_output_aliases=aliases, c...]
    unnamed x276 -> x122, local copies, waits for them, and re-layouts: 68.8 us -> 15.8 us
    ppermute x41, waiting for transfers between devices: 71.7 us -> 60.8 us  [across(): return lax.ppermute(value, 'dp', [(i, i ^ bit) for i in range(count)])]
    convert_element_type x10, other arithmetic: 17.3 us -> 28 us  [added(): return sum((a.astype(F32) for a in addends)).astype(BF16)]
  transfers between devices with their start and end apart: 61 -> 61, of which waited for: 18 -> 17; matrix products, arithmetic and copies ran while one was open for 11% -> 14% of each run, Pallas kernels for 36% -> 49%
where the time goes in v6:
time: 544 us; the launch traced here: 536 us
  Pallas kernels  264 us (49%)
  waiting for transfers between devices  103 us (19%)
  other arithmetic  73.7 us (14%)
  starting transfers between devices  66.8 us (12%)
  local copies, waits for them, and re-layouts  26.3 us (5%)
    pallas_call x31, Pallas kernels, call(): pl.pallas_call(body, out_shape=out_shape, input_output_aliases=aliases, c...  264 us
    ppermute x41, waiting for transfers between devices, across(): return lax.ppermute(value, 'dp', [(i, i ^ bit) for i in range(count)])  60.8 us
    ppermute x2, waiting for transfers between devices, gather_far(): down = lax.ppermute(chunks[3], 'mp', [(1, 0), (2, 1)])  32.1 us
    ppermute x41, starting transfers between devices, across(): return lax.ppermute(value, 'dp', [(i, i ^ bit) for i in range(count)])  30.1 us
    convert_element_type x10, other arithmetic, added(): return sum((a.astype(F32) for a in addends)).astype(BF16)  28 us
    ppermute x9, starting transfers between devices, ring(): lax.ppermute(value, 'mp', [(i, (i + k) % parts) for i in range(parts)])  16.1 us
    unnamed x122, local copies, waits for them, and re-layouts  15.8 us
  transfers between devices with their start and end apart: 61, of which 17 were waited for; matrix products, arithmetic and copies ran while one was open for 14% of the time, Pallas kernels for 49%

profile of v6, /device:TPU:0, one launch (start us, length us, event | category | flops | bytes accessed | tf_op | source)
XLA Modules:
  0.0 535.7 jit_solution(12718892374042365267)
XLA Ops:
  2.9 2.6 collective-permute-start.1
  5.4 1.6 collective-permute-start.3
  7.1 1.6 collective-permute-start.2
  10.9 15.5 %collective-permute-done.1.refs_2_ = bf16[256,1792]{1,0:T(8,128)(2,1)S(1)} collective-permute-done((bf16[256,1792]{1,0:T(8,128)(2,1)S(1)}, bf16[256,1792]{1,0:T(8,128)(2,1)S(1)}, u32[]{:S(2)}, u32[]{:S(2)}) %collective-permute-start.1) | collective-permute-done | bytes 917536 | tf_op jit(solution)/shard_map/ppermute | solution.py:703
  27.4 5.2 collective-permute-done.3.refs_4_
  33.6 1.7 collective-permute-start.7
  35.8 1.5 collective-permute-start.6
  37.4 2.3 copy.147.refs_8_
  39.7 17.2 %collective-permute-done.5.refs_3_ = bf16[256,1792]{1,0:T(8,128)(2,1)S(1)} collective-permute-done((bf16[256,1792]{1,0:T(8,128)(2,1)}, bf16[256,1792]{1,0:T(8,128)(2,1)S(1)}, u32[]{:S(2)}, u32[]{:S(2)}) %collective-permute-start.5) | collective-permute-done | bytes 917536 | tf_op jit(solution)/shard_map/ppermute | solution.py:703
  58.4 2.3 pad_maximum_fusion
  64.8 24.9 %collective-permute-done.12 = bf16[256,2048]{1,0:T(8,128)(2,1)S(1)} collective-permute-done((bf16[256,2048]{1,0:T(8,128)(2,1)}, bf16[256,2048]{1,0:T(8,128)(2,1)S(1)}, u32[]{:S(2)}, u32[]{:S(2)}) %collective-permute-start.12) | collective-permute-done | bytes 1048608 | tf_op jit(solution)/shard_map/ppermute | solution.py:718
  92.0 1.7 copy-done.17
  93.8 2.7 collective-permute-start.16
  96.6 1.5 collective-permute-start.15
  100.0 31.7 %project.2 = (bf16[2048,768]{1,0:T(8,128)(2,1)}, bf16[2048,1024]{1,0:T(8,128)(2,1)}, bf16[2048,1024]{1,0:T(8,128)(2,1)}, bf16[2048,2048]{1,0:T(8,128)(2,1)}, bf16[2048,2048]{1,0:T(8,128)(2,1)}) custom-call(s32[1]{0:T(128)} %bitcast.refs_0_, f32[1,1792]{1,0:T(1,128)} %maximum_convert_fusion.refs_1_, f32[1,2048]{1,0:T(1,128)} %bitcast.99, ...), custom_call_target="tpu_custom_call" | custom-call | tf_op jit(solution)/shard_map/project/pallas_call | solution.py:41
  132.6 1.9 collective-permute-start.17
  136.4 31.7 %project.3 = (bf16[2048,768]{1,0:T(8,128)(2,1)}, bf16[2048,1024]{1,0:T(8,128)(2,1)}, bf16[2048,1024]{1,0:T(8,128)(2,1)}, bf16[2048,2048]{1,0:T(8,128)(2,1)}, bf16[2048,2048]{1,0:T(8,128)(2,1)}) custom-call(s32[1]{0:T(128)} %bitcast.refs_0_, ...), custom_call_target="tpu_custom_call", output_to_operand_aliasing={{0}: (17, {}), {1}: (18, {}), {2}: (19, {}), {3}: (20, {}),... | custom-call | tf_op jit(solution)/shard_map/project/pallas_call | solution.py:41
  170.6 14.9 %attend.1 = (bf16[2048,256]{1,0:T(8,128)(2,1)}, f32[4,8,1024]{2,1,0:T(8,128)}) custom-call(bf16[2048,768]{1,0:T(8,128)(2,1)} %get-tuple-element.189.refs_6_.refs_0_.refs_1_.refs_2_, bf16[2048,768]{1,0:T(8,128)(2,1)} %get-tuple-element.189.refs_6_.refs_0_.refs_1_.refs_2_, bf16[2048,768]{1,0:T(8,128)(2,1)} %get-tuple-element.189.refs_6_.refs_0_.refs_1_.refs_2_, ...), custom_call_target="tpu_custom_call" | custom-call | tf_op jit(solution)/shard_map/attend/pallas_call | solution.py:41
  186.9 3.8 pad_maximum_fusion.1.refs_11_
  190.7 1.6 collective-permute-start.23
  192.4 1.8 collective-permute-start.24
  194.2 18.9 %branch_sums.1 = (bf16[4,256,2048]{2,1,0:T(8,128)(2,1)}, bf16[4,256,2048]{2,1,0:T(8,128)(2,1)}) custom-call(s32[1]{0:T(128)} %bitcast.refs_0_, bf16[2048,256]{1,0:T(8,128)(2,1)} %get-tuple-element.194.refs_10_.refs_1_.refs_2_.refs_4_, bf16[2048,1024]{1,0:T(8,128)(2,1)} %get-tuple-element.195.refs_2_.refs_3_, ...), custom_call_target="tpu_custom_call" | custom-call | tf_op jit(solution)/shard_map/branch_sums/pallas_call | solution.py:41
  213.1 7.2 %collective-permute-done.24 = bf16[256,2048]{1,0:T(8,128)(2,1)} collective-permute-done((bf16[256,2048]{1,0:T(8,128)(2,1)}, bf16[256,2048]{1,0:T(8,128)(2,1)}, u32[]{:S(2)}, u32[]{:S(2)}) %collective-permute-start.24) | collective-permute-done | bytes 1048608 | tf_op jit(solution)/shard_map/ppermute | solution.py:718
  220.4 2.9 add.230.refs_2_
  223.8 20.3 %grad_in.2 = (bf16[2048,256]{1,0:T(8,128)(2,1)}, bf16[2048,1024]{1,0:T(8,128)(2,1)}, bf16[2048,2048]{1,0:T(8,128)(2,1)}, f32[8,1024]{1,0:T(8,128)}, f32[8,2048]{1,0:T(8,128)}) custom-call(s32[1]{0:T(128)} %bitcast.refs_0_, bf16[2048,1024]{1,0:T(8,128)(2,1)} %get-tuple-element.217.refs_1_, bf16[256,2048]{1,0:T(8,128)(2,1)} %get-tuple-element.202.refs_2_, ...), custom_call_target="tpu_custom_call" | custom-call | tf_op jit(solution)/shard_map/grad_in/pallas_call | solution.py:41
  244.2 2.9 fusion.19.refs_20_
  247.1 4.5 collective-permute-start.27
  251.6 1.8 collective-permute-start.28
  253.9 20.2 %grad_in.3 = (bf16[2048,256]{1,0:T(8,128)(2,1)}, bf16[2048,1024]{1,0:T(8,128)(2,1)}, bf16[2048,2048]{1,0:T(8,128)(2,1)}, f32[8,1024]{1,0:T(8,128)}, f32[8,2048]{1,0:T(8,128)}) custom-call(s32[1]{0:T(128)} %bitcast.refs_0_, bf16[2048,1024]{1,0:T(8,128)(2,1)} %get-tuple-element.217.refs_1_, ...), custom_call_target="tpu_custom_call", output_to_operand_aliasing={{0}: (16, {}), {1}: (17, {}), {2}: (18, {})} | custom-call | tf_op jit(solution)/shard_map/grad_in/pallas_call | solution.py:41
  274.2 20.6 %weight_grads.3 = (bf16[2,1280,256]{2,1,0:T(8,128)(2,1)}, bf16[2,1280,256]{2,1,0:T(8,128)(2,1)}, bf16[1,1280,256]{2,1,0:T(8,128)(2,1)}, bf16[1,1280,256]{2,1,0:T...) custom-call(s32[8]{0:T(128)} %broadcast_xor_fusion.refs_0_, ...), custom_call_target="tpu_custom_call" | custom-call | tf_op jit(solution)/shard_map/weight_grads/pallas_call | solution.py:41
  296.9 5.6 %fusion.16 = (bf16[256,2048]{1,0:T(8,128)(2,1)}, bf16[256,2048]{1,0:T(8,128)(2,1)}) fusion(bf16[256,2048]{1,0:T(8,128)(2,1)} %get-tuple-element.229, bf16[4,256,2048]{2,1,0:T(8,128)(2,1)} %get-tuple-element.220, bf16[4,256,2048]{2,1,0:T(8,128)(2,1)} %get-tuple-element.213.refs_3_, bf16[256,2048]{1,0:T(8,128)(2,1)} %get-tuple-element.228), kind=kLoop, calls=%fused_computation.27 | loop fusion | flops 6291456 | bytes 8388608 | tf_op jit(solution)/shard_map/convert_element_type | solution.py:723
  303.4 25.2 %attend_back.1 = (bf16[2048,256]{1,0:T(8,128)(2,1)}, bf16[2048,256]{1,0:T(8,128)(2,1)}, bf16[2048,256]{1,0:T(8,128)(2,1)}, f32[4,8,128]{2,1,0:T(8,128)}) custom-call(bf16[2048,768]{1,0:T(8,128)(2,1)} %get-tuple-element.189.refs_6_.refs_0_.refs_1_.refs_2_, bf16[2048,768]{1,0:T(8,128)(2,1)} %get-tuple-element.189.refs_6_.refs_0_.refs_1_.refs_2_, ...), custom_call_target="tpu_custom_call" | custom-call | tf_op jit(solution)/shard_map/attend_back/pallas_call | solution.py:41
  329.1 3.7 collective-permute-start.30
  332.8 13.6 %grad_normed_sums.3 = (bf16[1,256,2048]{2,1,0:T(8,128)(2,1)}, bf16[1,256,2048]{2,1,0:T(8,128)(2,1)}, f32[8,2048]{1,0:T(8,128)}) custom-call(s32[1]{0:T(128)} %bitcast.refs_0_, bf16[2048,256]{1,0:T(8,128)(2,1)} %get-tuple-element.232.refs_2_.refs_1_, bf16[2048,256]{1,0:T(8,128)(2,1)} %get-tuple-element.235.refs_2_.refs_3_, ...), custom_call_target="tpu_custom_call" | custom-call | tf_op jit(solution)/shard_map/grad_normed_sums/pallas_call | solution.py:41
  347.5 2.1 add_convert_fusion.3.refs_16_
  352.7 2.1 add_convert_fusion.4.refs_15_
  357.0 20.1 %grad_normed_sums.4 = (bf16[2,256,2048]{2,1,0:T(8,128)(2,1)}, bf16[2,256,2048]{2,1,0:T(8,128)(2,1)}, f32[8,2048]{1,0:T(8,128)}) custom-call(s32[1]{0:T(128)} %bitcast.refs_0_, bf16[2048,256]{1,0:T(8,128)(2,1)} %get-tuple-element.232.refs_2_.refs_1_, bf16[2048,256]{1,0:T(8,128)(2,1)} %get-tuple-element.235.refs_2_.refs_3_, ...), custom_call_target="tpu_custom_call" | custom-call | tf_op jit(solution)/shard_map/grad_normed_sums/pallas_call | solution.py:41
  378.0 3.0 fusion.20.refs_15_
  381.0 2.3 collective-permute-start.39
  383.3 2.1 collective-permute-start.40
  385.5 2.2 fusion.21.refs_16_.refs_2_
  387.7 13.7 %grad_normed_sums.5 = (bf16[1,256,2048]{2,1,0:T(8,128)(2,1)}, bf16[1,256,2048]{2,1,0:T(8,128)(2,1)}, f32[8,2048]{1,0:T(8,128)}) custom-call(s32[1]{0:T(128)} %bitcast.refs_0_, bf16[2048,256]{1,0:T(8,128)(2,1)} %get-tuple-element.232.refs_2_.refs_1_, bf16[2048,256]{1,0:T(8,128)(2,1)} %get-tuple-element.235.refs_2_.refs_3_, ...), custom_call_target="tpu_custom_call" | custom-call | tf_op jit(solution)/shard_map/grad_normed_sums/pallas_call | solution.py:41
  402.4 1.6 collective-permute-start.38
  407.6 17.6 %weight_grads.4 = (bf16[2,256,1024]{2,1,0:T(8,128)(2,1)}, bf16[2,256,1024]{2,1,0:T(8,128)(2,1)}, bf16[1,256,1024]{2,1,0:T(8,128)(2,1)}, bf16[1,256,1024]{2,1,0:T...) custom-call(s32[8]{0:T(128)} %broadcast_xor_fusion.refs_0_, ...), custom_call_target="tpu_custom_call" | custom-call | tf_op jit(solution)/shard_map/weight_grads/pallas_call | solution.py:41
  428.7 5.5 %fusion.14 = (bf16[256,2048]{1,0:T(8,128)(2,1)}, bf16[256,2048]{1,0:T(8,128)(2,1)}) fusion(bf16[256,2048]{1,0:T(8,128)(2,1)} %get-tuple-element.269, bf16[2,256,2048]{2,1,0:T(8,128)(2,1)} %get-tuple-element.264, bf16[2,256,2048]{2,1,0:T(8,128)(2,1)} %get-tuple-element.255, bf16[256,2048]{1,0:T(8,128)(2,1)} %get-tuple-element.265), kind=kLoop, calls=%fused_computation.23 | loop fusion | flops 6291456 | bytes 8388608 | tf_op jit(solution)/shard_map/convert_element_type | solution.py:723
  434.4 1.7 slice_bitcast_fusion.1
  436.1 15.1 %weight_grads.5 = (bf16[2,256,768]{2,1,0:T(8,128)(2,1)}, bf16[2,256,768]{2,1,0:T(8,128)(2,1)}, bf16[1,256,768]{2,1,0:T(8,128)(2,1)}, bf16[1,256,768]{2,1,0:T(8,1...) custom-call(s32[8]{0:T(128)} %broadcast_xor_fusion.refs_0_, ...), custom_call_target="tpu_custom_call" | custom-call | tf_op jit(solution)/shard_map/weight_grads/pallas_call | solution.py:41
  454.5 2.0 add_convert_fusion.6
  457.7 2.0 add_convert_fusion.7
  462.6 1.6 maximum_select_fusion.1
  465.7 2.3 fusion.29
  468.0 3.6 collective-permute-start.47
  471.6 3.2 collective-permute-done.49.refs_0_
  474.9 13.0 %collective-permute-done.51.refs_3_ = bf16[2,256,768]{2,1,0:T(8,128)(2,1)} collective-permute-done((bf16[2,256,768]{2,1,0:T(8,128)(2,1)}, bf16[2,256,768]{2,1,0:T(8,128)(2,1)}, u32[]{:S(2)}, u32[]{:S(2)}) %collective-permute-start.51) | collective-permute-done | bytes 786464 | tf_op jit(solution)/shard_map/ppermute | solution.py:703
  487.9 2.6 collective-permute-done.52.refs_4_
  491.4 2.7 add_bitcast_fusion
  494.1 2.4 fusion.22
  496.4 1.9 add_convert_fusion.10
  500.4 2.9 collective-permute-start.55
  506.1 2.8 collective-permute-done.56
  511.7 7.4 %collective-permute-done.58 = bf16[1,256,768]{2,1,0:T(8,128)(2,1)} collective-permute-done((bf16[1,256,768]{2,1,0:T(8,128)(2,1)}, bf16[1,256,768]{2,1,0:T(8,128)(2,1)}, u32[]{:S(2)}, u32[]{:S(2)}) %collective-permute-start.58) | collective-permute-done | bytes 393248 | tf_op jit(solution)/shard_map/ppermute | solution.py:703
  523.1 1.6 maximum_select_fusion
  525.4 2.8 fusion.27
  528.2 5.1 fusion.8
  (293 shorter events, 67.1 us)
Async XLA Ops:
  0.6 97.5 %copy-start = (bf16[3,512]{1,0:T(4,128)(2,1)S(1)}, bf16[3,512]{1,0:T(4,128)(2,1)}, u32[]{:S(2)}) copy-start(bf16[3,512]{1,0:T(4,128)(2,1)} %param.22) | copy-start | bytes 9220
  2.3 4.8 collective-permute-start
  2.9 23.6 %collective-permute-start.1 = (bf16[256,1792]{1,0:T(8,128)(2,1)S(1)}, bf16[256,1792]{1,0:T(8,128)(2,1)S(1)}, u32[]{:S(2)}, u32[]{:S(2)}) collective-permute-start(bf16[256,1792]{1,0:T(8,128)(2,1)S(1)} %pad_maximum_fusion.3.refs_0_), channel_id=1, source_target_pairs={{0,8},{4,12},{8,0},{12,4},{16,24},{20,28},{24,16},{28,20},{1,9},{5... | collective-permute-start | bytes 2752520 | tf_op jit(solution)/shard_map/ppermute | solution.py:703
  5.4 27.1 %collective-permute-start.3 = (bf16[256,2048]{1,0:T(8,128)(2,1)S(1)}, bf16[256,2048]{1,0:T(8,128)(2,1)S(1)}, u32[]{:S(2)}, u32[]{:S(2)}) collective-permute-start(bf16[256,2048]{1,0:T(8,128)(2,1)S(1)} %copy-done.6), channel_id=1, source_target_pairs={{0,1},{1,2},{2,3},{3,0},{4,5},{5,6},{6,7},{7,4},{8,9},{9,10},{10,1... | collective-permute-start | bytes 3145736 | tf_op jit(solution)/shard_map/ppermute | solution.py:707
  7.1 26.4 %collective-permute-start.2 = (bf16[256,1792]{1,0:T(8,128)(2,1)S(1)}, bf16[256,1792]{1,0:T(8,128)(2,1)}, u32[]{:S(2)}, u32[]{:S(2)}) collective-permute-start(bf16[256,1792]{1,0:T(8,128)(2,1)S(1)} %collective-permute-done.refs_1_), channel_id=1, source_target_pairs={{0,16},{4,20},{8,24},{12,28},{16,0},{20,4},{24,8},{28,12},{1,17},{... | collective-permute-start | bytes 2752520 | tf_op jit(solution)/shard_map/ppermute | solution.py:703
  8.8 2.2 collective-permute-start.4
  10.9 22.6 %copy-start.10 = (bf16[1280,256]{1,0:T(8,128)(2,1)}, bf16[1280,256]{1,0:T(8,128)(2,1)S(1)}, u32[]{:S(2)}) copy-start(bf16[1280,256]{1,0:T(8,128)(2,1)S(1)} %collective-permute-done.4.refs_7_.refs_10_) | copy-start | bytes 1966084
  33.6 24.8 %collective-permute-start.7 = (bf16[256,2048]{1,0:T(8,128)(2,1)}, bf16[256,2048]{1,0:T(8,128)(2,1)}, u32[]{:S(2)}, u32[]{:S(2)}) collective-permute-start(bf16[256,2048]{1,0:T(8,128)(2,1)} %get-tuple-element.161), channel_id=1, source_target_pairs={{0,3},{1,0},{2,1},{3,2},{4,7},{5,4},{6,5},{7,6},{8,11},{9,8},{10,9... | collective-permute-start | bytes 3145736 | tf_op jit(solution)/shard_map/ppermute | solution.py:707
  35.3 21.6 %collective-permute-start.5 = (bf16[256,1792]{1,0:T(8,128)(2,1)}, bf16[256,1792]{1,0:T(8,128)(2,1)S(1)}, u32[]{:S(2)}, u32[]{:S(2)}) collective-permute-start(bf16[256,1792]{1,0:T(8,128)(2,1)} %get-tuple-element.157.refs_1_), channel_id=1, source_target_pairs={{0,8},{4,12},{8,0},{12,4},{16,24},{20,28},{24,16},{28,20},{1,9},{5... | collective-permute-start | bytes 2752520 | tf_op jit(solution)/shard_map/ppermute | solution.py:703
  35.8 21.1 %collective-permute-start.6 = (bf16[256,1792]{1,0:T(8,128)(2,1)}, bf16[256,1792]{1,0:T(8,128)(2,1)}, u32[]{:S(2)}, u32[]{:S(2)}) collective-permute-start(bf16[256,1792]{1,0:T(8,128)(2,1)} %get-tuple-element.156.refs_0_), channel_id=1, source_target_pairs={{0,16},{4,20},{8,24},{12,28},{16,0},{20,4},{24,8},{28,12},{1,17},{... | collective-permute-start | bytes 2752520 | tf_op jit(solution)/shard_map/ppermute | solution.py:703
  60.7 31.3 %collective-permute-start.8 = (bf16[3,256,2048]{2,1,0:T(8,128)(2,1)S(1)}, bf16[3,256,2048]{2,1,0:T(8,128)(2,1)S(1)}, u32[]{:S(2)}, u32[]{:S(2)}) collective-permute-start(bf16[3,256,2048]{2,1,0:T(8,128)(2,1)S(1)} %pad_maximum_fusion), channel_id=1, source_target_pairs={{0,4},{4,0},{8,12},{12,8},{16,20},{20,16},{24,28},{28,24},{1,5},{5... | collective-permute-start | bytes 9437192 | tf_op jit(solution)/shard_map/ppermute | solution.py:703
  60.8 4.0 collective-permute-start.11
  61.6 28.1 %collective-permute-start.12 = (bf16[256,2048]{1,0:T(8,128)(2,1)}, bf16[256,2048]{1,0:T(8,128)(2,1)S(1)}, u32[]{:S(2)}, u32[]{:S(2)}) collective-permute-start(bf16[256,2048]{1,0:T(8,128)(2,1)} %get-tuple-element.163.refs_9_), channel_id=1, source_target_pairs={{1,0},{2,1},{5,4},{6,5},{9,8},{10,9},{13,12},{14,13},{17,16},{18,1... | collective-permute-start | bytes 3145736 | tf_op jit(solution)/shard_map/ppermute | solution.py:718
  62.9 28.2 %collective-permute-start.10 = (bf16[256,1792]{1,0:T(8,128)(2,1)}, bf16[256,1792]{1,0:T(8,128)(2,1)S(1)}, u32[]{:S(2)}, u32[]{:S(2)}) collective-permute-start(bf16[256,1792]{1,0:T(8,128)(2,1)} %get-tuple-element.169.refs_5_), channel_id=1, source_target_pairs={{0,8},{4,12},{8,0},{12,4},{16,24},{20,28},{24,16},{28,20},{1,9},{5... | collective-permute-start | bytes 2752520 | tf_op jit(solution)/shard_map/ppermute | solution.py:703
  63.3 27.8 %collective-permute-start.9 = (bf16[256,1792]{1,0:T(8,128)(2,1)S(1)}, bf16[256,1792]{1,0:T(8,128)(2,1)S(1)}, u32[]{:S(2)}, u32[]{:S(2)}) collective-permute-start(bf16[256,1792]{1,0:T(8,128)(2,1)S(1)} %copy-done.5), channel_id=1, source_target_pairs={{0,16},{4,20},{8,24},{12,28},{16,0},{20,4},{24,8},{28,12},{1,17},{... | collective-permute-start | bytes 2752520 | tf_op jit(solution)/shard_map/ppermute | solution.py:703
  93.8 38.0 %collective-permute-start.16 = (bf16[256,2048]{1,0:T(8,128)(2,1)}, bf16[256,2048]{1,0:T(8,128)(2,1)}, u32[]{:S(2)}, u32[]{:S(2)}) collective-permute-start(bf16[256,2048]{1,0:T(8,128)(2,1)} %get-tuple-element.180.refs_19_.refs_4_), channel_id=1, source_target_pairs={{0,1},{1,2},{2,3},{3,0},{4,5},{5,6},{6,7},{7,4},{8,9},{9,10},{10,1... | collective-permute-start | bytes 3145736 | tf_op jit(solution)/shard_map/ppermute | solution.py:707
  96.5 35.2 %collective-permute-start.14 = (bf16[1280,256]{1,0:T(8,128)(2,1)}, bf16[1280,256]{1,0:T(8,128)(2,1)S(1)}, u32[]{:S(2)}, u32[]{:S(2)}) collective-permute-start(bf16[1280,256]{1,0:T(8,128)(2,1)} %get-tuple-element.186.refs_0_), channel_id=1, source_target_pairs={{0,8},{4,12},{8,0},{12,4},{16,24},{20,28},{24,16},{28,20},{1,9},{5... | collective-permute-start | bytes 1966088 | tf_op jit(solution)/shard_map/ppermute | solution.py:703
  96.6 35.1 %collective-permute-start.15 = (bf16[1280,256]{1,0:T(8,128)(2,1)}, bf16[1280,256]{1,0:T(8,128)(2,1)}, u32[]{:S(2)}, u32[]{:S(2)}) collective-permute-start(bf16[1280,256]{1,0:T(8,128)(2,1)} %get-tuple-element.187.refs_1_), channel_id=1, source_target_pairs={{0,16},{4,20},{8,24},{12,28},{16,0},{20,4},{24,8},{28,12},{1,17},{... | collective-permute-start | bytes 1966088 | tf_op jit(solution)/shard_map/ppermute | solution.py:703
  98.1 38.2 %collective-permute-start.13 = (bf16[256,2048]{1,0:T(8,128)(2,1)}, bf16[256,2048]{1,0:T(8,128)(2,1)}, u32[]{:S(2)}, u32[]{:S(2)}) collective-permute-start(bf16[256,2048]{1,0:T(8,128)(2,1)} %get-tuple-element.171.refs_10_), channel_id=1, source_target_pairs={{0,4},{4,0},{8,12},{12,8},{16,20},{20,16},{24,28},{28,24},{1,5},{5... | collective-permute-start | bytes 3145736 | tf_op jit(solution)/shard_map/ppermute | solution.py:703
  132.6 35.5 %collective-permute-start.17 = (bf16[1280,256]{1,0:T(8,128)(2,1)}, bf16[1280,256]{1,0:T(8,128)(2,1)S(1)}, u32[]{:S(2)}, u32[]{:S(2)}) collective-permute-start(bf16[1280,256]{1,0:T(8,128)(2,1)} %get-tuple-element.190.refs_1_), channel_id=1, source_target_pairs={{0,8},{4,12},{8,0},{12,4},{16,24},{20,28},{24,16},{28,20},{1,9},{5... | collective-permute-start | bytes 1966088 | tf_op jit(solution)/shard_map/ppermute | solution.py:703
  134.5 33.6 %collective-permute-start.18 = (bf16[1280,256]{1,0:T(8,128)(2,1)}, bf16[1280,256]{1,0:T(8,128)(2,1)}, u32[]{:S(2)}, u32[]{:S(2)}) collective-permute-start(bf16[1280,256]{1,0:T(8,128)(2,1)} %get-tuple-element.188.refs_22_.refs_0_), channel_id=1, source_target_pairs={{0,16},{4,20},{8,24},{12,28},{16,0},{20,4},{24,8},{28,12},{1,17},{... | collective-permute-start | bytes 1966088 | tf_op jit(solution)/shard_map/ppermute | solution.py:703
  135.0 50.6 %collective-permute-start.21 = (bf16[256,2048]{1,0:T(8,128)(2,1)}, bf16[256,2048]{1,0:T(8,128)(2,1)}, u32[]{:S(2)}, u32[]{:S(2)}) collective-permute-start(bf16[256,2048]{1,0:T(8,128)(2,1)} %get-tuple-element.202.refs_2_), channel_id=1, source_target_pairs={{0,3},{1,0},{2,1},{3,2},{4,7},{5,4},{6,5},{7,6},{8,11},{9,8},{10,9... | collective-permute-start | bytes 3145736 | tf_op jit(solution)/shard_map/ppermute | solution.py:707
  169.0 16.6 %collective-permute-start.19 = (bf16[1280,256]{1,0:T(8,128)(2,1)}, bf16[1280,256]{1,0:T(8,128)(2,1)S(1)}, u32[]{:S(2)}, u32[]{:S(2)}) collective-permute-start(bf16[1280,256]{1,0:T(8,128)(2,1)} %get-tuple-element.197.refs_2_), channel_id=1, source_target_pairs={{0,16},{4,20},{8,24},{12,28},{16,0},{20,4},{24,8},{28,12},{1,17},{... | collective-permute-start | bytes 1966088 | tf_op jit(solution)/shard_map/ppermute | solution.py:703
  170.5 16.4 %collective-permute-start.20 = (bf16[1280,256]{1,0:T(8,128)(2,1)}, bf16[1280,256]{1,0:T(8,128)(2,1)}, u32[]{:S(2)}, u32[]{:S(2)}) collective-permute-start(bf16[1280,256]{1,0:T(8,128)(2,1)} %get-tuple-element.200.refs_5_), channel_id=1, source_target_pairs={{0,8},{4,12},{8,0},{12,4},{16,24},{20,28},{24,16},{28,20},{1,9},{5... | collective-permute-start | bytes 1966088 | tf_op jit(solution)/shard_map/ppermute | solution.py:703
  190.7 32.6 %collective-permute-start.22 = (bf16[3,256,2048]{2,1,0:T(8,128)(2,1)}, bf16[3,256,2048]{2,1,0:T(8,128)(2,1)}, u32[]{:S(2)}, u32[]{:S(2)}) collective-permute-start(bf16[3,256,2048]{2,1,0:T(8,128)(2,1)} %pad_maximum_fusion.1.refs_11_), channel_id=1, source_target_pairs={{0,4},{4,0},{8,12},{12,8},{16,20},{20,16},{24,28},{28,24},{1,5},{5... | collective-permute-start | bytes 9437192 | tf_op jit(solution)/shard_map/ppermute | solution.py:703
  190.7 22.4 %collective-permute-start.23 = (bf16[256,2048]{1,0:T(8,128)(2,1)}, bf16[256,2048]{1,0:T(8,128)(2,1)}, u32[]{:S(2)}, u32[]{:S(2)}) collective-permute-start(bf16[256,2048]{1,0:T(8,128)(2,1)} %get-tuple-element.211.refs_3_), channel_id=1, source_target_pairs={{1,2},{2,3},{5,6},{6,7},{9,10},{10,11},{13,14},{14,15},{17,18},{18... | collective-permute-start | bytes 3145736 | tf_op jit(solution)/shard_map/ppermute | solution.py:717
  192.4 28.0 %collective-permute-start.24 = (bf16[256,2048]{1,0:T(8,128)(2,1)}, bf16[256,2048]{1,0:T(8,128)(2,1)}, u32[]{:S(2)}, u32[]{:S(2)}) collective-permute-start(bf16[256,2048]{1,0:T(8,128)(2,1)} %get-tuple-element.212.refs_4_), channel_id=1, source_target_pairs={{1,0},{2,1},{5,4},{6,5},{9,8},{10,9},{13,12},{14,13},{17,16},{18,1... | collective-permute-start | bytes 3145736 | tf_op jit(solution)/shard_map/ppermute | solution.py:718
  223.3 20.9 %collective-permute-start.25 = (bf16[4,256,2048]{2,1,0:T(8,128)(2,1)}, bf16[4,256,2048]{2,1,0:T(8,128)(2,1)}, u32[]{:S(2)}, u32[]{:S(2)}) collective-permute-start(bf16[4,256,2048]{2,1,0:T(8,128)(2,1)} %get-tuple-element.215.refs_14_), channel_id=1, source_target_pairs={{0,4},{4,0},{8,12},{12,8},{16,20},{20,16},{24,28},{28,24},{1,5},{5... | collective-permute-start | bytes 12582920 | tf_op jit(solution)/shard_map/ppermute | solution.py:703
  223.3 20.9 %collective-permute-start.26 = (bf16[256,2048]{1,0:T(8,128)(2,1)}, bf16[256,2048]{1,0:T(8,128)(2,1)}, u32[]{:S(2)}, u32[]{:S(2)}) collective-permute-start(bf16[256,2048]{1,0:T(8,128)(2,1)} %get-tuple-element.216.refs_5_), channel_id=1, source_target_pairs={{0,4},{4,0},{8,12},{12,8},{16,20},{20,16},{24,28},{28,24},{1,5},{5... | collective-permute-start | bytes 3145736 | tf_op jit(solution)/shard_map/ppermute | solution.py:703
  247.1 49.7 %collective-permute-start.27 = (bf16[256,2048]{1,0:T(8,128)(2,1)}, bf16[256,2048]{1,0:T(8,128)(2,1)}, u32[]{:S(2)}, u32[]{:S(2)}) collective-permute-start(bf16[256,2048]{1,0:T(8,128)(2,1)} %fusion.19.refs_20_), channel_id=1, source_target_pairs={{0,1},{1,2},{4,5},{5,6},{8,9},{9,10},{12,13},{13,14},{16,17},{17,1... | collective-permute-start | bytes 3145736 | tf_op jit(solution)/shard_map/ppermute | solution.py:727
  251.6 45.3 %collective-permute-start.28 = (bf16[256,2048]{1,0:T(8,128)(2,1)}, bf16[256,2048]{1,0:T(8,128)(2,1)}, u32[]{:S(2)}, u32[]{:S(2)}) collective-permute-start(bf16[256,2048]{1,0:T(8,128)(2,1)} %fusion.19.refs_20_), channel_id=1, source_target_pairs={{3,2},{2,1},{7,6},{6,5},{11,10},{10,9},{15,14},{14,13},{19,18},{18... | collective-permute-start | bytes 3145736 | tf_op jit(solution)/shard_map/ppermute | solution.py:728
  294.7 51.7 %collective-permute-start.31 = (bf16[2,1280,256]{2,1,0:T(8,128)(2,1)}, bf16[2,1280,256]{2,1,0:T(8,128)(2,1)}, u32[]{:S(2)}, u32[]{:S(2)}) collective-permute-start(bf16[2,1280,256]{2,1,0:T(8,128)(2,1)} %get-tuple-element.227.refs_2_.refs_9_), channel_id=1, source_target_pairs={{0,16},{4,20},{8,24},{12,28},{16,0},{20,4},{24,8},{28,12},{1,17},{... | collective-permute-start | bytes 3932168 | tf_op jit(solution)/shard_map/ppermute | solution.py:703
  295.8 50.6 %collective-permute-start.32 = (bf16[2,1280,256]{2,1,0:T(8,128)(2,1)}, bf16[2,1280,256]{2,1,0:T(8,128)(2,1)}, u32[]{:S(2)}, u32[]{:S(2)}) collective-permute-start(bf16[2,1280,256]{2,1,0:T(8,128)(2,1)} %get-tuple-element.241), channel_id=1, source_target_pairs={{0,8},{4,12},{8,0},{12,4},{16,24},{20,28},{24,16},{28,20},{1,9},{5... | collective-permute-start | bytes 3932168 | tf_op jit(solution)/shard_map/ppermute | solution.py:703
  302.5 26.6 %collective-permute-start.29 = (bf16[256,2048]{1,0:T(8,128)(2,1)}, bf16[256,2048]{1,0:T(8,128)(2,1)}, u32[]{:S(2)}, u32[]{:S(2)}) collective-permute-start(bf16[256,2048]{1,0:T(8,128)(2,1)} %get-tuple-element.304.refs_10_), channel_id=1, source_target_pairs={{0,1},{1,2},{2,3},{3,0},{4,5},{5,6},{6,7},{7,4},{8,9},{9,10},{10,1... | collective-permute-start | bytes 3145736 | tf_op jit(solution)/shard_map/ppermute | solution.py:707
  329.1 48.0 %collective-permute-start.30 = (bf16[256,2048]{1,0:T(8,128)(2,1)}, bf16[256,2048]{1,0:T(8,128)(2,1)}, u32[]{:S(2)}, u32[]{:S(2)}) collective-permute-start(bf16[256,2048]{1,0:T(8,128)(2,1)} %get-tuple-element.234), channel_id=1, source_target_pairs={{0,3},{1,0},{2,1},{3,2},{4,7},{5,4},{6,5},{7,6},{8,11},{9,8},{10,9... | collective-permute-start | bytes 3145736 | tf_op jit(solution)/shard_map/ppermute | solution.py:707
  349.6 27.5 %collective-permute-start.34 = (bf16[1,1280,256]{2,1,0:T(8,128)(2,1)}, bf16[1,1280,256]{2,1,0:T(8,128)(2,1)S(1)}, u32[]{:S(2)}, u32[]{:S(2)}) collective-permute-start(bf16[1,1280,256]{2,1,0:T(8,128)(2,1)} %add_convert_fusion.3.refs_16_), channel_id=1, source_target_pairs={{0,16},{4,20},{8,24},{12,28},{16,0},{20,4},{24,8},{28,12},{1,17},{... | collective-permute-start | bytes 1966088 | tf_op jit(solution)/shard_map/ppermute | solution.py:703
  352.2 24.9 %collective-permute-start.35 = (bf16[1,128,2048]{2,1,0:T(8,128)(2,1)}, bf16[1,128,2048]{2,1,0:T(8,128)(2,1)}, u32[]{:S(2)}, u32[]{:S(2)}) collective-permute-start(bf16[1,128,2048]{2,1,0:T(8,128)(2,1)} %get-tuple-element.312), channel_id=1, source_target_pairs={{0,4},{4,0},{8,12},{12,8},{16,20},{20,16},{24,28},{28,24},{1,5},{5... | collective-permute-start | bytes 1572872 | tf_op jit(solution)/shard_map/ppermute | solution.py:703
  352.2 24.9 %collective-permute-start.36 = (bf16[1,128,2048]{2,1,0:T(8,128)(2,1)}, bf16[1,128,2048]{2,1,0:T(8,128)(2,1)}, u32[]{:S(2)}, u32[]{:S(2)}) collective-permute-start(bf16[1,128,2048]{2,1,0:T(8,128)(2,1)} %get-tuple-element.311), channel_id=1, source_target_pairs={{0,4},{4,0},{8,12},{12,8},{16,20},{20,16},{24,28},{28,24},{1,5},{5... | collective-permute-start | bytes 1572872 | tf_op jit(solution)/shard_map/ppermute | solution.py:703
  354.8 22.4 %collective-permute-start.33 = (bf16[1,1280,256]{2,1,0:T(8,128)(2,1)}, bf16[1,1280,256]{2,1,0:T(8,128)(2,1)}, u32[]{:S(2)}, u32[]{:S(2)}) collective-permute-start(bf16[1,1280,256]{2,1,0:T(8,128)(2,1)} %add_convert_fusion.4.refs_15_), channel_id=1, source_target_pairs={{0,8},{4,12},{8,0},{12,4},{16,24},{20,28},{24,16},{28,20},{1,9},{5... | collective-permute-start | bytes 1966088 | tf_op jit(solution)/shard_map/ppermute | solution.py:703
  378.0 48.8 %collective-permute-start.37 = (bf16[2,256,2048]{2,1,0:T(8,128)(2,1)}, bf16[2,256,2048]{2,1,0:T(8,128)(2,1)}, u32[]{:S(2)}, u32[]{:S(2)}) collective-permute-start(bf16[2,256,2048]{2,1,0:T(8,128)(2,1)} %get-tuple-element.256), channel_id=1, source_target_pairs={{0,4},{4,0},{8,12},{12,8},{16,20},{20,16},{24,28},{28,24},{1,5},{5... | collective-permute-start | bytes 6291464 | tf_op jit(solution)/shard_map/ppermute | solution.py:703
  381.0 45.8 %collective-permute-start.39 = (bf16[256,2048]{1,0:T(8,128)(2,1)}, bf16[256,2048]{1,0:T(8,128)(2,1)}, u32[]{:S(2)}, u32[]{:S(2)}) collective-permute-start(bf16[256,2048]{1,0:T(8,128)(2,1)} %fusion.20.refs_15_), channel_id=1, source_target_pairs={{0,1},{1,2},{4,5},{5,6},{8,9},{9,10},{12,13},{13,14},{16,17},{17,1... | collective-permute-start | bytes 3145736 | tf_op jit(solution)/shard_map/ppermute | solution.py:727
  383.3 43.5 %collective-permute-start.40 = (bf16[256,2048]{1,0:T(8,128)(2,1)}, bf16[256,2048]{1,0:T(8,128)(2,1)}, u32[]{:S(2)}, u32[]{:S(2)}) collective-permute-start(bf16[256,2048]{1,0:T(8,128)(2,1)} %fusion.20.refs_15_), channel_id=1, source_target_pairs={{3,2},{2,1},{7,6},{6,5},{11,10},{10,9},{15,14},{14,13},{19,18},{18... | collective-permute-start | bytes 3145736 | tf_op jit(solution)/shard_map/ppermute | solution.py:728
  402.4 23.4 %collective-permute-start.38 = (f32[7936]{0:T(1024)S(1)}, f32[7936]{0:T(1024)S(1)}, u32[]{:S(2)}, u32[]{:S(2)}) collective-permute-start(f32[7936]{0:T(1024)S(1)} %pad_maximum_fusion.7.refs_4_), channel_id=1, source_target_pairs={{0,8},{4,12},{8,0},{12,4},{16,24},{20,28},{24,16},{28,20},{1,9},{5... | collective-permute-start | bytes 95240 | tf_op jit(solution)/shard_map/ppermute | solution.py:703
  425.2 26.0 %collective-permute-start.42 = (bf16[2,256,1024]{2,1,0:T(8,128)(2,1)}, bf16[2,256,1024]{2,1,0:T(8,128)(2,1)}, u32[]{:S(2)}, u32[]{:S(2)}) collective-permute-start(bf16[2,256,1024]{2,1,0:T(8,128)(2,1)} %get-tuple-element.263.refs_6_), channel_id=1, source_target_pairs={{0,16},{4,20},{8,24},{12,28},{16,0},{20,4},{24,8},{28,12},{1,17},{... | collective-permute-start | bytes 3145736 | tf_op jit(solution)/shard_map/ppermute | solution.py:703
  425.8 25.4 %collective-permute-start.43 = (bf16[2,256,1024]{2,1,0:T(8,128)(2,1)}, bf16[2,256,1024]{2,1,0:T(8,128)(2,1)}, u32[]{:S(2)}, u32[]{:S(2)}) collective-permute-start(bf16[2,256,1024]{2,1,0:T(8,128)(2,1)} %get-tuple-element.268), channel_id=1, source_target_pairs={{0,8},{4,12},{8,0},{12,4},{16,24},{20,28},{24,16},{28,20},{1,9},{5... | collective-permute-start | bytes 3145736 | tf_op jit(solution)/shard_map/ppermute | solution.py:703
  427.6 23.8 %collective-permute-start.45 = (f32[7936]{0:T(1024)S(1)}, f32[7936]{0:T(1024)S(1)}, u32[]{:S(2)}, u32[]{:S(2)}) collective-permute-start(f32[7936]{0:T(1024)S(1)} %fusion.26.refs_5_), channel_id=1, source_target_pairs={{0,16},{4,20},{8,24},{12,28},{16,0},{20,4},{24,8},{28,12},{1,17},{... | collective-permute-start | bytes 95240 | tf_op jit(solution)/shard_map/ppermute | solution.py:703
  428.7 22.7 %collective-permute-start.44 = (bf16[1280,256]{1,0:T(8,128)(2,1)}, bf16[1280,256]{1,0:T(8,128)(2,1)S(1)}, u32[]{:S(2)}, u32[]{:S(2)}) collective-permute-start(bf16[1280,256]{1,0:T(8,128)(2,1)} %get-tuple-element.272), channel_id=1, source_target_pairs={{0,4},{4,0},{8,12},{12,8},{16,20},{20,16},{24,28},{28,24},{1,5},{5... | collective-permute-start | bytes 1966088 | tf_op jit(solution)/shard_map/ppermute | solution.py:703
  434.2 31.5 %collective-permute-start.41 = (bf16[256,2048]{1,0:T(8,128)(2,1)}, bf16[256,2048]{1,0:T(8,128)(2,1)}, u32[]{:S(2)}, u32[]{:S(2)}) collective-permute-start(bf16[256,2048]{1,0:T(8,128)(2,1)} %get-tuple-element.306.refs_6_), channel_id=1, source_target_pairs={{0,1},{1,2},{2,3},{3,0},{4,5},{5,6},{6,7},{7,4},{8,9},{9,10},{10,1... | collective-permute-start | bytes 3145736 | tf_op jit(solution)/shard_map/ppermute | solution.py:707
  456.5 15.1 %collective-permute-start.50 = (bf16[1,256,1024]{2,1,0:T(8,128)(2,1)}, bf16[1,256,1024]{2,1,0:T(8,128)(2,1)}, u32[]{:S(2)}, u32[]{:S(2)}) collective-permute-start(bf16[1,256,1024]{2,1,0:T(8,128)(2,1)} %add_convert_fusion.6), channel_id=1, source_target_pairs={{0,16},{4,20},{8,24},{12,28},{16,0},{20,4},{24,8},{28,12},{1,17},{... | collective-permute-start | bytes 1572872 | tf_op jit(solution)/shard_map/ppermute | solution.py:703
  459.7 15.1 %collective-permute-start.49 = (bf16[1,256,1024]{2,1,0:T(8,128)(2,1)}, bf16[1,256,1024]{2,1,0:T(8,128)(2,1)}, u32[]{:S(2)}, u32[]{:S(2)}) collective-permute-start(bf16[1,256,1024]{2,1,0:T(8,128)(2,1)} %add_convert_fusion.7), channel_id=1, source_target_pairs={{0,8},{4,12},{8,0},{12,4},{16,24},{20,28},{24,16},{28,20},{1,9},{5... | collective-permute-start | bytes 1572872 | tf_op jit(solution)/shard_map/ppermute | solution.py:703
  460.4 27.5 %collective-permute-start.51 = (bf16[2,256,768]{2,1,0:T(8,128)(2,1)}, bf16[2,256,768]{2,1,0:T(8,128)(2,1)}, u32[]{:S(2)}, u32[]{:S(2)}) collective-permute-start(bf16[2,256,768]{2,1,0:T(8,128)(2,1)} %get-tuple-element.274.refs_4_), channel_id=1, source_target_pairs={{0,16},{4,20},{8,24},{12,28},{16,0},{20,4},{24,8},{28,12},{1,17},{... | collective-permute-start | bytes 2359304 | tf_op jit(solution)/shard_map/ppermute | solution.py:703
  461.9 28.6 %collective-permute-start.52 = (bf16[2,256,768]{2,1,0:T(8,128)(2,1)}, bf16[2,256,768]{2,1,0:T(8,128)(2,1)S(1)}, u32[]{:S(2)}, u32[]{:S(2)}) collective-permute-start(bf16[2,256,768]{2,1,0:T(8,128)(2,1)} %get-tuple-element.285), channel_id=1, source_target_pairs={{0,8},{4,12},{8,0},{12,4},{16,24},{20,28},{24,16},{28,20},{1,9},{5... | collective-permute-start | bytes 2359304 | tf_op jit(solution)/shard_map/ppermute | solution.py:703
  468.0 42.6 %collective-permute-start.47 = (bf16[128,2048]{1,0:T(8,128)(2,1)}, bf16[128,2048]{1,0:T(8,128)(2,1)}, u32[]{:S(2)}, u32[]{:S(2)}) collective-permute-start(bf16[128,2048]{1,0:T(8,128)(2,1)} %get-tuple-element.310), channel_id=1, source_target_pairs={{0,3},{1,0},{2,1},{3,2},{4,7},{5,4},{6,5},{7,6},{8,11},{9,8},{10,9... | collective-permute-start | bytes 1572872 | tf_op jit(solution)/shard_map/ppermute | solution.py:707
  471.6 53.1 %collective-permute-start.46 = (bf16[1,256,2048]{2,1,0:T(8,128)(2,1)}, bf16[1,256,2048]{2,1,0:T(8,128)(2,1)}, u32[]{:S(2)}, u32[]{:S(2)}) collective-permute-start(bf16[1,256,2048]{2,1,0:T(8,128)(2,1)} %get-tuple-element.275), channel_id=1, source_target_pairs={{0,4},{4,0},{8,12},{12,8},{16,20},{20,16},{24,28},{28,24},{1,5},{5... | collective-permute-start | bytes 3145736 | tf_op jit(solution)/shard_map/ppermute | solution.py:703
  491.4 7.8 %collective-permute-start.53 = (f32[7936]{0:T(1024)}, f32[7936]{0:T(1024)S(1)}, u32[]{:S(2)}, u32[]{:S(2)}) collective-permute-start(f32[7936]{0:T(1024)} %get-tuple-element.286), channel_id=1, source_target_pairs={{0,4},{4,0},{8,12},{12,8},{16,20},{20,16},{24,28},{28,24},{1,5},{5... | collective-permute-start | bytes 95240 | tf_op jit(solution)/shard_map/ppermute | solution.py:703
  499.1 35.8 %copy-start.51 = (f32[2048]{0:T(1024)}, f32[2048]{0:T(1024)S(1)}, u32[]{:S(2)}) copy-start(f32[2048]{0:T(1024)S(1)} %slice.274) | copy-start | bytes 24580
  499.2 5.7 %collective-permute-start.54 = (f32[4096]{0:T(1024)S(1)}, f32[4096]{0:T(1024)S(1)}, u32[]{:S(2)}, u32[]{:S(2)}) collective-permute-start(f32[4096]{0:T(1024)S(1)} %slice_add_fusion), channel_id=1, source_target_pairs={{0,1},{1,0},{2,3},{3,2},{4,5},{5,4},{6,7},{7,6},{8,9},{9,8},{10,11... | collective-permute-start | bytes 49160 | tf_op jit(solution)/shard_map/ppermute | solution.py:1055
  500.4 4.7 collective-permute-start.55
  503.4 5.5 %collective-permute-start.56 = (f32[4096]{0:T(1024)S(1)}, f32[4096]{0:T(1024)S(1)}, u32[]{:S(2)}, u32[]{:S(2)}) collective-permute-start(f32[4096]{0:T(1024)S(1)} %slice_add_fusion), channel_id=1, source_target_pairs={{0,3},{1,2},{2,1},{3,0},{4,7},{5,6},{6,5},{7,4},{8,11},{9,10},{10,... | collective-permute-start | bytes 49160 | tf_op jit(solution)/shard_map/ppermute | solution.py:1055
  504.9 17.0 %collective-permute-start.60 = (bf16[256,1024]{1,0:T(8,128)(2,1)}, bf16[256,1024]{1,0:T(8,128)(2,1)}, u32[]{:S(2)}, u32[]{:S(2)}) collective-permute-start(bf16[256,1024]{1,0:T(8,128)(2,1)} %fusion.22), channel_id=1, source_target_pairs={{0,4},{4,0},{8,12},{12,8},{16,20},{20,16},{24,28},{28,24},{1,5},{5... | collective-permute-start | bytes 1572872 | tf_op jit(solution)/shard_map/ppermute | solution.py:703
  505.1 15.3 %collective-permute-start.57 = (bf16[1,256,768]{2,1,0:T(8,128)(2,1)}, bf16[1,256,768]{2,1,0:T(8,128)(2,1)}, u32[]{:S(2)}, u32[]{:S(2)}) collective-permute-start(bf16[1,256,768]{2,1,0:T(8,128)(2,1)} %add_convert_fusion.10), channel_id=1, source_target_pairs={{0,8},{4,12},{8,0},{12,4},{16,24},{20,28},{24,16},{28,20},{1,9},{5... | collective-permute-start | bytes 1179656 | tf_op jit(solution)/shard_map/ppermute | solution.py:703
  508.9 10.1 %collective-permute-start.58 = (bf16[1,256,768]{2,1,0:T(8,128)(2,1)}, bf16[1,256,768]{2,1,0:T(8,128)(2,1)}, u32[]{:S(2)}, u32[]{:S(2)}) collective-permute-start(bf16[1,256,768]{2,1,0:T(8,128)(2,1)} %add_convert_fusion.9), channel_id=1, source_target_pairs={{0,16},{4,20},{8,24},{12,28},{16,0},{20,4},{24,8},{28,12},{1,17},{... | collective-permute-start | bytes 1179656 | tf_op jit(solution)/shard_map/ppermute | solution.py:703
  510.6 14.1 %collective-permute-start.48 = (bf16[128,2048]{1,0:T(8,128)(2,1)}, bf16[128,2048]{1,0:T(8,128)(2,1)S(1)}, u32[]{:S(2)}, u32[]{:S(2)}) collective-permute-start(bf16[128,2048]{1,0:T(8,128)(2,1)} %get-tuple-element.279), channel_id=1, source_target_pairs={{0,3},{1,0},{2,1},{3,2},{4,7},{5,4},{6,5},{7,6},{8,11},{9,8},{10,9... | collective-permute-start | bytes 1572872 | tf_op jit(solution)/shard_map/ppermute | solution.py:707
  520.3 13.1 %collective-permute-start.59 = (bf16[256,768]{1,0:T(8,128)(2,1)S(1)}, bf16[256,768]{1,0:T(8,128)(2,1)S(1)}, u32[]{:S(2)}, u32[]{:S(2)}) collective-permute-start(bf16[256,768]{1,0:T(8,128)(2,1)S(1)} %fusion.23), channel_id=1, source_target_pairs={{0,4},{4,0},{8,12},{12,8},{16,20},{20,16},{24,28},{28,24},{1,5},{5... | collective-permute-start | bytes 1179656 | tf_op jit(solution)/shard_map/ppermute | solution.py:703
  (56 other events, 204.8 us)

commit v7 on v5

--- a/solution.py
+++ b/solution.py
@@ -23,7 +23,7 @@
     )
 
 
-def call(kernel, name, operands, deps=(), scalars=(), vmem=2, **spec):
+def call(kernel, name, operands, deps=(), scalars=(), vmem=63, **spec):
     deps, many, lead = tuple(deps), len(operands), len(scalars)
 
     def body(*refs):
@@ -55,6 +55,7 @@
         "fence",
         values,
         deps,
+        vmem=2,
         in_specs=[ANY] * len(values),
         out_specs=[ANY] * len(values),
         out_shape=[jax.ShapeDtypeStruct(v.shape, v.dtype) for v in values],
@@ -98,6 +99,10 @@
         pltpu.make_async_copy(block, place(lax.bitwise_xor(me, j)), sems.at[j])
         for j, block in enumerate(blocks)
     ]
+
+
+def span(owner, size):
+    return pl.ds(pl.multiple_of(owner * size, size), size)
 
 
 def rows_at(ref, size):
@@ -226,7 +231,6 @@
         operands + list(earlier),
         deps,
         (at_mp,),
-        vmem=32,
         grid=(parts,),
         in_specs=[line(bias), line(gain), line(shift), table, table, table]
         + [ANY] * (len(chunks) + count + len(earlier)),
@@ -288,7 +292,6 @@
         "attend",
         [qkv, qkv, qkv],
         deps,
-        vmem=26,
         grid=(sequences * pairs,),
         in_specs=[at(0), at(1), at(2)],
         out_specs=[at(0), pl.BlockSpec((1, 8, length), lambda g: (g, 0, 0))],
@@ -384,7 +387,6 @@
         "attend_back",
         [qkv, qkv, qkv, grad, mixed, lse, *tables],
         deps,
-        vmem=26,
         grid=(sequences * pairs,),
         in_specs=[at(0), at(1), at(2), at(0), at(0), small, table, table, table],
         out_specs=[at(0)] * 3 + [pl.BlockSpec((1, 8, LANES), lambda g: (g, 0, 0))],
@@ -449,7 +451,6 @@
         [mixed, act, *blocks],
         deps,
         (at_mp,),
-        vmem=22,
         grid=(2 * turns,),
         in_specs=[
             pl.BlockSpec((rows, a.shape[1]), lambda i, at: (where(i, at), 0)) for a in (mixed, act)
@@ -524,7 +525,6 @@
         operands + list(earlier),
         deps,
         (at_mp,),
-        vmem=24,
         grid=(2 * turns,),
         in_specs=[out(hidden)] + [ANY] * (many + count + len(earlier)),
         out_specs=[out(width), out(hidden), out(model), total(hidden), total(model)],
@@ -543,7 +543,8 @@
 def grad_normed_kernel(
     count, turns, at_ref, gq_ref, gk_ref, gv_ref, gpre_ref, tokens_ref, *rest
 ):
-    blocks, (other_ref, own_ref, sum_ref, held, sems) = rest[:count], rest[count:]
+    blocks, others, rest = rest[:count], rest[count : count + turns], rest[count + turns :]
+    own_ref, sum_ref, held, sems = rest
     step = pl.program_id(0)
 
     @pl.when(step == 0)
@@ -559,7 +560,16 @@
     result = dot(g, held[...], 1, 1)
     sum_ref[0:1, :] += jnp.sum(result * normalized(tokens_ref[...]), axis=0, keepdims=True)
     sum_ref[1:2, :] += jnp.sum(result, axis=0, keepdims=True)
-    split_outputs(step, turns, result.astype(BF16), other_ref, own_ref)
+    result = result.astype(BF16)
+    for n, other_ref in enumerate(others):
+
+        @pl.when(step == n)
+        def _(other_ref=other_ref):
+            other_ref[...] = result
+
+    @pl.when(step >= turns)
+    def _():
+        own_ref[0] = result
 
 
 def grad_normed_sums(at_mp, gqkv, gpre, tokens, blocks, parts, places, deps):
@@ -573,69 +583,127 @@
         operands + list(blocks),
         deps,
         (at_mp,),
-        vmem=28,
         grid=(2 * turns,),
         in_specs=[
             pl.BlockSpec((rows, a.shape[1]), lambda i, at: (where(i, at), 0)) for a in operands
         ]
         + [ANY] * count,
-        out_specs=split_specs(rows, model, turns)
+        out_specs=[pl.BlockSpec((rows, model), lambda i, at: (0, 0))] * turns
+        + split_specs(rows, model, turns)[1:]
         + [pl.BlockSpec((8, model), lambda i, at: (0, 0))],
-        out_shape=[jax.ShapeDtypeStruct((turns, rows, model), BF16)] * 2
-        + [jax.ShapeDtypeStruct((8, model), F32)],
+        out_shape=[jax.ShapeDtypeStruct((rows, model), BF16)] * turns
+        + [
+            jax.ShapeDtypeStruct((turns, rows, model), BF16),
+            jax.ShapeDtypeStruct((8, model), F32),
+        ],
         scratch_shapes=[pltpu.VMEM((model, total), BF16), pltpu.SemaphoreType.DMA((count,))],
     )
 
 
-def weight_grad_kernel(sizes, left, at_ref, *refs):
-    ins, outs = refs[: len(refs) - len(sizes)], refs[len(refs) - len(sizes) :]
-    if left:
-        grad = jnp.concatenate([dot(ins[0][...], g[...], 0, 0) for g in ins[1:]], axis=1)
-    else:
-        grad = jnp.concatenate([dot(x[...], ins[-1][...], 0, 0) for x in ins[:-1]], axis=0)
-    grad = grad.astype(BF16)
-    first = 0
-    for size, out_ref in zip(sizes, outs):
-
-        @pl.when((pl.program_id(0) >= first) & (pl.program_id(0) < first + size))
-        def _(out_ref=out_ref):
-            out_ref[0] = grad
-
-        first += size
+def weight_grad_kernel(writes, left, rows, at_ref, cut_ref, *refs):
+    *refs, held, grad, sems = refs
+    whole, outs = refs[: len(refs) - len(writes)], refs[len(refs) - len(writes) :]
+    step, core, loads, first = pl.program_id(0), lax.rem(lax.axis_index("dp"), 2), [], 0
+    for ref in whole:
+        columns = pl.ds(first, ref.shape[1])
+        first += ref.shape[1]
+        for start in range(0, ref.shape[0], rows):
+            part = pl.ds(start, rows)
+            loads.append((ref.at[part], held.at[part, columns]))
+    loads = [pltpu.make_async_copy(*pair, sems.at[n]) for n, pair in enumerate(loads)]
+
+    @pl.when(step == 0)
+    def _():
+        for copy in loads:
+            copy.start()
+        for copy in loads:
+            copy.wait()
+
+    pair = (cut_ref[...], held[...]) if left else (held[...], cut_ref[...])
+    grad[...] = dot(*pair, 0, 0).astype(BF16)
+    size = cut_ref.shape[1] // 2
+    for half, steps, out_ref in writes_of(writes, outs):
+        here = functools.reduce(jnp.logical_or, [step == s for s in steps])
+
+        @pl.when(here)
+        def _(half=half, out_ref=out_ref):
+            mine = span(core if half == 0 else 1 - core, size)
+            out_ref[0] = grad[mine, :] if left else grad[:, mine]
+
+
+def writes_of(writes, outs):
+    return [(half, steps, out) for (half, steps), out in zip(writes, outs)]
 
 
 def weight_grads(me, xs, gs, count, deps, left):
-    plan = scatter_plan(count)
+    plan, chips = scatter_plan(count), count // 2
+    order = [j // 2 for s in plan[0] for j in s]
     sets = [(half, s) for s in range(len(plan[0])) for half in range(2)]
-    sizes = [len(plan[half][s]) for half, s in sets]
-    order = [j for half, s in sets for j in plan[half][s]]
-    owners = lax.bitwise_xor(me, jnp.array(order, jnp.int32))
+    writes = [(half, [order.index(j // 2) for j in plan[half][s]]) for half, s in sets]
+    table = []
+    for _, steps in writes:
+        for i in range(chips):
+            later = [w for w in steps if w >= i]
+            table.append(steps.index(min(later) if later else max(steps)))
+    owners = lax.bitwise_xor(me // 2, jnp.array(order, jnp.int32))
+    at = jnp.concatenate([owners, jnp.array(table, jnp.int32)])
     length, (cut, whole) = xs[0].shape[0], ((xs, gs) if left else (gs, xs))
-    size = cut[0].shape[1] // count
-    cut_spec = pl.BlockSpec((length, size), lambda i, at: (0, at[i]))
-    whole_specs = [pl.BlockSpec(a.shape, lambda i, at: (0, 0)) for a in whole]
-    full = sum(a.shape[1] for a in whole)
+    size, full = cut[0].shape[1] // count, sum(a.shape[1] for a in whole)
     shape = (size, full) if left else (full, size)
-
-    def out(first, many):
-        return pl.BlockSpec(
-            (1, *shape), lambda i, at: (jnp.clip(i - first, 0, many - 1), 0, 0)
-        )
-
-    firsts = [sum(sizes[:n]) for n in range(len(sizes))]
+    pieces = 8 // len(whole)
+
+    def out(n):
+        return pl.BlockSpec((1, *shape), lambda i, at: (at[chips * (n + 1) + i], 0, 0))
+
     outs = call(
-        functools.partial(weight_grad_kernel, sizes, left),
+        functools.partial(weight_grad_kernel, writes, left, length // pieces),
         "weight_grads",
-        [*xs, *gs],
+        [*cut, *whole],
         deps,
-        (owners,),
-        vmem=32,
-        grid=(count,),
-        in_specs=[cut_spec] + whole_specs if left else whole_specs + [cut_spec],
-        out_specs=[out(first, many) for first, many in zip(firsts, sizes)],
-        out_shape=[jax.ShapeDtypeStruct((many, *shape), BF16) for many in sizes],
+        (at,),
+        grid=(chips,),
+        in_specs=[pl.BlockSpec((length, 2 * size), lambda i, at: (0, at[i]))]
+        + [ANY] * len(whole),
+        out_specs=[out(n) for n in range(len(sets))],
+        out_shape=[
+            jax.ShapeDtypeStruct((len(plan[half][s]), *shape), BF16) for half, s in sets
+        ],
+        scratch_shapes=[
+            pltpu.VMEM((length, full), BF16),
+            pltpu.VMEM((2 * size, full) if left else (full, 2 * size), BF16),
+            pltpu.SemaphoreType.DMA((pieces * len(whole),)),
+        ],
     )
     return [[o for o, (half, _) in zip(outs, sets) if half == h] for h in range(2)]
+
+
+def norm_back_kernel(many, tokens_ref, dy_ref, gain_ref, *rest):
+    addends, out_ref = rest[:many], rest[many]
+    x = tokens_ref[...].astype(F32)
+    centered = x - jnp.mean(x, axis=1, keepdims=True)
+    inverse_std = lax.rsqrt(jnp.mean(centered * centered, axis=1, keepdims=True) + EPS)
+    normal = centered * inverse_std
+    scaled = sum(a[...].astype(F32) for a in addends) * gain_ref[...]
+    first_mean = jnp.mean(scaled, axis=1, keepdims=True)
+    second_mean = jnp.mean(scaled * normal, axis=1, keepdims=True)
+    back = (scaled - first_mean - normal * second_mean) * inverse_std
+    out_ref[...] = (dy_ref[...].astype(F32) + back).astype(BF16)
+
+
+def norm_back(tokens, dy, gain, addends, deps):
+    rows, model = tokens.shape
+    tile = min(64, rows)
+    part = pl.BlockSpec((tile, model), lambda i: (i, 0))
+    return call(
+        functools.partial(norm_back_kernel, len(addends)),
+        "norm_back",
+        [tokens, dy, gain, *addends],
+        deps,
+        grid=(rows // tile,),
+        in_specs=[part, part, pl.BlockSpec((1, model), lambda i: (0, 0))] + [part] * len(addends),
+        out_specs=part,
+        out_shape=jax.ShapeDtypeStruct((rows, model), BF16),
+    )
 
 
 def across(value, bit, count):
@@ -793,32 +861,32 @@
             [rank(dense_weight, 0, which, width), rank(down_weight, 0, which, hidden)], axis=0
         )
 
-    def stage(*arrays):
-        return jnp.stack(arrays), tuple([0, *near])
-
     near, places, pairs = near_shifts(nmp), list(range(nmp)), width // LANES
-    rows = BlockGather(row_pack(core), across(row_pack(1 - core), 1, ndp), ndp)
-    columns = BlockGather(column_pack(core), across(column_pack(1 - core), 1, ndp), ndp)
     head, tail = near[0], near[1:]
+    swap = lambda array: across(array, 1, ndp)
+    rows = BlockGather(row_pack(core), swap(row_pack(1 - core)), ndp)
+    columns = BlockGather(column_pack(core), swap(column_pack(1 - core)), ndp)
     came = {head: ring(tokens, head, nmp)}
+    other = [(swap(tokens), (0,))]
     rows.own_to(0)
-    came[head], begun = rows.fenced([came[head], tokens], columns.held.values())
+    came[head], begun = rows.fenced([came[head], tokens], [*columns.held.values(), other[0][0]])
     came.update({k: ring(begun, k, nmp) for k in tail})
+    other.append((swap(came[head]), (head,)))
     rows.own_to(1)
-    *held, cot = rows.fenced([*came.values(), cotangent])
+    *held, cot = rows.fenced([*came.values(), cotangent], [other[1][0]])
     came = dict(zip(near, held))
     own = [(tokens, (0,))] + [(came[k], (k,)) for k in near]
-    packed, shifts = stage(tokens, *held)
-    other = [(across(packed, 1, ndp), shifts)]
+    other += [(swap(came[k]), (k,)) for k in tail]
     far = gather_far(came, nmp)
     rows.rest()
     cot, *held = rows.fenced(
-        [cot, columns.held[0], columns.held[1]] + ([far] if nmp == 4 else []), [other[0][0]]
+        [cot, columns.held[0], columns.held[1]] + ([far] if nmp == 4 else []),
+        [array for array, _ in other[2:]],
     )
     columns.held = dict(enumerate(held[:2]))
     if nmp == 4:
         own.append((held[2], (2,)))
-        other.append((across(held[2], 1, ndp), (2,)))
+        other.append((swap(held[2]), (2,)))
 
     tables = rotary_tables(length)
     bias = jnp.concatenate(
@@ -830,37 +898,45 @@
     )
     gain, shift = norm_gain.astype(F32)[None, :], norm_bias.astype(F32)[None, :]
     came = {head: ring(cot, head, nmp)}
+    dy_other = [(swap(cot), (0,))]
     columns.own_to(0)
     common = (rows.blocks(), bias, gain, shift, tables, width, nmp)
     first = project(at_mp, 0, own, *common, (), [cot])
-    cot, came[head] = columns.fenced([cot, came[head]], [first[0]])
+    cot, came[head], begun = columns.fenced([cot, came[head], dy_other[0][0]], [first[0]])
+    dy_other = [(begun, (0,)), (swap(came[head]), (head,))]
     came.update({k: ring(cot, k, nmp) for k in tail})
     columns.own_to(1)
     qkv, act, slope, normed, token_rows = project(
         at_mp, 1, other, *common, first, [columns.held[0]]
     )
-    columns.fenced(deps=[qkv])
+    begun, *held = columns.fenced([dy_other[1][0], *came.values()], [qkv])
+    dy_other[1] = (begun, (head,))
+    came = dict(zip(near, held))
+    dy_own = [(cot, (0,))] + [(came[k], (k,)) for k in near]
+    dy_other += [(swap(came[k]), (k,)) for k in tail]
+    far = gather_far(came, nmp)
     columns.rest()
     mixed, lse = attend(qkv, length, block, [columns.held[0]])
-    held = columns.fenced(came.values(), [mixed])
-    came = dict(zip(near, held))
-    dy_own = [(cot, (0,))] + [(came[k], (k,)) for k in near]
-    packed, shifts = stage(cot, *held)
-    dy_packed = across(packed, 1, ndp)
-    far = gather_far(came, nmp)
+    begun = columns.fenced([array for array, _ in dy_other[2:]], [mixed])
+    dy_other[2:] = [(array, (k,)) for array, k in zip(begun, tail)]
     other_sums, own_sums = branch_sums(
-        at_mp, mixed, act, columns.blocks(), nmp, places, [packed]
-    )
-    dy_packed, other_sums, *far = fence(
-        [dy_packed, other_sums] + ([far] if nmp == 4 else []), [own_sums]
-    )
-    theirs = across(other_sums, 1, ndp)
-
-    dy_other = [(dy_packed, shifts)]
+        at_mp, mixed, act, columns.blocks(), nmp, places, [begun[0]]
+    )
+    other_sums, *far = fence([other_sums] + ([far] if nmp == 4 else []), [own_sums])
+    theirs = swap(other_sums)
+
     grad_a = grad_in(
-        at_mp, (dy_own, dy_other), slope, columns.blocks(), width, nmp, (0, 1), (), [other_sums]
-    )
-    far_other = [across(a, 1, ndp) for a in far]
+        at_mp,
+        ([c for c in dy_own if c[1][0] in (0, 1, nmp - 1)], [c for c in dy_other if c[1][0] in (0, 1, nmp - 1)]),
+        slope,
+        columns.blocks(),
+        width,
+        nmp,
+        (0, 1),
+        (),
+        far,
+    )
+    far_other = [swap(a) for a in far]
     theirs, *far_other = fence([theirs, *far_other], [grad_a[3]])
     shares = [[own_sums[k], theirs[k]] for k in places]
     farthest = [added(shares[2])] if nmp == 4 else []
@@ -881,14 +957,14 @@
         weight_grads(me, [mixed, act], [dy], ndp, [grad_b[3]], left=False), ndp
     )
 
-    def with_far(shares, moved):
+    def with_far(shares, moved, shifts):
         if moved:
             shares[1], shares[3] = shares[1] + [moved[0]], shares[3] + [moved[1]]
-        return {k: added(shares[k]) for k in near}
+        return {k: added(shares[k]) for k in shifts}
 
     if moved:
         moved = fence(moved, [column_grads.held[0][0][0]])
-    sums = with_far(shares, moved)
+    sums = with_far(shares, moved, near)
     brought = [ring(sums[head], head, nmp)]
     column_came = column_grads.send(0)
     gq, gk, gv, qkv_sums = attend_back(
@@ -905,35 +981,45 @@
     brought += [ring(a, k, nmp) for k, a in zip(tail, held)]
 
     def normed_part(part, deps):
-        return grad_normed_sums(
+        *other_part, own_part, sums = grad_normed_sums(
             at_mp, (gq, gk, gv), gpre, token_rows, rows.blocks(), nmp, part, deps
         )
+        return other_part, own_part, sums
 
     thirds = ([2], [1, 3], [0]) if nmp == 4 else (places[1:2], places[2:], places[:1])
     other_a, own_a, sums_a = normed_part(thirds[0], [brought[0]])
-    *column_came, other_a = fence([*column_came, other_a], [sums_a])
+    *column_came, other_a = fence([*column_came, *other_a], [sums_a])
     column_grads.arrive(0, column_came)
     column_grads.between()
-    column_came = column_grads.send(-1 + chip_steps)
-    most = other_a.shape[1] // 2
-    came_a = [across(p, 1, ndp) for p in (other_a[:, :most], other_a[:, most:])]
-    other_b, own_b, sums_b = normed_part(
-        thirds[1], [sums_a, *column_grads.ready(chip_steps - 1)]
-    )
-    brought[1:] = fence(brought[1:], [sums_b])
-    c0, c1, a0, a1, other_b = fence([*column_came, *came_a, other_b], [brought[1]])
+    column_came = column_grads.send(chip_steps - 1)
+    most = other_a.shape[0] // 2
+    came_a = [swap(p) for p in (other_a[:most], other_a[most:])]
+    up_grads = BlockScatter(
+        weight_grads(
+            me,
+            [normed],
+            [gpre],
+            ndp,
+            [sums_a, *column_grads.ready(chip_steps - 1)],
+            left=True,
+        ),
+        ndp,
+    )
+    brought[1:] = fence(brought[1:], [up_grads.held[0][0][0]])
+    c0, c1, a0, a1 = fence([*column_came, *came_a], [brought[1]])
     column_grads.arrive(chip_steps - 1, [c0, c1])
-    came_a = jnp.concatenate([a0, a1], axis=1)
-    came_b = across(other_b, 1, ndp)
     shares = [[] for _ in places]
-    for part, kept, got in ((thirds[0], own_a, came_a),):
-        for n, k in enumerate(part):
-            shares[k] = [kept[n], got[n]]
+    shares[thirds[0][0]] = [own_a[0], jnp.concatenate([a0, a1])]
     farthest = [added(shares[2])] if nmp == 4 else []
     moved = [a for f in farthest for a in send_far(f)]
-    other_c, own_c, sums_c = normed_part(
-        thirds[2], [sums_b, *farthest, column_grads.last()]
-    )
+    up_came = up_grads.send(0)
+    column_theirs = swap(column_grads.last())
+    other_b, own_b, sums_b = normed_part(
+        thirds[1], [sums_a, *farthest, up_grads.held[0][0][0], column_grads.last()]
+    )
+    column_theirs, *other_b = fence([column_theirs, *other_b], [sums_b])
+    came_b = [swap(other_b[0])]
+    other_c, own_c, sums_c = normed_part(thirds[2], [sums_b, column_theirs])
     qkv_sum = (
         qkv_sums.reshape(2, pairs, 8, LANES).sum(0)[:, :3, :].transpose(1, 0, 2).reshape(3 * width)
     )
@@ -944,51 +1030,68 @@
     bits = chip_bits(ndp)
     for bit in bits[:-2]:
         small = small + across(small, bit, ndp)
+    (other_c,) = other_c
+    u0, u1, *moved = fence([*up_came, *moved], [sums_c])
+    u0, u1 = fence([u0, u1])
+    up_grads.arrive(0, [u0, u1])
+    up_grads.between()
+    came_b0, small, other_c, *other_b[1:] = fence(
+        [came_b[0], small, other_c, *other_b[1:]], [u0]
+    )
+    came_b = [came_b0] + [swap(a) for a in other_b[1:]]
+    for n, k in enumerate(thirds[1]):
+        shares[k] = [own_b[n], came_b[n]]
+    if moved:
+        shares[1], shares[3] = shares[1] + [moved[0]], shares[3] + [moved[1]]
+    first_sum = added(shares[head])
+    came = {head: ring(first_sum, head, nmp)}
+    up_came = up_grads.send(chip_steps - 1)
     small_came = across(small, bits[-2], ndp)
-    up_grads = BlockScatter(
-        weight_grads(me, [normed], [gpre], ndp, [sums_c, small], left=True), ndp
-    )
-    came_b, other_c, column_last, small_came, *moved = fence(
-        [came_b, other_c, column_grads.last(), small_came, *moved], [up_grads.held[0][0][0]]
-    )
+    qkv_grads = BlockScatter(
+        weight_grads(
+            me,
+            [normed],
+            [gq, gk, gv],
+            ndp,
+            [sums_c, first_sum, *up_grads.ready(chip_steps - 1)],
+            left=True,
+        ),
+        ndp,
+    )
+    u0, u1, small_came, q0, q1, other_c, *held = fence(
+        [
+            *up_came,
+            small_came,
+            qkv_grads.held[0][0][0],
+            qkv_grads.held[1][0][0],
+            other_c,
+            *came_b[1:],
+        ]
+    )
+    for n, k in enumerate(thirds[1][1:]):
+        shares[k][1] = held[n]
+    up_grads.arrive(chip_steps - 1, [u0, u1])
+    qkv_grads.held[0][0], qkv_grads.held[1][0] = [q0], [q1]
+    qkv_came = qkv_grads.send(0)
     small = small + small_came
     small_came = across(small, bits[-1], ndp)
-    up_came = up_grads.send(0)
-    for n, k in enumerate(thirds[1]):
-        shares[k] = [own_b[n], came_b[n]]
-    sums = with_far(shares, moved)
-    came = {head: ring(sums[head], head, nmp)}
-    column_theirs = across(column_last, 1, ndp)
-    qkv_grads = BlockScatter(
-        weight_grads(me, [normed], [gq, gk, gv], ndp, [small, *sums.values()], left=True), ndp
-    )
-    *up_came, q0, q1, column_theirs, small_came = fence(
-        [*up_came, qkv_grads.held[0][0][0], qkv_grads.held[1][0][0], column_theirs, small_came]
-    )
-    qkv_grads.held[0][0], qkv_grads.held[1][0] = [q0], [q1]
-    up_grads.arrive(0, up_came)
-    up_grads.between()
-    up_came = up_grads.send(chip_steps - 1)
-    qkv_came = qkv_grads.send(0)
+    came_c = swap(other_c)
+    sums = {k: added(shares[k]) for k in tail}
+    came[head], up_last, *held = fence(
+        [came[head], up_grads.last(), *(sums[k] for k in tail)], [q0]
+    )
+    came.update({k: ring(a, k, nmp) for k, a in zip(tail, held)})
+    q0, q1, small_came, came_c, up_last = fence(
+        [*qkv_came, small_came, came_c, up_last], [came[head]]
+    )
+    qkv_grads.arrive(0, [q0, q1])
+    qkv_grads.between()
     small = small + small_came
-    came[head], other_c, small, *held = fence(
-        [came[head], other_c, small, *(sums[k] for k in tail)], [q0]
-    )
-    half = held[0].shape[0] // 2
-    early = [ring(a[:half], k, nmp) for k, a in zip(tail, held)]
-    u0, u1, small, *qkv_came = fence([*up_came, small, *qkv_came], [came[head]])
-    small_other = across(small, 1, ndp)
-    up_grads.arrive(chip_steps - 1, [u0, u1])
-    up_theirs = across(up_grads.last(), 1, ndp)
-    qkv_grads.arrive(0, qkv_came)
-    qkv_grads.between()
-    late = fence([*early, *(a[half:] for a in held)])
-    early, late = late[: len(tail)], late[len(tail) :]
-    late = [ring(a, k, nmp) for k, a in zip(tail, late)]
-    came.update({k: jnp.concatenate(pair) for k, *pair in zip(tail, early, late)})
-    came_c = across(other_c, 1, ndp)
-    qkv_grads.arrive(chip_steps - 1, qkv_grads.send(chip_steps - 1))
-    qkv_theirs = across(qkv_grads.last(), 1, ndp)
+    up_theirs = swap(up_last)
+    q0, q1, small = fence([*qkv_grads.send(chip_steps - 1), small])
+    qkv_grads.arrive(chip_steps - 1, [q0, q1])
+    small_other = swap(small)
+    qkv_theirs = swap(qkv_grads.last())
     norm_sums = small[: 2 * model] + small_other[: 2 * model]
     norm_sums = [norm_sums] + [
         lax.ppermute(norm_sums, "mp", [(i, i ^ j) for i in range(nmp)]) for j in range(1, nmp)
@@ -1032,16 +1135,9 @@
     )
     grad_up_bias = jnp.concatenate([even[3 * width :], odd[3 * width :]])
 
-    centered = local_inputs - jnp.mean(local_inputs, axis=1, keepdims=True)
-    inverse_std = lax.rsqrt(jnp.mean(centered * centered, axis=1, keepdims=True) + EPS)
-    normal_rows = centered * inverse_std
-    grad_rows = sum(a.astype(F32) for a in [own_c[0], came_c[0], *came.values()])
-    scaled = grad_rows * gain
-    first_mean = jnp.mean(scaled, axis=1, keepdims=True)
-    second_mean = jnp.mean(scaled * normal_rows, axis=1, keepdims=True)
-    grad_tokens = (
-        cotangent.astype(F32) + (scaled - first_mean - normal_rows * second_mean) * inverse_std
-    ).astype(BF16)
+    grad_tokens = norm_back(
+        tokens, cotangent, gain, [own_c[0], came_c, *came.values()], [qkv_theirs, small_other]
+    )
     return (
         output,
         grad_tokens,

time: 499 us -> 501 us (level)
  Pallas kernels: 175 us -> 219 us
  local copies, waits for them, and re-layouts: 78.1 us -> 46 us
  waiting for transfers between devices: 116 us -> 98.2 us
    pallas_call x31 -> x35, Pallas kernels: 175 us -> 219 us  [call(): pl.pallas_call(body, out_shape=out_shape, input_output_aliases=aliases, c...]
    unnamed x276 -> x162, local copies, waits for them, and re-layouts: 68.8 us -> 38.2 us
    ppermute x41 -> x46, waiting for transfers between devices: 71.7 us -> 48.9 us  [across(): return lax.ppermute(value, 'dp', [(i, i ^ bit) for i in range(count)])]
    ppermute x2, waiting for transfers between devices: 35 us -> 22.7 us  [gather_far(): down = lax.ppermute(chunks[3], 'mp', [(1, 0), (2, 1)])]
    ppermute x3, waiting for transfers between devices: 0.17 us -> 8.65 us  [on_device(): lax.ppermute(norm_sums, 'mp', [(i, i ^ j) for i in range(nmp)])]
    ppermute x9 -> x8, waiting for transfers between devices: 9.6 us -> 17.9 us  [ring(): lax.ppermute(value, 'mp', [(i, (i + k) % parts) for i in range(parts)])]
    convert_element_type x10 -> x11, other arithmetic: 17.3 us -> 24.7 us  [added(): return sum((a.astype(F32) for a in addends)).astype(BF16)]
    reduce_sum x3 -> x0, other arithmetic: 5.74 us -> none  [the longest x1 2.51 us: on_device(): first_mean = jnp.mean(scaled, axis=1, keepdims=True)]
  transfers between devices with their start and end apart: 61 -> 65, of which waited for: 18 -> 17; matrix products, arithmetic and copies ran while one was open for 11% -> 12% of each run, Pallas kernels for 36% -> 43%
where the time goes in v7:
time: 501 us; the launch traced here: 491 us
  Pallas kernels  219 us (44%)
  waiting for transfers between devices  98.2 us (20%)
  starting transfers between devices  69.9 us (14%)
  other arithmetic  56.2 us (11%)
  local copies, waits for them, and re-layouts  46 us (9%)
    pallas_call x35, Pallas kernels, call(): pl.pallas_call(body, out_shape=out_shape, input_output_aliases=aliases, c...  219 us
    ppermute x46, waiting for transfers between devices, across(): return lax.ppermute(value, 'dp', [(i, i ^ bit) for i in range(count)])  48.9 us
    unnamed x162, local copies, waits for them, and re-layouts  38.2 us
    ppermute x46, starting transfers between devices, across(): return lax.ppermute(value, 'dp', [(i, i ^ bit) for i in range(count)])  32.2 us
    convert_element_type x11, other arithmetic, added(): return sum((a.astype(F32) for a in addends)).astype(BF16)  24.7 us
    ppermute x2, waiting for transfers between devices, gather_far(): down = lax.ppermute(chunks[3], 'mp', [(1, 0), (2, 1)])  22.7 us
    ppermute x8, waiting for transfers between devices, ring(): lax.ppermute(value, 'mp', [(i, (i + k) % parts) for i in range(parts)])  17.9 us
    ppermute x8, starting transfers between devices, ring(): lax.ppermute(value, 'mp', [(i, (i + k) % parts) for i in range(parts)])  15.7 us
  transfers between devices with their start and end apart: 65, of which 17 were waited for; matrix products, arithmetic and copies ran while one was open for 12% of the time, Pallas kernels for 43%

profile of v7, /device:TPU:0, one launch (start us, length us, event | category | flops | bytes accessed | tf_op | source)
XLA Modules:
  0.0 491.0 jit_solution(9028236583167945712)
XLA Ops:
  3.8 2.6 collective-permute-start.4
  6.4 1.6 collective-permute-start.2
  8.1 1.6 collective-permute-start.3
  10.0 2.0 collective-permute-done.5.refs_7_.refs_10_
  12.0 16.9 %collective-permute-done.2.refs_2_ = bf16[256,1792]{1,0:T(8,128)(2,1)S(1)} collective-permute-done((bf16[256,1792]{1,0:T(8,128)(2,1)S(1)}, bf16[256,1792]{1,0:T(8,128)(2,1)S(1)}, u32[]{:S(2)}, u32[]{:S(2)}) %collective-permute-start.2) | collective-permute-done | bytes 917536 | tf_op jit(solution)/shard_map/ppermute | solution.py:710
  29.0 3.2 collective-permute-done.4.refs_4_
  32.2 1.8 collective-permute-start.9
  34.0 1.5 collective-permute-start.7
  35.5 1.5 collective-permute-start.8
  38.0 18.4 %collective-permute-done.7.refs_3_ = bf16[256,1792]{1,0:T(8,128)(2,1)S(1)} collective-permute-done((bf16[256,1792]{1,0:T(8,128)(2,1)S(1)}, bf16[256,1792]{1,0:T(8,128)(2,1)S(1)}, u32[]{:S(2)}, u32[]{:S(2)}) %collective-permute-start.7) | collective-permute-done | bytes 917536 | tf_op jit(solution)/shard_map/ppermute | solution.py:710
  60.8 1.6 collective-permute-start.11
  63.0 22.7 %collective-permute-done.14 = bf16[256,2048]{1,0:T(8,128)(2,1)S(1)} collective-permute-done((bf16[256,2048]{1,0:T(8,128)(2,1)S(1)}, bf16[256,2048]{1,0:T(8,128)(2,1)S(1)}, u32[]{:S(2)}, u32[]{:S(2)}) %collective-permute-start.14) | collective-permute-done | bytes 1048608 | tf_op jit(solution)/shard_map/ppermute | solution.py:725
  95.6 2.7 collective-permute-start.18
  98.3 1.5 collective-permute-start.16
  99.8 1.5 collective-permute-start.17
  103.1 19.7 %project.2 = (bf16[2048,768]{1,0:T(8,128)(2,1)}, bf16[2048,1024]{1,0:T(8,128)(2,1)}, bf16[2048,1024]{1,0:T(8,128)(2,1)}, bf16[2048,2048]{1,0:T(8,128)(2,1)}, bf16[2048,2048]{1,0:T(8,128)(2,1)}) custom-call(s32[1]{0:T(128)} %bitcast.refs_0_, f32[1,1792]{1,0:T(1,128)} %maximum_convert_fusion.refs_1_, f32[1,2048]{1,0:T(1,128)} %bitcast.86, f32[1,2048]{1,0:T(1,128)} %bitcast.89, ...), custom_call_target="tpu_custom_call" | custom-call | tf_op jit(solution)/shard_map/project/pallas_call | solution.py:41
  122.9 1.9 copy-done.2
  127.3 19.7 %project.3 = (bf16[2048,768]{1,0:T(8,128)(2,1)}, bf16[2048,1024]{1,0:T(8,128)(2,1)}, bf16[2048,1024]{1,0:T(8,128)(2,1)}, bf16[2048,2048]{1,0:T(8,128)(2,1)}, bf16[2048,2048]{1,0:T(8,128)(2,1)}) custom-call(s32[1]{0:T(128)} %bitcast.refs_0_, ...), custom_call_target="tpu_custom_call", output_to_operand_aliasing={{0}: (19, {}), {1}: (20, {}), {2}: (21, {}), {3}: (22, {}),... | custom-call | tf_op jit(solution)/shard_map/project/pallas_call | solution.py:41
  147.1 3.5 collective-permute-done.23.refs_8_
  150.6 1.9 copy-done.3
  154.5 1.7 collective-permute-start.27
  156.1 1.7 collective-permute-start.28
  159.7 15.0 %attend.1 = (bf16[2048,256]{1,0:T(8,128)(2,1)}, f32[4,8,1024]{2,1,0:T(8,128)}) custom-call(bf16[2048,768]{1,0:T(8,128)(2,1)} %get-tuple-element.199.refs_9_.refs_0_.refs_1_.refs_2_, bf16[2048,768]{1,0:T(8,128)(2,1)} %get-tuple-element.199.refs_9_.refs_0_.refs_1_.refs_2_, bf16[2048,768]{1,0:T(8,128)(2,1)} %get-tuple-element.199.refs_9_.refs_0_.refs_1_.refs_2_, ...), custom_call_target="tpu_custom_call" | custom-call | tf_op jit(solution)/shard_map/attend/pallas_call | solution.py:41
  177.7 18.8 %branch_sums.1 = (bf16[4,256,2048]{2,1,0:T(8,128)(2,1)}, bf16[4,256,2048]{2,1,0:T(8,128)(2,1)}) custom-call(s32[1]{0:T(128)} %bitcast.refs_0_, bf16[2048,256]{1,0:T(8,128)(2,1)} %get-tuple-element.206.refs_9_.refs_1_.refs_2_.refs_4_, bf16[2048,1024]{1,0:T(8,128)(2,1)} %get-tuple-element.207.refs_2_.refs_3_, bf16[1280,256]{1,0:T(8,128)(2,1)} %copy-done.8, ...), custom_call_target="tpu_custom_call" | custom-call | tf_op jit(solution)/shard_map/branch_sums/pallas_call | solution.py:41
  196.5 2.9 add.198.refs_1_
  199.4 2.2 copy-done.19
  202.1 12.8 %grad_in.2 = (bf16[2048,256]{1,0:T(8,128)(2,1)}, bf16[2048,1024]{1,0:T(8,128)(2,1)}, bf16[2048,2048]{1,0:T(8,128)(2,1)}, f32[8,1024]{1,0:T(8,128)}, f32[8,2048]{1,0:T(8,128)}) custom-call(s32[1]{0:T(128)} %bitcast.refs_0_, bf16[2048,1024]{1,0:T(8,128)(2,1)} %get-tuple-element.228.refs_1_, bf16[256,2048]{1,0:T(8,128)(2,1)} %get-tuple-element.204.refs_2_, ...), custom_call_target="tpu_custom_call" | custom-call | tf_op jit(solution)/shard_map/grad_in/pallas_call | solution.py:41
  215.8 2.9 fusion.11.refs_22_
  218.7 5.6 %collective-permute-start.31 = (bf16[256,2048]{1,0:T(8,128)(2,1)}, bf16[256,2048]{1,0:T(8,128)(2,1)}, u32[]{:S(2)}, u32[]{:S(2)}) collective-permute-start(bf16[256,2048]{1,0:T(8,128)(2,1)} %fusion.11.refs_22_), channel_id=1, source_target_pairs={{0,1},{1,2},{4,5},{5,6},{8,9},{9,10},{12,13},{13,14},{16,17},{17,1... | collective-permute-start | bytes 3145736 | tf_op jit(solution)/shard_map/ppermute | solution.py:734
  224.3 1.8 collective-permute-start.32
  226.7 13.1 %grad_in.3 = (bf16[2048,256]{1,0:T(8,128)(2,1)}, bf16[2048,1024]{1,0:T(8,128)(2,1)}, bf16[2048,2048]{1,0:T(8,128)(2,1)}, f32[8,1024]{1,0:T(8,128)}, f32[8,2048]{1,0:T(8,128)}) custom-call(s32[1]{0:T(128)} %bitcast.refs_0_, bf16[2048,1024]{1,0:T(8,128)(2,1)} %get-tuple-element.228.refs_1_, ...), custom_call_target="tpu_custom_call", output_to_operand_aliasing={{0}: (18, {}), {1}: (19, {}), {2}: (20, {})} | custom-call | tf_op jit(solution)/shard_map/grad_in/pallas_call | solution.py:41
  239.8 19.4 %weight_grads.3 = (bf16[2,1280,256]{2,1,0:T(8,128)(2,1)}, bf16[2,1280,256]{2,1,0:T(8,128)(2,1)}, bf16[1,1280,256]{2,1,0:T(8,128)(2,1)}, bf16[1,1280,256]{2,1,0:T...) custom-call(s32[28]{0:T(128)} %pad_add_fusion.refs_0_, ...), custom_call_target="tpu_custom_call" | custom-call | tf_op jit(solution)/shard_map/weight_grads/pallas_call | solution.py:41
  259.3 1.5 collective-permute-start.35
  263.0 5.6 %fusion.5 = (bf16[256,2048]{1,0:T(8,128)(2,1)}, bf16[256,2048]{1,0:T(8,128)(2,1)}) fusion(bf16[256,2048]{1,0:T(8,128)(2,1)} %get-tuple-element.241, bf16[4,256,2048]{2,1,0:T(8,128)(2,1)} %get-tuple-element.232, bf16[4,256,2048]{2,1,0:T(8,128)(2,1)} %get-tuple-element.223.refs_2_, bf16[256,2048]{1,0:T(8,128)(2,1)} %get-tuple-element.240), kind=kLoop, calls=%fused_computation.11 | loop fusion | flops 6291456 | bytes 8388608 | tf_op jit(solution)/shard_map/convert_element_type | solution.py:730
  269.4 25.2 %attend_back.1 = (bf16[2048,256]{1,0:T(8,128)(2,1)}, bf16[2048,256]{1,0:T(8,128)(2,1)}, bf16[2048,256]{1,0:T(8,128)(2,1)}, f32[4,8,128]{2,1,0:T(8,128)}) custom-call(bf16[2048,768]{1,0:T(8,128)(2,1)} %get-tuple-element.199.refs_9_.refs_0_.refs_1_.refs_2_, bf16[2048,768]{1,0:T(8,128)(2,1)} %get-tuple-element.199.refs_9_.refs_0_.refs_1_.refs_2_, ...), custom_call_target="tpu_custom_call" | custom-call | tf_op jit(solution)/shard_map/attend_back/pallas_call | solution.py:41
  296.2 2.9 collective-permute-start.34
  299.1 11.2 %grad_normed_sums.3 = (bf16[256,2048]{1,0:T(8,128)(2,1)}, bf16[1,256,2048]{2,1,0:T(8,128)(2,1)}, f32[8,2048]{1,0:T(8,128)}) custom-call(s32[1]{0:T(128)} %bitcast.refs_0_, bf16[2048,256]{1,0:T(8,128)(2,1)} %get-tuple-element.244.refs_2_.refs_1_, bf16[2048,256]{1,0:T(8,128)(2,1)} %get-tuple-element.249.refs_2_.refs_3_, ...), custom_call_target="tpu_custom_call" | custom-call | tf_op jit(solution)/shard_map/grad_normed_sums/pallas_call | solution.py:41
  313.4 2.3 add_convert_fusion.2.refs_5_
  318.4 2.1 add_convert_fusion.3.refs_4_
  322.7 16.5 %weight_grads.4 = (bf16[2,256,1024]{2,1,0:T(8,128)(2,1)}, bf16[2,256,1024]{2,1,0:T(8,128)(2,1)}, bf16[1,256,1024]{2,1,0:T(8,128)(2,1)}, bf16[1,256,1024]{2,1,0:T...) custom-call(s32[28]{0:T(128)} %pad_add_fusion.refs_0_, ...), custom_call_target="tpu_custom_call" | custom-call | tf_op jit(solution)/shard_map/weight_grads/pallas_call | solution.py:41
  343.1 2.2 fusion.12.refs_17_
  345.3 2.5 fusion.4.refs_15_
  347.8 16.7 %grad_normed_sums.4 = (bf16[256,2048]{1,0:T(8,128)(2,1)}, bf16[256,2048]{1,0:T(8,128)(2,1)}, bf16[2,256,2048]{2,1,0:T(8,128)(2,1)}, f32[8,2048]{1,0:T(8,128)}) custom-call(s32[1]{0:T(128)} %bitcast.refs_0_, bf16[2048,256]{1,0:T(8,128)(2,1)} %get-tuple-element.244.refs_2_.refs_1_, bf16[2048,256]{1,0:T(8,128)(2,1)} %get-tuple-element.249.refs_2_.refs_3_, ...), custom_call_target="tpu_custom_call" | custom-call | tf_op jit(solution)/shard_map/grad_normed_sums/pallas_call | solution.py:41
  364.5 2.8 collective-permute-start.44
  367.4 1.9 collective-permute-start.45
  369.3 1.7 convert_add_fusion.3
  373.6 4.0 fusion.10
  378.6 11.2 %grad_normed_sums.5 = (bf16[256,2048]{1,0:T(8,128)(2,1)}, bf16[1,256,2048]{2,1,0:T(8,128)(2,1)}, f32[8,2048]{1,0:T(8,128)}) custom-call(s32[1]{0:T(128)} %bitcast.refs_0_, bf16[2048,256]{1,0:T(8,128)(2,1)} %get-tuple-element.244.refs_2_.refs_1_, bf16[2048,256]{1,0:T(8,128)(2,1)} %get-tuple-element.249.refs_2_.refs_3_, ...), custom_call_target="tpu_custom_call" | custom-call | tf_op jit(solution)/shard_map/grad_normed_sums/pallas_call | solution.py:41
  389.8 1.6 slice.283
  394.3 2.0 add_convert_fusion.5.refs_8_
  397.5 2.0 add_convert_fusion.6.refs_7_
  401.5 2.9 fusion.3.refs_6_
  404.5 13.8 %weight_grads.5 = (bf16[2,256,768]{2,1,0:T(8,128)(2,1)}, bf16[2,256,768]{2,1,0:T(8,128)(2,1)}, bf16[1,256,768]{2,1,0:T(8,128)(2,1)}, bf16[1,256,768]{2,1,0:T(8,1...) custom-call(s32[28]{0:T(128)} %pad_add_fusion.refs_0_, ...), custom_call_target="tpu_custom_call" | custom-call | tf_op jit(solution)/shard_map/weight_grads/pallas_call | solution.py:41
  418.3 3.5 collective-permute-start.55
  425.9 1.6 maximum_select_fusion.1
  430.5 2.1 fusion.1.refs_2_
  434.1 10.7 %collective-permute-done.55.refs_0_ = bf16[256,2048]{1,0:T(8,128)(2,1)S(1)} collective-permute-done((bf16[256,2048]{1,0:T(8,128)(2,1)}, bf16[256,2048]{1,0:T(8,128)(2,1)S(1)}, u32[]{:S(2)}, u32[]{:S(2)}) %collective-permute-start.55) | collective-permute-done | bytes 1048608 | tf_op jit(solution)/shard_map/ppermute | solution.py:714
  444.8 3.5 collective-permute-done.51.refs_0_
  453.6 2.3 add_bitcast_fusion
  456.0 4.3 collective-permute-done.58.refs_1_
  464.6 3.4 collective-permute-start.63
  469.2 8.6 %collective-permute-done.61 = f32[4096]{0:T(1024)} collective-permute-done((f32[4096]{0:T(1024)}, f32[4096]{0:T(1024)}, u32[]{:S(2)}, u32[]{:S(2)}) %collective-permute-start.61) | collective-permute-done | bytes 16416 | tf_op jit(solution)/shard_map/ppermute | solution.py:1097
  480.4 1.6 maximum_select_fusion
  484.6 5.4 %norm_back.1 = bf16[256,2048]{1,0:T(8,128)(2,1)} custom-call(bf16[256,2048]{1,0:T(8,128)(2,1)} %refs_0_.1, bf16[256,2048]{1,0:T(8,128)(2,1)} %refs_1_.1, f32[1,2048]{1,0:T(1,128)} %bitcast.88, bf16[256,2048]{1,0:T(8,128)(2,1)} %bitcast.85, bf16[256,2048]{1,0:T(8,128)(2,1)} %copy-done.31, bf16[256,2048]{1,0:T(8,128)(2,1)} %copy-done.21, ...), custom_call_target="tpu_custom_call" | custom-call | tf_op jit(solution)/shard_map/norm_back/pallas_call | solution.py:41
  (338 shorter events, 83.2 us)
Async XLA Ops:
  2.3 5.8 %collective-permute-start.1 = (bf16[256,1792]{1,0:T(8,128)(2,1)S(1)}, bf16[256,1792]{1,0:T(8,128)(2,1)S(1)}, u32[]{:S(2)}, u32[]{:S(2)}) collective-permute-start(bf16[256,1792]{1,0:T(8,128)(2,1)S(1)} %pad_maximum_fusion.2), channel_id=1, source_target_pairs={{0,4},{4,0},{8,12},{12,8},{16,20},{20,16},{24,28},{28,24},{1,5},{5... | collective-permute-start | bytes 2752520 | tf_op jit(solution)/shard_map/ppermute | solution.py:710
  3.3 25.6 %collective-permute-start = (bf16[256,2048]{1,0:T(8,128)(2,1)S(1)}, bf16[256,2048]{1,0:T(8,128)(2,1)S(1)}, u32[]{:S(2)}, u32[]{:S(2)}) collective-permute-start(bf16[256,2048]{1,0:T(8,128)(2,1)S(1)} %copy-done.43), channel_id=1, source_target_pairs={{0,4},{4,0},{8,12},{12,8},{16,20},{20,16},{24,28},{28,24},{1,5},{5... | collective-permute-start | bytes 3145736 | tf_op jit(solution)/shard_map/ppermute | solution.py:710
  3.8 28.4 %collective-permute-start.4 = (bf16[256,2048]{1,0:T(8,128)(2,1)S(1)}, bf16[256,2048]{1,0:T(8,128)(2,1)S(1)}, u32[]{:S(2)}, u32[]{:S(2)}) collective-permute-start(bf16[256,2048]{1,0:T(8,128)(2,1)S(1)} %copy-done.43), channel_id=1, source_target_pairs={{0,1},{1,2},{2,3},{3,0},{4,5},{5,6},{6,7},{7,4},{8,9},{9,10},{10,1... | collective-permute-start | bytes 3145736 | tf_op jit(solution)/shard_map/ppermute | solution.py:714
  6.4 22.5 %collective-permute-start.2 = (bf16[256,1792]{1,0:T(8,128)(2,1)S(1)}, bf16[256,1792]{1,0:T(8,128)(2,1)S(1)}, u32[]{:S(2)}, u32[]{:S(2)}) collective-permute-start(bf16[256,1792]{1,0:T(8,128)(2,1)S(1)} %pad_maximum_fusion.1.refs_0_), channel_id=1, source_target_pairs={{0,8},{4,12},{8,0},{12,4},{16,24},{20,28},{24,16},{28,20},{1,9},{5... | collective-permute-start | bytes 2752520 | tf_op jit(solution)/shard_map/ppermute | solution.py:710
  8.1 24.2 %collective-permute-start.3 = (bf16[256,1792]{1,0:T(8,128)(2,1)S(1)}, bf16[256,1792]{1,0:T(8,128)(2,1)S(1)}, u32[]{:S(2)}, u32[]{:S(2)}) collective-permute-start(bf16[256,1792]{1,0:T(8,128)(2,1)S(1)} %collective-permute-done.1.refs_1_), channel_id=1, source_target_pairs={{0,16},{4,20},{8,24},{12,28},{16,0},{20,4},{24,8},{28,12},{1,17},{... | collective-permute-start | bytes 2752520 | tf_op jit(solution)/shard_map/ppermute | solution.py:710
  9.7 2.3 collective-permute-start.5
  32.2 25.4 %collective-permute-start.6 = (bf16[256,2048]{1,0:T(8,128)(2,1)S(1)}, bf16[256,2048]{1,0:T(8,128)(2,1)S(1)}, u32[]{:S(2)}, u32[]{:S(2)}) collective-permute-start(bf16[256,2048]{1,0:T(8,128)(2,1)S(1)} %get-tuple-element.166.refs_6_), channel_id=1, source_target_pairs={{0,4},{4,0},{8,12},{12,8},{16,20},{20,16},{24,28},{28,24},{1,5},{5... | collective-permute-start | bytes 3145736 | tf_op jit(solution)/shard_map/ppermute | solution.py:710
  32.2 25.6 %collective-permute-start.9 = (bf16[256,2048]{1,0:T(8,128)(2,1)S(1)}, bf16[256,2048]{1,0:T(8,128)(2,1)S(1)}, u32[]{:S(2)}, u32[]{:S(2)}) collective-permute-start(bf16[256,2048]{1,0:T(8,128)(2,1)S(1)} %get-tuple-element.171), channel_id=1, source_target_pairs={{0,3},{1,0},{2,1},{3,2},{4,7},{5,4},{6,5},{7,6},{8,11},{9,8},{10,9... | collective-permute-start | bytes 3145736 | tf_op jit(solution)/shard_map/ppermute | solution.py:714
  34.0 22.4 %collective-permute-start.7 = (bf16[256,1792]{1,0:T(8,128)(2,1)S(1)}, bf16[256,1792]{1,0:T(8,128)(2,1)S(1)}, u32[]{:S(2)}, u32[]{:S(2)}) collective-permute-start(bf16[256,1792]{1,0:T(8,128)(2,1)S(1)} %get-tuple-element.168.refs_1_), channel_id=1, source_target_pairs={{0,8},{4,12},{8,0},{12,4},{16,24},{20,28},{24,16},{28,20},{1,9},{5... | collective-permute-start | bytes 2752520 | tf_op jit(solution)/shard_map/ppermute | solution.py:710
  35.5 22.1 %collective-permute-start.8 = (bf16[256,1792]{1,0:T(8,128)(2,1)S(1)}, bf16[256,1792]{1,0:T(8,128)(2,1)S(1)}, u32[]{:S(2)}, u32[]{:S(2)}) collective-permute-start(bf16[256,1792]{1,0:T(8,128)(2,1)S(1)} %get-tuple-element.167.refs_0_), channel_id=1, source_target_pairs={{0,16},{4,20},{8,24},{12,28},{16,0},{20,4},{24,8},{28,12},{1,17},{... | collective-permute-start | bytes 2752520 | tf_op jit(solution)/shard_map/ppermute | solution.py:710
  58.7 4.4 collective-permute-start.13
  59.4 26.3 %collective-permute-start.14 = (bf16[256,2048]{1,0:T(8,128)(2,1)S(1)}, bf16[256,2048]{1,0:T(8,128)(2,1)S(1)}, u32[]{:S(2)}, u32[]{:S(2)}) collective-permute-start(bf16[256,2048]{1,0:T(8,128)(2,1)S(1)} %get-tuple-element.172.refs_9_), channel_id=1, source_target_pairs={{1,0},{2,1},{5,4},{6,5},{9,8},{10,9},{13,12},{14,13},{17,16},{18,1... | collective-permute-start | bytes 3145736 | tf_op jit(solution)/shard_map/ppermute | solution.py:725
  60.7 26.4 %collective-permute-start.10 = (bf16[256,2048]{1,0:T(8,128)(2,1)S(1)}, bf16[256,2048]{1,0:T(8,128)(2,1)S(1)}, u32[]{:S(2)}, u32[]{:S(2)}) collective-permute-start(bf16[256,2048]{1,0:T(8,128)(2,1)S(1)} %get-tuple-element.172.refs_9_), channel_id=1, source_target_pairs={{0,4},{4,0},{8,12},{12,8},{16,20},{20,16},{24,28},{28,24},{1,5},{5... | collective-permute-start | bytes 3145736 | tf_op jit(solution)/shard_map/ppermute | solution.py:710
  60.8 26.3 %collective-permute-start.11 = (bf16[256,1792]{1,0:T(8,128)(2,1)S(1)}, bf16[256,1792]{1,0:T(8,128)(2,1)S(1)}, u32[]{:S(2)}, u32[]{:S(2)}) collective-permute-start(bf16[256,1792]{1,0:T(8,128)(2,1)S(1)} %get-tuple-element.175.refs_2_), channel_id=1, source_target_pairs={{0,16},{4,20},{8,24},{12,28},{16,0},{20,4},{24,8},{28,12},{1,17},{... | collective-permute-start | bytes 2752520 | tf_op jit(solution)/shard_map/ppermute | solution.py:710
  62.3 24.7 %collective-permute-start.12 = (bf16[256,1792]{1,0:T(8,128)(2,1)S(1)}, bf16[256,1792]{1,0:T(8,128)(2,1)S(1)}, u32[]{:S(2)}, u32[]{:S(2)}) collective-permute-start(bf16[256,1792]{1,0:T(8,128)(2,1)S(1)} %get-tuple-element.178.refs_5_), channel_id=1, source_target_pairs={{0,8},{4,12},{8,0},{12,4},{16,24},{20,28},{24,16},{28,20},{1,9},{5... | collective-permute-start | bytes 2752520 | tf_op jit(solution)/shard_map/ppermute | solution.py:710
  95.6 27.3 %collective-permute-start.18 = (bf16[256,2048]{1,0:T(8,128)(2,1)}, bf16[256,2048]{1,0:T(8,128)(2,1)}, u32[]{:S(2)}, u32[]{:S(2)}) collective-permute-start(bf16[256,2048]{1,0:T(8,128)(2,1)} %get-tuple-element.190.refs_19_.refs_4_), channel_id=1, source_target_pairs={{0,1},{1,2},{2,3},{3,0},{4,5},{5,6},{6,7},{7,4},{8,9},{9,10},{10,1... | collective-permute-start | bytes 3145736 | tf_op jit(solution)/shard_map/ppermute | solution.py:714
  98.3 24.6 %collective-permute-start.19 = (bf16[256,2048]{1,0:T(8,128)(2,1)}, bf16[256,2048]{1,0:T(8,128)(2,1)}, u32[]{:S(2)}, u32[]{:S(2)}) collective-permute-start(bf16[256,2048]{1,0:T(8,128)(2,1)} %get-tuple-element.190.refs_19_.refs_4_), channel_id=1, source_target_pairs={{0,4},{4,0},{8,12},{12,8},{16,20},{20,16},{24,28},{28,24},{1,5},{5... | collective-permute-start | bytes 3145736 | tf_op jit(solution)/shard_map/ppermute | solution.py:710
  98.3 24.5 %collective-permute-start.16 = (bf16[1280,256]{1,0:T(8,128)(2,1)S(1)}, bf16[1280,256]{1,0:T(8,128)(2,1)}, u32[]{:S(2)}, u32[]{:S(2)}) collective-permute-start(bf16[1280,256]{1,0:T(8,128)(2,1)S(1)} %get-tuple-element.196.refs_0_), channel_id=1, source_target_pairs={{0,8},{4,12},{8,0},{12,4},{16,24},{20,28},{24,16},{28,20},{1,9},{5... | collective-permute-start | bytes 1966088 | tf_op jit(solution)/shard_map/ppermute | solution.py:710
  99.8 23.1 %collective-permute-start.17 = (bf16[1280,256]{1,0:T(8,128)(2,1)}, bf16[1280,256]{1,0:T(8,128)(2,1)}, u32[]{:S(2)}, u32[]{:S(2)}) collective-permute-start(bf16[1280,256]{1,0:T(8,128)(2,1)} %get-tuple-element.197.refs_1_), channel_id=1, source_target_pairs={{0,16},{4,20},{8,24},{12,28},{16,0},{20,4},{24,8},{28,12},{1,17},{... | collective-permute-start | bytes 1966088 | tf_op jit(solution)/shard_map/ppermute | solution.py:710
  103.1 24.2 %collective-permute-start.15 = (bf16[256,2048]{1,0:T(8,128)(2,1)}, bf16[256,2048]{1,0:T(8,128)(2,1)}, u32[]{:S(2)}, u32[]{:S(2)}) collective-permute-start(bf16[256,2048]{1,0:T(8,128)(2,1)} %get-tuple-element.181.refs_10_), channel_id=1, source_target_pairs={{0,4},{4,0},{8,12},{12,8},{16,20},{20,16},{24,28},{28,24},{1,5},{5... | collective-permute-start | bytes 3145736 | tf_op jit(solution)/shard_map/ppermute | solution.py:710
  124.7 22.4 %collective-permute-start.22 = (bf16[256,2048]{1,0:T(8,128)(2,1)}, bf16[256,2048]{1,0:T(8,128)(2,1)}, u32[]{:S(2)}, u32[]{:S(2)}) collective-permute-start(bf16[256,2048]{1,0:T(8,128)(2,1)} %get-tuple-element.203.refs_7_), channel_id=1, source_target_pairs={{0,4},{4,0},{8,12},{12,8},{16,20},{20,16},{24,28},{28,24},{1,5},{5... | collective-permute-start | bytes 3145736 | tf_op jit(solution)/shard_map/ppermute | solution.py:710
  125.2 25.4 %collective-permute-start.23 = (bf16[256,2048]{1,0:T(8,128)(2,1)}, bf16[256,2048]{1,0:T(8,128)(2,1)}, u32[]{:S(2)}, u32[]{:S(2)}) collective-permute-start(bf16[256,2048]{1,0:T(8,128)(2,1)} %get-tuple-element.204.refs_2_), channel_id=1, source_target_pairs={{0,3},{1,0},{2,1},{3,2},{4,7},{5,4},{6,5},{7,6},{8,11},{9,8},{10,9... | collective-permute-start | bytes 3145736 | tf_op jit(solution)/shard_map/ppermute | solution.py:714
  126.3 20.8 %collective-permute-start.20 = (bf16[1280,256]{1,0:T(8,128)(2,1)}, bf16[1280,256]{1,0:T(8,128)(2,1)}, u32[]{:S(2)}, u32[]{:S(2)}) collective-permute-start(bf16[1280,256]{1,0:T(8,128)(2,1)} %get-tuple-element.200.refs_1_), channel_id=1, source_target_pairs={{0,8},{4,12},{8,0},{12,4},{16,24},{20,28},{24,16},{28,20},{1,9},{5... | collective-permute-start | bytes 1966088 | tf_op jit(solution)/shard_map/ppermute | solution.py:710
  126.8 20.3 %collective-permute-start.21 = (bf16[1280,256]{1,0:T(8,128)(2,1)S(1)}, bf16[1280,256]{1,0:T(8,128)(2,1)}, u32[]{:S(2)}, u32[]{:S(2)}) collective-permute-start(bf16[1280,256]{1,0:T(8,128)(2,1)S(1)} %get-tuple-element.198.refs_24_.refs_0_), channel_id=1, source_target_pairs={{0,16},{4,20},{8,24},{12,28},{16,0},{20,4},{24,8},{28,12},{1,17},{... | collective-permute-start | bytes 1966088 | tf_op jit(solution)/shard_map/ppermute | solution.py:710
  154.4 21.2 %collective-permute-start.26 = (bf16[256,2048]{1,0:T(8,128)(2,1)}, bf16[256,2048]{1,0:T(8,128)(2,1)}, u32[]{:S(2)}, u32[]{:S(2)}) collective-permute-start(bf16[256,2048]{1,0:T(8,128)(2,1)} %get-tuple-element.213.refs_4_), channel_id=1, source_target_pairs={{0,4},{4,0},{8,12},{12,8},{16,20},{20,16},{24,28},{28,24},{1,5},{5... | collective-permute-start | bytes 3145736 | tf_op jit(solution)/shard_map/ppermute | solution.py:710
  154.5 42.1 %collective-permute-start.27 = (bf16[256,2048]{1,0:T(8,128)(2,1)}, bf16[256,2048]{1,0:T(8,128)(2,1)}, u32[]{:S(2)}, u32[]{:S(2)}) collective-permute-start(bf16[256,2048]{1,0:T(8,128)(2,1)} %get-tuple-element.225.refs_3_), channel_id=1, source_target_pairs={{1,2},{2,3},{5,6},{6,7},{9,10},{10,11},{13,14},{14,15},{17,18},{18... | collective-permute-start | bytes 3145736 | tf_op jit(solution)/shard_map/ppermute | solution.py:724
  156.1 40.4 %collective-permute-start.28 = (bf16[256,2048]{1,0:T(8,128)(2,1)}, bf16[256,2048]{1,0:T(8,128)(2,1)}, u32[]{:S(2)}, u32[]{:S(2)}) collective-permute-start(bf16[256,2048]{1,0:T(8,128)(2,1)} %get-tuple-element.213.refs_4_), channel_id=1, source_target_pairs={{1,0},{2,1},{5,4},{6,5},{9,8},{10,9},{13,12},{14,13},{17,16},{18,1... | collective-permute-start | bytes 3145736 | tf_op jit(solution)/shard_map/ppermute | solution.py:725
  157.9 17.5 %collective-permute-start.24 = (bf16[1280,256]{1,0:T(8,128)(2,1)}, bf16[1280,256]{1,0:T(8,128)(2,1)}, u32[]{:S(2)}, u32[]{:S(2)}) collective-permute-start(bf16[1280,256]{1,0:T(8,128)(2,1)} %get-tuple-element.209.refs_2_), channel_id=1, source_target_pairs={{0,16},{4,20},{8,24},{12,28},{16,0},{20,4},{24,8},{28,12},{1,17},{... | collective-permute-start | bytes 1966088 | tf_op jit(solution)/shard_map/ppermute | solution.py:710
  158.5 17.2 %collective-permute-start.25 = (bf16[1280,256]{1,0:T(8,128)(2,1)}, bf16[1280,256]{1,0:T(8,128)(2,1)}, u32[]{:S(2)}, u32[]{:S(2)}) collective-permute-start(bf16[1280,256]{1,0:T(8,128)(2,1)} %get-tuple-element.212.refs_5_), channel_id=1, source_target_pairs={{0,8},{4,12},{8,0},{12,4},{16,24},{20,28},{24,16},{28,20},{1,9},{5... | collective-permute-start | bytes 1966088 | tf_op jit(solution)/shard_map/ppermute | solution.py:710
  201.6 13.3 %collective-permute-start.29 = (bf16[4,256,2048]{2,1,0:T(8,128)(2,1)}, bf16[4,256,2048]{2,1,0:T(8,128)(2,1)}, u32[]{:S(2)}, u32[]{:S(2)}) collective-permute-start(bf16[4,256,2048]{2,1,0:T(8,128)(2,1)} %get-tuple-element.226), channel_id=1, source_target_pairs={{0,4},{4,0},{8,12},{12,8},{16,20},{20,16},{24,28},{28,24},{1,5},{5... | collective-permute-start | bytes 12582920 | tf_op jit(solution)/shard_map/ppermute | solution.py:710
  201.6 13.3 %collective-permute-start.30 = (bf16[256,2048]{1,0:T(8,128)(2,1)}, bf16[256,2048]{1,0:T(8,128)(2,1)}, u32[]{:S(2)}, u32[]{:S(2)}) collective-permute-start(bf16[256,2048]{1,0:T(8,128)(2,1)} %get-tuple-element.227.refs_16_.refs_5_), channel_id=1, source_target_pairs={{0,4},{4,0},{8,12},{12,8},{16,20},{20,16},{24,28},{28,24},{1,5},{5... | collective-permute-start | bytes 3145736 | tf_op jit(solution)/shard_map/ppermute | solution.py:710
  218.7 43.0 %collective-permute-start.31 = (bf16[256,2048]{1,0:T(8,128)(2,1)}, bf16[256,2048]{1,0:T(8,128)(2,1)}, u32[]{:S(2)}, u32[]{:S(2)}) collective-permute-start(bf16[256,2048]{1,0:T(8,128)(2,1)} %fusion.11.refs_22_), channel_id=1, source_target_pairs={{0,1},{1,2},{4,5},{5,6},{8,9},{9,10},{12,13},{13,14},{16,17},{17,1... | collective-permute-start | bytes 3145736 | tf_op jit(solution)/shard_map/ppermute | solution.py:734
  224.3 37.5 %collective-permute-start.32 = (bf16[256,2048]{1,0:T(8,128)(2,1)}, bf16[256,2048]{1,0:T(8,128)(2,1)}, u32[]{:S(2)}, u32[]{:S(2)}) collective-permute-start(bf16[256,2048]{1,0:T(8,128)(2,1)} %fusion.11.refs_22_), channel_id=1, source_target_pairs={{3,2},{2,1},{7,6},{6,5},{11,10},{10,9},{15,14},{14,13},{19,18},{18... | collective-permute-start | bytes 3145736 | tf_op jit(solution)/shard_map/ppermute | solution.py:735
  259.3 51.1 %collective-permute-start.35 = (bf16[2,1280,256]{2,1,0:T(8,128)(2,1)}, bf16[2,1280,256]{2,1,0:T(8,128)(2,1)}, u32[]{:S(2)}, u32[]{:S(2)}) collective-permute-start(bf16[2,1280,256]{2,1,0:T(8,128)(2,1)} %get-tuple-element.239.refs_2_.refs_9_), channel_id=1, source_target_pairs={{0,16},{4,20},{8,24},{12,28},{16,0},{20,4},{24,8},{28,12},{1,17},{... | collective-permute-start | bytes 3932168 | tf_op jit(solution)/shard_map/ppermute | solution.py:710
  260.8 49.6 %collective-permute-start.36 = (bf16[2,1280,256]{2,1,0:T(8,128)(2,1)}, bf16[2,1280,256]{2,1,0:T(8,128)(2,1)}, u32[]{:S(2)}, u32[]{:S(2)}) collective-permute-start(bf16[2,1280,256]{2,1,0:T(8,128)(2,1)} %get-tuple-element.254), channel_id=1, source_target_pairs={{0,8},{4,12},{8,0},{12,4},{16,24},{20,28},{24,16},{28,20},{1,9},{5... | collective-permute-start | bytes 3932168 | tf_op jit(solution)/shard_map/ppermute | solution.py:710
  268.6 26.3 %collective-permute-start.33 = (bf16[256,2048]{1,0:T(8,128)(2,1)}, bf16[256,2048]{1,0:T(8,128)(2,1)}, u32[]{:S(2)}, u32[]{:S(2)}) collective-permute-start(bf16[256,2048]{1,0:T(8,128)(2,1)} %get-tuple-element.321.refs_10_), channel_id=1, source_target_pairs={{0,1},{1,2},{2,3},{3,0},{4,5},{5,6},{6,7},{7,4},{8,9},{9,10},{10,1... | collective-permute-start | bytes 3145736 | tf_op jit(solution)/shard_map/ppermute | solution.py:714
  296.2 43.1 %collective-permute-start.34 = (bf16[256,2048]{1,0:T(8,128)(2,1)}, bf16[256,2048]{1,0:T(8,128)(2,1)}, u32[]{:S(2)}, u32[]{:S(2)}) collective-permute-start(bf16[256,2048]{1,0:T(8,128)(2,1)} %get-tuple-element.246), channel_id=1, source_target_pairs={{0,3},{1,0},{2,1},{3,2},{4,7},{5,4},{6,5},{7,6},{8,11},{9,8},{10,9... | collective-permute-start | bytes 3145736 | tf_op jit(solution)/shard_map/ppermute | solution.py:714
  315.7 27.3 %collective-permute-start.38 = (bf16[1,1280,256]{2,1,0:T(8,128)(2,1)}, bf16[1,1280,256]{2,1,0:T(8,128)(2,1)S(1)}, u32[]{:S(2)}, u32[]{:S(2)}) collective-permute-start(bf16[1,1280,256]{2,1,0:T(8,128)(2,1)} %add_convert_fusion.2.refs_5_), channel_id=1, source_target_pairs={{0,16},{4,20},{8,24},{12,28},{16,0},{20,4},{24,8},{28,12},{1,17},{... | collective-permute-start | bytes 1966088 | tf_op jit(solution)/shard_map/ppermute | solution.py:710
  317.8 24.2 %collective-permute-start.39 = (bf16[128,2048]{1,0:T(8,128)(2,1)}, bf16[128,2048]{1,0:T(8,128)(2,1)}, u32[]{:S(2)}, u32[]{:S(2)}) collective-permute-start(bf16[128,2048]{1,0:T(8,128)(2,1)} %get-tuple-element.323), channel_id=1, source_target_pairs={{0,4},{4,0},{8,12},{12,8},{16,20},{20,16},{24,28},{28,24},{1,5},{5... | collective-permute-start | bytes 1572872 | tf_op jit(solution)/shard_map/ppermute | solution.py:710
  317.8 25.1 %collective-permute-start.40 = (bf16[128,2048]{1,0:T(8,128)(2,1)}, bf16[128,2048]{1,0:T(8,128)(2,1)}, u32[]{:S(2)}, u32[]{:S(2)}) collective-permute-start(bf16[128,2048]{1,0:T(8,128)(2,1)} %get-tuple-element.322), channel_id=1, source_target_pairs={{0,4},{4,0},{8,12},{12,8},{16,20},{20,16},{24,28},{28,24},{1,5},{5... | collective-permute-start | bytes 1572872 | tf_op jit(solution)/shard_map/ppermute | solution.py:710
  320.4 22.5 %collective-permute-start.37 = (bf16[1,1280,256]{2,1,0:T(8,128)(2,1)}, bf16[1,1280,256]{2,1,0:T(8,128)(2,1)}, u32[]{:S(2)}, u32[]{:S(2)}) collective-permute-start(bf16[1,1280,256]{2,1,0:T(8,128)(2,1)} %add_convert_fusion.3.refs_4_), channel_id=1, source_target_pairs={{0,8},{4,12},{8,0},{12,4},{16,24},{20,28},{24,16},{28,20},{1,9},{5... | collective-permute-start | bytes 1966088 | tf_op jit(solution)/shard_map/ppermute | solution.py:710
  339.3 53.1 %collective-permute-start.42 = (bf16[2,256,1024]{2,1,0:T(8,128)(2,1)}, bf16[2,256,1024]{2,1,0:T(8,128)(2,1)}, u32[]{:S(2)}, u32[]{:S(2)}) collective-permute-start(bf16[2,256,1024]{2,1,0:T(8,128)(2,1)} %get-tuple-element.259.refs_1_.refs_16_), channel_id=1, source_target_pairs={{0,16},{4,20},{8,24},{12,28},{16,0},{20,4},{24,8},{28,12},{1,17},{... | collective-permute-start | bytes 3145736 | tf_op jit(solution)/shard_map/ppermute | solution.py:710
  342.0 50.4 %collective-permute-start.43 = (bf16[2,256,1024]{2,1,0:T(8,128)(2,1)}, bf16[2,256,1024]{2,1,0:T(8,128)(2,1)}, u32[]{:S(2)}, u32[]{:S(2)}) collective-permute-start(bf16[2,256,1024]{2,1,0:T(8,128)(2,1)} %get-tuple-element.272), channel_id=1, source_target_pairs={{0,8},{4,12},{8,0},{12,4},{16,24},{20,28},{24,16},{28,20},{1,9},{5... | collective-permute-start | bytes 3145736 | tf_op jit(solution)/shard_map/ppermute | solution.py:710
  345.3 26.8 %collective-permute-start.41 = (bf16[1280,256]{1,0:T(8,128)(2,1)}, bf16[1280,256]{1,0:T(8,128)(2,1)S(1)}, u32[]{:S(2)}, u32[]{:S(2)}) collective-permute-start(bf16[1280,256]{1,0:T(8,128)(2,1)} %fusion.12.refs_17_), channel_id=1, source_target_pairs={{0,4},{4,0},{8,12},{12,8},{16,20},{20,16},{24,28},{28,24},{1,5},{5... | collective-permute-start | bytes 1966088 | tf_op jit(solution)/shard_map/ppermute | solution.py:710
  364.5 27.9 %collective-permute-start.44 = (bf16[256,2048]{1,0:T(8,128)(2,1)}, bf16[256,2048]{1,0:T(8,128)(2,1)}, u32[]{:S(2)}, u32[]{:S(2)}) collective-permute-start(bf16[256,2048]{1,0:T(8,128)(2,1)} %fusion.4.refs_15_), channel_id=1, source_target_pairs={{0,1},{1,2},{4,5},{5,6},{8,9},{9,10},{12,13},{13,14},{16,17},{17,1... | collective-permute-start | bytes 3145736 | tf_op jit(solution)/shard_map/ppermute | solution.py:734
  367.4 25.1 %collective-permute-start.45 = (bf16[256,2048]{1,0:T(8,128)(2,1)}, bf16[256,2048]{1,0:T(8,128)(2,1)}, u32[]{:S(2)}, u32[]{:S(2)}) collective-permute-start(bf16[256,2048]{1,0:T(8,128)(2,1)} %fusion.4.refs_15_), channel_id=1, source_target_pairs={{3,2},{2,1},{7,6},{6,5},{11,10},{10,9},{15,14},{14,13},{19,18},{18... | collective-permute-start | bytes 3145736 | tf_op jit(solution)/shard_map/ppermute | solution.py:735
  372.1 21.1 %collective-permute-start.48 = (bf16[256,2048]{1,0:T(8,128)(2,1)}, bf16[256,2048]{1,0:T(8,128)(2,1)}, u32[]{:S(2)}, u32[]{:S(2)}) collective-permute-start(bf16[256,2048]{1,0:T(8,128)(2,1)} %get-tuple-element.279), channel_id=1, source_target_pairs={{0,4},{4,0},{8,12},{12,8},{16,20},{20,16},{24,28},{28,24},{1,5},{5... | collective-permute-start | bytes 3145736 | tf_op jit(solution)/shard_map/ppermute | solution.py:710
  393.3 28.5 %collective-permute-start.50 = (bf16[256,2048]{1,0:T(8,128)(2,1)}, bf16[256,2048]{1,0:T(8,128)(2,1)}, u32[]{:S(2)}, u32[]{:S(2)}) collective-permute-start(bf16[256,2048]{1,0:T(8,128)(2,1)} %get-tuple-element.292), channel_id=1, source_target_pairs={{0,4},{4,0},{8,12},{12,8},{16,20},{20,16},{24,28},{28,24},{1,5},{5... | collective-permute-start | bytes 3145736 | tf_op jit(solution)/shard_map/ppermute | solution.py:710
  396.3 25.4 %collective-permute-start.47 = (bf16[1,256,1024]{2,1,0:T(8,128)(2,1)}, bf16[1,256,1024]{2,1,0:T(8,128)(2,1)}, u32[]{:S(2)}, u32[]{:S(2)}) collective-permute-start(bf16[1,256,1024]{2,1,0:T(8,128)(2,1)} %add_convert_fusion.5.refs_8_), channel_id=1, source_target_pairs={{0,16},{4,20},{8,24},{12,28},{16,0},{20,4},{24,8},{28,12},{1,17},{... | collective-permute-start | bytes 1572872 | tf_op jit(solution)/shard_map/ppermute | solution.py:710
  399.5 22.3 %collective-permute-start.46 = (bf16[1,256,1024]{2,1,0:T(8,128)(2,1)}, bf16[1,256,1024]{2,1,0:T(8,128)(2,1)S(1)}, u32[]{:S(2)}, u32[]{:S(2)}) collective-permute-start(bf16[1,256,1024]{2,1,0:T(8,128)(2,1)} %add_convert_fusion.6.refs_7_), channel_id=1, source_target_pairs={{0,8},{4,12},{8,0},{12,4},{16,24},{20,28},{24,16},{28,20},{1,9},{5... | collective-permute-start | bytes 1572872 | tf_op jit(solution)/shard_map/ppermute | solution.py:710
  400.4 21.3 %collective-permute-start.49 = (f32[7936]{0:T(1024)S(1)}, f32[7936]{0:T(1024)S(1)}, u32[]{:S(2)}, u32[]{:S(2)}) collective-permute-start(f32[7936]{0:T(1024)S(1)} %get-tuple-element.285), channel_id=1, source_target_pairs={{0,8},{4,12},{8,0},{12,4},{16,24},{20,28},{24,16},{28,20},{1,9},{5... | collective-permute-start | bytes 95240 | tf_op jit(solution)/shard_map/ppermute | solution.py:710
  418.3 26.5 %collective-permute-start.55 = (bf16[256,2048]{1,0:T(8,128)(2,1)}, bf16[256,2048]{1,0:T(8,128)(2,1)S(1)}, u32[]{:S(2)}, u32[]{:S(2)}) collective-permute-start(bf16[256,2048]{1,0:T(8,128)(2,1)} %fusion.3.refs_6_), channel_id=1, source_target_pairs={{0,1},{1,2},{2,3},{3,0},{4,5},{5,6},{6,7},{7,4},{8,9},{9,10},{10,1... | collective-permute-start | bytes 3145736 | tf_op jit(solution)/shard_map/ppermute | solution.py:714
  425.8 23.0 %collective-permute-start.54 = (bf16[256,2048]{1,0:T(8,128)(2,1)}, bf16[256,2048]{1,0:T(8,128)(2,1)S(1)}, u32[]{:S(2)}, u32[]{:S(2)}) collective-permute-start(bf16[256,2048]{1,0:T(8,128)(2,1)} %get-tuple-element.296), channel_id=1, source_target_pairs={{0,4},{4,0},{8,12},{12,8},{16,20},{20,16},{24,28},{28,24},{1,5},{5... | collective-permute-start | bytes 3145736 | tf_op jit(solution)/shard_map/ppermute | solution.py:710
  427.5 17.3 %collective-permute-start.53 = (f32[7936]{0:T(1024)S(1)}, f32[7936]{0:T(1024)S(1)}, u32[]{:S(2)}, u32[]{:S(2)}) collective-permute-start(f32[7936]{0:T(1024)S(1)} %add.229), channel_id=1, source_target_pairs={{0,16},{4,20},{8,24},{12,28},{16,0},{20,4},{24,8},{28,12},{1,17},{... | collective-permute-start | bytes 95240 | tf_op jit(solution)/shard_map/ppermute | solution.py:710
  428.4 19.8 %collective-permute-start.51 = (bf16[2,256,768]{2,1,0:T(8,128)(2,1)S(1)}, bf16[2,256,768]{2,1,0:T(8,128)(2,1)S(1)}, u32[]{:S(2)}, u32[]{:S(2)}) collective-permute-start(bf16[2,256,768]{2,1,0:T(8,128)(2,1)S(1)} %copy-done.35), channel_id=1, source_target_pairs={{0,16},{4,20},{8,24},{12,28},{16,0},{20,4},{24,8},{28,12},{1,17},{... | collective-permute-start | bytes 2359304 | tf_op jit(solution)/shard_map/ppermute | solution.py:710
  429.5 19.3 %collective-permute-start.52 = (bf16[2,256,768]{2,1,0:T(8,128)(2,1)S(1)}, bf16[2,256,768]{2,1,0:T(8,128)(2,1)S(1)}, u32[]{:S(2)}, u32[]{:S(2)}) collective-permute-start(bf16[2,256,768]{2,1,0:T(8,128)(2,1)S(1)} %copy-done.38), channel_id=1, source_target_pairs={{0,8},{4,12},{8,0},{12,4},{16,24},{20,28},{24,16},{28,20},{1,9},{5... | collective-permute-start | bytes 2359304 | tf_op jit(solution)/shard_map/ppermute | solution.py:710
  450.2 10.1 %collective-permute-start.58 = (bf16[1,256,768]{2,1,0:T(8,128)(2,1)S(1)}, bf16[1,256,768]{2,1,0:T(8,128)(2,1)S(1)}, u32[]{:S(2)}, u32[]{:S(2)}) collective-permute-start(bf16[1,256,768]{2,1,0:T(8,128)(2,1)S(1)} %add_convert_fusion.8), channel_id=1, source_target_pairs={{0,16},{4,20},{8,24},{12,28},{16,0},{20,4},{24,8},{28,12},{1,17},{... | collective-permute-start | bytes 1179656 | tf_op jit(solution)/shard_map/ppermute | solution.py:710
  451.3 9.8 %collective-permute-start.57 = (bf16[1,256,768]{2,1,0:T(8,128)(2,1)S(1)}, bf16[1,256,768]{2,1,0:T(8,128)(2,1)S(1)}, u32[]{:S(2)}, u32[]{:S(2)}) collective-permute-start(bf16[1,256,768]{2,1,0:T(8,128)(2,1)S(1)} %add_convert_fusion.9), channel_id=1, source_target_pairs={{0,8},{4,12},{8,0},{12,4},{16,24},{20,28},{24,16},{28,20},{1,9},{5... | collective-permute-start | bytes 1179656 | tf_op jit(solution)/shard_map/ppermute | solution.py:710
  453.2 31.4 %collective-permute-start.56 = (bf16[256,2048]{1,0:T(8,128)(2,1)S(1)}, bf16[256,2048]{1,0:T(8,128)(2,1)}, u32[]{:S(2)}, u32[]{:S(2)}) collective-permute-start(bf16[256,2048]{1,0:T(8,128)(2,1)S(1)} %get-tuple-element.304), channel_id=1, source_target_pairs={{0,3},{1,0},{2,1},{3,2},{4,7},{5,4},{6,5},{7,6},{8,11},{9,8},{10,9... | collective-permute-start | bytes 3145736 | tf_op jit(solution)/shard_map/ppermute | solution.py:714
  455.9 23.4 %collective-permute-start.64 = (bf16[256,1024]{1,0:T(8,128)(2,1)S(1)}, bf16[256,1024]{1,0:T(8,128)(2,1)}, u32[]{:S(2)}, u32[]{:S(2)}) collective-permute-start(bf16[256,1024]{1,0:T(8,128)(2,1)S(1)} %get-tuple-element.319), channel_id=1, source_target_pairs={{0,4},{4,0},{8,12},{12,8},{16,20},{20,16},{24,28},{28,24},{1,5},{5... | collective-permute-start | bytes 1572872 | tf_op jit(solution)/shard_map/ppermute | solution.py:710
  463.6 14.3 %collective-permute-start.61 = (f32[4096]{0:T(1024)}, f32[4096]{0:T(1024)}, u32[]{:S(2)}, u32[]{:S(2)}) collective-permute-start(f32[4096]{0:T(1024)} %slice_add_fusion), channel_id=1, source_target_pairs={{0,1},{1,0},{2,3},{3,2},{4,5},{5,4},{6,7},{7,6},{8,9},{9,8},{10,11... | collective-permute-start | bytes 49160 | tf_op jit(solution)/shard_map/ppermute | solution.py:1097
  463.7 14.2 %collective-permute-start.62 = (f32[4096]{0:T(1024)}, f32[4096]{0:T(1024)}, u32[]{:S(2)}, u32[]{:S(2)}) collective-permute-start(f32[4096]{0:T(1024)} %slice_add_fusion), channel_id=1, source_target_pairs={{0,2},{1,3},{2,0},{3,1},{4,6},{5,7},{6,4},{7,5},{8,10},{9,11},{10,... | collective-permute-start | bytes 49160 | tf_op jit(solution)/shard_map/ppermute | solution.py:1097
  464.6 13.3 %collective-permute-start.63 = (f32[4096]{0:T(1024)}, f32[4096]{0:T(1024)}, u32[]{:S(2)}, u32[]{:S(2)}) collective-permute-start(f32[4096]{0:T(1024)} %slice_add_fusion), channel_id=1, source_target_pairs={{0,3},{1,2},{2,1},{3,0},{4,7},{5,6},{6,5},{7,4},{8,11},{9,10},{10,... | collective-permute-start | bytes 49160 | tf_op jit(solution)/shard_map/ppermute | solution.py:1097
  477.9 4.1 collective-permute-start.59
  (80 other events, 473.3 us)

commit v8 on v7

v8 whole, which is shorter than its diff:
```python
import functools

import jax
import jax.numpy as jnp
import numpy as np
from jax import lax
from jax.experimental import pallas as pl
from jax.experimental.pallas import tpu as pltpu
from jax.sharding import PartitionSpec as P

HEAD_DIM = 64
ROT = 32
EPS = 1e-05
LANES = 128
F32 = jnp.float32
BF16 = jnp.bfloat16
HBM = pl.BlockSpec(memory_space=pltpu.HBM)


def dot(lhs, rhs, lhs_dim, rhs_dim):
    return lax.dot_general(
        lhs, rhs, (((lhs_dim,), (rhs_dim,)), ((), ())), preferred_element_type=F32
    )


def call(kernel, name, operands, deps=(), scalars=(), vmem=63, **spec):
    deps, many, lead = tuple(deps), len(operands), len(scalars)

    def body(*refs):
        kernel(*refs[: lead + many], *refs[lead + many + len(deps) :])

    in_specs = list(spec.pop("in_specs")) + [HBM] * len(deps)
    out_shape, aliases = spec.pop("out_shape"), spec.pop("input_output_aliases", {})
    if scalars:
        grid_spec = pltpu.PrefetchScalarGridSpec(
            num_scalar_prefetch=lead, in_specs=in_specs, **spec
        )
        spec = {"grid_spec": grid_spec}
    else:
        spec["in_specs"] = in_specs
    return pl.pallas_call(
        body,
        out_shape=out_shape,
        input_output_aliases=aliases,
        compiler_params=pltpu.CompilerParams(vmem_limit_bytes=vmem << 20),
        cost_estimate=pl.CostEstimate(flops=0, transcendentals=0, bytes_accessed=0),
        name=name,
        **spec,
    )(*scalars, *operands, *deps)


def fence(values, deps=()):
    return call(
        lambda *refs: None,
        "fence",
        values,
        deps,
        in_specs=[HBM] * len(values),
        out_specs=[HBM] * len(values),
        out_shape=[jax.ShapeDtypeStruct(v.shape, v.dtype) for v in values],
        input_output_aliases={n: n for n in range(len(values))},
    )


def rotary_tables(length):
    positions = np.arange(length, dtype=np.float32)
    frequency = 10000.0 ** (-np.arange(ROT // 2, dtype=np.float64) * 2.0 / ROT)
    angles = positions[:, None] * frequency.astype(np.float32)[None, :]
    cosine, sine = np.cos(angles.astype(np.float64)), np.sin(angles.astype(np.float64))
    rest = HEAD_DIM - ROT
    none = np.zeros((length, ROT // 2))
    ones, zeros = np.ones((length, rest)), np.zeros((length, rest))
    straight = np.concatenate([cosine, cosine, ones], axis=1)
    left = np.concatenate([-sine, none, zeros], axis=1)
    right = np.concatenate([none, sine, zeros], axis=1)
    return [
        jnp.asarray(np.concatenate([t, t], axis=1).astype(np.float32))
        for t in (straight, left, right)
    ]


def rotated(u, straight, left, right, sign):
    half = ROT // 2
    turned = pltpu.roll(u, LANES - half, 1) * left + pltpu.roll(u, half, 1) * right
    return u * straight + sign * turned


def normalized(x):
    x = x.astype(F32)
    centered = x - jnp.mean(x, axis=1, keepdims=True)
    variance = jnp.mean(centered * centered, axis=1, keepdims=True)
    return centered * lax.rsqrt(variance + EPS)


def block_copies(blocks, place, sems):
    me = lax.axis_index("dp")
    return [
        pltpu.make_async_copy(block, place(lax.bitwise_xor(me, j)), sems.at[j])
        for j, block in enumerate(blocks)
    ]


def span(owner, size):
    return pl.ds(pl.multiple_of(owner * size, size), size)


def rows_at(ref, size):
    return lambda owner: ref.at[pl.ds(pl.multiple_of(owner * size, size), size)]


def columns_at(ref, size):
    return lambda owner: ref.at[:, pl.ds(pl.multiple_of(owner * size, size), size)]


def project_kernel(setup, x_ref, bias_ref, gain_ref, shift_ref, cos_ref, left_ref, right_ref, *rest):
    count, width, hidden = setup
    blocks = rest[:count]
    qkv_ref, act_ref, slope_ref, normed_ref, held, sems = rest[-6:]

    @pl.when(pl.program_id(0) == 0)
    def _():
        loads = block_copies(blocks, rows_at(held, blocks[0].shape[0]), sems)
        for copy in loads:
            copy.start()
        for copy in loads:
            copy.wait()

    x = (normalized(x_ref[...]) * gain_ref[...] + shift_ref[...]).astype(BF16)
    normed_ref[...] = x
    root = 0.7978845608028654
    for t in range((3 * width + hidden) // width):
        columns = slice(t * width, (t + 1) * width)
        y = dot(x, held[:, columns], 1, 0) + bias_ref[:, columns]
        if t < 3:
            for g in range(width // LANES):
                part = y[:, g * LANES : (g + 1) * LANES]
                if t < 2:
                    part = rotated(part, cos_ref[...], left_ref[...], right_ref[...], 1.0)
                if t == 0:
                    part = part * HEAD_DIM**-0.5
                start = t * width + g * LANES
                qkv_ref[:, start : start + LANES] = part.astype(BF16)
        else:
            columns = slice((t - 3) * width, (t - 2) * width)
            square = y * y
            turn = jnp.tanh(root * y * (1.0 + 0.044715 * square))
            half = 0.5 * (1.0 + turn)
            act_ref[:, columns] = (y * half).astype(BF16)
            slope = half * (1.0 + y * (1.0 - turn) * (root + (3.0 * 0.044715 * root) * square))
            slope_ref[:, columns] = slope.astype(BF16)


def project(sequence, x, blocks, bias, gain, shift, tables, width, tile, earlier, deps):
    (length, model), total, count = x.shape, blocks[0].shape[1], len(blocks)
    hidden, steps = total - 3 * width, length // tile
    rows = lambda w: pl.BlockSpec((tile, w), lambda i: (i, 0))
    out = lambda w: pl.BlockSpec((tile, w), lambda i: (sequence * steps + i, 0))
    line = lambda a: pl.BlockSpec(a.shape, lambda i: (0, 0))
    widths = (3 * width, hidden, hidden, model)
    operands = [x, bias, gain, shift, *tables, *blocks]
    return call(
        functools.partial(project_kernel, (count, width, hidden)),
        "project",
        operands + list(earlier),
        deps,
        grid=(steps,),
        in_specs=[rows(model), line(bias), line(gain), line(shift)]
        + [rows(LANES)] * 3
        + [HBM] * (count + len(earlier)),
        out_specs=[out(w) for w in widths],
        out_shape=[jax.ShapeDtypeStruct((2 * length, w), BF16) for w in widths],
        input_output_aliases={len(operands) + n: n for n in range(len(earlier))},
        scratch_shapes=[pltpu.VMEM((model, total), BF16), pltpu.SemaphoreType.DMA((count,))],
    )


def attend_kernel(block, q_ref, k_ref, v_ref, out_ref, lse_ref):
    length = q_ref.shape[0]
    lane = lax.broadcasted_iota(jnp.int32, (1, LANES), 1)
    key = lax.broadcasted_iota(jnp.int32, (block, block), 0)
    causal = key <= lax.broadcasted_iota(jnp.int32, (block, block), 1)
    for i in range(length // block):
        rows, before = pl.ds(i * block, block), pl.ds(0, i * block)
        results = []
        for h in range(2):
            mine = (lane < HEAD_DIM) if h == 0 else (lane >= HEAD_DIM)
            query = jnp.where(mine, q_ref[rows, :], 0)
            near = jnp.where(causal, dot(k_ref[rows, :], query, 1, 1), -1e30)
            highest = jnp.max(near, axis=0, keepdims=True)
            if i:
                far = dot(k_ref[before, :], query, 1, 1)
                highest = jnp.maximum(highest, jnp.max(far, axis=0, keepdims=True))
            near = jnp.exp(near - highest)
            total = jnp.sum(near, axis=0, keepdims=True)
            if i:
                far = jnp.exp(far - highest)
                total = total + jnp.sum(far, axis=0, keepdims=True)
            inverse = 1.0 / total
            result = dot((near * inverse).astype(BF16), v_ref[rows, :], 0, 0)
            if i:
                result = result + dot((far * inverse).astype(BF16), v_ref[before, :], 0, 0)
            results.append(result)
            lse_ref[0, h : h + 1, rows] = highest + jnp.log(total)
        out_ref[rows, :] = jnp.where(lane < HEAD_DIM, results[0], results[1]).astype(BF16)


def pair_specs(length, pairs):
    return lambda off: pl.BlockSpec(
        (length, LANES), lambda g: (g // pairs, off * pairs + g % pairs)
    )


def attend(qkv, length, block, deps):
    width, sequences = qkv.shape[1] // 3, qkv.shape[0] // length
    pairs = width // LANES
    at = pair_specs(length, pairs)
    return call(
        functools.partial(attend_kernel, block),
        "attend",
        [qkv, qkv, qkv],
        deps,
        grid=(sequences * pairs,),
        in_specs=[at(0), at(1), at(2)],
        out_specs=[at(0), pl.BlockSpec((1, 8, length), lambda g: (g, 0, 0))],
        out_shape=[
            jax.ShapeDtypeStruct((qkv.shape[0], width), BF16),
            jax.ShapeDtypeStruct((sequences * pairs, 8, length), F32),
        ],
    )


def attend_back_kernel(
    block,
    q_ref,
    k_ref,
    v_ref,
    grad_ref,
    mixed_ref,
    lse_ref,
    cos_ref,
    left_ref,
    right_ref,
    gq_ref,
    gk_ref,
    gv_ref,
    sum_ref,
    gk_sum,
    gv_sum,
):
    length = q_ref.shape[0]
    lane = lax.broadcasted_iota(jnp.int32, (1, LANES), 1)
    key = lax.broadcasted_iota(jnp.int32, (block, block), 0)
    causal = key <= lax.broadcasted_iota(jnp.int32, (block, block), 1)
    count = length // block
    sum_ref[...] = jnp.zeros_like(sum_ref)

    def put(ref, which, rows, value):
        value = value.astype(BF16)
        ref[rows, :] = value
        sum_ref[0, which : which + 1, :] += jnp.sum(value.astype(F32), axis=0, keepdims=True)

    def unrotated(value, rows):
        return rotated(value, cos_ref[rows, :], left_ref[rows, :], right_ref[rows, :], -1.0)

    for i in reversed(range(count)):
        rows = pl.ds(i * block, block)
        product = grad_ref[rows, :].astype(F32) * mixed_ref[rows, :].astype(F32)
        gq = None
        for h in range(2):
            mine = (lane < HEAD_DIM) if h == 0 else (lane >= HEAD_DIM)
            query = jnp.where(mine, q_ref[rows, :], 0)
            grad = jnp.where(mine, grad_ref[rows, :], 0)
            ones = jnp.where(mine, jnp.ones((8, LANES), F32), 0.0)
            delta = lax.dot_general(
                ones,
                product,
                (((1,), (1,)), ((), ())),
                precision=lax.Precision.HIGHEST,
                preferred_element_type=F32,
            )[0:1, :]
            lse = lse_ref[0, h : h + 1, rows]
            for j in range(i + 1):
                keys = pl.ds(j * block, block)
                key_rows = k_ref[keys, :]
                probs = jnp.exp(dot(key_rows, query, 1, 1) - lse)
                if j == i:
                    probs = jnp.where(causal, probs, 0.0)
                gprobs = dot(v_ref[keys, :], grad, 1, 1)
                gscores = (probs * (gprobs - delta)).astype(BF16)
                gv, gk = dot(probs.astype(BF16), grad, 1, 0), dot(gscores, query, 1, 0)
                if i == count - 1 and h == 0:
                    gv_sum[keys, :] = gv
                    gk_sum[keys, :] = gk
                else:
                    gv_sum[keys, :] += gv
                    gk_sum[keys, :] += gk
                part = dot(gscores, jnp.where(mine, key_rows, 0), 0, 0)
                gq = part if gq is None else gq + part
        put(gq_ref, 0, rows, unrotated(gq * HEAD_DIM**-0.5, rows))
    for i in range(count):
        rows = pl.ds(i * block, block)
        put(gk_ref, 1, rows, unrotated(gk_sum[rows, :], rows))
        put(gv_ref, 2, rows, gv_sum[rows, :])


def attend_back(qkv, grad, mixed, lse, tables, length, block, deps):
    width, sequences = qkv.shape[1] // 3, qkv.shape[0] // length
    pairs = width // LANES
    at = pair_specs(length, pairs)
    table = pl.BlockSpec((length, LANES), lambda g: (0, 0))
    small = pl.BlockSpec((1, 8, length), lambda g: (g, 0, 0))
    return call(
        functools.partial(attend_back_kernel, block),
        "attend_back",
        [qkv, qkv, qkv, grad, mixed, lse, *tables],
        deps,
        grid=(sequences * pairs,),
        in_specs=[at(0), at(1), at(2), at(0), at(0), small, table, table, table],
        out_specs=[at(0)] * 3 + [pl.BlockSpec((1, 8, LANES), lambda g: (g, 0, 0))],
        out_shape=[jax.ShapeDtypeStruct((qkv.shape[0], width), BF16)] * 3
        + [jax.ShapeDtypeStruct((sequences * pairs, 8, LANES), F32)],
        scratch_shapes=[pltpu.VMEM((length, LANES), F32)] * 2,
    )


def by_sequence(tile, width, steps):
    return [
        pl.BlockSpec((tile, width), lambda i: (jnp.minimum(i, steps - 1), 0)),
        pl.BlockSpec((tile, width), lambda i: (jnp.maximum(i - steps, 0), 0)),
    ]


def other_first(tile, width, steps):
    return pl.BlockSpec((tile, width), lambda i: ((i + steps) % (2 * steps), 0))


def put_by_sequence(step, steps, value, other_ref, own_ref):
    @pl.when(step < steps)
    def _():
        other_ref[...] = value

    @pl.when(step >= steps)
    def _():
        own_ref[...] = value


def branch_kernel(count, steps, mixed_ref, act_ref, *rest):
    blocks, (other_ref, own_ref, held, sems) = rest[:count], rest[count:]
    step = pl.program_id(0)

    @pl.when(step == 0)
    def _():
        loads = block_copies(blocks, columns_at(held, blocks[0].shape[1]), sems)
        for copy in loads:
            copy.start()
        for copy in loads:
            copy.wait()

    x = jnp.concatenate([mixed_ref[...], act_ref[...]], axis=1)
    put_by_sequence(step, steps, dot(x, held[...], 1, 0).astype(BF16), other_ref, own_ref)


def branch_sums(mixed, act, blocks, tile, deps):
    length, count = mixed.shape[0] // 2, len(blocks)
    inner, model, steps = blocks[0].shape[0], count * blocks[0].shape[1], length // tile
    return call(
        functools.partial(branch_kernel, count, steps),
        "branch_sums",
        [mixed, act, *blocks],
        deps,
        grid=(2 * steps,),
        in_specs=[other_first(tile, a.shape[1], steps) for a in (mixed, act)] + [HBM] * count,
        out_specs=by_sequence(tile, model, steps),
        out_shape=[jax.ShapeDtypeStruct((length, model), BF16)] * 2,
        scratch_shapes=[pltpu.VMEM((inner, model), BF16), pltpu.SemaphoreType.DMA((count,))],
    )


def grad_in_kernel(setup, dy_ref, slope_ref, *rest):
    count, width, hidden = setup
    blocks = rest[:count]
    gmixed_ref, gpre_ref, gsum_ref, dsum_ref, held, sems = rest[-6:]

    @pl.when(pl.program_id(0) == 0)
    def _():
        loads = block_copies(blocks, columns_at(held, blocks[0].shape[1]), sems)
        for copy in loads:
            copy.start()
        gsum_ref[...] = jnp.zeros_like(gsum_ref)
        dsum_ref[...] = jnp.zeros_like(dsum_ref)
        for copy in loads:
            copy.wait()

    dy = dy_ref[...]
    gmixed_ref[...] = dot(dy, held[:width, :], 1, 1).astype(BF16)
    for start in range(0, hidden, width):
        part = slice(start, start + width)
        gact = dot(dy, held[width + start : 2 * width + start, :], 1, 1)
        gpre = (gact * slope_ref[:, part].astype(F32)).astype(BF16)
        gpre_ref[:, part] = gpre
        gsum_ref[0:1, part] += jnp.sum(gpre.astype(F32), axis=0, keepdims=True)
    dsum_ref[0:1, :] += jnp.sum(dy.astype(F32), axis=0, keepdims=True)


def grad_in(sequence, dy, slope, blocks, width, tile, earlier, deps):
    (length, model), hidden, count = dy.shape, slope.shape[1], len(blocks)
    steps = length // tile
    out = lambda w: pl.BlockSpec((tile, w), lambda i: (sequence * steps + i, 0))
    total = lambda w: pl.BlockSpec((8, w), lambda i: (0, 0))
    operands = [dy, slope, *blocks]
    return call(
        functools.partial(grad_in_kernel, (count, width, hidden)),
        "grad_in",
        operands + list(earlier),
        deps,
        grid=(steps,),
        in_specs=[pl.BlockSpec((tile, model), lambda i: (i, 0)), out(hidden)]
        + [HBM] * (count + len(earlier)),
        out_specs=[out(width), out(hidden), total(hidden), total(model)],
        out_shape=[jax.ShapeDtypeStruct((2 * length, w), BF16) for w in (width, hidden)]
        + [jax.ShapeDtypeStruct((8, w), F32) for w in (hidden, model)],
        input_output_aliases={len(operands) + n: n for n in range(len(earlier))},
        scratch_shapes=[
            pltpu.VMEM((width + hidden, model), BF16),
            pltpu.SemaphoreType.DMA((count,)),
        ],
    )


def grad_normed_kernel(
    count, steps, half, gq_ref, gk_ref, gv_ref, gpre_ref, x_other_ref, x_own_ref, *rest
):
    blocks, (early_ref, late_ref, own_ref, sum_ref, held, normal, sems) = rest[:count], rest[count:]
    step, size, few = pl.program_id(0), blocks[0].shape[0], count // 2
    me = lax.axis_index("dp")

    @pl.when(step == 0)
    def _():
        for start in (True, False):
            for j, block in enumerate(blocks):
                owner = lax.bitwise_xor(me, j) - half * few

                @pl.when((owner >= 0) & (owner < few))
                def _(start=start, j=j, block=block, owner=owner):
                    copy = pltpu.make_async_copy(block, held.at[span(owner, size)], sems.at[j])
                    if start:
                        copy.start()
                    else:
                        copy.wait()

        sum_ref[...] = jnp.zeros_like(sum_ref)

    columns = slice(half * few * size, (half + 1) * few * size)

    @pl.when(step < steps)
    def _():
        normal[...] = normalized(x_other_ref[...])[:, columns]

    @pl.when(step >= steps)
    def _():
        normal[...] = normalized(x_own_ref[...])[:, columns]

    g = jnp.concatenate([gq_ref[...], gk_ref[...], gv_ref[...], gpre_ref[...]], axis=1)
    result = dot(g, held[...], 1, 1)
    sum_ref[0:1, :] += jnp.sum(result * normal[...], axis=0, keepdims=True)
    sum_ref[1:2, :] += jnp.sum(result, axis=0, keepdims=True)
    result = result.astype(BF16)
    for n, ref in enumerate((early_ref, late_ref)):

        @pl.when(step // (steps // 2) == n)
        def _(ref=ref):
            ref[...] = result

    @pl.when(step >= steps)
    def _():
        own_ref[...] = result


def grad_normed_sums(half, gqkv, gpre, x_own, x_other, blocks, tile, deps):
    (length, model), count, total = x_own.shape, len(blocks), blocks[0].shape[1]
    steps, part = length // tile, model // 2
    few = steps // 2
    operands = [*gqkv, gpre]
    return call(
        functools.partial(grad_normed_kernel, count, steps, half),
        "grad_normed_sums",
        operands + [x_other, x_own, *blocks],
        deps,
        grid=(2 * steps,),
        in_specs=[other_first(tile, a.shape[1], steps) for a in operands]
        + by_sequence(tile, model, steps)
        + [HBM] * count,
        out_specs=[
            pl.BlockSpec((tile, part), lambda i: (jnp.minimum(i, few - 1), 0)),
            pl.BlockSpec((tile, part), lambda i: (jnp.clip(i - few, 0, few - 1), 0)),
        ]
        + by_sequence(tile, part, steps)[1:]
        + [pl.BlockSpec((8, part), lambda i: (0, 0))],
        out_shape=[jax.ShapeDtypeStruct((length // 2, part), BF16)] * 2
        + [jax.ShapeDtypeStruct((length, part), BF16), jax.ShapeDtypeStruct((8, part), F32)],
        scratch_shapes=[
            pltpu.VMEM((part, total), BF16),
            pltpu.VMEM((tile, part), F32),
            pltpu.SemaphoreType.DMA((count,)),
        ],
    )


def weight_grad_kernel(writes, left, rows, many, at_ref, *refs):
    cuts, (*refs, held, grad, sems) = refs[:many], refs[many:]
    whole, outs = refs[: len(refs) - len(writes)], refs[len(refs) - len(writes) :]
    step, core, loads, first = pl.program_id(0), lax.rem(lax.axis_index("dp"), 2), [], 0
    for ref in whole:
        columns = pl.ds(first, ref.shape[1])
        first += ref.shape[1]
        for start in range(0, ref.shape[0], rows):
            part = pl.ds(start, rows)
            loads.append((ref.at[part], held.at[part, columns]))
    loads = [pltpu.make_async_copy(*pair, sems.at[n]) for n, pair in enumerate(loads)]

    @pl.when(step == 0)
    def _():
        for copy in loads:
            copy.start()
        for copy in loads:
            copy.wait()

    cut = jnp.concatenate([ref[...] for ref in cuts], axis=0)
    pair = (cut, held[...]) if left else (held[...], cut)
    grad[...] = dot(*pair, 0, 0).astype(BF16)
    size = cut.shape[1] // 2
    for half, steps, out_ref in writes_of(writes, outs):
        here = functools.reduce(jnp.logical_or, [step == s for s in steps])

        @pl.when(here)
        def _(half=half, out_ref=out_ref):
            mine = span(core if half == 0 else 1 - core, size)
            out_ref[0] = grad[mine, :] if left else grad[:, mine]


def writes_of(writes, outs):
    return [(half, steps, out) for (half, steps), out in zip(writes, outs)]


def weight_grads(me, xs, gs, count, deps, left):
    plan, chips = scatter_plan(count), count // 2
    order = [j // 2 for s in plan[0] for j in s]
    sets = [(half, s) for s in range(len(plan[0])) for half in range(2)]
    writes = [(half, [order.index(j // 2) for j in plan[half][s]]) for half, s in sets]
    table = []
    for _, steps in writes:
        for i in range(chips):
            later = [w for w in steps if w >= i]
            table.append(steps.index(min(later) if later else max(steps)))
    owners = lax.bitwise_xor(me // 2, jnp.array(order, jnp.int32))
    at = jnp.concatenate([owners, jnp.array(table, jnp.int32)])
    cut, whole = (xs, gs) if left else (gs, xs)
    length = whole[0].shape[0]
    size, full = cut[0].shape[1] // count, sum(a.shape[1] for a in whole)
    shape = (size, full) if left else (full, size)
    pieces = 8 // len(whole)

    def out(n):
        return pl.BlockSpec((1, *shape), lambda i, at: (at[chips * (n + 1) + i], 0, 0))

    outs = call(
        functools.partial(weight_grad_kernel, writes, left, length // pieces, len(cut)),
        "weight_grads",
        [*cut, *whole],
        deps,
        (at,),
        grid=(chips,),
        in_specs=[pl.BlockSpec((a.shape[0], 2 * size), lambda i, at: (0, at[i])) for a in cut]
        + [HBM] * len(whole),
        out_specs=[out(n) for n in range(len(sets))],
        out_shape=[
            jax.ShapeDtypeStruct((len(plan[half][s]), *shape), BF16) for half, s in sets
        ],
        scratch_shapes=[
            pltpu.VMEM((length, full), BF16),
            pltpu.VMEM((2 * size, full) if left else (full, 2 * size), BF16),
            pltpu.SemaphoreType.DMA((pieces * len(whole),)),
        ],
    )
    return [[o for o, (half, _) in zip(outs, sets) if half == h] for h in range(2)]


def norm_back_kernel(tokens_ref, dy_ref, gain_ref, left_ref, right_ref, out_ref):
    x = tokens_ref[...].astype(F32)
    centered = x - jnp.mean(x, axis=1, keepdims=True)
    inverse_std = lax.rsqrt(jnp.mean(centered * centered, axis=1, keepdims=True) + EPS)
    normal = centered * inverse_std
    grad = jnp.concatenate([left_ref[...], right_ref[...]], axis=1).astype(F32)
    scaled = grad * gain_ref[...]
    first_mean = jnp.mean(scaled, axis=1, keepdims=True)
    second_mean = jnp.mean(scaled * normal, axis=1, keepdims=True)
    back = (scaled - first_mean - normal * second_mean) * inverse_std
    out_ref[...] = (dy_ref[...].astype(F32) + back).astype(BF16)


def norm_back(tokens, dy, gain, halves, deps):
    rows, model = tokens.shape
    tile = min(64, rows)
    part = lambda w: pl.BlockSpec((tile, w), lambda i: (i, 0))
    return call(
        norm_back_kernel,
        "norm_back",
        [tokens, dy, gain, *halves],
        deps,
        grid=(rows // tile,),
        in_specs=[part(model), part(model), pl.BlockSpec((1, model), lambda i: (0, 0))]
        + [part(model // 2)] * 2,
        out_specs=part(model),
        out_shape=jax.ShapeDtypeStruct((rows, model), BF16),
    )


def across(value, bit, count):
    return lax.ppermute(value, "dp", [(i, i ^ bit) for i in range(count)])


def added(addends):
    return sum(a.astype(F32) for a in addends).astype(BF16)


def chip_bits(count):
    bits, bit = [], 2
    while bit < count:
        bits.append(bit)
        bit *= 2
    return bits


class BlockGather:
    def __init__(self, own, sibling, count):
        self.held, self.count = {0: own, 1: sibling}, count
        self.orders = (chip_bits(count), chip_bits(count)[::-1])

    def own_to(self, s):
        if s < len(self.orders[0]):
            for half in range(2):
                bit = self.orders[half][s]
                self.held[half ^ bit] = across(self.held[half], bit, self.count)

    def rest(self):
        for s in range(1, len(self.orders[0])):
            for half in range(2):
                order = self.orders[half]
                for j in [j for j in self.held if j % 2 == half]:
                    if j ^ order[s] not in self.held and not any(j & b for b in order[s:]):
                        self.held[j ^ order[s]] = across(self.held[j], order[s], self.count)

    def fenced(self, others=(), deps=()):
        keys = sorted(self.held)
        values = fence([self.held[j] for j in keys] + list(others), deps)
        self.held = dict(zip(keys, values))
        return values[len(keys) :]

    def blocks(self):
        return [self.held[j] for j in range(self.count)]


def scatter_orders(count):
    return (chip_bits(count)[::-1], chip_bits(count))


def scatter_plan(count):
    plan = []
    for half, order in enumerate(scatter_orders(count)):
        sets, rest = [[half]], [half]
        for bit in reversed(order):
            sets.insert(0, [j ^ bit for j in rest])
            rest = sets[0] + rest
        plan.append(sets)
    return plan


class BlockScatter:
    def __init__(self, halves, count):
        self.count, self.orders = count, scatter_orders(count)
        self.held = [[[a] for a in arrays] for arrays in halves]
        self.steps = len(self.orders[0])

    def total(self, half, s):
        if len(self.held[half][s]) > 1:
            self.held[half][s] = [added(self.held[half][s])]
        return self.held[half][s][0]

    def ready(self, s):
        return [self.total(half, s) for half in range(2)]

    def send(self, s):
        return [across(self.total(h, s), self.orders[h][s], self.count) for h in range(2)]

    def arrive(self, s, came):
        for half in range(2):
            first = 0
            for later in self.held[half][s + 1 :]:
                many = later[0].shape[0]
                later.append(came[half][first : first + many])
                first += many

    def between(self):
        for s in range(1, self.steps - 1):
            self.arrive(s, self.send(s))

    def last(self):
        return self.total(1, -1)[0]

    def finish(self, theirs):
        return sum(a[0].astype(F32) for a in self.held[0][-1]), theirs.astype(F32)


def on_device(
    tokens,
    norm_gain,
    norm_bias,
    qkv_weight,
    qkv_bias,
    dense_weight,
    dense_bias,
    up_weight,
    up_bias,
    down_weight,
    down_bias,
    cotangent,
    *,
    ndp,
    nmp,
):
    me = lax.axis_index("dp")
    core = me % 2
    length, model = tokens.shape[0] * nmp, tokens.shape[1]
    tile, block = min(256, length), min(512, length)
    width, hidden = qkv_weight.shape[2] // 2, up_weight.shape[1] // 2
    chip_steps = len(chip_bits(ndp))
    rank = lambda array, axis, which, size: lax.dynamic_slice_in_dim(
        array, which * size, size, axis
    )

    def row_pack(which):
        qkv = rank(qkv_weight, 2, which, width)
        return jnp.concatenate([qkv[0], qkv[1], qkv[2], rank(up_weight, 1, which, hidden)], axis=1)

    def column_pack(which):
        return jnp.concatenate(
            [rank(dense_weight, 0, which, width), rank(down_weight, 0, which, hidden)], axis=0
        )

    pairs = width // LANES
    swap = lambda array: across(array, 1, ndp)
    line_gather = lambda array: lax.all_gather(array, "mp", axis=0, tiled=True)
    line_scatter = lambda array: lax.psum_scatter(array, "mp", scatter_dimension=0, tiled=True)
    x_own, dy_own = line_gather(tokens), line_gather(cotangent)
    rows = BlockGather(row_pack(core), swap(row_pack(1 - core)), ndp)
    columns = BlockGather(column_pack(core), swap(column_pack(1 - core)), ndp)
    rows.own_to(0)
    rows.fenced(deps=columns.held.values())
    rows.own_to(1)
    rows.fenced()
    rows.rest()
    x_own, *held = fence([x_own, columns.held[0], columns.held[1]], rows.blocks())
    columns.held = dict(enumerate(held))

    tables = rotary_tables(length)
    bias = jnp.concatenate(
        [
            rank(qkv_bias, 1, core, width).astype(F32).reshape(1, 3 * width),
            rank(up_bias[None, :], 1, core, hidden).astype(F32),
        ],
        axis=1,
    )
    gain, shift = norm_gain.astype(F32)[None, :], norm_bias.astype(F32)[None, :]
    x_other = swap(x_own)
    columns.own_to(0)
    common = (rows.blocks(), bias, gain, shift, tables, width, tile)
    first = project(0, x_own, *common, (), [columns.held[0]])
    (x_other,) = columns.fenced([x_other], [first[0]])
    columns.own_to(1)
    qkv, act, slope, normed = project(1, x_other, *common, first, [columns.held[0]])
    columns.fenced(deps=[qkv])
    columns.rest()
    mixed, lse = attend(qkv, length, block, [columns.held[0]])
    columns.fenced(deps=[mixed])
    other_sums, own_sums = branch_sums(mixed, act, columns.blocks(), tile, [])
    other_sums, dy_own = fence([other_sums, dy_own], [own_sums])
    theirs = swap(other_sums)
    dy_other = swap(dy_own)

    grads = (slope, columns.blocks(), width, tile)
    grad_a = grad_in(0, dy_own, *grads, (), [own_sums])
    theirs, dy_other = fence([theirs, dy_other], [grad_a[2]])
    total = added([own_sums, theirs])
    branches = line_scatter(total)
    gmixed, gpre, *grad_b = grad_in(1, dy_other, *grads, grad_a[:2], [total])
    column_grads = BlockScatter(
        weight_grads(me, [mixed, act], [dy_own, dy_other], ndp, [grad_b[0]], left=False), ndp
    )
    column_came = column_grads.send(0)
    gq, gk, gv, qkv_sums = attend_back(
        qkv, gmixed, mixed, lse, tables, length, block, [column_grads.held[0][0][0]]
    )

    def normed_half(half, deps):
        *other, own, sums = grad_normed_sums(
            half, (gq, gk, gv), gpre, x_own, x_other, rows.blocks(), tile, deps
        )
        return other, own, sums

    other_a, own_a, sums_a = normed_half(0, [column_grads.held[0][0][0]])
    c0, c1, *other_a = fence([*column_came, *other_a], [sums_a])
    column_came = [c0, c1]
    column_grads.arrive(0, column_came)
    column_grads.between()
    column_came = column_grads.send(chip_steps - 1)
    theirs_a = [swap(a) for a in other_a]
    up_grads = BlockScatter(
        weight_grads(
            me, [normed], [gpre], ndp, [sums_a, *column_grads.ready(chip_steps - 1)], left=True
        ),
        ndp,
    )
    c0, c1, branches, u0, u1, *theirs_a = fence(
        [*column_came, branches, *(up_grads.held[h][0][0] for h in range(2)), *theirs_a]
    )
    up_grads.held[0][0], up_grads.held[1][0] = [u0], [u1]
    column_grads.arrive(chip_steps - 1, [c0, c1])
    total_a = added([own_a, jnp.concatenate(theirs_a)])
    half_a = line_scatter(total_a)
    up_came = up_grads.send(0)
    column_theirs = swap(column_grads.last())
    other_b, own_b, sums_b = normed_half(1, [u0, total_a, column_grads.last()])
    *other_b, column_theirs = fence([*other_b, column_theirs], [sums_b])
    theirs_b = [swap(a) for a in other_b]
    qkv_sum = (
        qkv_sums.reshape(2, pairs, 8, LANES).sum(0)[:, :3, :].transpose(1, 0, 2).reshape(3 * width)
    )
    norm_sums = jnp.concatenate([sums_a[:2], sums_b[:2]], axis=1).reshape(2 * model)
    small = jnp.concatenate(
        [norm_sums, qkv_sum, grad_a[2][0] + grad_b[0][0], grad_a[3][0] + grad_b[1][0]]
    )
    bits = chip_bits(ndp)
    for bit in bits[:-2]:
        small = small + across(small, bit, ndp)
    small_came = across(small, bits[-2], ndp)
    qkv_grads = BlockScatter(
        weight_grads(me, [normed], [gq, gk, gv], ndp, [small, other_b[0]], left=True), ndp
    )
    u0, u1 = fence(up_came, [qkv_grads.held[0][0][0]])
    for _ in range(3):
        u0, u1 = fence([u0, u1])
    small_came, q0, q1, *theirs_b = fence(
        [small_came, *(qkv_grads.held[h][0][0] for h in range(2)), *theirs_b], [u0]
    )
    half_b = line_scatter(added([own_b, jnp.concatenate(theirs_b)]))
    up_grads.arrive(0, [u0, u1])
    up_grads.between()
    qkv_grads.held[0][0], qkv_grads.held[1][0] = [q0], [q1]
    up_came = up_grads.send(chip_steps - 1)
    qkv_came = qkv_grads.send(0)
    small = small + small_came
    small_came = across(small, bits[-1], ndp)
    u0, u1, q0, q1, small_came, column_theirs, branches, half_a = fence(
        [*up_came, *qkv_came, small_came, column_theirs, branches, half_a]
    )
    up_grads.arrive(chip_steps - 1, [u0, u1])
    up_theirs = swap(up_grads.last())
    qkv_grads.arrive(0, [q0, q1])
    qkv_grads.between()
    small = small + small_came
    q0, q1, small = fence([*qkv_grads.send(chip_steps - 1), small])
    qkv_grads.arrive(chip_steps - 1, [q0, q1])
    small_other = swap(small)
    qkv_theirs = swap(qkv_grads.last())
    norm_sums = small[: 2 * model] + small_other[: 2 * model]
    norm_sums = [norm_sums] + [
        lax.ppermute(norm_sums, "mp", [(i, i ^ j) for i in range(nmp)]) for j in range(1, nmp)
    ]
    while len(norm_sums) > 1:
        norm_sums = [a + b for a, b in zip(norm_sums[::2], norm_sums[1::2])]
    norm_sums = norm_sums[0]

    output = (
        tokens.astype(F32)
        + branches.astype(F32)
        + (dense_bias.astype(F32) + down_bias.astype(F32))[None, :]
    ).astype(BF16)

    def both(mine, theirs, axis):
        return jnp.where(
            core == 0,
            jnp.concatenate([mine, theirs], axis=axis),
            jnp.concatenate([theirs, mine], axis=axis),
        )

    mine, theirs = column_grads.finish(column_theirs)
    owned_dense = both(mine[:width], theirs[:width], 0)
    owned_down = both(mine[width:], theirs[width:], 0)
    owned_up = both(*up_grads.finish(up_theirs), 1)
    mine, theirs = qkv_grads.finish(qkv_theirs)
    owned_qkv = jnp.stack(
        [
            both(mine[:, c * width : (c + 1) * width], theirs[:, c * width : (c + 1) * width], 1)
            for c in range(3)
        ]
    )

    inner = 3 * width + hidden
    grad_out_bias = small[2 * model + inner :]
    here, there = (a[2 * model : 2 * model + inner] for a in (small, small_other))
    even, odd = jnp.where(core == 0, here, there), jnp.where(core == 0, there, here)
    grad_qkv_bias = jnp.concatenate(
        [a[: 3 * width].reshape(3, width) for a in (even, odd)], axis=1
    )
    grad_up_bias = jnp.concatenate([even[3 * width :], odd[3 * width :]])

    grad_tokens = norm_back(tokens, cotangent, gain, [half_a, half_b], [qkv_theirs, small_other])
    return (
        output,
        grad_tokens,
        norm_sums[:model],
        norm_sums[model:],
        owned_qkv,
        grad_qkv_bias,
        owned_dense,
        grad_out_bias,
        owned_up,
        grad_up_bias,
        owned_down,
        grad_out_bias,
    )


def solution(mesh):
    return jax.shard_map(
        functools.partial(on_device, ndp=mesh.shape["dp"], nmp=mesh.shape["mp"]),
        mesh=mesh,
        in_specs=(
            P(("dp", "mp"), None),
            P(),
            P(),
            P(None, "dp", "mp"),
            P(None, "mp"),
            P("mp", "dp"),
            P(),
            P("dp", "mp"),
            P("mp"),
            P("mp", "dp"),
            P(),
            P(("dp", "mp"), None),
        ),
        out_specs=(
            P(("dp", "mp"), None),
            P(("dp", "mp"), None),
            P(),
            P(),
            P(None, "dp", "mp"),
            P(None, "mp"),
            P("mp", "dp"),
            P(),
            P("dp", "mp"),
            P("mp"),
            P("mp", "dp"),
            P(),
        ),
        check_vma=False,
    )
```

time: 501 us -> 451 us (0.900)
  starting transfers between devices: 69.9 us -> 40 us
  local copies, waits for them, and re-layouts: 46 us -> 18.1 us
  between operations: 2.16 us -> 14.9 us
  Pallas kernels: 219 us -> 226 us
  waiting for transfers between devices: 98.2 us -> 92.6 us
    ppermute x16 -> x0, waiting for transfers between devices: 40.7 us -> none  [the longest x2 22.7 us: gather_far(): down = lax.ppermute(chunks[3], 'mp', [(1, 0), (2, 1)])]
    ppermute x16 -> x0, starting transfers between devices: 33.3 us -> none  [the longest x8 15.7 us: ring(): lax.ppermute(value, 'mp', [(i, (i + k) % parts) for i in range(parts)])]
    ppermute x46 -> x39, waiting for transfers between devices: 48.9 us -> 78.8 us  [across(): return lax.ppermute(value, 'dp', [(i, i ^ bit) for i in range(count)])]
    unnamed x162 -> x102, local copies, waits for them, and re-layouts: 38.2 us -> 12.5 us
    all_gather x0 -> x2, waiting for transfers between devices: none -> 12.1 us  [on_device(): line_gather = lambda array: lax.all_gather(array, 'mp', axis=0, tiled=True)]
    ppermute x3, waiting for transfers between devices: 8.65 us -> 0.9 us  [on_device(): lax.ppermute(norm_sums, 'mp', [(i, i ^ j) for i in range(nmp)])]
    pallas_call x35 -> x31, Pallas kernels: 219 us -> 226 us  [call(): pl.pallas_call(body, out_shape=out_shape, input_output_aliases=aliases, c...]
    ppermute x46 -> x39, starting transfers between devices: 32.2 us -> 36.2 us  [across(): return lax.ppermute(value, 'dp', [(i, i ^ bit) for i in range(count)])]
  transfers between devices with their start and end apart: 65 -> 47, of which waited for: 17 -> 13; matrix products, arithmetic and copies ran while one was open for 12% -> 11% of each run, Pallas kernels for 43% -> 50%
where the time goes in v8:
time: 451 us; the launch traced here: 445 us
  Pallas kernels  226 us (50%)
  waiting for transfers between devices  92.6 us (21%)
  other arithmetic  53.9 us (12%)
  starting transfers between devices  40 us (9%)
  local copies, waits for them, and re-layouts  18.1 us (4%)
  between operations  14.9 us (3%)
    pallas_call x31, Pallas kernels, call(): pl.pallas_call(body, out_shape=out_shape, input_output_aliases=aliases, c...  226 us
    ppermute x39, waiting for transfers between devices, across(): return lax.ppermute(value, 'dp', [(i, i ^ bit) for i in range(count)])  78.8 us
    ppermute x39, starting transfers between devices, across(): return lax.ppermute(value, 'dp', [(i, i ^ bit) for i in range(count)])  36.2 us
    convert_element_type x9, other arithmetic, added(): return sum((a.astype(F32) for a in addends)).astype(BF16)  26.8 us
    unnamed x102, local copies, waits for them, and re-layouts  12.5 us
    all_gather x2, waiting for transfers between devices, on_device(): line_gather = lambda array: lax.all_gather(array, 'mp', axis=0, tiled=True)  12.1 us
  transfers between devices with their start and end apart: 47, of which 13 were waited for; matrix products, arithmetic and copies ran while one was open for 11% of the time, Pallas kernels for 50%

profile of v8, /device:TPU:0, one launch (start us, length us, event | category | flops | bytes accessed | tf_op | source)
XLA Modules:
  0.0 445.0 jit_solution(2538491623387260749)
XLA Ops:
  8.0 1.3 dynamic-slice_bitcast_fusion.2
  10.1 2.6 collective-permute-start.2
  12.7 2.2 collective-permute-start.3
  16.0 1.2 collective-permute-done.refs_5_.refs_2_
  17.2 16.4 %collective-permute-done.2.refs_2_ = bf16[256,1792]{1,0:T(8,128)(2,1)S(1)} collective-permute-done((bf16[256,1792]{1,0:T(8,128)(2,1)S(1)}, bf16[256,1792]{1,0:T(8,128)(2,1)S(1)}, u32[]{:S(2)}, u32[]{:S(2)}) %collective-permute-start.2) | collective-permute-done | bytes 917536 | tf_op jit(solution)/shard_map/ppermute | solution.py:619
  34.6 1.2 collective-permute-done.3.refs_3_
  35.7 1.7 collective-permute-start.4
  37.5 1.5 collective-permute-start.5
  39.0 18.9 %collective-permute-done.4.refs_3_ = bf16[256,1792]{1,0:T(8,128)(2,1)S(1)} collective-permute-done((bf16[256,1792]{1,0:T(8,128)(2,1)}, bf16[256,1792]{1,0:T(8,128)(2,1)S(1)}, u32[]{:S(2)}, u32[]{:S(2)}) %collective-permute-start.4) | collective-permute-done | bytes 917536 | tf_op jit(solution)/shard_map/ppermute | solution.py:619
  57.8 1.2 collective-permute-done.5.refs_4_
  59.1 1.5 collective-permute-start.6
  60.6 1.1 collective-permute-start.7
  61.8 18.3 %collective-permute-done.6.refs_9_.refs_13_.refs_12_ = bf16[256,1792]{1,0:T(8,128)(2,1)S(1)} collective-permute-done((bf16[256,1792]{1,0:T(8,128)(2,1)}, bf16[256,1792]{1,0:T(8,128)(2,1)S(1)}, u32[]{:S(2)}, u32[]{:S(2)}) %collective-permute-start.6) | collective-permute-done | bytes 917536 | tf_op jit(solution)/shard_map/ppermute | solution.py:619
  81.0 12.1 %all-gather.3.cloned.1.call-done.refs_0_ = bf16[1024,2048]{1,0:T(8,128)(2,1)} async-done(((bf16[256,2048]{1,0:T(8,128)(2,1)}), bf16[1024,2048]{1,0:T(8,128)(2,1)}) %all-gather.3.cloned.1.call-update) | async-done | bytes 4194320 | tf_op jit(solution)/shard_map/all_gather | solution.py:752
  93.2 1.6 collective-permute-start.8
  94.8 1.5 collective-permute-start.9
  98.1 18.8 %project.2 = (bf16[2048,768]{1,0:T(8,128)(2,1)}, bf16[2048,1024]{1,0:T(8,128)(2,1)}, bf16[2048,1024]{1,0:T(8,128)(2,1)}, bf16[2048,2048]{1,0:T(8,128)(2,1)}) custom-call(bf16[1024,2048]{1,0:T(8,128)(2,1)} %get-tuple-element.148.refs_0_.refs_5_, f32[1,1792]{1,0:T(1,128)} %maximum_convert_fusion.refs_1_, f32[1,2048]{1,0:T(1,128)} %bitcast.56, ...), custom_call_target="tpu_custom_call" | custom-call | tf_op jit(solution)/shard_map/project/pallas_call | solution.py:41
  118.5 18.2 %project.3 = (bf16[2048,768]{1,0:T(8,128)(2,1)}, bf16[2048,1024]{1,0:T(8,128)(2,1)}, bf16[2048,1024]{1,0:T(8,128)(2,1)}, bf16[2048,2048]{1,0:T(8,128)(2,1)}) custom-call(bf16[1024,2048]{1,0:T(8,128)(2,1)} %get-tuple-element.150.refs_0_.refs_4_, ...), custom_call_target="tpu_custom_call", output_to_operand_aliasing={{0}: (15, {}), {1}: (16, {}), {2}: (17, {}), {3}: (18, {})} | custom-call | tf_op jit(solution)/shard_map/project/pallas_call | solution.py:41
  137.6 1.9 collective-permute-start.13
  139.4 1.4 collective-permute-start.14
  140.9 15.0 %attend.1 = (bf16[2048,256]{1,0:T(8,128)(2,1)}, f32[4,8,1024]{2,1,0:T(8,128)}) custom-call(bf16[2048,768]{1,0:T(8,128)(2,1)} %get-tuple-element.156.refs_6_.refs_0_.refs_1_.refs_2_, bf16[2048,768]{1,0:T(8,128)(2,1)} %get-tuple-element.156.refs_6_.refs_0_.refs_1_.refs_2_, bf16[2048,768]{1,0:T(8,128)(2,1)} %get-tuple-element.156.refs_6_.refs_0_.refs_1_.refs_2_, ...), custom_call_target="tpu_custom_call" | custom-call | tf_op jit(solution)/shard_map/attend/pallas_call | solution.py:41
  156.7 18.7 %branch_sums.1 = (bf16[1024,2048]{1,0:T(8,128)(2,1)}, bf16[1024,2048]{1,0:T(8,128)(2,1)}) custom-call(bf16[2048,256]{1,0:T(8,128)(2,1)} %get-tuple-element.161.refs_8_.refs_0_.refs_3_.refs_4_, bf16[2048,1024]{1,0:T(8,128)(2,1)} %get-tuple-element.162.refs_1_.refs_4_, bf16[1280,256]{1,0:T(8,128)(2,1)} %get-tuple-element.168.refs_2_, ...), custom_call_target="tpu_custom_call" | custom-call | tf_op jit(solution)/shard_map/branch_sums/pallas_call | solution.py:41
  176.0 11.8 %grad_in.2 = (bf16[2048,256]{1,0:T(8,128)(2,1)}, bf16[2048,1024]{1,0:T(8,128)(2,1)}, f32[8,1024]{1,0:T(8,128)}, f32[8,2048]{1,0:T(8,128)}) custom-call(bf16[1024,2048]{1,0:T(8,128)(2,1)} %get-tuple-element.179.refs_0_.refs_1_, bf16[2048,1024]{1,0:T(8,128)(2,1)} %get-tuple-element.180.refs_1_, bf16[1280,256]{1,0:T(8,128)(2,1)} %get-tuple-element.168.refs_2_, ...), custom_call_target="tpu_custom_call" | custom-call | tf_op jit(solution)/shard_map/grad_in/pallas_call | solution.py:41
  187.9 1.2 collective-permute-done.16.refs_1_
  189.0 7.7 %add_convert_fusion.refs_12_ = bf16[1024,2048]{1,0:T(8,128)(2,1)} fusion(bf16[1024,2048]{1,0:T(8,128)(2,1)} %get-tuple-element.185, bf16[1024,2048]{1,0:T(8,128)(2,1)} %get-tuple-element.177.refs_2_.refs_10_), kind=kLoop, calls=%fused_computation | loop fusion | flops 8388608 | bytes 12582912 | tf_op jit(solution)/shard_map/convert_element_type | solution.py:623
  198.0 12.1 %grad_in.3 = (bf16[2048,256]{1,0:T(8,128)(2,1)}, bf16[2048,1024]{1,0:T(8,128)(2,1)}, f32[8,1024]{1,0:T(8,128)}, f32[8,2048]{1,0:T(8,128)}) custom-call(bf16[1024,2048]{1,0:T(8,128)(2,1)} %get-tuple-element.182.refs_0_.refs_2_, bf16[2048,1024]{1,0:T(8,128)(2,1)} %get-tuple-element.180.refs_1_, ...), custom_call_target="tpu_custom_call", output_to_operand_aliasing={{0}: (10, {}), {1}: (11, {})} | custom-call | tf_op jit(solution)/shard_map/grad_in/pallas_call | solution.py:41
  210.1 19.5 %weight_grads.3 = (bf16[2,1280,256]{2,1,0:T(8,128)(2,1)}, bf16[2,1280,256]{2,1,0:T(8,128)(2,1)}, bf16[1,1280,256]{2,1,0:T(8,128)(2,1)}, bf16[1,1280,256]{2,1,0:T...) custom-call(s32[28]{0:T(128)} %pad_add_fusion.refs_0_, ...), custom_call_target="tpu_custom_call" | custom-call | tf_op jit(solution)/shard_map/weight_grads/pallas_call | solution.py:41
  230.7 25.2 %attend_back.1 = (bf16[2048,256]{1,0:T(8,128)(2,1)}, bf16[2048,256]{1,0:T(8,128)(2,1)}, bf16[2048,256]{1,0:T(8,128)(2,1)}, f32[4,8,128]{2,1,0:T(8,128)}) custom-call(bf16[2048,768]{1,0:T(8,128)(2,1)} %get-tuple-element.156.refs_6_.refs_0_.refs_1_.refs_2_, bf16[2048,768]{1,0:T(8,128)(2,1)} %get-tuple-element.156.refs_6_.refs_0_.refs_1_.refs_2_, ...), custom_call_target="tpu_custom_call" | custom-call | tf_op jit(solution)/shard_map/attend_back/pallas_call | solution.py:41
  255.9 31.0 %grad_normed_sums.2 = (bf16[512,1024]{1,0:T(8,128)(2,1)}, bf16[512,1024]{1,0:T(8,128)(2,1)}, bf16[1024,1024]{1,0:T(8,128)(2,1)}, f32[8,1024]{1,0:T(8,128)}) custom-call(bf16[2048,256]{1,0:T(8,128)(2,1)} %get-tuple-element.191.refs_0_.refs_2_, bf16[2048,256]{1,0:T(8,128)(2,1)} %get-tuple-element.192.refs_1_.refs_3_, ...), custom_call_target="tpu_custom_call" | custom-call | tf_op jit(solution)/shard_map/grad_normed_sums/pallas_call | solution.py:41
  286.9 1.1 copy-done.30
  288.0 2.1 add_convert_fusion.6.refs_4_
  290.1 1.7 collective-permute-start.19
  292.3 2.1 add_convert_fusion.5.refs_5_
  294.4 1.3 collective-permute-start.20
  295.7 16.5 %weight_grads.4 = (bf16[2,256,1024]{2,1,0:T(8,128)(2,1)}, bf16[2,256,1024]{2,1,0:T(8,128)(2,1)}, bf16[1,256,1024]{2,1,0:T(8,128)(2,1)}, bf16[1,256,1024]{2,1,0:T...) custom-call(s32[28]{0:T(128)} %pad_add_fusion.refs_0_, ...), custom_call_target="tpu_custom_call" | custom-call | tf_op jit(solution)/shard_map/weight_grads/pallas_call | solution.py:41
  313.0 4.5 %add_convert_fusion.2.refs_15_ = bf16[1024,1024]{1,0:T(8,128)(2,1)} fusion(bf16[1024,1024]{1,0:T(8,128)(2,1)} %get-tuple-element.209, bf16[512,1024]{1,0:T(8,128)(2,1)} %get-tuple-element.211, bf16[512,1024]{1,0:T(8,128)(2,1)} %get-tuple-element.210), kind=kLoop, calls=%fused_computation.2 | loop fusion | flops 7340032 | bytes 6291456 | tf_op jit(solution)/shard_map/convert_element_type | solution.py:623
  319.8 2.3 fusion.refs_16_
  324.1 20.5 %grad_normed_sums.3 = (bf16[512,1024]{1,0:T(8,128)(2,1)}, bf16[512,1024]{1,0:T(8,128)(2,1)}, bf16[1024,1024]{1,0:T(8,128)(2,1)}, f32[8,1024]{1,0:T(8,128)}) custom-call(bf16[2048,256]{1,0:T(8,128)(2,1)} %get-tuple-element.191.refs_0_.refs_2_, bf16[2048,256]{1,0:T(8,128)(2,1)} %get-tuple-element.192.refs_1_.refs_3_, ...), custom_call_target="tpu_custom_call" | custom-call | tf_op jit(solution)/shard_map/grad_normed_sums/pallas_call | solution.py:41
  345.4 1.7 collective-permute-start.28
  348.5 1.7 convert_add_fusion
  352.0 13.8 %weight_grads.5 = (bf16[2,256,768]{2,1,0:T(8,128)(2,1)}, bf16[2,256,768]{2,1,0:T(8,128)(2,1)}, bf16[1,256,768]{2,1,0:T(8,128)(2,1)}, bf16[1,256,768]{2,1,0:T(8,1...) custom-call(s32[28]{0:T(128)} %pad_add_fusion.refs_0_, ...), custom_call_target="tpu_custom_call" | custom-call | tf_op jit(solution)/shard_map/weight_grads/pallas_call | solution.py:41
  366.9 2.0 add_convert_fusion.9
  369.9 1.7 collective-permute-start.31
  371.6 1.4 collective-permute-start.32
  373.0 1.4 add_convert_fusion.8
  375.8 1.4 collective-permute-start.33
  377.2 4.5 %add_convert_fusion.1 = bf16[1024,1024]{1,0:T(8,128)(2,1)} fusion(bf16[1024,1024]{1,0:T(8,128)(2,1)} %get-tuple-element.240, bf16[512,1024]{1,0:T(8,128)(2,1)} %get-tuple-element.242, bf16[512,1024]{1,0:T(8,128)(2,1)} %get-tuple-element.241), kind=kLoop, calls=%fused_computation.1 | loop fusion | flops 7340032 | bytes 6291456 | tf_op jit(solution)/shard_map/convert_element_type | solution.py:623
  381.7 2.3 collective-permute-done.26.refs_0_
  384.0 16.8 %collective-permute-done.27.refs_1_ = bf16[1,256,1024]{2,1,0:T(8,128)(2,1)S(1)} collective-permute-done((bf16[1,256,1024]{2,1,0:T(8,128)(2,1)S(1)}, bf16[1,256,1024]{2,1,0:T(8,128)(2,1)S(1)}, u32[]{:S(2)}, u32[]{:S(2)}) %collective-permute-start.27) | collective-permute-done | bytes 524320 | tf_op jit(solution)/shard_map/ppermute | solution.py:619
  403.0 1.3 add_convert_fusion.12
  404.3 1.8 collective-permute-start.34
  406.1 1.2 add_convert_fusion.11
  407.3 1.5 collective-permute-start.35
  408.8 2.2 fusion.1
  411.7 1.6 maximum_select_fusion.1
  414.0 1.4 add_convert_fusion.3
  416.2 2.4 add_bitcast_fusion
  418.7 1.3 fusion.2
  420.5 1.4 add_bitcast_fusion.1
  422.3 3.3 collective-permute-start.38
  428.4 1.1 convert_element_type.240
  429.6 1.6 maximum_select_fusion
  431.9 1.3 pad_maximum_fusion
  433.2 4.6 %norm_back.1 = bf16[256,2048]{1,0:T(8,128)(2,1)} custom-call(bf16[256,2048]{1,0:T(8,128)(2,1)} %refs_0_.1, bf16[256,2048]{1,0:T(8,128)(2,1)} %refs_1_.1, f32[1,2048]{1,0:T(1,128)} %bitcast.58, bf16[256,1024]{1,0:T(8,128)(2,1)} %get-tuple-element.239.refs_3_, bf16[256,1024]{1,0:T(8,128)(2,1)} %reduce-scatter.8.cloned.1.call-done.refs_4_, ...), custom_call_target="tpu_custom_call" | custom-call | tf_op jit(solution)/shard_map/norm_back/pallas_call | solution.py:41
  (240 shorter events, 34.9 us)
Async XLA Ops:
  7.2 89.1 %copy-start = (bf16[3,512]{1,0:T(4,128)(2,1)S(1)}, bf16[3,512]{1,0:T(4,128)(2,1)}, u32[]{:S(2)}) copy-start(bf16[3,512]{1,0:T(4,128)(2,1)} %param.25) | copy-start | bytes 9220
  7.2 85.9 %all-gather.3.cloned.1.call-start = ((), (), s32[]{:S(2)}) async-start(), calls=%async_computation.3 | async-start | bytes 5242880 | tf_op jit(solution)/shard_map/all_gather | solution.py:752
  7.9 167.5 %all-gather.5.cloned.1.call-start = ((), (), s32[]{:S(2)}) async-start(), calls=%async_computation.4 | async-start | bytes 5242880 | tf_op jit(solution)/shard_map/all_gather | solution.py:752
  9.5 5.5 %copy-start.35 = (bf16[512,256]{1,0:T(8,128)(2,1)S(1)}, bf16[512,256]{1,0:T(8,128)(2,1)}, u32[]{:S(2)}) copy-start(bf16[512,256]{1,0:T(8,128)(2,1)} %param.26) | copy-start | bytes 786436
  9.5 3.2 collective-permute-start.1
  10.1 6.0 %copy-start.2 = (bf16[256,1792]{1,0:T(8,128)(2,1)}, bf16[256,1792]{1,0:T(8,128)(2,1)S(1)}, u32[]{:S(2)}) copy-start(bf16[256,1792]{1,0:T(8,128)(2,1)S(1)} %pad_maximum_fusion.1.refs_0_) | copy-start | bytes 2752516
  10.1 23.6 %collective-permute-start.2 = (bf16[256,1792]{1,0:T(8,128)(2,1)S(1)}, bf16[256,1792]{1,0:T(8,128)(2,1)S(1)}, u32[]{:S(2)}, u32[]{:S(2)}) collective-permute-start(bf16[256,1792]{1,0:T(8,128)(2,1)S(1)} %pad_maximum_fusion.1.refs_0_), channel_id=1, source_target_pairs={{0,8},{4,12},{8,0},{12,4},{16,24},{20,28},{24,16},{28,20},{1,9},{5... | collective-permute-start | bytes 2752520 | tf_op jit(solution)/shard_map/ppermute | solution.py:619
  12.7 20.9 %copy-start.3 = (bf16[256,1792]{1,0:T(8,128)(2,1)}, bf16[256,1792]{1,0:T(8,128)(2,1)S(1)}, u32[]{:S(2)}) copy-start(bf16[256,1792]{1,0:T(8,128)(2,1)S(1)} %collective-permute-done.1.refs_1_) | copy-start | bytes 2752516
  12.7 23.0 %collective-permute-start.3 = (bf16[256,1792]{1,0:T(8,128)(2,1)S(1)}, bf16[256,1792]{1,0:T(8,128)(2,1)}, u32[]{:S(2)}, u32[]{:S(2)}) collective-permute-start(bf16[256,1792]{1,0:T(8,128)(2,1)S(1)} %collective-permute-done.1.refs_1_), channel_id=1, source_target_pairs={{0,16},{4,20},{8,24},{12,28},{16,0},{20,4},{24,8},{28,12},{1,17},{... | collective-permute-start | bytes 2752520 | tf_op jit(solution)/shard_map/ppermute | solution.py:619
  15.1 2.2 collective-permute-start
  17.2 16.4 %copy-start.5 = (bf16[1280,256]{1,0:T(8,128)(2,1)}, bf16[1280,256]{1,0:T(8,128)(2,1)S(1)}, u32[]{:S(2)}) copy-start(bf16[1280,256]{1,0:T(8,128)(2,1)S(1)} %collective-permute-done.refs_5_.refs_2_) | copy-start | bytes 1966084
  35.7 22.1 %collective-permute-start.4 = (bf16[256,1792]{1,0:T(8,128)(2,1)}, bf16[256,1792]{1,0:T(8,128)(2,1)S(1)}, u32[]{:S(2)}, u32[]{:S(2)}) collective-permute-start(bf16[256,1792]{1,0:T(8,128)(2,1)} %get-tuple-element.137.refs_1_), channel_id=1, source_target_pairs={{0,8},{4,12},{8,0},{12,4},{16,24},{20,28},{24,16},{28,20},{1,9},{5... | collective-permute-start | bytes 2752520 | tf_op jit(solution)/shard_map/ppermute | solution.py:619
  37.5 21.6 %collective-permute-start.5 = (bf16[256,1792]{1,0:T(8,128)(2,1)}, bf16[256,1792]{1,0:T(8,128)(2,1)}, u32[]{:S(2)}, u32[]{:S(2)}) collective-permute-start(bf16[256,1792]{1,0:T(8,128)(2,1)} %get-tuple-element.136.refs_0_), channel_id=1, source_target_pairs={{0,16},{4,20},{8,24},{12,28},{16,0},{20,4},{24,8},{28,12},{1,17},{... | collective-permute-start | bytes 2752520 | tf_op jit(solution)/shard_map/ppermute | solution.py:619
  59.1 21.0 %collective-permute-start.6 = (bf16[256,1792]{1,0:T(8,128)(2,1)}, bf16[256,1792]{1,0:T(8,128)(2,1)S(1)}, u32[]{:S(2)}, u32[]{:S(2)}) collective-permute-start(bf16[256,1792]{1,0:T(8,128)(2,1)} %get-tuple-element.142.refs_5_.refs_9_.refs_8_), channel_id=1, source_target_pairs={{0,16},{4,20},{8,24},{12,28},{16,0},{20,4},{24,8},{28,12},{1,17},{... | collective-permute-start | bytes 2752520 | tf_op jit(solution)/shard_map/ppermute | solution.py:619
  60.6 20.4 %collective-permute-start.7 = (bf16[256,1792]{1,0:T(8,128)(2,1)}, bf16[256,1792]{1,0:T(8,128)(2,1)}, u32[]{:S(2)}, u32[]{:S(2)}) collective-permute-start(bf16[256,1792]{1,0:T(8,128)(2,1)} %get-tuple-element.145.refs_8_.refs_12_.refs_11_), channel_id=1, source_target_pairs={{0,8},{4,12},{8,0},{12,4},{16,24},{20,28},{24,16},{28,20},{1,9},{5... | collective-permute-start | bytes 2752520 | tf_op jit(solution)/shard_map/ppermute | solution.py:619
  61.7 250.6 %reduce-scatter.4.cloned.1.call-start = ((), (), s32[]{:S(2)}) async-start(), calls=%async_computation.5 | async-start | bytes 5242880 | tf_op jit(solution)/shard_map/reduce_scatter | solution.py:753
  80.1 13.0 %copy-start.8 = (bf16[256,1792]{1,0:T(8,128)(2,1)}, bf16[256,1792]{1,0:T(8,128)(2,1)S(1)}, u32[]{:S(2)}) copy-start(bf16[256,1792]{1,0:T(8,128)(2,1)S(1)} %collective-permute-done.6.refs_9_.refs_13_.refs_12_) | copy-start | bytes 2752516
  93.1 3.8 copy-start.44
  93.1 23.8 %collective-permute-start.10 = (bf16[1024,2048]{1,0:T(8,128)(2,1)}, bf16[1024,2048]{1,0:T(8,128)(2,1)}, u32[]{:S(2)}, u32[]{:S(2)}) collective-permute-start(bf16[1024,2048]{1,0:T(8,128)(2,1)} %get-tuple-element.148.refs_0_.refs_5_), channel_id=1, source_target_pairs={{0,4},{4,0},{8,12},{12,8},{16,20},{20,16},{24,28},{28,24},{1,5},{5... | collective-permute-start | bytes 12582920 | tf_op jit(solution)/shard_map/ppermute | solution.py:619
  93.2 23.7 %collective-permute-start.8 = (bf16[1280,256]{1,0:T(8,128)(2,1)}, bf16[1280,256]{1,0:T(8,128)(2,1)S(1)}, u32[]{:S(2)}, u32[]{:S(2)}) collective-permute-start(bf16[1280,256]{1,0:T(8,128)(2,1)} %get-tuple-element.146.refs_15_.refs_0_), channel_id=1, source_target_pairs={{0,8},{4,12},{8,0},{12,4},{16,24},{20,28},{24,16},{28,20},{1,9},{5... | collective-permute-start | bytes 1966088 | tf_op jit(solution)/shard_map/ppermute | solution.py:619
  94.8 22.2 %collective-permute-start.9 = (bf16[1280,256]{1,0:T(8,128)(2,1)}, bf16[1280,256]{1,0:T(8,128)(2,1)}, u32[]{:S(2)}, u32[]{:S(2)}) collective-permute-start(bf16[1280,256]{1,0:T(8,128)(2,1)} %get-tuple-element.147.refs_1_), channel_id=1, source_target_pairs={{0,16},{4,20},{8,24},{12,28},{16,0},{20,4},{24,8},{28,12},{1,17},{... | collective-permute-start | bytes 1966088 | tf_op jit(solution)/shard_map/ppermute | solution.py:619
  117.8 18.9 %collective-permute-start.11 = (bf16[1280,256]{1,0:T(8,128)(2,1)}, bf16[1280,256]{1,0:T(8,128)(2,1)S(1)}, u32[]{:S(2)}, u32[]{:S(2)}) collective-permute-start(bf16[1280,256]{1,0:T(8,128)(2,1)} %get-tuple-element.157.refs_1_), channel_id=1, source_target_pairs={{0,8},{4,12},{8,0},{12,4},{16,24},{20,28},{24,16},{28,20},{1,9},{5... | collective-permute-start | bytes 1966088 | tf_op jit(solution)/shard_map/ppermute | solution.py:619
  118.3 18.4 %collective-permute-start.12 = (bf16[1280,256]{1,0:T(8,128)(2,1)}, bf16[1280,256]{1,0:T(8,128)(2,1)}, u32[]{:S(2)}, u32[]{:S(2)}) collective-permute-start(bf16[1280,256]{1,0:T(8,128)(2,1)} %get-tuple-element.154.refs_19_.refs_0_), channel_id=1, source_target_pairs={{0,16},{4,20},{8,24},{12,28},{16,0},{20,4},{24,8},{28,12},{1,17},{... | collective-permute-start | bytes 1966088 | tf_op jit(solution)/shard_map/ppermute | solution.py:619
  137.6 18.3 %collective-permute-start.13 = (bf16[1280,256]{1,0:T(8,128)(2,1)}, bf16[1280,256]{1,0:T(8,128)(2,1)S(1)}, u32[]{:S(2)}, u32[]{:S(2)}) collective-permute-start(bf16[1280,256]{1,0:T(8,128)(2,1)} %get-tuple-element.164.refs_2_), channel_id=1, source_target_pairs={{0,16},{4,20},{8,24},{12,28},{16,0},{20,4},{24,8},{28,12},{1,17},{... | collective-permute-start | bytes 1966088 | tf_op jit(solution)/shard_map/ppermute | solution.py:619
  139.4 16.4 %collective-permute-start.14 = (bf16[1280,256]{1,0:T(8,128)(2,1)}, bf16[1280,256]{1,0:T(8,128)(2,1)}, u32[]{:S(2)}, u32[]{:S(2)}) collective-permute-start(bf16[1280,256]{1,0:T(8,128)(2,1)} %get-tuple-element.167.refs_5_), channel_id=1, source_target_pairs={{0,8},{4,12},{8,0},{12,4},{16,24},{20,28},{24,16},{28,20},{1,9},{5... | collective-permute-start | bytes 1966088 | tf_op jit(solution)/shard_map/ppermute | solution.py:619
  175.5 12.4 %collective-permute-start.15 = (bf16[1024,2048]{1,0:T(8,128)(2,1)}, bf16[1024,2048]{1,0:T(8,128)(2,1)}, u32[]{:S(2)}, u32[]{:S(2)}) collective-permute-start(bf16[1024,2048]{1,0:T(8,128)(2,1)} %get-tuple-element.178), channel_id=1, source_target_pairs={{0,4},{4,0},{8,12},{12,8},{16,20},{20,16},{24,28},{28,24},{1,5},{5... | collective-permute-start | bytes 12582920 | tf_op jit(solution)/shard_map/ppermute | solution.py:619
  175.5 13.5 %collective-permute-start.16 = (bf16[1024,2048]{1,0:T(8,128)(2,1)}, bf16[1024,2048]{1,0:T(8,128)(2,1)}, u32[]{:S(2)}, u32[]{:S(2)}) collective-permute-start(bf16[1024,2048]{1,0:T(8,128)(2,1)} %get-tuple-element.179.refs_0_.refs_1_), channel_id=1, source_target_pairs={{0,4},{4,0},{8,12},{12,8},{16,20},{20,16},{24,28},{28,24},{1,5},{5... | collective-permute-start | bytes 12582920 | tf_op jit(solution)/shard_map/ppermute | solution.py:619
  196.8 205.3 %reduce-scatter.6.cloned.1.call-start = ((), (), s32[]{:S(2)}) async-start(), calls=%async_computation.6 | async-start | bytes 2621440 | tf_op jit(solution)/shard_map/reduce_scatter | solution.py:753
  229.6 57.3 %collective-permute-start.17 = (bf16[2,1280,256]{2,1,0:T(8,128)(2,1)}, bf16[2,1280,256]{2,1,0:T(8,128)(2,1)}, u32[]{:S(2)}, u32[]{:S(2)}) collective-permute-start(bf16[2,1280,256]{2,1,0:T(8,128)(2,1)} %get-tuple-element.190.refs_9_.refs_14_), channel_id=1, source_target_pairs={{0,16},{4,20},{8,24},{12,28},{16,0},{20,4},{24,8},{28,12},{1,17},{... | collective-permute-start | bytes 3932168 | tf_op jit(solution)/shard_map/ppermute | solution.py:619
  230.3 56.5 %collective-permute-start.18 = (bf16[2,1280,256]{2,1,0:T(8,128)(2,1)}, bf16[2,1280,256]{2,1,0:T(8,128)(2,1)}, u32[]{:S(2)}, u32[]{:S(2)}) collective-permute-start(bf16[2,1280,256]{2,1,0:T(8,128)(2,1)} %get-tuple-element.196), channel_id=1, source_target_pairs={{0,8},{4,12},{8,0},{12,4},{16,24},{20,28},{24,16},{28,20},{1,9},{5... | collective-permute-start | bytes 3932168 | tf_op jit(solution)/shard_map/ppermute | solution.py:619
  286.9 5.4 %copy-start.29 = (bf16[1,1280,256]{2,1,0:T(8,128)(2,1)S(1)}, bf16[1,1280,256]{2,1,0:T(8,128)(2,1)}, u32[]{:S(2)}) copy-start(bf16[1,1280,256]{2,1,0:T(8,128)(2,1)} %get-tuple-element.200) | copy-start | bytes 1966084
  290.1 22.1 %collective-permute-start.19 = (bf16[1,1280,256]{2,1,0:T(8,128)(2,1)}, bf16[1,1280,256]{2,1,0:T(8,128)(2,1)}, u32[]{:S(2)}, u32[]{:S(2)}) collective-permute-start(bf16[1,1280,256]{2,1,0:T(8,128)(2,1)} %add_convert_fusion.6.refs_4_), channel_id=1, source_target_pairs={{0,8},{4,12},{8,0},{12,4},{16,24},{20,28},{24,16},{28,20},{1,9},{5... | collective-permute-start | bytes 1966088 | tf_op jit(solution)/shard_map/ppermute | solution.py:619
  291.8 20.5 %collective-permute-start.21 = (bf16[512,1024]{1,0:T(8,128)(2,1)}, bf16[512,1024]{1,0:T(8,128)(2,1)}, u32[]{:S(2)}, u32[]{:S(2)}) collective-permute-start(bf16[512,1024]{1,0:T(8,128)(2,1)} %get-tuple-element.205), channel_id=1, source_target_pairs={{0,4},{4,0},{8,12},{12,8},{16,20},{20,16},{24,28},{28,24},{1,5},{5... | collective-permute-start | bytes 3145736 | tf_op jit(solution)/shard_map/ppermute | solution.py:619
  291.8 20.5 %collective-permute-start.22 = (bf16[512,1024]{1,0:T(8,128)(2,1)}, bf16[512,1024]{1,0:T(8,128)(2,1)}, u32[]{:S(2)}, u32[]{:S(2)}) collective-permute-start(bf16[512,1024]{1,0:T(8,128)(2,1)} %get-tuple-element.206), channel_id=1, source_target_pairs={{0,4},{4,0},{8,12},{12,8},{16,20},{20,16},{24,28},{28,24},{1,5},{5... | collective-permute-start | bytes 3145736 | tf_op jit(solution)/shard_map/ppermute | solution.py:619
  294.4 17.8 %collective-permute-start.20 = (bf16[1,1280,256]{2,1,0:T(8,128)(2,1)}, bf16[1,1280,256]{2,1,0:T(8,128)(2,1)S(1)}, u32[]{:S(2)}, u32[]{:S(2)}) collective-permute-start(bf16[1,1280,256]{2,1,0:T(8,128)(2,1)} %add_convert_fusion.5.refs_5_), channel_id=1, source_target_pairs={{0,16},{4,20},{8,24},{12,28},{16,0},{20,4},{24,8},{28,12},{1,17},{... | collective-permute-start | bytes 1966088 | tf_op jit(solution)/shard_map/ppermute | solution.py:619
  317.6 115.6 %reduce-scatter.8.cloned.1.call-start = ((), (), s32[]{:S(2)}) async-start(), calls=%async_computation.7 | async-start | bytes 2621440 | tf_op jit(solution)/shard_map/reduce_scatter | solution.py:753
  322.1 25.0 %collective-permute-start.25 = (bf16[1280,256]{1,0:T(8,128)(2,1)}, bf16[1280,256]{1,0:T(8,128)(2,1)S(1)}, u32[]{:S(2)}, u32[]{:S(2)}) collective-permute-start(bf16[1280,256]{1,0:T(8,128)(2,1)} %fusion.refs_16_), channel_id=1, source_target_pairs={{0,4},{4,0},{8,12},{12,8},{16,20},{20,16},{24,28},{28,24},{1,5},{5... | collective-permute-start | bytes 1966088 | tf_op jit(solution)/shard_map/ppermute | solution.py:619
  323.0 42.8 %collective-permute-start.23 = (bf16[2,256,1024]{2,1,0:T(8,128)(2,1)}, bf16[2,256,1024]{2,1,0:T(8,128)(2,1)}, u32[]{:S(2)}, u32[]{:S(2)}) collective-permute-start(bf16[2,256,1024]{2,1,0:T(8,128)(2,1)} %get-tuple-element.207.refs_14_), channel_id=1, source_target_pairs={{0,16},{4,20},{8,24},{12,28},{16,0},{20,4},{24,8},{28,12},{1,17},{... | collective-permute-start | bytes 3145736 | tf_op jit(solution)/shard_map/ppermute | solution.py:619
  323.7 42.1 %collective-permute-start.24 = (bf16[2,256,1024]{2,1,0:T(8,128)(2,1)}, bf16[2,256,1024]{2,1,0:T(8,128)(2,1)}, u32[]{:S(2)}, u32[]{:S(2)}) collective-permute-start(bf16[2,256,1024]{2,1,0:T(8,128)(2,1)} %get-tuple-element.208), channel_id=1, source_target_pairs={{0,8},{4,12},{8,0},{12,4},{16,24},{20,28},{24,16},{28,20},{1,9},{5... | collective-permute-start | bytes 3145736 | tf_op jit(solution)/shard_map/ppermute | solution.py:619
  345.4 6.6 %copy-start.39 = (f32[7936]{0:T(1024)}, f32[7936]{0:T(1024)S(1)}, u32[]{:S(2)}) copy-start(f32[7936]{0:T(1024)S(1)} %pad_maximum_fusion.5.refs_5_) | copy-start | bytes 95236
  345.4 23.9 %collective-permute-start.28 = (f32[7936]{0:T(1024)S(1)}, f32[7936]{0:T(1024)S(1)}, u32[]{:S(2)}, u32[]{:S(2)}) collective-permute-start(f32[7936]{0:T(1024)S(1)} %pad_maximum_fusion.5.refs_5_), channel_id=1, source_target_pairs={{0,8},{4,12},{8,0},{12,4},{16,24},{20,28},{24,16},{28,20},{1,9},{5... | collective-permute-start | bytes 95240 | tf_op jit(solution)/shard_map/ppermute | solution.py:619
  348.0 21.3 %collective-permute-start.29 = (bf16[512,1024]{1,0:T(8,128)(2,1)}, bf16[512,1024]{1,0:T(8,128)(2,1)}, u32[]{:S(2)}, u32[]{:S(2)}) collective-permute-start(bf16[512,1024]{1,0:T(8,128)(2,1)} %get-tuple-element.220.refs_6_), channel_id=1, source_target_pairs={{0,4},{4,0},{8,12},{12,8},{16,20},{20,16},{24,28},{28,24},{1,5},{5... | collective-permute-start | bytes 3145736 | tf_op jit(solution)/shard_map/ppermute | solution.py:619
  348.0 21.3 %collective-permute-start.30 = (bf16[512,1024]{1,0:T(8,128)(2,1)}, bf16[512,1024]{1,0:T(8,128)(2,1)}, u32[]{:S(2)}, u32[]{:S(2)}) collective-permute-start(bf16[512,1024]{1,0:T(8,128)(2,1)} %get-tuple-element.232), channel_id=1, source_target_pairs={{0,4},{4,0},{8,12},{12,8},{16,20},{20,16},{24,28},{28,24},{1,5},{5... | collective-permute-start | bytes 3145736 | tf_op jit(solution)/shard_map/ppermute | solution.py:619
  368.9 15.1 %collective-permute-start.26 = (bf16[1,256,1024]{2,1,0:T(8,128)(2,1)}, bf16[1,256,1024]{2,1,0:T(8,128)(2,1)}, u32[]{:S(2)}, u32[]{:S(2)}) collective-permute-start(bf16[1,256,1024]{2,1,0:T(8,128)(2,1)} %add_convert_fusion.9), channel_id=1, source_target_pairs={{0,8},{4,12},{8,0},{12,4},{16,24},{20,28},{24,16},{28,20},{1,9},{5... | collective-permute-start | bytes 1572872 | tf_op jit(solution)/shard_map/ppermute | solution.py:619
  369.9 31.3 %collective-permute-start.31 = (bf16[2,256,768]{2,1,0:T(8,128)(2,1)}, bf16[2,256,768]{2,1,0:T(8,128)(2,1)S(1)}, u32[]{:S(2)}, u32[]{:S(2)}) collective-permute-start(bf16[2,256,768]{2,1,0:T(8,128)(2,1)} %get-tuple-element.233), channel_id=1, source_target_pairs={{0,16},{4,20},{8,24},{12,28},{16,0},{20,4},{24,8},{28,12},{1,17},{... | collective-permute-start | bytes 2359304 | tf_op jit(solution)/shard_map/ppermute | solution.py:619
  371.6 29.7 %collective-permute-start.32 = (bf16[2,256,768]{2,1,0:T(8,128)(2,1)}, bf16[2,256,768]{2,1,0:T(8,128)(2,1)S(1)}, u32[]{:S(2)}, u32[]{:S(2)}) collective-permute-start(bf16[2,256,768]{2,1,0:T(8,128)(2,1)} %get-tuple-element.234), channel_id=1, source_target_pairs={{0,8},{4,12},{8,0},{12,4},{16,24},{20,28},{24,16},{28,20},{1,9},{5... | collective-permute-start | bytes 2359304 | tf_op jit(solution)/shard_map/ppermute | solution.py:619
  374.4 26.5 %collective-permute-start.27 = (bf16[1,256,1024]{2,1,0:T(8,128)(2,1)S(1)}, bf16[1,256,1024]{2,1,0:T(8,128)(2,1)S(1)}, u32[]{:S(2)}, u32[]{:S(2)}) collective-permute-start(bf16[1,256,1024]{2,1,0:T(8,128)(2,1)S(1)} %add_convert_fusion.8), channel_id=1, source_target_pairs={{0,16},{4,20},{8,24},{12,28},{16,0},{20,4},{24,8},{28,12},{1,17},{... | collective-permute-start | bytes 1572872 | tf_op jit(solution)/shard_map/ppermute | solution.py:619
  375.8 25.4 %collective-permute-start.33 = (f32[7936]{0:T(1024)S(1)}, f32[7936]{0:T(1024)S(1)}, u32[]{:S(2)}, u32[]{:S(2)}) collective-permute-start(f32[7936]{0:T(1024)S(1)} %fusion.4), channel_id=1, source_target_pairs={{0,16},{4,20},{8,24},{12,28},{16,0},{20,4},{24,8},{28,12},{1,17},{... | collective-permute-start | bytes 95240 | tf_op jit(solution)/shard_map/ppermute | solution.py:619
  403.0 5.8 %copy-start.23 = (bf16[1,256,1024]{2,1,0:T(8,128)(2,1)S(1)}, bf16[1,256,1024]{2,1,0:T(8,128)(2,1)}, u32[]{:S(2)}) copy-start(bf16[1,256,1024]{2,1,0:T(8,128)(2,1)} %get-tuple-element.259) | copy-start | bytes 1572868
  403.0 5.8 %copy-start.33 = (bf16[1,256,1024]{2,1,0:T(8,128)(2,1)S(1)}, bf16[1,256,1024]{2,1,0:T(8,128)(2,1)}, u32[]{:S(2)}) copy-start(bf16[1,256,1024]{2,1,0:T(8,128)(2,1)} %get-tuple-element.258) | copy-start | bytes 1572868
  403.0 8.0 %copy-start.12 = (bf16[1280,256]{1,0:T(8,128)(2,1)S(1)}, bf16[1280,256]{1,0:T(8,128)(2,1)}, u32[]{:S(2)}) copy-start(bf16[1280,256]{1,0:T(8,128)(2,1)} %get-tuple-element.255) | copy-start | bytes 1966084
  404.3 14.3 %collective-permute-start.34 = (bf16[1,256,768]{2,1,0:T(8,128)(2,1)S(1)}, bf16[1,256,768]{2,1,0:T(8,128)(2,1)}, u32[]{:S(2)}, u32[]{:S(2)}) collective-permute-start(bf16[1,256,768]{2,1,0:T(8,128)(2,1)S(1)} %add_convert_fusion.12), channel_id=1, source_target_pairs={{0,8},{4,12},{8,0},{12,4},{16,24},{20,28},{24,16},{28,20},{1,9},{5... | collective-permute-start | bytes 1179656 | tf_op jit(solution)/shard_map/ppermute | solution.py:619
  407.3 11.4 %collective-permute-start.35 = (bf16[1,256,768]{2,1,0:T(8,128)(2,1)S(1)}, bf16[1,256,768]{2,1,0:T(8,128)(2,1)}, u32[]{:S(2)}, u32[]{:S(2)}) collective-permute-start(bf16[1,256,768]{2,1,0:T(8,128)(2,1)S(1)} %add_convert_fusion.11), channel_id=1, source_target_pairs={{0,16},{4,20},{8,24},{12,28},{16,0},{20,4},{24,8},{28,12},{1,17},{... | collective-permute-start | bytes 1179656 | tf_op jit(solution)/shard_map/ppermute | solution.py:619
  411.7 16.7 %collective-permute-start.41 = (bf16[256,1024]{1,0:T(8,128)(2,1)}, bf16[256,1024]{1,0:T(8,128)(2,1)}, u32[]{:S(2)}, u32[]{:S(2)}) collective-permute-start(bf16[256,1024]{1,0:T(8,128)(2,1)} %fusion.1), channel_id=1, source_target_pairs={{0,4},{4,0},{8,12},{12,8},{16,20},{20,16},{24,28},{28,24},{1,5},{5... | collective-permute-start | bytes 1572872 | tf_op jit(solution)/shard_map/ppermute | solution.py:619
  415.4 3.3 copy-start.18
  420.0 11.2 %collective-permute-start.36 = (bf16[256,768]{1,0:T(8,128)(2,1)S(1)}, bf16[256,768]{1,0:T(8,128)(2,1)S(1)}, u32[]{:S(2)}, u32[]{:S(2)}) collective-permute-start(bf16[256,768]{1,0:T(8,128)(2,1)S(1)} %fusion.2), channel_id=1, source_target_pairs={{0,4},{4,0},{8,12},{12,8},{16,20},{20,16},{24,28},{28,24},{1,5},{5... | collective-permute-start | bytes 1179656 | tf_op jit(solution)/shard_map/ppermute | solution.py:619
  420.0 2.0 collective-permute-start.37
  421.9 7.6 %copy-start.16 = (f32[256,1024]{1,0:T(8,128)S(1)}, f32[256,1024]{1,0:T(8,128)}, u32[]{:S(2)}) copy-start(f32[256,1024]{1,0:T(8,128)} %add_bitcast_fusion) | copy-start | bytes 3145732
  422.0 15.7 %copy-start.41 = (f32[2048]{0:T(1024)}, f32[2048]{0:T(1024)S(1)}, u32[]{:S(2)}) copy-start(f32[2048]{0:T(1024)S(1)} %slice.214) | copy-start | bytes 24580
  422.0 9.1 %copy-start.40 = (f32[7936]{0:T(1024)}, f32[7936]{0:T(1024)S(1)}, u32[]{:S(2)}) copy-start(f32[7936]{0:T(1024)S(1)} %collective-permute-done.37.refs_6_) | copy-start | bytes 95236
  422.1 4.8 %collective-permute-start.39 = (f32[4096]{0:T(1024)S(1)}, f32[4096]{0:T(1024)S(1)}, u32[]{:S(2)}, u32[]{:S(2)}) collective-permute-start(f32[4096]{0:T(1024)S(1)} %slice_add_fusion), channel_id=1, source_target_pairs={{0,2},{1,3},{2,0},{3,1},{4,6},{5,7},{6,4},{7,5},{8,10},{9,11},{10,... | collective-permute-start | bytes 49160 | tf_op jit(solution)/shard_map/ppermute | solution.py:877
  422.2 5.5 %collective-permute-start.40 = (f32[4096]{0:T(1024)S(1)}, f32[4096]{0:T(1024)S(1)}, u32[]{:S(2)}, u32[]{:S(2)}) collective-permute-start(f32[4096]{0:T(1024)S(1)} %slice_add_fusion), channel_id=1, source_target_pairs={{0,3},{1,2},{2,1},{3,0},{4,7},{5,6},{6,5},{7,4},{8,11},{9,10},{10,... | collective-permute-start | bytes 49160 | tf_op jit(solution)/shard_map/ppermute | solution.py:877
  422.3 5.5 %collective-permute-start.38 = (f32[4096]{0:T(1024)S(1)}, f32[4096]{0:T(1024)S(1)}, u32[]{:S(2)}, u32[]{:S(2)}) collective-permute-start(f32[4096]{0:T(1024)S(1)} %slice_add_fusion), channel_id=1, source_target_pairs={{0,1},{1,0},{2,3},{3,2},{4,5},{5,4},{6,7},{7,6},{8,9},{9,8},{10,11... | collective-permute-start | bytes 49160 | tf_op jit(solution)/shard_map/ppermute | solution.py:877
  433.2 5.2 %copy-start.1 = (bf16[3,512]{1,0:T(4,128)(2,1)S(1)}, bf16[3,512]{1,0:T(4,128)(2,1)}, u32[]{:S(2)}) copy-start(bf16[3,512]{1,0:T(4,128)(2,1)} %param.25) | copy-start | bytes 9220
  (33 other events, 49.7 us)
Sparse Core Ops, SparseCore 0:
  9.6 83.4 all-gather.2
  94.7 79.2 all-gather.4
  196.9 73.7 reduce-scatter.3
  317.7 40.5 reduce-scatter.5
  381.9 40.3 reduce-scatter.7
